TPU v7x, 32 devices: a whole 2x2x4 slice. The times are simulated.
32 devices in a mesh: loc: 32 (over z, y, x, core).
Axes of the slice: x: 2, y: 2, z: 4, core: 2. Of those that a mesh axis runs over, the one named last changes fastest.
Arguments:
- points: float32 [3, 32768], P(None, 'loc'), may hold values from -1 to 1, as said below
- right_sides: float32 [16, 32768], P(None, 'loc')
- skeleton: int32 [4, 8192], P(None, 'loc'), may hold values from 0 to 1023, as said below
- lengthscale: float32 [1], replicated, may hold values from 0.10606602 to 0.26516503
- far_length: float32 [1], replicated, may hold values from 0.4 to 1
- signal: float32 [1], replicated, may hold values from 0.00024414062 to 0.0009765625
- noise_var: float32 [1], replicated, may hold values from 0.5 to 2
Outputs:
- solution: float32 [16, 32768], P(None, 'loc')
- residual: float32 [16, 32768], P(None, 'loc')
- slope_image: float32 [16, 32768], P(None, 'loc')
- trace_terms: float32 [16], replicated
Inputs may be any that keep to these rules, and one draw needn't show every extreme that they name: `points`: unit vectors. `skeleton`: each leaf's 256 entries of a level rise, the j-th in the range j*1024/256 to (j+1)*1024/256 - 1.
All inputs are finite; a program needn't handle non-finite values.
Results may differ from a plain program's by a relative error of at most 0.002.
Values may be sent and summed in bfloat16 or wider, within the bound.
No kernel may reach another device: no remote copies, remote signals or barrier semaphores. Data moves between devices by JAX's collectives and lax.ppermute only.
A program may use at most 64 MiB of HBM per device.

v0:
```python
import jax
import jax.numpy as jnp
from jax import lax
from jax.sharding import PartitionSpec as P

ITERS = 2


root_three = 1.7320508075688772
tile_rows = 512


def extended(shard, sides, width):
    for axis, dim in sides:
        count, length = (lax.axis_size(axis), shard.shape[dim])
        up = [(i, (i + 1) % count) for i in range(count - 1)]
        down = [(j, i) for i, j in up]
        last = lax.slice_in_dim(shard, length - width, length, axis=dim)
        leading = lax.slice_in_dim(shard, 0, width, axis=dim)
        before = lax.ppermute(last, axis, up)
        after = lax.ppermute(leading, axis, down)
        shard = jnp.concatenate([before, shard, after], axis=dim)
    return shard


def partner(value, axis, bit):
    mask = 2**bit
    pairs = [(source, source ^ mask) for source in range(lax.axis_size(axis))]
    return lax.ppermute(value, axis, pairs)


def kernel_pair(row_pts, col_pts, length):
    diff_a = row_pts[0][:, None] - col_pts[0][None, :]
    diff_b = row_pts[1][:, None] - col_pts[1][None, :]
    diff_c = row_pts[2][:, None] - col_pts[2][None, :]
    radius = jnp.sqrt(diff_a * diff_a + diff_b * diff_b + diff_c * diff_c)
    scaled = root_three * radius / length
    decay = jnp.exp(-scaled)
    return ((1.0 + scaled) * decay, scaled * scaled * decay)


def contract_rows(vectors, matrix):
    return lax.dot_general(
        vectors, matrix, (((1,), (1,)), ((), ())), preferred_element_type=jnp.float32
    )


def make_block(row_pts, col_pts, length, fwd_vecs):
    row_count = row_pts.shape[1]
    tile_size = min(tile_rows, row_count)
    tile_count = row_count // tile_size
    tile_pts_all = row_pts.reshape(3, tile_count, tile_size).transpose(1, 0, 2)
    back_init = jnp.zeros((1, 1), jnp.float32)

    def one_tile(back_sum, inputs):
        tile_pts, back_tile = inputs
        kernel_vals, slope_vals = kernel_pair(tile_pts, col_pts, length)
        slope_half = slope_vals.astype(jnp.bfloat16)
        forward = contract_rows(fwd_vecs, slope_half)
        return (back_sum, (kernel_vals.astype(jnp.bfloat16), forward))

    backward, outputs = lax.scan(one_tile, back_init, (tile_pts_all, tile_pts_all))
    kernel_block = outputs[0].reshape(row_count, col_pts.shape[1])
    forward = outputs[1].transpose(1, 0, 2).reshape(fwd_vecs.shape[0], row_count)
    return (kernel_block, forward, backward)


def shards(points, right_sides, skeleton, lengthscale, far_length, signal, noise_var):
    length = lengthscale[0]
    far_len = far_length[0]
    signal_var = signal[0]
    nugget = noise_var[0]
    probe_count, row_count = right_sides.shape
    level_count = skeleton.shape[0]
    rank_size = skeleton.shape[1]
    point_total = row_count * lax.axis_size("loc")
    far_scale = 1.0 / (rank_size * rank_size * level_count)
    wide_pts = extended(points, (("loc", 1),), row_count)
    near_cols = [wide_pts[:, :row_count], points, wide_pts[:, 2 * row_count :]]
    own_skel = [jnp.take(points, skeleton[level_id], axis=1) for level_id in range(level_count)]
    couplings = []
    for level_id in range(level_count):
        partner_skel = partner(own_skel[level_id], "loc", level_id + 1)
        couplings.append(kernel_pair(partner_skel, own_skel[level_id], far_len)[0])

    def side_vectors(vec_half):
        widened = extended(vec_half, (("loc", 1),), row_count)
        return [widened[:, :row_count], vec_half, widened[:, 2 * row_count :]]

    def far_part(vec_half, bases):
        result = jnp.zeros(vec_half.shape, jnp.float32)
        for level_id in range(level_count):
            coefs_own = contract_rows(vec_half, bases[level_id])
            remote_coefs = partner(coefs_own, "loc", level_id + 1)
            mixed_half = jnp.dot(
                remote_coefs, couplings[level_id], precision=lax.Precision.HIGHEST
            ).astype(jnp.bfloat16)
            result = result + jnp.dot(
                mixed_half, bases[level_id], preferred_element_type=jnp.float32
            )
        return far_scale * result

    bases = [
        kernel_pair(own_skel[level_id], points, far_len)[0].astype(jnp.bfloat16)
        for level_id in range(level_count)
    ]
    vec_half = jnp.concatenate([right_sides, jnp.ones((1, row_count), jnp.float32)], axis=0).astype(
        jnp.bfloat16
    )
    side_list = side_vectors(vec_half)
    blocks = []
    kernel_part = far_part(vec_half, bases)
    slope_sum = jnp.zeros((probe_count, row_count), jnp.float32)
    for col_id in range(3):
        kernel_block, forward, backward = make_block(
            points, near_cols[col_id], length, side_list[col_id][:probe_count]
        )
        blocks.append(kernel_block)
        kernel_part = kernel_part + contract_rows(side_list[col_id], kernel_block)
        slope_sum = slope_sum + forward
    row_sums = kernel_part[probe_count:]
    slope_image = signal_var * slope_sum
    first_image = nugget * right_sides + signal_var * (
        kernel_part[:probe_count] + row_sums * right_sides
    )
    solution = jnp.zeros_like(right_sides)
    residual = right_sides
    norm_now, curvature = lax.psum(
        (jnp.sum(residual * residual, axis=1), jnp.sum(residual * first_image, axis=1)), "loc"
    )
    alpha = norm_now / curvature
    direction = residual
    along = first_image
    trace_terms = jnp.zeros((probe_count,), jnp.float32)
    for sweep in range(ITERS):
        solution = solution + alpha[:, None] * direction
        residual = residual - alpha[:, None] * along
        if sweep + 1 < ITERS:
            half_now = residual.astype(jnp.bfloat16)
            sides_now = side_vectors(half_now)
            kernel_now = far_part(half_now, bases)
            for operate_col_id in range(len(blocks)):
                kernel_now = kernel_now + contract_rows(
                    sides_now[operate_col_id], blocks[operate_col_id]
                )
            image = nugget * residual + signal_var * (kernel_now + row_sums * residual)
            norm_next, curvature, held_sum, fresh_sum, older_sum = lax.psum(
                (
                    jnp.sum(residual * residual, axis=1),
                    jnp.sum(residual * image, axis=1),
                    jnp.sum(solution * slope_image, axis=1),
                    jnp.sum(residual * slope_image, axis=1),
                    jnp.sum(direction * slope_image, axis=1),
                ),
                "loc",
            )
            ratio = norm_next / norm_now
            alpha = norm_next / (curvature - ratio * norm_next / alpha)
            direction = residual + ratio[:, None] * direction
            along = image + ratio[:, None] * along
            norm_now = norm_next
            trace_terms = (held_sum + alpha * (fresh_sum + ratio * older_sum)) / point_total
    return (solution, residual, slope_image, trace_terms)


def solution(mesh):
    placed = (P(None, "loc"), P(None, "loc"), P(None, "loc"), P(), P(), P(), P())
    return jax.shard_map(
        shards,
        mesh=mesh,
        in_specs=placed,
        out_specs=(P(None, "loc"), P(None, "loc"), P(None, "loc"), P()),
        check_vma=False,
    )
```

profile of v0, /device:TPU:0, one launch (start us, length us, event | category | flops | bytes accessed | tf_op | source)
XLA Modules:
  0.0 202.2 jit_solution(7344995155433927192)
XLA Ops:
  0.6 2.5 %collective-permute-start.9 = (f32[3,1024]{1,0:T(4,128)}, f32[3,1024]{1,0:T(4,128)S(1)}, u32[]{:S(2)}, u32[]{:S(2)}) collective-permute-start(f32[3,1024]{1,0:T(4,128)} %param.15), channel_id=1, source_target_pairs={{0,1},{1,2},{2,3},{3,4},{4,5},{5,6},{6,7},{7,8},{8,9},{9,10},{10,1... | collective-permute-start | bytes 36872 | tf_op jit(solution)/shard_map/ppermute | solution.py:20
  5.8 3.7 %collective-permute-start.7 = (f32[3,256]{0,1:T(8,128)S(1)}, f32[3,256]{0,1:T(8,128)S(1)}, u32[]{:S(2)}, u32[]{:S(2)}) collective-permute-start(f32[3,256]{0,1:T(8,128)S(1)} %select_bitcast_fusion), channel_id=1, source_target_pairs={{0,16},{1,17},{2,18},{3,19},{4,20},{5,21},{6,22},{7,23},{8,24},{9,... | collective-permute-start | bytes 9224 | tf_op jit(solution)/shard_map/ppermute | solution.py:29
  19.7 12.4 %while.37 = (s32[]{:T(128)}, bf16[2,512,1024]{2,1,0:T(8,128)(2,1)S(1)}, f32[2,16,512]{2,1,0:T(8,128)S(1)}, f32[2,3,512]{2,1,0:T(4,128)}, f32[3,1024]{1,0:T(4,128...) while((s32[]{:T(128)}, ...), condition=%wide.region_5.7_spmd, body=%wide.region_4.6_spmd.sunk | while | flops 31457284 | bytes 1188001 | solution.py:62
  21.4 2.2 %fusion.135 = bf16[2,512,1024]{2,1,0:T(8,128)(2,1)S(1)} fusion(bf16[2,512,1024]{2,1,0:T(8,128)(2,1)S(1)} %get-tuple-element.415, s32[]{:T(128)} %get-tuple-element.414, f32[]{:T(128)} %get-tuple-element.430, f32[1024]{0:T(1024)S(1)} %bitcast.195, f32[512]{0:T(512)S(1)} %bitcast.215, f32[1024]{0:T(1024)S(1)} %bitcast.197, f32[512]{0:T(512)S(1)} %bitcast.213, ...), kind=kLoop, calls=%fused_computation.24.clone.1 | loop fusion | flops 7340032 | bytes 1067016 | tf_op jit(solution)/shard_map/while/body/jit(dynamic_update_index_in_dim)/dynamic_update_slice | solution.py:62
  23.6 2.3 %fusion.136 = f32[2,16,512]{2,1,0:T(8,128)S(1)} fusion(f32[2,16,512]{2,1,0:T(8,128)S(1)} %get-tuple-element.416, s32[]{:T(128)} %get-tuple-element.414, bf16[16,1024]{1,0:T(8,128)(2,1)S(1)} %get-tuple-element.431, f32[]{:T(128)} %get-tuple-element.430, f32[1024]{0:T(1024)S(1)} %bitcast.196, f32[512]{0:T(512)S(1)} %bitcast.216, ...), kind=kOutput, calls=%fused_computation.23.clone.1 | convolution fusion | flops 24117248 | bytes 83976 | tf_op jit(solution)/shard_map/while/body/eval_jaxpr/dot_general | solution.py:43
  27.6 2.2 %fusion.135 = bf16[2,512,1024]{2,1,0:T(8,128)(2,1)S(1)} fusion(bf16[2,512,1024]{2,1,0:T(8,128)(2,1)S(1)} %get-tuple-element.415, s32[]{:T(128)} %get-tuple-element.414, f32[]{:T(128)} %get-tuple-element.430, f32[1024]{0:T(1024)S(1)} %bitcast.195, f32[512]{0:T(512)S(1)} %bitcast.215, f32[1024]{0:T(1024)S(1)} %bitcast.197, f32[512]{0:T(512)S(1)} %bitcast.213, ...), kind=kLoop, calls=%fused_computation.24.clone.1 | loop fusion | flops 7340032 | bytes 1067016 | tf_op jit(solution)/shard_map/while/body/jit(dynamic_update_index_in_dim)/dynamic_update_slice | solution.py:62
  29.8 2.3 %fusion.136 = f32[2,16,512]{2,1,0:T(8,128)S(1)} fusion(f32[2,16,512]{2,1,0:T(8,128)S(1)} %get-tuple-element.416, s32[]{:T(128)} %get-tuple-element.414, bf16[16,1024]{1,0:T(8,128)(2,1)S(1)} %get-tuple-element.431, f32[]{:T(128)} %get-tuple-element.430, f32[1024]{0:T(1024)S(1)} %bitcast.196, f32[512]{0:T(512)S(1)} %bitcast.216, ...), kind=kOutput, calls=%fused_computation.23.clone.1 | convolution fusion | flops 24117248 | bytes 83976 | tf_op jit(solution)/shard_map/while/body/eval_jaxpr/dot_general | solution.py:43
  45.2 4.2 %collective-permute-start = (f32[17,256]{1,0:T(8,128)}, f32[17,256]{1,0:T(8,128)S(1)}, u32[]{:S(2)}, u32[]{:S(2)}) collective-permute-start(f32[17,256]{1,0:T(8,128)} %fusion.47), channel_id=1, source_target_pairs={{0,2},{1,3},{2,0},{3,1},{4,6},{5,7},{6,4},{7,5},{8,10},{9,11},{10,... | collective-permute-start | bytes 52232 | tf_op jit(solution)/shard_map/ppermute | solution.py:29
  51.5 2.8 %collective-permute-start.2 = (f32[17,256]{1,0:T(8,128)}, f32[17,256]{1,0:T(8,128)S(1)}, u32[]{:S(2)}, u32[]{:S(2)}) collective-permute-start(f32[17,256]{1,0:T(8,128)} %fusion.45), channel_id=1, source_target_pairs={{0,4},{1,5},{2,6},{3,7},{4,0},{5,1},{6,2},{7,3},{8,12},{9,13},{10,... | collective-permute-start | bytes 52232 | tf_op jit(solution)/shard_map/ppermute | solution.py:29
  56.3 2.9 %collective-permute-start.4 = (f32[17,256]{1,0:T(8,128)S(1)}, f32[17,256]{1,0:T(8,128)S(1)}, u32[]{:S(2)}, u32[]{:S(2)}) collective-permute-start(f32[17,256]{1,0:T(8,128)S(1)} %copy-done.6), channel_id=1, source_target_pairs={{0,8},{1,9},{2,10},{3,11},{4,12},{5,13},{6,14},{7,15},{8,0},{9,1},... | collective-permute-start | bytes 52232 | tf_op jit(solution)/shard_map/ppermute | solution.py:29
  67.5 10.7 %while.36 = (s32[]{:T(128)}, bf16[2,512,1024]{2,1,0:T(8,128)(2,1)S(1)}, f32[2,16,512]{2,1,0:T(8,128)S(1)}, f32[2,3,512]{2,1,0:T(4,128)}, f32[3,1024]{1,0:T(4,128...) while((s32[]{:T(128)}, ...), condition=%wide.region_3.5_spmd, body=%wide.region_2.4_spmd.sunk | while | flops 31457284 | bytes 1188001 | solution.py:62
  68.3 2.2 %fusion.131 = bf16[2,512,1024]{2,1,0:T(8,128)(2,1)S(1)} fusion(bf16[2,512,1024]{2,1,0:T(8,128)(2,1)S(1)} %get-tuple-element.448, s32[]{:T(128)} %get-tuple-element.447, f32[]{:T(128)} %get-tuple-element.463, f32[1024]{0:T(1024)S(1)} %bitcast.201, f32[512]{0:T(512)S(1)} %bitcast.221, f32[1024]{0:T(1024)S(1)} %bitcast.203, f32[512]{0:T(512)S(1)} %bitcast.219, ...), kind=kLoop, calls=%fused_computation.8.clone.1 | loop fusion | flops 7340032 | bytes 1067016 | tf_op jit(solution)/shard_map/while/body/jit(dynamic_update_index_in_dim)/dynamic_update_slice | solution.py:62
  70.5 2.3 %fusion.132 = f32[2,16,512]{2,1,0:T(8,128)S(1)} fusion(f32[2,16,512]{2,1,0:T(8,128)S(1)} %get-tuple-element.449, s32[]{:T(128)} %get-tuple-element.447, bf16[16,1024]{1,0:T(8,128)(2,1)S(1)} %get-tuple-element.464, f32[]{:T(128)} %get-tuple-element.463, f32[1024]{0:T(1024)S(1)} %bitcast.202, f32[512]{0:T(512)S(1)} %bitcast.222, ...), kind=kOutput, calls=%fused_computation.7.clone.1 | convolution fusion | flops 24117248 | bytes 83976 | tf_op jit(solution)/shard_map/while/body/eval_jaxpr/dot_general | solution.py:43
  73.6 2.2 %fusion.131 = bf16[2,512,1024]{2,1,0:T(8,128)(2,1)S(1)} fusion(bf16[2,512,1024]{2,1,0:T(8,128)(2,1)S(1)} %get-tuple-element.448, s32[]{:T(128)} %get-tuple-element.447, f32[]{:T(128)} %get-tuple-element.463, f32[1024]{0:T(1024)S(1)} %bitcast.201, f32[512]{0:T(512)S(1)} %bitcast.221, f32[1024]{0:T(1024)S(1)} %bitcast.203, f32[512]{0:T(512)S(1)} %bitcast.219, ...), kind=kLoop, calls=%fused_computation.8.clone.1 | loop fusion | flops 7340032 | bytes 1067016 | tf_op jit(solution)/shard_map/while/body/jit(dynamic_update_index_in_dim)/dynamic_update_slice | solution.py:62
  75.8 2.3 %fusion.132 = f32[2,16,512]{2,1,0:T(8,128)S(1)} fusion(f32[2,16,512]{2,1,0:T(8,128)S(1)} %get-tuple-element.449, s32[]{:T(128)} %get-tuple-element.447, bf16[16,1024]{1,0:T(8,128)(2,1)S(1)} %get-tuple-element.464, f32[]{:T(128)} %get-tuple-element.463, f32[1024]{0:T(1024)S(1)} %bitcast.202, f32[512]{0:T(512)S(1)} %bitcast.222, ...), kind=kOutput, calls=%fused_computation.7.clone.1 | convolution fusion | flops 24117248 | bytes 83976 | tf_op jit(solution)/shard_map/while/body/eval_jaxpr/dot_general | solution.py:43
  79.7 10.7 %while.38 = (s32[]{:T(128)}, bf16[2,512,1024]{2,1,0:T(8,128)(2,1)S(1)}, f32[2,16,512]{2,1,0:T(8,128)S(1)}, f32[2,3,512]{2,1,0:T(4,128)}, f32[3,1024]{1,0:T(4,128...) while((s32[]{:T(128)}, ...), condition=%wide.region_7.9_spmd, body=%wide.region_6.8_spmd.sunk | while | flops 31457284 | bytes 1188001 | solution.py:62
  82.8 2.3 %fusion.140 = f32[2,16,512]{2,1,0:T(8,128)S(1)} fusion(f32[2,16,512]{2,1,0:T(8,128)S(1)} %get-tuple-element.482, s32[]{:T(128)} %get-tuple-element.480, bf16[16,1024]{1,0:T(8,128)(2,1)S(1)} %get-tuple-element.497, f32[]{:T(128)} %get-tuple-element.496, f32[1024]{0:T(1024)S(1)} %bitcast.208, f32[512]{0:T(512)S(1)} %bitcast.228, ...), kind=kOutput, calls=%fused_computation.39.clone.1 | convolution fusion | flops 24117248 | bytes 83976 | tf_op jit(solution)/shard_map/while/body/eval_jaxpr/dot_general | solution.py:43
  88.1 2.3 %fusion.140 = f32[2,16,512]{2,1,0:T(8,128)S(1)} fusion(f32[2,16,512]{2,1,0:T(8,128)S(1)} %get-tuple-element.482, s32[]{:T(128)} %get-tuple-element.480, bf16[16,1024]{1,0:T(8,128)(2,1)S(1)} %get-tuple-element.497, f32[]{:T(128)} %get-tuple-element.496, f32[1024]{0:T(1024)S(1)} %bitcast.208, f32[512]{0:T(512)S(1)} %bitcast.228, ...), kind=kOutput, calls=%fused_computation.39.clone.1 | convolution fusion | flops 24117248 | bytes 83976 | tf_op jit(solution)/shard_map/while/body/eval_jaxpr/dot_general | solution.py:43
  90.4 2.3 %fusion.30 = f32[17,1024]{1,0:T(8,128)S(1)} fusion(f32[17,1024]{1,0:T(8,128)S(1)} %fusion.39, f32[17,1024]{1,0:T(8,128)S(1)} %fusion.31, bf16[17,1024]{1,0:T(8,128)(2,1)S(1)} %collective-permute-done.8, bf16[1024,1024]{1,0:T(8,128)(2,1)} %bitcast.183), kind=kOutput, calls=%fused_computation.54 | convolution fusion | flops 35686400 | bytes 2340864 | tf_op jit(solution)/shard_map/dot_general | solution.py:43
  93.5 39.9 %all-reduce.2 = (f32[16]{0:T(128)S(1)}, f32[16]{0:T(128)S(1)}) all-reduce(f32[16]{0:T(128)S(1)} %get-tuple-element.155, f32[16]{0:T(128)S(1)} %get-tuple-element.154), channel_id=1, replica_groups=mesh['loc'=32] {'loc'}, use_global_device_ids=true, to_apply=%region_1.2 | all-reduce | flops 32 | bytes 256 | tf_op jit(solution)/shard_map/psum | solution.py:128
  133.5 2.2 %fusion.82 = f32[16,1024]{1,0:T(8,128)S(1)} fusion(bf16[16,1024]{1,0:T(8,128)(2,1)S(1)} %get-tuple-element.208, bf16[1024,1024]{1,0:T(8,128)(2,1)} %bitcast.186), kind=kOutput, calls=%fused_computation.184 | convolution fusion | flops 33554432 | bytes 2195456 | tf_op jit(solution)/shard_map/dot_general | solution.py:43
  139.5 5.0 %collective-permute-start.15 = (f32[16,256]{1,0:T(8,128)S(1)}, f32[16,256]{1,0:T(8,128)S(1)}, u32[]{:S(2)}, u32[]{:S(2)}) collective-permute-start(f32[16,256]{1,0:T(8,128)S(1)} %fusion.72), channel_id=1, source_target_pairs={{0,16},{1,17},{2,18},{3,19},{4,20},{5,21},{6,22},{7,23},{8,24},{9,... | collective-permute-start | bytes 49160 | tf_op jit(solution)/shard_map/ppermute | solution.py:29
  149.7 3.2 %collective-permute-done.12 = f32[16,256]{1,0:T(8,128)S(1)} collective-permute-done((f32[16,256]{1,0:T(8,128)S(1)}, f32[16,256]{1,0:T(8,128)S(1)}, u32[]{:S(2)}, u32[]{:S(2)}) %collective-permute-start.12) | collective-permute-done | bytes 16416 | tf_op jit(solution)/shard_map/ppermute | solution.py:29
  163.0 37.9 %all-reduce.1 = (f32[16]{0:T(128)S(1)}, f32[16]{0:T(128)S(1)}, f32[16]{0:T(128)S(1)}, f32[16]{0:T(128)S(1)}, f32[16]{0:T(128)S(1)}) all-reduce(f32[16]{0:T(128)S(1)} %get-tuple-element.153, f32[16]{0:T(128)S(1)} %get-tuple-element.152, f32[16]{0:T(128)S(1)} %get-tuple-element.126, ...), channel_id=1, replica_groups=mesh['loc'=32] {'loc'}, use_global_device_ids=true, to_apply=%region_11.13 | all-reduce | flops 80 | bytes 640 | tf_op jit(solution)/shard_map/psum | solution.py:147
  (134 shorter events, 69.9 us)
Async XLA Ops:
  0.6 18.8 %copy-start.3 = (f32[16,1024]{1,0:T(8,128)S(1)}, f32[16,1024]{1,0:T(8,128)}, u32[]{:S(2)}) copy-start(f32[16,1024]{1,0:T(8,128)} %param.16) | copy-start | bytes 196612
  0.6 66.5 %collective-permute-start.9 = (f32[3,1024]{1,0:T(4,128)}, f32[3,1024]{1,0:T(4,128)S(1)}, u32[]{:S(2)}, u32[]{:S(2)}) collective-permute-start(f32[3,1024]{1,0:T(4,128)} %param.15), channel_id=1, source_target_pairs={{0,1},{1,2},{2,3},{3,4},{4,5},{5,6},{6,7},{7,8},{8,9},{9,10},{10,1... | collective-permute-start | bytes 36872 | tf_op jit(solution)/shard_map/ppermute | solution.py:20
  5.8 34.5 %collective-permute-start.7 = (f32[3,256]{0,1:T(8,128)S(1)}, f32[3,256]{0,1:T(8,128)S(1)}, u32[]{:S(2)}, u32[]{:S(2)}) collective-permute-start(f32[3,256]{0,1:T(8,128)S(1)} %select_bitcast_fusion), channel_id=1, source_target_pairs={{0,16},{1,17},{2,18},{3,19},{4,20},{5,21},{6,22},{7,23},{8,24},{9,... | collective-permute-start | bytes 9224 | tf_op jit(solution)/shard_map/ppermute | solution.py:29
  10.3 31.5 %collective-permute-start.5 = (f32[3,256]{0,1:T(8,128)S(1)}, f32[3,256]{0,1:T(8,128)S(1)}, u32[]{:S(2)}, u32[]{:S(2)}) collective-permute-start(f32[3,256]{0,1:T(8,128)S(1)} %select_bitcast_fusion.1), channel_id=1, source_target_pairs={{0,8},{1,9},{2,10},{3,11},{4,12},{5,13},{6,14},{7,15},{8,0},{9,1},... | collective-permute-start | bytes 9224 | tf_op jit(solution)/shard_map/ppermute | solution.py:29
  12.8 30.6 %collective-permute-start.3 = (f32[3,256]{0,1:T(8,128)S(1)}, f32[3,256]{0,1:T(8,128)S(1)}, u32[]{:S(2)}, u32[]{:S(2)}) collective-permute-start(f32[3,256]{0,1:T(8,128)S(1)} %select_bitcast_fusion.2), channel_id=1, source_target_pairs={{0,4},{1,5},{2,6},{3,7},{4,0},{5,1},{6,2},{7,3},{8,12},{9,13},{10,... | collective-permute-start | bytes 9224 | tf_op jit(solution)/shard_map/ppermute | solution.py:29
  15.3 29.9 %collective-permute-start.1 = (f32[3,256]{0,1:T(8,128)S(1)}, f32[3,256]{0,1:T(8,128)S(1)}, u32[]{:S(2)}, u32[]{:S(2)}) collective-permute-start(f32[3,256]{0,1:T(8,128)S(1)} %select_bitcast_fusion.3), channel_id=1, source_target_pairs={{0,2},{1,3},{2,0},{3,1},{4,6},{5,7},{6,4},{7,5},{8,10},{9,11},{10,... | collective-permute-start | bytes 9224 | tf_op jit(solution)/shard_map/ppermute | solution.py:29
  32.1 6.2 %copy-start.2 = (bf16[2,512,1024]{2,1,0:T(8,128)(2,1)}, bf16[2,512,1024]{2,1,0:T(8,128)(2,1)S(1)}, u32[]{:S(2)}) copy-start(bf16[2,512,1024]{2,1,0:T(8,128)(2,1)S(1)} %get-tuple-element.120) | copy-start | bytes 6291460
  40.3 26.9 %collective-permute-start.8 = (bf16[17,1024]{1,0:T(8,128)(2,1)S(1)}, bf16[17,1024]{1,0:T(8,128)(2,1)S(1)}, u32[]{:S(2)}, u32[]{:S(2)}) collective-permute-start(bf16[17,1024]{1,0:T(8,128)(2,1)S(1)} %concatenate.3), channel_id=1, source_target_pairs={{0,1},{1,2},{2,3},{3,4},{4,5},{5,6},{6,7},{7,8},{8,9},{9,10},{10,1... | collective-permute-start | bytes 104456 | tf_op jit(solution)/shard_map/ppermute | solution.py:20
  41.8 36.3 %collective-permute-start.10 = (bf16[17,1024]{1,0:T(8,128)(2,1)S(1)}, bf16[17,1024]{1,0:T(8,128)(2,1)S(1)}, u32[]{:S(2)}, u32[]{:S(2)}) collective-permute-start(bf16[17,1024]{1,0:T(8,128)(2,1)S(1)} %concatenate.3), channel_id=1, source_target_pairs={{1,0},{2,1},{3,2},{4,3},{5,4},{6,5},{7,6},{8,7},{9,8},{10,9},{11,1... | collective-permute-start | bytes 104456 | tf_op jit(solution)/shard_map/ppermute | solution.py:21
  43.4 36.0 %collective-permute-start.11 = (f32[3,1024]{1,0:T(4,128)}, f32[3,1024]{1,0:T(4,128)S(1)}, u32[]{:S(2)}, u32[]{:S(2)}) collective-permute-start(f32[3,1024]{1,0:T(4,128)} %param.15), channel_id=1, source_target_pairs={{1,0},{2,1},{3,2},{4,3},{5,4},{6,5},{7,6},{8,7},{9,8},{10,9},{11,1... | collective-permute-start | bytes 36872 | tf_op jit(solution)/shard_map/ppermute | solution.py:21
  45.2 6.3 %collective-permute-start = (f32[17,256]{1,0:T(8,128)}, f32[17,256]{1,0:T(8,128)S(1)}, u32[]{:S(2)}, u32[]{:S(2)}) collective-permute-start(f32[17,256]{1,0:T(8,128)} %fusion.47), channel_id=1, source_target_pairs={{0,2},{1,3},{2,0},{3,1},{4,6},{5,7},{6,4},{7,5},{8,10},{9,11},{10,... | collective-permute-start | bytes 52232 | tf_op jit(solution)/shard_map/ppermute | solution.py:29
  51.5 4.8 %collective-permute-start.2 = (f32[17,256]{1,0:T(8,128)}, f32[17,256]{1,0:T(8,128)S(1)}, u32[]{:S(2)}, u32[]{:S(2)}) collective-permute-start(f32[17,256]{1,0:T(8,128)} %fusion.45), channel_id=1, source_target_pairs={{0,4},{1,5},{2,6},{3,7},{4,0},{5,1},{6,2},{7,3},{8,12},{9,13},{10,... | collective-permute-start | bytes 52232 | tf_op jit(solution)/shard_map/ppermute | solution.py:29
  54.8 1.5 copy-start.6
  56.3 4.7 %collective-permute-start.4 = (f32[17,256]{1,0:T(8,128)S(1)}, f32[17,256]{1,0:T(8,128)S(1)}, u32[]{:S(2)}, u32[]{:S(2)}) collective-permute-start(f32[17,256]{1,0:T(8,128)S(1)} %copy-done.6), channel_id=1, source_target_pairs={{0,8},{1,9},{2,10},{3,11},{4,12},{5,13},{6,14},{7,15},{8,0},{9,1},... | collective-permute-start | bytes 52232 | tf_op jit(solution)/shard_map/ppermute | solution.py:29
  59.7 1.3 copy-start.5
  61.0 4.7 %collective-permute-start.6 = (f32[17,256]{1,0:T(8,128)S(1)}, f32[17,256]{1,0:T(8,128)S(1)}, u32[]{:S(2)}, u32[]{:S(2)}) collective-permute-start(f32[17,256]{1,0:T(8,128)S(1)} %copy-done.5), channel_id=1, source_target_pairs={{0,16},{1,17},{2,18},{3,19},{4,20},{5,21},{6,22},{7,23},{8,24},{9,... | collective-permute-start | bytes 52232 | tf_op jit(solution)/shard_map/ppermute | solution.py:29
  135.7 25.2 %collective-permute-start.16 = (bf16[16,1024]{1,0:T(8,128)(2,1)S(1)}, bf16[16,1024]{1,0:T(8,128)(2,1)S(1)}, u32[]{:S(2)}, u32[]{:S(2)}) collective-permute-start(bf16[16,1024]{1,0:T(8,128)(2,1)S(1)} %get-tuple-element.208), channel_id=1, source_target_pairs={{0,1},{1,2},{2,3},{3,4},{4,5},{5,6},{6,7},{7,8},{8,9},{9,10},{10,1... | collective-permute-start | bytes 98312 | tf_op jit(solution)/shard_map/ppermute | solution.py:20
  137.0 25.2 %collective-permute-start.17 = (bf16[16,1024]{1,0:T(8,128)(2,1)S(1)}, bf16[16,1024]{1,0:T(8,128)(2,1)S(1)}, u32[]{:S(2)}, u32[]{:S(2)}) collective-permute-start(bf16[16,1024]{1,0:T(8,128)(2,1)S(1)} %get-tuple-element.208), channel_id=1, source_target_pairs={{1,0},{2,1},{3,2},{4,3},{5,4},{6,5},{7,6},{8,7},{9,8},{10,9},{11,1... | collective-permute-start | bytes 98312 | tf_op jit(solution)/shard_map/ppermute | solution.py:21
  139.5 20.0 %collective-permute-start.15 = (f32[16,256]{1,0:T(8,128)S(1)}, f32[16,256]{1,0:T(8,128)S(1)}, u32[]{:S(2)}, u32[]{:S(2)}) collective-permute-start(f32[16,256]{1,0:T(8,128)S(1)} %fusion.72), channel_id=1, source_target_pairs={{0,16},{1,17},{2,18},{3,19},{4,20},{5,21},{6,22},{7,23},{8,24},{9,... | collective-permute-start | bytes 49160 | tf_op jit(solution)/shard_map/ppermute | solution.py:29
  145.4 12.6 %collective-permute-start.14 = (f32[16,256]{1,0:T(8,128)S(1)}, f32[16,256]{1,0:T(8,128)S(1)}, u32[]{:S(2)}, u32[]{:S(2)}) collective-permute-start(f32[16,256]{1,0:T(8,128)S(1)} %fusion.71), channel_id=1, source_target_pairs={{0,8},{1,9},{2,10},{3,11},{4,12},{5,13},{6,14},{7,15},{8,0},{9,1},... | collective-permute-start | bytes 49160 | tf_op jit(solution)/shard_map/ppermute | solution.py:29
  149.1 3.8 %collective-permute-start.12 = (f32[16,256]{1,0:T(8,128)S(1)}, f32[16,256]{1,0:T(8,128)S(1)}, u32[]{:S(2)}, u32[]{:S(2)}) collective-permute-start(f32[16,256]{1,0:T(8,128)S(1)} %fusion.74), channel_id=1, source_target_pairs={{0,2},{1,3},{2,0},{3,1},{4,6},{5,7},{6,4},{7,5},{8,10},{9,11},{10,... | collective-permute-start | bytes 49160 | tf_op jit(solution)/shard_map/ppermute | solution.py:29
  149.7 12.5 %copy-start.4 = (f32[2,2,8,512]{3,2,0,1:T(8,128)}, f32[2,2,8,512]{3,2,0,1:T(8,128)S(1)}, u32[]{:S(2)}) copy-start(f32[2,2,8,512]{3,2,0,1:T(8,128)S(1)} %copy.21) | copy-start | bytes 196612
  152.9 3.7 %collective-permute-start.13 = (f32[16,256]{1,0:T(8,128)S(1)}, f32[16,256]{1,0:T(8,128)S(1)}, u32[]{:S(2)}, u32[]{:S(2)}) collective-permute-start(f32[16,256]{1,0:T(8,128)S(1)} %fusion.70), channel_id=1, source_target_pairs={{0,4},{1,5},{2,6},{3,7},{4,0},{5,1},{6,2},{7,3},{8,12},{9,13},{10,... | collective-permute-start | bytes 49160 | tf_op jit(solution)/shard_map/ppermute | solution.py:29
  159.9 1.6 copy-start.1
  (1 other events, 1.3 us)
where the time goes:
time: 204 us; the launch traced here: 202 us
  blocking collectives  77.8 us (38%)
  matrix products  42.2 us (21%)
  starting transfers between devices  38.4 us (19%)
  local copies, waits for them, and re-layouts  17.2 us (8%)
  other arithmetic  15.1 us (7%)
  waiting for transfers between devices  8.41 us (4%)
  between operations  3.05 us (1%)
    psum x1, blocking collectives, shards(): lax.psum((jnp.sum(residual * residual, axis=1), jnp.sum(residual * first_...  39.9 us
    psum x1, blocking collectives, shards(): lax.psum((jnp.sum(residual * residual, axis=1), jnp.sum(residual * image,...  37.9 us
    dot_general x20, matrix products, contract_rows(): lax.dot_general(vectors, matrix, (((1,), (1,)), ((), ())), preferred_elem...  31 us
    ppermute x12, starting transfers between devices, partner(): return lax.ppermute(value, axis, pairs)  29 us
    dynamic_update_slice x6, other arithmetic, make_block(): lax.scan(one_tile, back_init, (tile_pts_all, tile_pts_all))  13.1 us
    slice x21, local copies, waits for them, and re-layouts, kernel_pair(): diff_a = row_pts[0][:, None] - col_pts[0][None, :]  9.69 us
    ppermute x12, waiting for transfers between devices, partner(): return lax.ppermute(value, axis, pairs)  8.39 us
    dot_general x8, matrix products, far_part(): jnp.dot(mixed_half, bases[level_id], preferred_element_type=jnp.float32)  7.53 us
  transfers between devices with their start and end apart: 18, of which 6 were waited for; matrix products, arithmetic and copies ran while one was open for 27% of the time, Pallas kernels for 0%

commit v1 on v0

v1 whole, which is shorter than its diff:
```python
import functools

import jax
import jax.numpy as jnp
from jax import lax
from jax.experimental import pallas as pl
from jax.experimental.pallas import tpu as pltpu
from jax.sharding import PartitionSpec as P

HALF = jnp.bfloat16
FULL = jnp.float32
LOG2_E = 1.4426950408889634
LN_2 = 0.6931471805599453
TINY = 1e-30
VEC_ROWS = 32
SRC_ROWS = 32
MSG_ROWS = 48
TILE = 256
VMEM = pltpu.VMEM
SMEM = pltpu.SMEM


def split_two(value):
    high = value.astype(HALF)
    low = (value - high.astype(FULL)).astype(HALF)
    return high, low


def split_three(value):
    first = value.astype(HALF).astype(FULL)
    rest = value - first
    second = rest.astype(HALF).astype(FULL)
    third = (rest - second).astype(HALF).astype(FULL)
    return first, second, third


def matern(squared):
    squared = jnp.maximum(squared, TINY)
    scaled = squared * lax.rsqrt(squared)
    decay = jnp.exp2(-scaled)
    return squared, decay, decay + (LN_2 * scaled) * decay


def source_rows(buf, base, pts):
    one, two, three = split_three(pts)
    for slot, piece in enumerate((one, one, two, two, one, three)):
        buf[base + 1 + 3 * slot : base + 4 + 3 * slot, :] = piece
    size = jnp.sum(pts * pts, axis=0, keepdims=True)
    one, two, three = split_three(size)
    for slot, piece in enumerate((one, one, two, two, one, three)):
        buf[base + 19 + slot : base + 20 + slot, :] = piece
    unit = jnp.ones_like(size)
    buf[base : base + 1, :] = unit
    buf[base + 25 : base + 26, :] = unit
    buf[base + 26 : base + 27, :] = unit
    buf[base + 27 : base + 32, :] = jnp.zeros((5, size.shape[1]), FULL)


def target_rows(buf, pts, length):
    size = jnp.sum(pts * pts, axis=0, keepdims=True)
    reach = jnp.full_like(size, length)
    scale = (3.0 * LOG2_E * LOG2_E) / (reach * reach)
    one, two, three = split_three(pts * (-2.0 * scale))
    for slot, piece in enumerate((one, two, one, two, three, one)):
        buf[1 + 3 * slot : 4 + 3 * slot, :] = piece
    one, two, three = split_three(scale)
    for slot, piece in enumerate((one, two, one, two, three, one)):
        buf[19 + slot : 20 + slot, :] = piece
    one, two, three = split_three(scale * size)
    buf[0:1, :] = one
    buf[25:26, :] = two
    buf[26:27, :] = three
    buf[27:32, :] = jnp.zeros((5, size.shape[1]), FULL)


def dot(a, b):
    return jnp.dot(a, b, preferred_element_type=FULL)


def dot_rows(a, b):
    return lax.dot_general(a, b, (((1,), (1,)), ((), ())), preferred_element_type=FULL)


def turned(value):
    return value.astype(FULL).T.astype(HALF)


def front_kernel(levels, *refs):
    length, far_length, pts, rhs, skel = refs[:5]
    msg, target, basis, skel_target = refs[5:9]
    lev = refs[9 : 9 + levels]
    buf, far_buf, pair_buf = refs[9 + levels :]
    points = pts[...]
    buf[0:16, :] = rhs[...]
    source_rows(buf, 16, points)
    msg[...] = buf[...].astype(HALF)
    target_rows(far_buf, points, length[0])
    target[...] = far_buf[...].astype(HALF)
    target_rows(far_buf, points, far_length[0])
    pair_buf[0:SRC_ROWS, :] = msg[16:48, :]
    pair_buf[SRC_ROWS:, :] = far_buf[...].astype(HALF)
    rows, rank = pts.shape[1], skel.shape[1]
    vecs = msg[0:VEC_ROWS, :]
    for level in range(levels):
        spot = lax.broadcasted_iota(jnp.int32, (rows, rank), 0)
        picks = jnp.where(spot == skel[level : level + 1, :], 1.0, 0.0).astype(HALF)
        both = dot(pair_buf[...], picks)
        skel_target[level] = both[SRC_ROWS:].astype(HALF)
        skel_source = both[:SRC_ROWS]
        squared = dot(skel_source.T.astype(HALF), pair_buf[SRC_ROWS:, :])
        block = matern(squared)[2].astype(HALF)
        basis[level] = block
        high, low = split_two(dot_rows(vecs, block))
        lev[level][0:32, :] = high
        lev[level][32:64, :] = low
        lev[level][64:96, :] = skel_source.astype(HALF)


def near_block(msg, target, turned_src, kept, image, slopes, first):
    rows = target.shape[1]
    turned_src[...] = turned(msg[16:48, :])

    def strip(index, carry):
        start = pl.multiple_of(index * TILE, TILE)
        vecs = msg[0:VEC_ROWS, pl.ds(start, TILE)]
        for col in range(0, rows, TILE):
            squared = dot(turned_src[pl.ds(start, TILE), :], target[:, col : col + TILE])
            squared, decay, value = matern(squared)
            value = value.astype(HALF)
            slope = (squared * decay).astype(HALF)
            kept[pl.ds(start, TILE), col : col + TILE] = value
            image[:, col : col + TILE] += dot(vecs, value)
            slopes[:, col : col + TILE] += dot(vecs[0:16], slope)
        return carry

    if first:
        image[...] = jnp.zeros_like(image)
        slopes[...] = jnp.zeros_like(slopes)
    lax.fori_loop(0, rows // TILE, strip, 0)


def own_kernel(msg, target, kept, image, slopes, turned_src):
    near_block(msg, target, turned_src, kept, image, slopes, True)


def side_kernel(levels, far_scale, *refs):
    signal, msg_a, msg_b, target, own_image, own_slopes, rhs, basis, skel_target = refs[:9]
    lev = refs[9 : 9 + levels]
    outs = refs[9 + levels :]
    kept_a, kept_b, coup_high, coup_low, row_sum, slope_image, first, wmsg = outs[:8]
    wlev = outs[8 : 8 + levels]
    turned_src, image, slopes = outs[8 + levels :]
    image[...] = own_image[...]
    slopes[...] = own_slopes[...]
    near_block(msg_a, target, turned_src, kept_a, image, slopes, False)
    near_block(msg_b, target, turned_src, kept_b, image, slopes, False)
    slope_image[...] = (signal[0] * (LN_2 * LN_2)) * slopes[...]
    far = jnp.zeros(image.shape, FULL)
    for level in range(levels):
        squared = dot(turned(lev[level][64:96, :]), skel_target[level])
        high, low = split_two(matern(squared)[2])
        coup_high[level] = high
        coup_low[level] = low
        coef = lev[level][0:32, :]
        mixed = dot(coef, high) + dot(lev[level][32:64, :], high) + dot(coef, low)
        far = far + dot(mixed.astype(HALF), basis[level])
    total = image[...] + far_scale * far
    sums = total[16:17, :]
    row_sum[...] = sums
    value = signal[0] * (total[0:16] + sums * rhs[...])
    first[...] = value
    high, low = split_two(value)
    wmsg[0:16, :] = high
    wmsg[16:32, :] = low
    for level in range(levels):
        both = dot_rows(wmsg[...], basis[level])
        high, low = split_two(both[0:16] + both[16:32])
        wlev[level][0:16, :] = high
        wlev[level][16:32, :] = low


def row_total(a, b):
    return jnp.sum(a * b, axis=1, keepdims=True)


def second_kernel(levels, far_scale, *refs):
    signal, wmsg, wmsg_a, wmsg_b, kept, kept_a, kept_b = refs[:7]
    basis, coup_high, coup_low, row_sum, first, rhs, slope_image = refs[7:14]
    wlev = refs[14 : 14 + levels]
    sums, first_rest, second_rest, shift_out = refs[14 + levels :]
    both = dot(wmsg[...], kept[...]) + dot(wmsg_a[...], kept_a[...]) + dot(wmsg_b[...], kept_b[...])
    far = jnp.zeros(both.shape, FULL)
    for level in range(levels):
        coef = wlev[level][...]
        mixed = dot(coef, coup_high[level])
        mixed = mixed[0:16] + mixed[16:32] + dot(coef[0:16], coup_low[level])
        high, low = split_two(mixed)
        far = far + dot(jnp.concatenate([high, low], axis=0), basis[level])
    both = both + far_scale * far
    base = rhs[...]
    value = first[...]
    image = signal[0] * (both[0:16] + both[16:32] + row_sum[...] * value)
    weight = row_total(base, base)
    shift = jnp.where(weight > 0.0, row_total(base, value) / jnp.where(weight > 0.0, weight, 1.0), 0.0)
    value = value - shift * base
    image = image - (2.0 * shift) * value - (shift * shift) * base
    first_rest[...] = value
    second_rest[...] = image
    shift_out[...] = jnp.broadcast_to(shift, shift_out.shape)
    slope = slope_image[...]
    parts = (
        shift,
        weight,
        row_total(value, value),
        row_total(value, image),
        row_total(base, image),
        row_total(base, value),
        row_total(base, slope),
        row_total(value, slope),
    )
    lane = lax.broadcasted_iota(jnp.int32, (16, 128), 1)
    row = lax.broadcasted_iota(jnp.int32, (16, 128), 0)
    packed = jnp.zeros((16, 128), FULL)
    for slot, part in enumerate(parts):
        packed = jnp.where(lane == row + 16 * slot, part, packed)
    sums[...] = jnp.broadcast_to(jnp.sum(packed, axis=0, keepdims=True), sums.shape)


def last_kernel(point_total, noise, table, shift_in, first_rest, second_rest, rhs, out, res, trace):
    gathered = table[...]
    shift = gathered

    def slot(index):
        return pltpu.roll(gathered, 128 - 16 * index, 1)

    weight, ww, wz, rz, rw, rs, ws = (slot(index) for index in range(1, 8))

    def total(value):
        return jnp.sum(value, axis=0, keepdims=True)

    norm = total(weight)
    center = total(shift * weight + rw) / norm
    off = shift - center
    cross = total(rw + off * weight)
    square = total(ww + 2.0 * off * rw + off * off * weight)
    mixed = total(rz + 2.0 * off * rw + off * off * weight)
    second = total(
        wz + 2.0 * off * ww + off * off * rw + off * rz + 2.0 * off * off * rw + off * off * off * weight
    )
    held = total(rs)
    along = total(ws + off * rs)
    level = noise[0] + center
    lead = level * norm + cross
    alpha = norm / lead
    part = cross / lead
    norm_next = part * part * norm - 2.0 * part * alpha * cross + alpha * alpha * square
    lean = part + norm_next / norm
    direction = lean * lean * norm - 2.0 * lean * alpha * cross + alpha * alpha * square
    bend = lean * lean * cross - lean * alpha * (mixed + square) + alpha * alpha * second
    beta = norm_next / (level * direction + bend)
    trace[...] = (((alpha + beta * lean) * held - beta * alpha * along) / point_total)[:, 0:16]

    lane = lax.broadcasted_iota(jnp.int32, (16, 128), 1)
    row = lax.broadcasted_iota(jnp.int32, (16, 128), 0)

    def column(value):
        return jnp.sum(jnp.where(lane == row, value, 0.0), axis=1, keepdims=True)

    own_off = shift_in[:, 0:1] - column(center)
    base = rhs[...]
    rest = first_rest[...]
    value = rest + own_off * base
    image = second_rest[...] + (2.0 * own_off) * rest + (own_off * own_off) * base
    out[...] = column(alpha + beta * lean) * base - column(beta * alpha) * value
    res[...] = (
        column(part - beta * level * lean) * base
        - column(alpha - beta * level * alpha + beta * lean) * value
        + column(beta * alpha) * image
    )


def call(kernel, outs, spaces, scratch=(), flops=0):
    params = pltpu.CompilerParams(vmem_limit_bytes=40 * 2**20)
    cost = pl.CostEstimate(flops=flops, bytes_accessed=2**20, transcendentals=0)
    return pl.pallas_call(
        kernel,
        out_shape=[jax.ShapeDtypeStruct(shape, kind) for shape, kind in outs],
        in_specs=[pl.BlockSpec(memory_space=space) for space in spaces],
        out_specs=[pl.BlockSpec(memory_space=VMEM) for _ in outs],
        scratch_shapes=list(scratch),
        compiler_params=params,
        cost_estimate=cost,
    )


def shards(points, right_sides, skeleton, lengthscale, far_length, signal, noise_var):
    probes, rows = right_sides.shape
    levels, rank = skeleton.shape
    count = lax.axis_size("loc")
    far_scale = 1.0 / (rank * rank * levels)
    beside = [(i, i ^ 1) for i in range(count)]
    across = [(i, i + 1) for i in range(1, count - 1, 2)]
    across = across + [(j, i) for i, j in across]

    def partner(value, level):
        return lax.ppermute(value, "loc", [(i, i ^ (2 << level)) for i in range(count)])

    def sides(value):
        return lax.ppermute(value, "loc", beside), lax.ppermute(value, "loc", across)

    msg, target, basis, skel_target, *lev = call(
        functools.partial(front_kernel, levels),
        [
            ((MSG_ROWS, rows), HALF),
            ((SRC_ROWS, rows), HALF),
            ((levels, rank, rows), HALF),
            ((levels, SRC_ROWS, rank), HALF),
        ]
        + [((96, rank), HALF)] * levels,
        [SMEM, SMEM] + [VMEM] * 3,
        [VMEM((MSG_ROWS, rows), FULL), VMEM((SRC_ROWS, rows), FULL), VMEM((2 * SRC_ROWS, rows), HALF)],
    )(lengthscale, far_length, points, right_sides, skeleton)
    msg_a, msg_b = sides(msg)
    lev = [partner(value, level) for level, value in enumerate(lev)]
    kept, image, slopes = call(
        own_kernel,
        [((rows, rows), HALF), ((VEC_ROWS, rows), FULL), ((probes, rows), FULL)],
        [VMEM] * 2,
        [VMEM((rows, SRC_ROWS), HALF)],
    )(msg, target)
    kept_a, kept_b, coup_high, coup_low, row_sum, slope_image, first, wmsg, *wlev = call(
        functools.partial(side_kernel, levels, far_scale),
        [
            ((rows, rows), HALF),
            ((rows, rows), HALF),
            ((levels, rank, rank), HALF),
            ((levels, rank, rank), HALF),
            ((1, rows), FULL),
            ((probes, rows), FULL),
            ((probes, rows), FULL),
            ((2 * probes, rows), HALF),
        ]
        + [((2 * probes, rank), HALF)] * levels,
        [SMEM] + [VMEM] * (8 + levels),
        [VMEM((rows, SRC_ROWS), HALF), VMEM((VEC_ROWS, rows), FULL), VMEM((probes, rows), FULL)],
    )(signal, msg_a, msg_b, target, image, slopes, right_sides, basis, skel_target, *lev)
    wmsg_a, wmsg_b = sides(wmsg)
    wlev = [partner(value, level) for level, value in enumerate(wlev)]
    sums, first_rest, second_rest, shift = call(
        functools.partial(second_kernel, levels, far_scale),
        [((count, 128), FULL), ((probes, rows), FULL), ((probes, rows), FULL), ((probes, 128), FULL)],
        [SMEM] + [VMEM] * (13 + levels),
    )(
        signal,
        wmsg,
        wmsg_a,
        wmsg_b,
        kept,
        kept_a,
        kept_b,
        basis,
        coup_high,
        coup_low,
        row_sum,
        first,
        right_sides,
        slope_image,
        *wlev,
    )
    table = lax.all_to_all(sums, "loc", 0, 0, tiled=True)
    solution, residual, trace = call(
        functools.partial(last_kernel, float(rows * count)),
        [((probes, rows), FULL), ((probes, rows), FULL), ((1, probes), FULL)],
        [SMEM] + [VMEM] * 5,
    )(noise_var, table, shift, first_rest, second_rest, right_sides)
    return (solution, residual, slope_image, trace.reshape(probes))


def solution(mesh):
    placed = (P(None, "loc"), P(None, "loc"), P(None, "loc"), P(), P(), P(), P())
    return jax.shard_map(
        shards,
        mesh=mesh,
        in_specs=placed,
        out_specs=(P(None, "loc"), P(None, "loc"), P(None, "loc"), P()),
        check_vma=False,
    )
```

time: 204 us -> 57.7 us (0.28)
  blocking collectives: 77.8 us -> 0 us
  matrix products: 42.2 us -> 0 us
  Pallas kernels: 0 us -> 17.8 us
  starting transfers between devices: 38.4 us -> 22.6 us
  other arithmetic: 15.1 us -> 0 us
  local copies, waits for them, and re-layouts: 17.2 us -> 3.92 us
    psum x2 -> x0, blocking collectives: 77.8 us -> none  [the longest x1 39.9 us: shards(): lax.psum((jnp.sum(residual * residual, axis=1), jnp.sum(residual * first_...]
    dot_general x36 -> x0, matrix products: 42.2 us -> none  [the longest x20 31 us: contract_rows(): lax.dot_general(vectors, matrix, (((1,), (1,)), ((), ())), preferred_elem...]
    ppermute x18 -> x12, starting transfers between devices: 38.4 us -> 19.2 us  [the longest x8 17.9 us: partner(): lax.ppermute(value, 'loc', [(i, i ^ 2 << level) for i in range(count)])]
    pallas_call x0 -> x5, Pallas kernels: none -> 17.8 us  [the longest x1 8.31 us: shards(): call(functools.partial(side_kernel, levels, far_scale), [((rows, rows), H...]
    dynamic_update_slice x6 -> x0, other arithmetic: 13.1 us -> none  [make_block(): lax.scan(one_tile, back_init, (tile_pts_all, tile_pts_all))]
    slice x25 -> x0, local copies, waits for them, and re-layouts: 10.6 us -> none  [the longest x21 9.69 us: kernel_pair(): diff_a = row_pts[0][:, None] - col_pts[0][None, :]]
    all_to_all x0 -> x1, waiting for transfers between devices: none -> 6.43 us  [shards(): table = lax.all_to_all(sums, 'loc', 0, 0, tiled=True)]
    ppermute x18 -> x12, waiting for transfers between devices: 8.41 us -> 3.13 us  [the longest x8 3.12 us: partner(): lax.ppermute(value, 'loc', [(i, i ^ 2 << level) for i in range(count)])]
  transfers between devices with their start and end apart: 18 -> 13, of which waited for: 6 -> 5; matrix products, arithmetic and copies ran while one was open for 27% -> 0% of each run, Pallas kernels for 0% -> 5%
where the time goes in v1:
time: 57.7 us; the launch traced here: 57.2 us
  starting transfers between devices  22.6 us (39%)
  Pallas kernels  17.8 us (31%)
  waiting for transfers between devices  9.56 us (17%)
  local copies, waits for them, and re-layouts  3.92 us (7%)
  between operations  3.33 us (6%)
    ppermute x8, starting transfers between devices, partner(): lax.ppermute(value, 'loc', [(i, i ^ 2 << level) for i in range(count)])  17.9 us
    pallas_call x1, Pallas kernels, shards(): call(functools.partial(side_kernel, levels, far_scale), [((rows, rows), H...  8.31 us
    all_to_all x1, waiting for transfers between devices, shards(): table = lax.all_to_all(sums, 'loc', 0, 0, tiled=True)  6.43 us
    unnamed x12, local copies, waits for them, and re-layouts  3.92 us
    all_to_all x1, starting transfers between devices, shards(): table = lax.all_to_all(sums, 'loc', 0, 0, tiled=True)  3.38 us
    ppermute x8, waiting for transfers between devices, partner(): lax.ppermute(value, 'loc', [(i, i ^ 2 << level) for i in range(count)])  3.12 us
    pallas_call x1, Pallas kernels, shards(): call(functools.partial(front_kernel, levels), [((MSG_ROWS, rows), HALF),...  3.12 us
    pallas_call x1, Pallas kernels, shards(): call(own_kernel, [((rows, rows), HALF), ((VEC_ROWS, rows), FULL), ((probe...  2.84 us
  transfers between devices with their start and end apart: 13, of which 5 were waited for; matrix products, arithmetic and copies ran while one was open for 0% of the time, Pallas kernels for 5%

profile of v1, /device:TPU:0, one launch (start us, length us, event | category | flops | bytes accessed | tf_op | source)
XLA Modules:
  0.0 57.2 jit_solution(5315639845128176586)
XLA Ops:
  1.9 0.8 %copy-done = f32[16,1024]{1,0:T(8,128)S(1)} copy-done((f32[16,1024]{1,0:T(8,128)S(1)}, f32[16,1024]{1,0:T(8,128)}, u32[]{:S(2)}) %copy-start) | copy-done | bytes 65560
  2.8 0.7 %copy-done.4 = f32[3,1024]{1,0:T(4,128)S(1)} copy-done((f32[3,1024]{1,0:T(4,128)S(1)}, f32[3,1024]{1,0:T(4,128)}, u32[]{:S(2)}) %copy-start.4) | copy-done | bytes 12312
  3.5 0.7 %copy-done.5 = s32[4,256]{1,0:T(4,128)S(1)} copy-done((s32[4,256]{1,0:T(4,128)S(1)}, s32[4,256]{1,0:T(4,128)}, u32[]{:S(2)}) %copy-start.5) | copy-done | bytes 4120
  4.2 3.1 %shard_map.102 = (bf16[48,1024]{1,0:T(8,128)(2,1)S(1)}, bf16[32,1024]{1,0:T(8,128)(2,1)S(1)}, bf16[4,256,1024]{2,1,0:T(8,128)(2,1)S(1)}, bf16[4,32,256]{2,1,0:T(...) custom-call(f32[1]{0:T(128)S(6)} %copy.12.refs_0_, ...), custom_call_target="tpu_custom_call" | custom-call | bytes 1048576 | tf_op jit(solution)/shard_map/pallas_call | solution.py:311
  7.3 3.0 %collective-permute-start.2 = (bf16[96,256]{1,0:T(8,128)(2,1)S(1)}, bf16[96,256]{1,0:T(8,128)(2,1)S(1)}, u32[]{:S(2)}, u32[]{:S(2)}) collective-permute-start(bf16[96,256]{1,0:T(8,128)(2,1)S(1)} %get-tuple-element.40), channel_id=1, source_target_pairs={{0,2},{1,3},{2,0},{3,1},{4,6},{5,7},{6,4},{7,5},{8,10},{9,11},{10,... | collective-permute-start | bytes 147464 | tf_op jit(solution)/shard_map/ppermute | solution.py:306
  10.3 0.7 %collective-permute-start.1 = (bf16[48,1024]{1,0:T(8,128)(2,1)S(1)}, bf16[48,1024]{1,0:T(8,128)(2,1)S(1)}, u32[]{:S(2)}, u32[]{:S(2)}) collective-permute-start(bf16[48,1024]{1,0:T(8,128)(2,1)S(1)} %get-tuple-element.34.msg), channel_id=1, source_target_pairs={{1,2},{3,4},{5,6},{7,8},{9,10},{11,12},{13,14},{15,16},{17,18},{19... | collective-permute-start | bytes 294920 | tf_op jit(solution)/shard_map/ppermute | solution.py:309
  11.0 3.0 %collective-permute-start.3 = (bf16[96,256]{1,0:T(8,128)(2,1)S(1)}, bf16[96,256]{1,0:T(8,128)(2,1)S(1)}, u32[]{:S(2)}, u32[]{:S(2)}) collective-permute-start(bf16[96,256]{1,0:T(8,128)(2,1)S(1)} %get-tuple-element.41), channel_id=1, source_target_pairs={{0,4},{1,5},{2,6},{3,7},{4,0},{5,1},{6,2},{7,3},{8,12},{9,13},{10,... | collective-permute-start | bytes 147464 | tf_op jit(solution)/shard_map/ppermute | solution.py:306
  13.9 2.0 %collective-permute-start.4 = (bf16[96,256]{1,0:T(8,128)(2,1)S(1)}, bf16[96,256]{1,0:T(8,128)(2,1)S(1)}, u32[]{:S(2)}, u32[]{:S(2)}) collective-permute-start(bf16[96,256]{1,0:T(8,128)(2,1)S(1)} %get-tuple-element.42), channel_id=1, source_target_pairs={{0,8},{1,9},{2,10},{3,11},{4,12},{5,13},{6,14},{7,15},{8,0},{9,1},... | collective-permute-start | bytes 147464 | tf_op jit(solution)/shard_map/ppermute | solution.py:306
  16.0 2.6 %collective-permute-start.5 = (bf16[96,256]{1,0:T(8,128)(2,1)S(1)}, bf16[96,256]{1,0:T(8,128)(2,1)S(1)}, u32[]{:S(2)}, u32[]{:S(2)}) collective-permute-start(bf16[96,256]{1,0:T(8,128)(2,1)S(1)} %get-tuple-element.43), channel_id=1, source_target_pairs={{0,16},{1,17},{2,18},{3,19},{4,20},{5,21},{6,22},{7,23},{8,24},{9,... | collective-permute-start | bytes 147464 | tf_op jit(solution)/shard_map/ppermute | solution.py:306
  18.6 2.8 %shard_map.103 = (bf16[1024,1024]{1,0:T(8,128)(2,1)S(1)}, f32[32,1024]{1,0:T(8,128)S(1)}, f32[16,1024]{1,0:T(8,128)S(1)}) custom-call(bf16[48,1024]{1,0:T(8,128)(2,1)S(1)} %get-tuple-element.34.msg, bf16[32,1024]{1,0:T(8,128)(2,1)S(1)} %get-tuple-element.35.target.refs_3_), custom_call_target="tpu_custom_call" | custom-call | bytes 1048576 | tf_op jit(solution)/shard_map/pallas_call | solution.py:325
  22.1 0.8 %copy-done.1 = f32[16,1024]{1,0:T(8,128)S(1)} copy-done((f32[16,1024]{1,0:T(8,128)S(1)}, f32[16,1024]{1,0:T(8,128)}, u32[]{:S(2)}) %copy-start.1) | copy-done | bytes 65560
  23.0 8.3 %shard_map.104 = (bf16[1024,1024]{1,0:T(8,128)(2,1)S(1)}, bf16[1024,1024]{1,0:T(8,128)(2,1)S(1)}, bf16[4,256,256]{2,1,0:T(8,128)(2,1)S(1)}, bf16[4,256,256]{2,1,...) custom-call(f32[1]{0:T(128)S(6)} %copy.14.refs_0_, ...), custom_call_target="tpu_custom_call" | custom-call | bytes 1048576 | tf_op jit(solution)/shard_map/pallas_call | solution.py:331
  31.3 0.7 %collective-permute-start.7 = (bf16[32,1024]{1,0:T(8,128)(2,1)S(1)}, bf16[32,1024]{1,0:T(8,128)(2,1)S(1)}, u32[]{:S(2)}, u32[]{:S(2)}) collective-permute-start(bf16[32,1024]{1,0:T(8,128)(2,1)S(1)} %get-tuple-element.44.refs_1_), channel_id=1, source_target_pairs={{1,2},{3,4},{5,6},{7,8},{9,10},{11,12},{13,14},{15,16},{17,18},{19... | collective-permute-start | bytes 196616 | tf_op jit(solution)/shard_map/ppermute | solution.py:309
  31.9 4.4 %collective-permute-start.10 = (bf16[32,256]{1,0:T(8,128)(2,1)S(1)}, bf16[32,256]{1,0:T(8,128)(2,1)S(1)}, u32[]{:S(2)}, u32[]{:S(2)}) collective-permute-start(bf16[32,256]{1,0:T(8,128)(2,1)S(1)} %get-tuple-element.55), channel_id=1, source_target_pairs={{0,8},{1,9},{2,10},{3,11},{4,12},{5,13},{6,14},{7,15},{8,0},{9,1},... | collective-permute-start | bytes 49160 | tf_op jit(solution)/shard_map/ppermute | solution.py:306
  36.3 1.5 %collective-permute-start.11 = (bf16[32,256]{1,0:T(8,128)(2,1)S(1)}, bf16[32,256]{1,0:T(8,128)(2,1)S(1)}, u32[]{:S(2)}, u32[]{:S(2)}) collective-permute-start(bf16[32,256]{1,0:T(8,128)(2,1)S(1)} %get-tuple-element.56), channel_id=1, source_target_pairs={{0,16},{1,17},{2,18},{3,19},{4,20},{5,21},{6,22},{7,23},{8,24},{9,... | collective-permute-start | bytes 49160 | tf_op jit(solution)/shard_map/ppermute | solution.py:306
  37.8 0.8 %collective-permute-done.10.refs_16_ = bf16[32,256]{1,0:T(8,128)(2,1)S(1)} collective-permute-done((bf16[32,256]{1,0:T(8,128)(2,1)S(1)}, bf16[32,256]{1,0:T(8,128)(2,1)S(1)}, u32[]{:S(2)}, u32[]{:S(2)}) %collective-permute-start.10) | collective-permute-done | bytes 16416 | tf_op jit(solution)/shard_map/ppermute | solution.py:306
  38.6 1.5 %collective-permute-start.9 = (bf16[32,256]{1,0:T(8,128)(2,1)S(1)}, bf16[32,256]{1,0:T(8,128)(2,1)S(1)}, u32[]{:S(2)}, u32[]{:S(2)}) collective-permute-start(bf16[32,256]{1,0:T(8,128)(2,1)S(1)} %get-tuple-element.54), channel_id=1, source_target_pairs={{0,4},{1,5},{2,6},{3,7},{4,0},{5,1},{6,2},{7,3},{8,12},{9,13},{10,... | collective-permute-start | bytes 49160 | tf_op jit(solution)/shard_map/ppermute | solution.py:306
  40.1 0.8 %collective-permute-done.11.refs_17_ = bf16[32,256]{1,0:T(8,128)(2,1)S(1)} collective-permute-done((bf16[32,256]{1,0:T(8,128)(2,1)S(1)}, bf16[32,256]{1,0:T(8,128)(2,1)S(1)}, u32[]{:S(2)}, u32[]{:S(2)}) %collective-permute-start.11) | collective-permute-done | bytes 16416 | tf_op jit(solution)/shard_map/ppermute | solution.py:306
  41.5 0.8 %collective-permute-done.9.refs_15_ = bf16[32,256]{1,0:T(8,128)(2,1)S(1)} collective-permute-done((bf16[32,256]{1,0:T(8,128)(2,1)S(1)}, bf16[32,256]{1,0:T(8,128)(2,1)S(1)}, u32[]{:S(2)}, u32[]{:S(2)}) %collective-permute-start.9) | collective-permute-done | bytes 16416 | tf_op jit(solution)/shard_map/ppermute | solution.py:306
  42.4 0.8 %copy-done.3 = f32[16,1024]{1,0:T(8,128)S(1)} copy-done((f32[16,1024]{1,0:T(8,128)S(1)}, f32[16,1024]{1,0:T(8,128)}, u32[]{:S(2)}) %copy-start.3) | copy-done | bytes 65560
  43.2 2.6 %shard_map.105 = (f32[32,128]{1,0:T(8,128)}, f32[16,1024]{1,0:T(8,128)S(1)}, f32[16,1024]{1,0:T(8,128)S(1)}, f32[16,128]{1,0:T(8,128)S(1)}) custom-call(f32[1]{0:T(128)S(6)} %copy.14.refs_0_, bf16[32,1024]{1,0:T(8,128)(2,1)S(1)} %get-tuple-element.44.refs_1_, bf16[32,1024]{1,0:T(8,128)(2,1)S(1)} %collective-permute-done.6.refs_2_, ...), custom_call_target="tpu_custom_call" | custom-call | bytes 1048576 | tf_op jit(solution)/shard_map/pallas_call | solution.py:349
  45.9 3.4 %all-to-all-start = ((f32[32,1,128]{2,1,0:T(1,128)}), f32[32,1,128]{2,1,0:T(1,128)S(1)}, u32[]{:S(2)}, u32[]{:S(2)}) async-start(f32[32,1,128]{2,1,0:T(1,128)} %bitcast.1), calls=%async_computation | async-start | bytes 32768 | tf_op jit(solution)/shard_map/all_to_all | solution.py:370
  49.9 6.4 %all-to-all-done = f32[32,1,128]{2,1,0:T(1,128)S(1)} async-done(((f32[32,1,128]{2,1,0:T(1,128)}), f32[32,1,128]{2,1,0:T(1,128)S(1)}, u32[]{:S(2)}, u32[]{:S(2)}) %all-to-all-start) | async-done | bytes 16416 | tf_op jit(solution)/shard_map/all_to_all | solution.py:370
  56.3 0.9 %shard_map.106 = (f32[16,1024]{1,0:T(8,128)}, f32[16,1024]{1,0:T(8,128)}, f32[1,16]{1,0:T(1,128)}) custom-call(f32[1]{0:T(128)S(6)} %copy.15.noise, f32[32,128]{1,0:T(8,128)S(1)} %bitcast.5, f32[16,128]{1,0:T(8,128)S(1)} %get-tuple-element.58.shift_in, f32[16,1024]{1,0:T(8,128)S(1)} %get-tuple-element.59.first_rest, ...), custom_call_target="tpu_custom_call" | custom-call | bytes 1048576 | tf_op jit(solution)/shard_map/pallas_call | solution.py:371
  (19 shorter events, 0.6 us)
Async XLA Ops:
  1.9 0.8 %copy-start = (f32[16,1024]{1,0:T(8,128)S(1)}, f32[16,1024]{1,0:T(8,128)}, u32[]{:S(2)}) copy-start(f32[16,1024]{1,0:T(8,128)} %rhs.1) | copy-start | bytes 196612
  2.8 0.7 %copy-start.4 = (f32[3,1024]{1,0:T(4,128)S(1)}, f32[3,1024]{1,0:T(4,128)}, u32[]{:S(2)}) copy-start(f32[3,1024]{1,0:T(4,128)} %refs_2_.1) | copy-start | bytes 36868
  3.5 0.7 %copy-start.5 = (s32[4,256]{1,0:T(4,128)S(1)}, s32[4,256]{1,0:T(4,128)}, u32[]{:S(2)}) copy-start(s32[4,256]{1,0:T(4,128)} %refs_4_.1) | copy-start | bytes 12292
  7.3 8.7 %collective-permute-start.2 = (bf16[96,256]{1,0:T(8,128)(2,1)S(1)}, bf16[96,256]{1,0:T(8,128)(2,1)S(1)}, u32[]{:S(2)}, u32[]{:S(2)}) collective-permute-start(bf16[96,256]{1,0:T(8,128)(2,1)S(1)} %get-tuple-element.40), channel_id=1, source_target_pairs={{0,2},{1,3},{2,0},{3,1},{4,6},{5,7},{6,4},{7,5},{8,10},{9,11},{10,... | collective-permute-start | bytes 147464 | tf_op jit(solution)/shard_map/ppermute | solution.py:306
  10.3 11.8 %collective-permute-start = (bf16[48,1024]{1,0:T(8,128)(2,1)S(1)}, bf16[48,1024]{1,0:T(8,128)(2,1)S(1)}, u32[]{:S(2)}, u32[]{:S(2)}) collective-permute-start(bf16[48,1024]{1,0:T(8,128)(2,1)S(1)} %get-tuple-element.34.msg), channel_id=1, source_target_pairs={{0,1},{1,0},{2,3},{3,2},{4,5},{5,4},{6,7},{7,6},{8,9},{9,8},{10,11... | collective-permute-start | bytes 294920 | tf_op jit(solution)/shard_map/ppermute | solution.py:309
  10.3 11.8 %collective-permute-start.1 = (bf16[48,1024]{1,0:T(8,128)(2,1)S(1)}, bf16[48,1024]{1,0:T(8,128)(2,1)S(1)}, u32[]{:S(2)}, u32[]{:S(2)}) collective-permute-start(bf16[48,1024]{1,0:T(8,128)(2,1)S(1)} %get-tuple-element.34.msg), channel_id=1, source_target_pairs={{1,2},{3,4},{5,6},{7,8},{9,10},{11,12},{13,14},{15,16},{17,18},{19... | collective-permute-start | bytes 294920 | tf_op jit(solution)/shard_map/ppermute | solution.py:309
  11.0 11.1 %collective-permute-start.3 = (bf16[96,256]{1,0:T(8,128)(2,1)S(1)}, bf16[96,256]{1,0:T(8,128)(2,1)S(1)}, u32[]{:S(2)}, u32[]{:S(2)}) collective-permute-start(bf16[96,256]{1,0:T(8,128)(2,1)S(1)} %get-tuple-element.41), channel_id=1, source_target_pairs={{0,4},{1,5},{2,6},{3,7},{4,0},{5,1},{6,2},{7,3},{8,12},{9,13},{10,... | collective-permute-start | bytes 147464 | tf_op jit(solution)/shard_map/ppermute | solution.py:306
  13.9 8.1 %collective-permute-start.4 = (bf16[96,256]{1,0:T(8,128)(2,1)S(1)}, bf16[96,256]{1,0:T(8,128)(2,1)S(1)}, u32[]{:S(2)}, u32[]{:S(2)}) collective-permute-start(bf16[96,256]{1,0:T(8,128)(2,1)S(1)} %get-tuple-element.42), channel_id=1, source_target_pairs={{0,8},{1,9},{2,10},{3,11},{4,12},{5,13},{6,14},{7,15},{8,0},{9,1},... | collective-permute-start | bytes 147464 | tf_op jit(solution)/shard_map/ppermute | solution.py:306
  16.0 6.1 %collective-permute-start.5 = (bf16[96,256]{1,0:T(8,128)(2,1)S(1)}, bf16[96,256]{1,0:T(8,128)(2,1)S(1)}, u32[]{:S(2)}, u32[]{:S(2)}) collective-permute-start(bf16[96,256]{1,0:T(8,128)(2,1)S(1)} %get-tuple-element.43), channel_id=1, source_target_pairs={{0,16},{1,17},{2,18},{3,19},{4,20},{5,21},{6,22},{7,23},{8,24},{9,... | collective-permute-start | bytes 147464 | tf_op jit(solution)/shard_map/ppermute | solution.py:306
  22.1 0.8 %copy-start.1 = (f32[16,1024]{1,0:T(8,128)S(1)}, f32[16,1024]{1,0:T(8,128)}, u32[]{:S(2)}) copy-start(f32[16,1024]{1,0:T(8,128)} %rhs.1) | copy-start | bytes 196612
  31.3 11.1 %collective-permute-start.6 = (bf16[32,1024]{1,0:T(8,128)(2,1)S(1)}, bf16[32,1024]{1,0:T(8,128)(2,1)S(1)}, u32[]{:S(2)}, u32[]{:S(2)}) collective-permute-start(bf16[32,1024]{1,0:T(8,128)(2,1)S(1)} %get-tuple-element.44.refs_1_), channel_id=1, source_target_pairs={{0,1},{1,0},{2,3},{3,2},{4,5},{5,4},{6,7},{7,6},{8,9},{9,8},{10,11... | collective-permute-start | bytes 196616 | tf_op jit(solution)/shard_map/ppermute | solution.py:309
  31.3 11.1 %collective-permute-start.7 = (bf16[32,1024]{1,0:T(8,128)(2,1)S(1)}, bf16[32,1024]{1,0:T(8,128)(2,1)S(1)}, u32[]{:S(2)}, u32[]{:S(2)}) collective-permute-start(bf16[32,1024]{1,0:T(8,128)(2,1)S(1)} %get-tuple-element.44.refs_1_), channel_id=1, source_target_pairs={{1,2},{3,4},{5,6},{7,8},{9,10},{11,12},{13,14},{15,16},{17,18},{19... | collective-permute-start | bytes 196616 | tf_op jit(solution)/shard_map/ppermute | solution.py:309
  31.9 6.7 %collective-permute-start.10 = (bf16[32,256]{1,0:T(8,128)(2,1)S(1)}, bf16[32,256]{1,0:T(8,128)(2,1)S(1)}, u32[]{:S(2)}, u32[]{:S(2)}) collective-permute-start(bf16[32,256]{1,0:T(8,128)(2,1)S(1)} %get-tuple-element.55), channel_id=1, source_target_pairs={{0,8},{1,9},{2,10},{3,11},{4,12},{5,13},{6,14},{7,15},{8,0},{9,1},... | collective-permute-start | bytes 49160 | tf_op jit(solution)/shard_map/ppermute | solution.py:306
  36.3 4.6 %collective-permute-start.11 = (bf16[32,256]{1,0:T(8,128)(2,1)S(1)}, bf16[32,256]{1,0:T(8,128)(2,1)S(1)}, u32[]{:S(2)}, u32[]{:S(2)}) collective-permute-start(bf16[32,256]{1,0:T(8,128)(2,1)S(1)} %get-tuple-element.56), channel_id=1, source_target_pairs={{0,16},{1,17},{2,18},{3,19},{4,20},{5,21},{6,22},{7,23},{8,24},{9,... | collective-permute-start | bytes 49160 | tf_op jit(solution)/shard_map/ppermute | solution.py:306
  37.8 3.7 %collective-permute-start.8 = (bf16[32,256]{1,0:T(8,128)(2,1)S(1)}, bf16[32,256]{1,0:T(8,128)(2,1)S(1)}, u32[]{:S(2)}, u32[]{:S(2)}) collective-permute-start(bf16[32,256]{1,0:T(8,128)(2,1)S(1)} %get-tuple-element.53), channel_id=1, source_target_pairs={{0,2},{1,3},{2,0},{3,1},{4,6},{5,7},{6,4},{7,5},{8,10},{9,11},{10,... | collective-permute-start | bytes 49160 | tf_op jit(solution)/shard_map/ppermute | solution.py:306
  38.6 3.7 %collective-permute-start.9 = (bf16[32,256]{1,0:T(8,128)(2,1)S(1)}, bf16[32,256]{1,0:T(8,128)(2,1)S(1)}, u32[]{:S(2)}, u32[]{:S(2)}) collective-permute-start(bf16[32,256]{1,0:T(8,128)(2,1)S(1)} %get-tuple-element.54), channel_id=1, source_target_pairs={{0,4},{1,5},{2,6},{3,7},{4,0},{5,1},{6,2},{7,3},{8,12},{9,13},{10,... | collective-permute-start | bytes 49160 | tf_op jit(solution)/shard_map/ppermute | solution.py:306
  42.4 0.8 %copy-start.3 = (f32[16,1024]{1,0:T(8,128)S(1)}, f32[16,1024]{1,0:T(8,128)}, u32[]{:S(2)}) copy-start(f32[16,1024]{1,0:T(8,128)} %get-tuple-element.32.refs_13_) | copy-start | bytes 196612
  43.2 13.1 %copy-start.2 = (f32[16,1024]{1,0:T(8,128)S(1)}, f32[16,1024]{1,0:T(8,128)}, u32[]{:S(2)}) copy-start(f32[16,1024]{1,0:T(8,128)} %rhs.1) | copy-start | bytes 196612
  45.9 10.5 %all-to-all-start = ((f32[32,1,128]{2,1,0:T(1,128)}), f32[32,1,128]{2,1,0:T(1,128)S(1)}, u32[]{:S(2)}, u32[]{:S(2)}) async-start(f32[32,1,128]{2,1,0:T(1,128)} %bitcast.1), calls=%async_computation | async-start | bytes 32768 | tf_op jit(solution)/shard_map/all_to_all | solution.py:370

commit v2 on v1

v2 whole, which is shorter than its diff:
```python
import functools

import jax
import jax.numpy as jnp
from jax import lax
from jax.experimental import pallas as pl
from jax.experimental.pallas import tpu as pltpu
from jax.sharding import PartitionSpec as P

HALF = jnp.bfloat16
FULL = jnp.float32
LOG2_E = 1.4426950408889634
ROOT_THREE = 1.7320508075688772
TINY = 1e-30
SRC_ROWS = 32
MSG_ROWS = 64
VEC_ROWS = 48
TILE = 128
VMEM = pltpu.VMEM
SMEM = pltpu.SMEM


def split_two(value):
    high = value.astype(HALF)
    low = (value - high.astype(FULL)).astype(HALF)
    return high, low


def split_three(value):
    first = value.astype(HALF).astype(FULL)
    rest = value - first
    second = rest.astype(HALF).astype(FULL)
    third = (rest - second).astype(HALF).astype(FULL)
    return first, second, third


def rate_of(length):
    return ROOT_THREE / length


def matern(squared, rate):
    squared = jnp.maximum(squared, TINY)
    radius = squared * lax.rsqrt(squared)
    decay = jnp.exp2(radius * (-LOG2_E * rate))
    falling = radius * decay
    return decay + rate * falling, radius * falling


def excess(pts):
    total = jnp.full((1, pts.shape[1]), -1.0, FULL)
    lost = jnp.zeros_like(total)
    small = jnp.zeros_like(total)
    for axis in range(3):
        value = pts[axis : axis + 1, :]
        head = value.astype(HALF).astype(FULL)
        tail = value - head
        small = small + tail * tail
        for term in (head * head, 2.0 * head * tail):
            grown = total + term
            back = grown - total
            lost = lost + ((total - (grown - back)) + (term - back))
            total = grown
    return total + (lost + small)


def write_rows(buf, base, pts, source):
    over = excess(pts)
    first = over.astype(HALF).astype(FULL)
    second = over - first
    unit = jnp.ones_like(over)
    if source:
        rows = (unit, unit, unit, first, second)
        order = (0, 0, 0, 1, 1, 1, 2, 2, 2)
        pieces = split_three(pts)
    else:
        rows = (unit + unit, first, second, unit, unit)
        order = (0, 1, 2, 0, 1, 2, 0, 1, 2)
        pieces = split_three(-2.0 * pts)
    for slot, row in enumerate(rows):
        buf[base + slot : base + slot + 1, :] = row
    for slot, index in enumerate(order):
        start = base + 5 + 3 * slot
        buf[start : start + 3, :] = pieces[index]


def dot(a, b):
    return jnp.dot(a, b, preferred_element_type=FULL)


def dot_rows(a, b):
    return lax.dot_general(a, b, (((1,), (1,)), ((), ())), preferred_element_type=FULL)


def turned(value):
    return value.astype(FULL).T.astype(HALF)


def merged(both):
    return jnp.concatenate([both[0:16] + both[16:32], both[32:48]], axis=0)


def front_kernel(levels, *refs):
    far_length, pts_in, rhs_in, skel_in = refs[:4]
    msg, target, basis, skel_target, rhs = refs[4:9]
    lev = refs[9 : 9 + levels]
    buf, pair_buf, turned_src, pts, skel, sems = refs[9 + levels :]
    copies = [
        pltpu.make_async_copy(source, dest, sems.at[index])
        for index, (source, dest) in enumerate(((pts_in, pts), (skel_in, skel), (rhs_in, rhs)))
    ]
    for copy in copies:
        copy.start()
    copies[0].wait()
    points = pts[...]
    write_rows(buf, 0, points, False)
    target[...] = buf[...].astype(HALF)
    pair_buf[SRC_ROWS:, :] = buf[...].astype(HALF)
    write_rows(buf, 0, points, True)
    pair_buf[0:SRC_ROWS, :] = buf[...].astype(HALF)
    msg[32:64, :] = buf[...].astype(HALF)
    rows, rank = pts.shape[1], skel.shape[1]
    copies[1].wait()
    for level in range(levels):
        spot = lax.broadcasted_iota(jnp.int32, (rows, rank), 0)
        picks = jnp.where(spot == skel[level : level + 1, :], 1.0, 0.0).astype(HALF)
        both = dot(pair_buf[...], picks)
        skel_target[level] = both[SRC_ROWS:].astype(HALF)
        skel_source = both[:SRC_ROWS]
        lev[level][64:96, :] = skel_source.astype(HALF)
        turned_src[level * rank : (level + 1) * rank, :] = skel_source.T.astype(HALF)
    rate = rate_of(far_length[0])
    for col in range(0, rows, TILE):
        squared = dot(turned_src[...], target[:, col : col + TILE])
        basis[:, col : col + TILE] = matern(squared, rate)[0].astype(HALF)
    copies[2].wait()
    high, low = split_two(rhs[...])
    msg[0:16, :] = low
    msg[16:32, :] = high
    coef = merged(dot_rows(msg[0:VEC_ROWS, :], basis[...]))
    for level in range(levels):
        high, low = split_two(coef[:, level * rank : (level + 1) * rank])
        lev[level][0:32, :] = high
        lev[level][32:64, :] = low


def near_block(msg, target, turned_src, rate, kept):
    rows = target.shape[1]
    turned_src[...] = turned(msg[32:64, :])
    for col in range(0, rows, TILE):
        squared = dot(turned_src[...], target[:, col : col + TILE])
        value, slope = matern(squared, rate)
        value = value.astype(HALF)
        kept[:, col : col + TILE] = value
        pair = jnp.concatenate([value, slope.astype(HALF)], axis=1)
        total = dot(msg[0:VEC_ROWS, :], pair)
        yield slice(col, col + TILE), merged(total[:, :TILE]), total[16:32, TILE:]


def own_kernel(length, msg, target, kept, image, slopes, turned_src):
    for span, part, slope in near_block(msg, target, turned_src, rate_of(length[0]), kept):
        image[:, span] = part
        slopes[:, span] = slope


def side_kernel(levels, far_scale, *refs):
    length, far_length, signal, msg_a, msg_b, target, image, slopes, rhs, basis, skel_target = refs[:11]
    lev = refs[11 : 11 + levels]
    outs = refs[11 + levels :]
    kept_a, kept_b, coup_high, coup_low, row_sum, slope_image, slope_copy, first, wmsg = outs[:9]
    wlev = outs[9 : 9 + levels]
    turned_a, turned_b = outs[9 + levels :]
    rank = skel_target.shape[2]
    far_rate = rate_of(far_length[0])
    rate = rate_of(length[0])
    mixed = []
    for level in range(levels):
        squared = dot(turned(lev[level][64:96, :]), skel_target[level])
        high, low = split_two(matern(squared, far_rate)[0])
        coup_high[level] = high
        coup_low[level] = low
        both = dot(lev[level][0:64, :], high)
        part = both[0:32] + both[32:64] + dot(lev[level][0:32, :], low)
        mixed.append(jnp.concatenate(split_two(part), axis=0))
    far = dot(jnp.concatenate(mixed, axis=1), basis[...])
    far = far_scale * (far[0:32] + far[32:64])
    factor = signal[0] * (rate * rate)
    side_a = near_block(msg_a, target, turned_a, rate, kept_a)
    side_b = near_block(msg_b, target, turned_b, rate, kept_b)
    for (span, image_a, slopes_a), (_, image_b, slopes_b) in zip(side_a, side_b):
        slope = factor * (slopes[:, span] + slopes_a + slopes_b)
        slope_image[:, span] = slope
        slope_copy[:, span] = slope
        total = image[:, span] + image_a + image_b + far[:, span]
        sums = total[16:17, :]
        row_sum[:, span] = sums
        value = signal[0] * (total[0:16] + sums * rhs[:, span])
        first[:, span] = value
        high, low = split_two(value)
        wmsg[0:16, span] = high
        wmsg[16:32, span] = low
    both = dot_rows(wmsg[...], basis[...])
    high, low = split_two(both[0:16] + both[16:32])
    for level in range(levels):
        span = slice(level * rank, (level + 1) * rank)
        wlev[level][0:16, :] = high[:, span]
        wlev[level][16:32, :] = low[:, span]


def row_total(a, b):
    return jnp.sum(a * b, axis=1, keepdims=True)


def second_kernel(levels, far_scale, *refs):
    signal, wmsg, wmsg_a, wmsg_b, kept, kept_a, kept_b = refs[:7]
    basis, coup_high, coup_low, row_sum, first, rhs, slope_image = refs[7:14]
    wlev = refs[14 : 14 + levels]
    sums, first_rest, second_rest, shift_out = refs[14 + levels :]
    both = dot(wmsg[...], kept[...]) + dot(wmsg_a[...], kept_a[...]) + dot(wmsg_b[...], kept_b[...])
    pieces = []
    for level in range(levels):
        coef = wlev[level][...]
        mixed = dot(coef, coup_high[level])
        mixed = mixed[0:16] + mixed[16:32] + dot(coef[0:16], coup_low[level])
        pieces.append(jnp.concatenate(split_two(mixed), axis=0))
    both = both + far_scale * dot(jnp.concatenate(pieces, axis=1), basis[...])
    base = rhs[...]
    value = first[...]
    image = signal[0] * (both[0:16] + both[16:32] + row_sum[...] * value)
    weight = row_total(base, base)
    shift = jnp.where(weight > 0.0, row_total(base, value) / jnp.where(weight > 0.0, weight, 1.0), 0.0)
    value = value - shift * base
    image = image - (2.0 * shift) * value - (shift * shift) * base
    first_rest[...] = value
    second_rest[...] = image
    shift_out[...] = jnp.broadcast_to(shift, shift_out.shape)
    slope = slope_image[...]
    parts = (
        shift,
        weight,
        row_total(value, value),
        row_total(value, image),
        row_total(base, image),
        row_total(base, value),
        row_total(base, slope),
        row_total(value, slope),
    )
    lane = lax.broadcasted_iota(jnp.int32, (16, 128), 1)
    row = lax.broadcasted_iota(jnp.int32, (16, 128), 0)
    packed = jnp.zeros((16, 128), FULL)
    for slot, part in enumerate(parts):
        packed = jnp.where(lane == row + 16 * slot, part, packed)
    sums[...] = jnp.broadcast_to(jnp.sum(packed, axis=0, keepdims=True), sums.shape)


def last_kernel(point_total, noise, table, shift_in, first_rest, second_rest, rhs, out, res, trace):
    gathered = table[...]
    shift = gathered

    def slot(index):
        return pltpu.roll(gathered, 128 - 16 * index, 1)

    weight, ww, wz, rz, rw, rs, ws = (slot(index) for index in range(1, 8))

    def total(value):
        return jnp.sum(value, axis=0, keepdims=True)

    norm = total(weight)
    center = total(shift * weight + rw) / norm
    off = shift - center
    cross = total(rw + off * weight)
    square = total(ww + 2.0 * off * rw + off * off * weight)
    mixed = total(rz + 2.0 * off * rw + off * off * weight)
    second = total(
        wz + 2.0 * off * ww + off * off * rw + off * rz + 2.0 * off * off * rw + off * off * off * weight
    )
    held = total(rs)
    along = total(ws + off * rs)
    level = noise[0] + center
    lead = level * norm + cross
    alpha = norm / lead
    part = cross / lead
    norm_next = part * part * norm - 2.0 * part * alpha * cross + alpha * alpha * square
    lean = part + norm_next / norm
    direction = lean * lean * norm - 2.0 * lean * alpha * cross + alpha * alpha * square
    bend = lean * lean * cross - lean * alpha * (mixed + square) + alpha * alpha * second
    beta = norm_next / (level * direction + bend)
    trace[...] = (((alpha + beta * lean) * held - beta * alpha * along) / point_total)[:, 0:16]

    lane = lax.broadcasted_iota(jnp.int32, (16, 128), 1)
    row = lax.broadcasted_iota(jnp.int32, (16, 128), 0)

    def column(value):
        return jnp.sum(jnp.where(lane == row, value, 0.0), axis=1, keepdims=True)

    own_off = shift_in[:, 0:1] - column(center)
    base = rhs[...]
    rest = first_rest[...]
    value = rest + own_off * base
    image = second_rest[...] + (2.0 * own_off) * rest + (own_off * own_off) * base
    out[...] = column(alpha + beta * lean) * base - column(beta * alpha) * value
    res[...] = (
        column(part - beta * level * lean) * base
        - column(alpha - beta * level * alpha + beta * lean) * value
        + column(beta * alpha) * image
    )


def call(kernel, outs, spaces, scratch=(), flops=0):
    params = pltpu.CompilerParams(vmem_limit_bytes=40 * 2**20)
    cost = pl.CostEstimate(flops=flops, bytes_accessed=2**20, transcendentals=0)
    return pl.pallas_call(
        kernel,
        out_shape=[jax.ShapeDtypeStruct(shape, kind) for shape, kind in outs],
        in_specs=[pl.BlockSpec(memory_space=space) for space in spaces],
        out_specs=[pl.BlockSpec(memory_space=VMEM) for _ in outs],
        scratch_shapes=list(scratch),
        compiler_params=params,
        cost_estimate=cost,
    )


def shards(points, right_sides, skeleton, lengthscale, far_length, signal, noise_var):
    probes, rows = right_sides.shape
    levels, rank = skeleton.shape
    count = lax.axis_size("loc")
    far_scale = 1.0 / (rank * rank * levels)
    beside = [(i, i ^ 1) for i in range(count)]
    across = [(i, i + 1) for i in range(1, count - 1, 2)]
    across = across + [(j, i) for i, j in across]

    def partner(value, level):
        return lax.ppermute(value, "loc", [(i, i ^ (2 << level)) for i in range(count)])

    def sides(value):
        return lax.ppermute(value, "loc", beside), lax.ppermute(value, "loc", across)

    msg, target, basis, skel_target, rhs, *lev = call(
        functools.partial(front_kernel, levels),
        [
            ((MSG_ROWS, rows), HALF),
            ((SRC_ROWS, rows), HALF),
            ((levels * rank, rows), HALF),
            ((levels, SRC_ROWS, rank), HALF),
            ((probes, rows), FULL),
        ]
        + [((96, rank), HALF)] * levels,
        [SMEM] + [pltpu.HBM] * 3,
        [
            VMEM((SRC_ROWS, rows), FULL),
            VMEM((2 * SRC_ROWS, rows), HALF),
            VMEM((levels * rank, SRC_ROWS), HALF),
            VMEM(points.shape, FULL),
            VMEM(skeleton.shape, jnp.int32),
            pltpu.SemaphoreType.DMA((3,)),
        ],
    )(far_length, points, right_sides, skeleton)
    msg_a, msg_b = sides(msg)
    lev = [partner(value, level) for level, value in enumerate(lev)]
    kept, image, slopes = call(
        own_kernel,
        [((rows, rows), HALF), ((32, rows), FULL), ((probes, rows), FULL)],
        [SMEM] + [VMEM] * 2,
        [VMEM((rows, SRC_ROWS), HALF)],
    )(lengthscale, msg, target)
    kept_a, kept_b, coup_high, coup_low, row_sum, slope_image, slope_copy, first, wmsg, *wlev = call(
        functools.partial(side_kernel, levels, far_scale),
        [
            ((rows, rows), HALF),
            ((rows, rows), HALF),
            ((levels, rank, rank), HALF),
            ((levels, rank, rank), HALF),
            ((1, rows), FULL),
            ((probes, rows), FULL),
            ((probes, rows), FULL),
            ((probes, rows), FULL),
            ((2 * probes, rows), HALF),
        ]
        + [((2 * probes, rank), HALF)] * levels,
        [SMEM] * 3 + [VMEM] * (8 + levels),
        [VMEM((rows, SRC_ROWS), HALF)] * 2,
    )(lengthscale, far_length, signal, msg_a, msg_b, target, image, slopes, rhs, basis, skel_target, *lev)
    wmsg_a, wmsg_b = sides(wmsg)
    wlev = [partner(value, level) for level, value in enumerate(wlev)]
    sums, first_rest, second_rest, shift = call(
        functools.partial(second_kernel, levels, far_scale),
        [((count, 128), FULL), ((probes, rows), FULL), ((probes, rows), FULL), ((probes, 128), FULL)],
        [SMEM] + [VMEM] * (13 + levels),
    )(
        signal,
        wmsg,
        wmsg_a,
        wmsg_b,
        kept,
        kept_a,
        kept_b,
        basis,
        coup_high,
        coup_low,
        row_sum,
        first,
        rhs,
        slope_copy,
        *wlev,
    )
    table = lax.all_to_all(sums, "loc", 0, 0, tiled=True)
    solution, residual, trace = call(
        functools.partial(last_kernel, float(rows * count)),
        [((probes, rows), FULL), ((probes, rows), FULL), ((1, probes), FULL)],
        [SMEM] + [VMEM] * 5,
    )(noise_var, table, shift, first_rest, second_rest, rhs)
    return (solution, residual, slope_image, trace.reshape(probes))


def solution(mesh):
    placed = (P(None, "loc"), P(None, "loc"), P(None, "loc"), P(), P(), P(), P())
    return jax.shard_map(
        shards,
        mesh=mesh,
        in_specs=placed,
        out_specs=(P(None, "loc"), P(None, "loc"), P(None, "loc"), P()),
        check_vma=False,
    )
```

time: 57.7 us -> 56 us (0.971)
  Pallas kernels: 17.8 us -> 14.7 us
  starting transfers between devices: 22.6 us -> 25.7 us
  local copies, waits for them, and re-layouts: 3.92 us -> 2.24 us
    ppermute x8, starting transfers between devices: 17.9 us -> 20 us  [partner(): lax.ppermute(value, 'loc', [(i, i ^ 2 << level) for i in range(count)])]
    pallas_call x1, Pallas kernels: 8.31 us -> 6.25 us  [shards(): call(functools.partial(side_kernel, levels, far_scale), [((rows, rows), H...]
    unnamed x12 -> x6, local copies, waits for them, and re-layouts: 3.92 us -> 2.24 us
    pallas_call x1, Pallas kernels: 2.84 us -> 2.01 us  [shards(): call(own_kernel, [((rows, rows), HALF), ((32, rows), FULL), ((probes, row...]
    ppermute x2, starting transfers between devices: 0.01 us -> 0.67 us  [sides(): lax.ppermute(value, 'loc', beside)]
  transfers between devices with their start and end apart: 13 -> 13, of which waited for: 5 -> 5; matrix products, arithmetic and copies ran while one was open for 0% -> 0% of each run, Pallas kernels for 5% -> 4%
where the time goes in v2:
time: 56 us; the launch traced here: 55.6 us
  starting transfers between devices  25.7 us (46%)
  Pallas kernels  14.7 us (26%)
  waiting for transfers between devices  9.64 us (17%)
  between operations  3.32 us (6%)
  local copies, waits for them, and re-layouts  2.24 us (4%)
    ppermute x8, starting transfers between devices, partner(): lax.ppermute(value, 'loc', [(i, i ^ 2 << level) for i in range(count)])  20 us
    all_to_all x1, waiting for transfers between devices, shards(): table = lax.all_to_all(sums, 'loc', 0, 0, tiled=True)  6.43 us
    pallas_call x1, Pallas kernels, shards(): call(functools.partial(side_kernel, levels, far_scale), [((rows, rows), H...  6.25 us
    all_to_all x1, starting transfers between devices, shards(): table = lax.all_to_all(sums, 'loc', 0, 0, tiled=True)  3.7 us
    pallas_call x1, Pallas kernels, shards(): call(functools.partial(front_kernel, levels), [((MSG_ROWS, rows), HALF),...  3.2 us
    ppermute x8, waiting for transfers between devices, partner(): lax.ppermute(value, 'loc', [(i, i ^ 2 << level) for i in range(count)])  3.2 us
    pallas_call x1, Pallas kernels, shards(): call(functools.partial(second_kernel, levels, far_scale), [((count, 128),...  2.36 us
    unnamed x6, local copies, waits for them, and re-layouts  2.24 us
  transfers between devices with their start and end apart: 13, of which 5 were waited for; matrix products, arithmetic and copies ran while one was open for 0% of the time, Pallas kernels for 4%

profile of v2, /device:TPU:0, one launch (start us, length us, event | category | flops | bytes accessed | tf_op | source)
XLA Modules:
  0.0 55.6 jit_solution(1887015098206667363)
XLA Ops:
  1.3 0.8 %copy-done = f32[16,1024]{1,0:T(8,128)S(1)} copy-done((f32[16,1024]{1,0:T(8,128)S(1)}, f32[16,1024]{1,0:T(8,128)}, u32[]{:S(2)}) %copy-start) | copy-done | bytes 65560
  2.1 0.7 %copy-done.1 = f32[3,1024]{1,0:T(4,128)S(1)} copy-done((f32[3,1024]{1,0:T(4,128)S(1)}, f32[3,1024]{1,0:T(4,128)}, u32[]{:S(2)}) %copy-start.1) | copy-done | bytes 12312
  2.8 0.7 %copy-done.2 = s32[4,256]{1,0:T(4,128)S(1)} copy-done((s32[4,256]{1,0:T(4,128)S(1)}, s32[4,256]{1,0:T(4,128)}, u32[]{:S(2)}) %copy-start.2) | copy-done | bytes 4120
  3.5 3.2 %shard_map.102 = (bf16[64,1024]{1,0:T(8,128)(2,1)S(1)}, bf16[32,1024]{1,0:T(8,128)(2,1)S(1)}, bf16[1024,1024]{1,0:T(8,128)(2,1)S(1)}, bf16[4,32,256]{2,1,0:T(8,1...) custom-call(f32[1]{0:T(128)S(6)} %copy.13.refs_0_.refs_1_, ...), custom_call_target="tpu_custom_call" | custom-call | bytes 1048576 | tf_op jit(solution)/shard_map/pallas_call | solution.py:337
  7.3 0.7 %collective-permute-start.1 = (bf16[64,1024]{1,0:T(8,128)(2,1)S(1)}, bf16[64,1024]{1,0:T(8,128)(2,1)S(1)}, u32[]{:S(2)}, u32[]{:S(2)}) collective-permute-start(bf16[64,1024]{1,0:T(8,128)(2,1)S(1)} %get-tuple-element.36.msg), channel_id=1, source_target_pairs={{1,2},{3,4},{5,6},{7,8},{9,10},{11,12},{13,14},{15,16},{17,18},{19... | collective-permute-start | bytes 393224 | tf_op jit(solution)/shard_map/ppermute | solution.py:335
  7.9 3.8 %collective-permute-start.2 = (bf16[96,256]{1,0:T(8,128)(2,1)S(1)}, bf16[96,256]{1,0:T(8,128)(2,1)S(1)}, u32[]{:S(2)}, u32[]{:S(2)}) collective-permute-start(bf16[96,256]{1,0:T(8,128)(2,1)S(1)} %get-tuple-element.43), channel_id=1, source_target_pairs={{0,2},{1,3},{2,0},{3,1},{4,6},{5,7},{6,4},{7,5},{8,10},{9,11},{10,... | collective-permute-start | bytes 147464 | tf_op jit(solution)/shard_map/ppermute | solution.py:332
  11.7 2.1 %collective-permute-start.3 = (bf16[96,256]{1,0:T(8,128)(2,1)S(1)}, bf16[96,256]{1,0:T(8,128)(2,1)S(1)}, u32[]{:S(2)}, u32[]{:S(2)}) collective-permute-start(bf16[96,256]{1,0:T(8,128)(2,1)S(1)} %get-tuple-element.44), channel_id=1, source_target_pairs={{0,4},{1,5},{2,6},{3,7},{4,0},{5,1},{6,2},{7,3},{8,12},{9,13},{10,... | collective-permute-start | bytes 147464 | tf_op jit(solution)/shard_map/ppermute | solution.py:332
  13.9 1.6 %collective-permute-start.4 = (bf16[96,256]{1,0:T(8,128)(2,1)S(1)}, bf16[96,256]{1,0:T(8,128)(2,1)S(1)}, u32[]{:S(2)}, u32[]{:S(2)}) collective-permute-start(bf16[96,256]{1,0:T(8,128)(2,1)S(1)} %get-tuple-element.45), channel_id=1, source_target_pairs={{0,8},{1,9},{2,10},{3,11},{4,12},{5,13},{6,14},{7,15},{8,0},{9,1},... | collective-permute-start | bytes 147464 | tf_op jit(solution)/shard_map/ppermute | solution.py:332
  15.5 0.7 %collective-permute-done.2.refs_11_ = bf16[96,256]{1,0:T(8,128)(2,1)S(1)} collective-permute-done((bf16[96,256]{1,0:T(8,128)(2,1)S(1)}, bf16[96,256]{1,0:T(8,128)(2,1)S(1)}, u32[]{:S(2)}, u32[]{:S(2)}) %collective-permute-start.2) | collective-permute-done | bytes 49184 | tf_op jit(solution)/shard_map/ppermute | solution.py:332
  16.2 3.8 %collective-permute-start.5 = (bf16[96,256]{1,0:T(8,128)(2,1)S(1)}, bf16[96,256]{1,0:T(8,128)(2,1)S(1)}, u32[]{:S(2)}, u32[]{:S(2)}) collective-permute-start(bf16[96,256]{1,0:T(8,128)(2,1)S(1)} %get-tuple-element.46), channel_id=1, source_target_pairs={{0,16},{1,17},{2,18},{3,19},{4,20},{5,21},{6,22},{7,23},{8,24},{9,... | collective-permute-start | bytes 147464 | tf_op jit(solution)/shard_map/ppermute | solution.py:332
  21.3 2.0 %shard_map.103 = (bf16[1024,1024]{1,0:T(8,128)(2,1)S(1)}, f32[32,1024]{1,0:T(8,128)S(1)}, f32[16,1024]{1,0:T(8,128)S(1)}) custom-call(f32[1]{0:T(128)S(6)} %copy.12.length.refs_0_, bf16[64,1024]{1,0:T(8,128)(2,1)S(1)} %get-tuple-element.36.msg, bf16[32,1024]{1,0:T(8,128)(2,1)S(1)} %get-tuple-element.37.target.refs_5_), custom_call_target="tpu_custom_call" | custom-call | bytes 1048576 | tf_op jit(solution)/shard_map/pallas_call | solution.py:359
  23.4 6.2 %shard_map.104 = (bf16[1024,1024]{1,0:T(8,128)(2,1)S(1)}, bf16[1024,1024]{1,0:T(8,128)(2,1)S(1)}, bf16[4,256,256]{2,1,0:T(8,128)(2,1)S(1)}, bf16[4,256,256]{2,1,...) custom-call(f32[1]{0:T(128)S(6)} %copy.12.length.refs_0_, ...), custom_call_target="tpu_custom_call" | custom-call | bytes 1048576 | tf_op jit(solution)/shard_map/pallas_call | solution.py:365
  29.8 0.7 %collective-permute-start.7 = (bf16[32,1024]{1,0:T(8,128)(2,1)S(1)}, bf16[32,1024]{1,0:T(8,128)(2,1)S(1)}, u32[]{:S(2)}, u32[]{:S(2)}) collective-permute-start(bf16[32,1024]{1,0:T(8,128)(2,1)S(1)} %get-tuple-element.47.refs_1_), channel_id=1, source_target_pairs={{1,2},{3,4},{5,6},{7,8},{9,10},{11,12},{13,14},{15,16},{17,18},{19... | collective-permute-start | bytes 196616 | tf_op jit(solution)/shard_map/ppermute | solution.py:335
  30.4 4.8 %collective-permute-start.10 = (bf16[32,256]{1,0:T(8,128)(2,1)S(1)}, bf16[32,256]{1,0:T(8,128)(2,1)S(1)}, u32[]{:S(2)}, u32[]{:S(2)}) collective-permute-start(bf16[32,256]{1,0:T(8,128)(2,1)S(1)} %get-tuple-element.58), channel_id=1, source_target_pairs={{0,8},{1,9},{2,10},{3,11},{4,12},{5,13},{6,14},{7,15},{8,0},{9,1},... | collective-permute-start | bytes 49160 | tf_op jit(solution)/shard_map/ppermute | solution.py:332
  35.2 1.6 %collective-permute-start.11 = (bf16[32,256]{1,0:T(8,128)(2,1)S(1)}, bf16[32,256]{1,0:T(8,128)(2,1)S(1)}, u32[]{:S(2)}, u32[]{:S(2)}) collective-permute-start(bf16[32,256]{1,0:T(8,128)(2,1)S(1)} %get-tuple-element.59), channel_id=1, source_target_pairs={{0,16},{1,17},{2,18},{3,19},{4,20},{5,21},{6,22},{7,23},{8,24},{9,... | collective-permute-start | bytes 49160 | tf_op jit(solution)/shard_map/ppermute | solution.py:332
  36.9 1.0 %collective-permute-start.8 = (bf16[32,256]{1,0:T(8,128)(2,1)S(1)}, bf16[32,256]{1,0:T(8,128)(2,1)S(1)}, u32[]{:S(2)}, u32[]{:S(2)}) collective-permute-start(bf16[32,256]{1,0:T(8,128)(2,1)S(1)} %get-tuple-element.56), channel_id=1, source_target_pairs={{0,2},{1,3},{2,0},{3,1},{4,6},{5,7},{6,4},{7,5},{8,10},{9,11},{10,... | collective-permute-start | bytes 49160 | tf_op jit(solution)/shard_map/ppermute | solution.py:332
  37.8 1.3 %collective-permute-start.9 = (bf16[32,256]{1,0:T(8,128)(2,1)S(1)}, bf16[32,256]{1,0:T(8,128)(2,1)S(1)}, u32[]{:S(2)}, u32[]{:S(2)}) collective-permute-start(bf16[32,256]{1,0:T(8,128)(2,1)S(1)} %get-tuple-element.57), channel_id=1, source_target_pairs={{0,4},{1,5},{2,6},{3,7},{4,0},{5,1},{6,2},{7,3},{8,12},{9,13},{10,... | collective-permute-start | bytes 49160 | tf_op jit(solution)/shard_map/ppermute | solution.py:332
  39.1 0.8 %collective-permute-done.11.refs_17_ = bf16[32,256]{1,0:T(8,128)(2,1)S(1)} collective-permute-done((bf16[32,256]{1,0:T(8,128)(2,1)S(1)}, bf16[32,256]{1,0:T(8,128)(2,1)S(1)}, u32[]{:S(2)}, u32[]{:S(2)}) %collective-permute-start.11) | collective-permute-done | bytes 16416 | tf_op jit(solution)/shard_map/ppermute | solution.py:332
  39.9 0.7 %collective-permute-done.8.refs_14_ = bf16[32,256]{1,0:T(8,128)(2,1)S(1)} collective-permute-done((bf16[32,256]{1,0:T(8,128)(2,1)S(1)}, bf16[32,256]{1,0:T(8,128)(2,1)S(1)}, u32[]{:S(2)}, u32[]{:S(2)}) %collective-permute-start.8) | collective-permute-done | bytes 16416 | tf_op jit(solution)/shard_map/ppermute | solution.py:332
  40.6 1.0 %collective-permute-done.9.refs_15_ = bf16[32,256]{1,0:T(8,128)(2,1)S(1)} collective-permute-done((bf16[32,256]{1,0:T(8,128)(2,1)S(1)}, bf16[32,256]{1,0:T(8,128)(2,1)S(1)}, u32[]{:S(2)}, u32[]{:S(2)}) %collective-permute-start.9) | collective-permute-done | bytes 16416 | tf_op jit(solution)/shard_map/ppermute | solution.py:332
  41.6 2.4 %shard_map.105 = (f32[32,128]{1,0:T(8,128)}, f32[16,1024]{1,0:T(8,128)S(1)}, f32[16,1024]{1,0:T(8,128)S(1)}, f32[16,128]{1,0:T(8,128)S(1)}) custom-call(f32[1]{0:T(128)S(6)} %copy.14.refs_2_.refs_0_, bf16[32,1024]{1,0:T(8,128)(2,1)S(1)} %get-tuple-element.47.refs_1_, bf16[32,1024]{1,0:T(8,128)(2,1)S(1)} %collective-permute-done.6.refs_2_, ...), custom_call_target="tpu_custom_call" | custom-call | bytes 1048576 | tf_op jit(solution)/shard_map/pallas_call | solution.py:384
  43.9 3.7 %all-to-all-start = ((f32[32,1,128]{2,1,0:T(1,128)}), f32[32,1,128]{2,1,0:T(1,128)S(1)}, u32[]{:S(2)}, u32[]{:S(2)}) async-start(f32[32,1,128]{2,1,0:T(1,128)} %bitcast.1), calls=%async_computation | async-start | bytes 32768 | tf_op jit(solution)/shard_map/all_to_all | solution.py:405
  48.3 6.4 %all-to-all-done = f32[32,1,128]{2,1,0:T(1,128)S(1)} async-done(((f32[32,1,128]{2,1,0:T(1,128)}), f32[32,1,128]{2,1,0:T(1,128)S(1)}, u32[]{:S(2)}, u32[]{:S(2)}) %all-to-all-start) | async-done | bytes 16416 | tf_op jit(solution)/shard_map/all_to_all | solution.py:405
  54.7 0.9 %shard_map.106 = (f32[16,1024]{1,0:T(8,128)}, f32[16,1024]{1,0:T(8,128)}, f32[1,16]{1,0:T(1,128)}) custom-call(f32[1]{0:T(128)S(6)} %copy.15.noise, f32[32,128]{1,0:T(8,128)S(1)} %bitcast.5, f32[16,128]{1,0:T(8,128)S(1)} %get-tuple-element.61.shift_in, f32[16,1024]{1,0:T(8,128)S(1)} %get-tuple-element.62.first_rest, ...), custom_call_target="tpu_custom_call" | custom-call | bytes 1048576 | tf_op jit(solution)/shard_map/pallas_call | solution.py:406
  (13 shorter events, 0.7 us)
Async XLA Ops:
  1.3 0.8 %copy-start = (f32[16,1024]{1,0:T(8,128)S(1)}, f32[16,1024]{1,0:T(8,128)}, u32[]{:S(2)}) copy-start(f32[16,1024]{1,0:T(8,128)} %refs_2_.2) | copy-start | bytes 196612
  2.1 0.7 %copy-start.1 = (f32[3,1024]{1,0:T(4,128)S(1)}, f32[3,1024]{1,0:T(4,128)}, u32[]{:S(2)}) copy-start(f32[3,1024]{1,0:T(4,128)} %refs_1_.2) | copy-start | bytes 36868
  2.8 0.7 %copy-start.2 = (s32[4,256]{1,0:T(4,128)S(1)}, s32[4,256]{1,0:T(4,128)}, u32[]{:S(2)}) copy-start(s32[4,256]{1,0:T(4,128)} %refs_3_.1) | copy-start | bytes 12292
  6.7 16.6 %collective-permute-start = (bf16[64,1024]{1,0:T(8,128)(2,1)S(1)}, bf16[64,1024]{1,0:T(8,128)(2,1)S(1)}, u32[]{:S(2)}, u32[]{:S(2)}) collective-permute-start(bf16[64,1024]{1,0:T(8,128)(2,1)S(1)} %get-tuple-element.36.msg), channel_id=1, source_target_pairs={{0,1},{1,0},{2,3},{3,2},{4,5},{5,4},{6,7},{7,6},{8,9},{9,8},{10,11... | collective-permute-start | bytes 393224 | tf_op jit(solution)/shard_map/ppermute | solution.py:335
  7.3 16.1 %collective-permute-start.1 = (bf16[64,1024]{1,0:T(8,128)(2,1)S(1)}, bf16[64,1024]{1,0:T(8,128)(2,1)S(1)}, u32[]{:S(2)}, u32[]{:S(2)}) collective-permute-start(bf16[64,1024]{1,0:T(8,128)(2,1)S(1)} %get-tuple-element.36.msg), channel_id=1, source_target_pairs={{1,2},{3,4},{5,6},{7,8},{9,10},{11,12},{13,14},{15,16},{17,18},{19... | collective-permute-start | bytes 393224 | tf_op jit(solution)/shard_map/ppermute | solution.py:335
  7.9 8.2 %collective-permute-start.2 = (bf16[96,256]{1,0:T(8,128)(2,1)S(1)}, bf16[96,256]{1,0:T(8,128)(2,1)S(1)}, u32[]{:S(2)}, u32[]{:S(2)}) collective-permute-start(bf16[96,256]{1,0:T(8,128)(2,1)S(1)} %get-tuple-element.43), channel_id=1, source_target_pairs={{0,2},{1,3},{2,0},{3,1},{4,6},{5,7},{6,4},{7,5},{8,10},{9,11},{10,... | collective-permute-start | bytes 147464 | tf_op jit(solution)/shard_map/ppermute | solution.py:332
  11.7 11.6 %collective-permute-start.3 = (bf16[96,256]{1,0:T(8,128)(2,1)S(1)}, bf16[96,256]{1,0:T(8,128)(2,1)S(1)}, u32[]{:S(2)}, u32[]{:S(2)}) collective-permute-start(bf16[96,256]{1,0:T(8,128)(2,1)S(1)} %get-tuple-element.44), channel_id=1, source_target_pairs={{0,4},{1,5},{2,6},{3,7},{4,0},{5,1},{6,2},{7,3},{8,12},{9,13},{10,... | collective-permute-start | bytes 147464 | tf_op jit(solution)/shard_map/ppermute | solution.py:332
  13.9 9.5 %collective-permute-start.4 = (bf16[96,256]{1,0:T(8,128)(2,1)S(1)}, bf16[96,256]{1,0:T(8,128)(2,1)S(1)}, u32[]{:S(2)}, u32[]{:S(2)}) collective-permute-start(bf16[96,256]{1,0:T(8,128)(2,1)S(1)} %get-tuple-element.45), channel_id=1, source_target_pairs={{0,8},{1,9},{2,10},{3,11},{4,12},{5,13},{6,14},{7,15},{8,0},{9,1},... | collective-permute-start | bytes 147464 | tf_op jit(solution)/shard_map/ppermute | solution.py:332
  16.2 7.2 %collective-permute-start.5 = (bf16[96,256]{1,0:T(8,128)(2,1)S(1)}, bf16[96,256]{1,0:T(8,128)(2,1)S(1)}, u32[]{:S(2)}, u32[]{:S(2)}) collective-permute-start(bf16[96,256]{1,0:T(8,128)(2,1)S(1)} %get-tuple-element.46), channel_id=1, source_target_pairs={{0,16},{1,17},{2,18},{3,19},{4,20},{5,21},{6,22},{7,23},{8,24},{9,... | collective-permute-start | bytes 147464 | tf_op jit(solution)/shard_map/ppermute | solution.py:332
  29.6 11.9 %collective-permute-start.6 = (bf16[32,1024]{1,0:T(8,128)(2,1)S(1)}, bf16[32,1024]{1,0:T(8,128)(2,1)S(1)}, u32[]{:S(2)}, u32[]{:S(2)}) collective-permute-start(bf16[32,1024]{1,0:T(8,128)(2,1)S(1)} %get-tuple-element.47.refs_1_), channel_id=1, source_target_pairs={{0,1},{1,0},{2,3},{3,2},{4,5},{5,4},{6,7},{7,6},{8,9},{9,8},{10,11... | collective-permute-start | bytes 196616 | tf_op jit(solution)/shard_map/ppermute | solution.py:335
  29.8 11.8 %collective-permute-start.7 = (bf16[32,1024]{1,0:T(8,128)(2,1)S(1)}, bf16[32,1024]{1,0:T(8,128)(2,1)S(1)}, u32[]{:S(2)}, u32[]{:S(2)}) collective-permute-start(bf16[32,1024]{1,0:T(8,128)(2,1)S(1)} %get-tuple-element.47.refs_1_), channel_id=1, source_target_pairs={{1,2},{3,4},{5,6},{7,8},{9,10},{11,12},{13,14},{15,16},{17,18},{19... | collective-permute-start | bytes 196616 | tf_op jit(solution)/shard_map/ppermute | solution.py:335
  30.4 7.4 %collective-permute-start.10 = (bf16[32,256]{1,0:T(8,128)(2,1)S(1)}, bf16[32,256]{1,0:T(8,128)(2,1)S(1)}, u32[]{:S(2)}, u32[]{:S(2)}) collective-permute-start(bf16[32,256]{1,0:T(8,128)(2,1)S(1)} %get-tuple-element.58), channel_id=1, source_target_pairs={{0,8},{1,9},{2,10},{3,11},{4,12},{5,13},{6,14},{7,15},{8,0},{9,1},... | collective-permute-start | bytes 49160 | tf_op jit(solution)/shard_map/ppermute | solution.py:332
  35.2 4.6 %collective-permute-start.11 = (bf16[32,256]{1,0:T(8,128)(2,1)S(1)}, bf16[32,256]{1,0:T(8,128)(2,1)S(1)}, u32[]{:S(2)}, u32[]{:S(2)}) collective-permute-start(bf16[32,256]{1,0:T(8,128)(2,1)S(1)} %get-tuple-element.59), channel_id=1, source_target_pairs={{0,16},{1,17},{2,18},{3,19},{4,20},{5,21},{6,22},{7,23},{8,24},{9,... | collective-permute-start | bytes 49160 | tf_op jit(solution)/shard_map/ppermute | solution.py:332
  36.9 3.7 %collective-permute-start.8 = (bf16[32,256]{1,0:T(8,128)(2,1)S(1)}, bf16[32,256]{1,0:T(8,128)(2,1)S(1)}, u32[]{:S(2)}, u32[]{:S(2)}) collective-permute-start(bf16[32,256]{1,0:T(8,128)(2,1)S(1)} %get-tuple-element.56), channel_id=1, source_target_pairs={{0,2},{1,3},{2,0},{3,1},{4,6},{5,7},{6,4},{7,5},{8,10},{9,11},{10,... | collective-permute-start | bytes 49160 | tf_op jit(solution)/shard_map/ppermute | solution.py:332
  37.8 3.7 %collective-permute-start.9 = (bf16[32,256]{1,0:T(8,128)(2,1)S(1)}, bf16[32,256]{1,0:T(8,128)(2,1)S(1)}, u32[]{:S(2)}, u32[]{:S(2)}) collective-permute-start(bf16[32,256]{1,0:T(8,128)(2,1)S(1)} %get-tuple-element.57), channel_id=1, source_target_pairs={{0,4},{1,5},{2,6},{3,7},{4,0},{5,1},{6,2},{7,3},{8,12},{9,13},{10,... | collective-permute-start | bytes 49160 | tf_op jit(solution)/shard_map/ppermute | solution.py:332
  43.9 10.8 %all-to-all-start = ((f32[32,1,128]{2,1,0:T(1,128)}), f32[32,1,128]{2,1,0:T(1,128)S(1)}, u32[]{:S(2)}, u32[]{:S(2)}) async-start(f32[32,1,128]{2,1,0:T(1,128)} %bitcast.1), calls=%async_computation | async-start | bytes 32768 | tf_op jit(solution)/shard_map/all_to_all | solution.py:405

commit v3 on v2

--- a/solution.py
+++ b/solution.py
@@ -12,6 +12,7 @@
 LOG2_E = 1.4426950408889634
 ROOT_THREE = 1.7320508075688772
 TINY = 1e-30
+SCALE = 2.0**-10
 SRC_ROWS = 32
 MSG_ROWS = 64
 VEC_ROWS = 48
@@ -34,14 +35,11 @@
     return first, second, third
 
 
-def rate_of(length):
-    return ROOT_THREE / length
-
-
-def matern(squared, rate):
+def matern(squared, rates):
+    rate, falling_rate = rates
     squared = jnp.maximum(squared, TINY)
     radius = squared * lax.rsqrt(squared)
-    decay = jnp.exp2(radius * (-LOG2_E * rate))
+    decay = jnp.exp2(radius * falling_rate)
     falling = radius * decay
     return decay + rate * falling, radius * falling
 
@@ -100,40 +98,35 @@
 
 
 def front_kernel(levels, *refs):
-    far_length, pts_in, rhs_in, skel_in = refs[:4]
-    msg, target, basis, skel_target, rhs = refs[4:9]
-    lev = refs[9 : 9 + levels]
-    buf, pair_buf, turned_src, pts, skel, sems = refs[9 + levels :]
-    copies = [
-        pltpu.make_async_copy(source, dest, sems.at[index])
-        for index, (source, dest) in enumerate(((pts_in, pts), (skel_in, skel), (rhs_in, rhs)))
-    ]
-    for copy in copies:
-        copy.start()
-    copies[0].wait()
-    points = pts[...]
+    length, far_length, given = refs[:3]
+    msg, target, basis, skel_target, numbers = refs[3:8]
+    lev = refs[8 : 8 + levels]
+    buf, pair_buf, turned_src = refs[8 + levels :]
+    points = given[16:19, :]
+    for slot, value in enumerate((length[0], far_length[0])):
+        lengths = jnp.full((1, 128), value, FULL)
+        numbers[slot : slot + 1, :] = ROOT_THREE / lengths
+        numbers[slot + 2 : slot + 3, :] = (-LOG2_E * ROOT_THREE) / lengths
     write_rows(buf, 0, points, False)
     target[...] = buf[...].astype(HALF)
     pair_buf[SRC_ROWS:, :] = buf[...].astype(HALF)
     write_rows(buf, 0, points, True)
     pair_buf[0:SRC_ROWS, :] = buf[...].astype(HALF)
     msg[32:64, :] = buf[...].astype(HALF)
-    rows, rank = pts.shape[1], skel.shape[1]
-    copies[1].wait()
+    rows, rank = points.shape[1], skel_target.shape[2]
     for level in range(levels):
-        spot = lax.broadcasted_iota(jnp.int32, (rows, rank), 0)
-        picks = jnp.where(spot == skel[level : level + 1, :], 1.0, 0.0).astype(HALF)
+        spot = lax.broadcasted_iota(jnp.int32, (rows, rank), 0).astype(FULL)
+        picks = jnp.where(spot == given[24 + level : 25 + level, 0:rank], 1.0, 0.0).astype(HALF)
         both = dot(pair_buf[...], picks)
         skel_target[level] = both[SRC_ROWS:].astype(HALF)
         skel_source = both[:SRC_ROWS]
         lev[level][64:96, :] = skel_source.astype(HALF)
         turned_src[level * rank : (level + 1) * rank, :] = skel_source.T.astype(HALF)
-    rate = rate_of(far_length[0])
+    rates = numbers[1:2, :], numbers[3:4, :]
     for col in range(0, rows, TILE):
         squared = dot(turned_src[...], target[:, col : col + TILE])
-        basis[:, col : col + TILE] = matern(squared, rate)[0].astype(HALF)
-    copies[2].wait()
-    high, low = split_two(rhs[...])
+        basis[:, col : col + TILE] = matern(squared, rates)[0].astype(HALF)
+    high, low = split_two(given[0:16, :])
     msg[0:16, :] = low
     msg[16:32, :] = high
     coef = merged(dot_rows(msg[0:VEC_ROWS, :], basis[...]))
@@ -143,12 +136,12 @@
         lev[level][32:64, :] = low
 
 
-def near_block(msg, target, turned_src, rate, kept):
+def near_block(msg, target, turned_src, rates, kept):
     rows = target.shape[1]
     turned_src[...] = turned(msg[32:64, :])
     for col in range(0, rows, TILE):
         squared = dot(turned_src[...], target[:, col : col + TILE])
-        value, slope = matern(squared, rate)
+        value, slope = matern(squared, rates)
         value = value.astype(HALF)
         kept[:, col : col + TILE] = value
         pair = jnp.concatenate([value, slope.astype(HALF)], axis=1)
@@ -156,26 +149,27 @@
         yield slice(col, col + TILE), merged(total[:, :TILE]), total[16:32, TILE:]
 
 
-def own_kernel(length, msg, target, kept, image, slopes, turned_src):
-    for span, part, slope in near_block(msg, target, turned_src, rate_of(length[0]), kept):
+def own_kernel(numbers, msg, target, kept, image, slopes, turned_src):
+    rates = numbers[0:1, :], numbers[2:3, :]
+    for span, part, slope in near_block(msg, target, turned_src, rates, kept):
         image[:, span] = part
         slopes[:, span] = slope
 
 
 def side_kernel(levels, far_scale, *refs):
-    length, far_length, signal, msg_a, msg_b, target, image, slopes, rhs, basis, skel_target = refs[:11]
-    lev = refs[11 : 11 + levels]
-    outs = refs[11 + levels :]
-    kept_a, kept_b, coup_high, coup_low, row_sum, slope_image, slope_copy, first, wmsg = outs[:9]
-    wlev = outs[9 : 9 + levels]
-    turned_a, turned_b = outs[9 + levels :]
+    numbers, msg_a, msg_b, target, image, slopes, given, basis, skel_target = refs[:9]
+    lev = refs[9 : 9 + levels]
+    outs = refs[9 + levels :]
+    kept_a, kept_b, coup_high, coup_low, row_sum, slope_sum, first, wmsg = outs[:8]
+    wlev = outs[8 : 8 + levels]
+    turned_a, turned_b = outs[8 + levels :]
     rank = skel_target.shape[2]
-    far_rate = rate_of(far_length[0])
-    rate = rate_of(length[0])
+    rates = numbers[0:1, :], numbers[2:3, :]
+    far_rates = [jnp.concatenate([numbers[row : row + 1, :]] * (rank // 128), axis=1) for row in (1, 3)]
     mixed = []
     for level in range(levels):
         squared = dot(turned(lev[level][64:96, :]), skel_target[level])
-        high, low = split_two(matern(squared, far_rate)[0])
+        high, low = split_two(matern(squared, far_rates)[0])
         coup_high[level] = high
         coup_low[level] = low
         both = dot(lev[level][0:64, :], high)
@@ -183,17 +177,14 @@
         mixed.append(jnp.concatenate(split_two(part), axis=0))
     far = dot(jnp.concatenate(mixed, axis=1), basis[...])
     far = far_scale * (far[0:32] + far[32:64])
-    factor = signal[0] * (rate * rate)
-    side_a = near_block(msg_a, target, turned_a, rate, kept_a)
-    side_b = near_block(msg_b, target, turned_b, rate, kept_b)
+    side_a = near_block(msg_a, target, turned_a, rates, kept_a)
+    side_b = near_block(msg_b, target, turned_b, rates, kept_b)
     for (span, image_a, slopes_a), (_, image_b, slopes_b) in zip(side_a, side_b):
-        slope = factor * (slopes[:, span] + slopes_a + slopes_b)
-        slope_image[:, span] = slope
-        slope_copy[:, span] = slope
+        slope_sum[:, span] = slopes[:, span] + slopes_a + slopes_b
         total = image[:, span] + image_a + image_b + far[:, span]
         sums = total[16:17, :]
         row_sum[:, span] = sums
-        value = signal[0] * (total[0:16] + sums * rhs[:, span])
+        value = SCALE * (total[0:16] + sums * given[0:16, span])
         first[:, span] = value
         high, low = split_two(value)
         wmsg[0:16, span] = high
@@ -211,10 +202,10 @@
 
 
 def second_kernel(levels, far_scale, *refs):
-    signal, wmsg, wmsg_a, wmsg_b, kept, kept_a, kept_b = refs[:7]
-    basis, coup_high, coup_low, row_sum, first, rhs, slope_image = refs[7:14]
-    wlev = refs[14 : 14 + levels]
-    sums, first_rest, second_rest, shift_out = refs[14 + levels :]
+    wmsg, wmsg_a, wmsg_b, kept, kept_a, kept_b = refs[:6]
+    basis, coup_high, coup_low, row_sum, first, given, slope_sum = refs[6:13]
+    wlev = refs[13 : 13 + levels]
+    sums, first_rest, second_rest, shift_out = refs[13 + levels :]
     both = dot(wmsg[...], kept[...]) + dot(wmsg_a[...], kept_a[...]) + dot(wmsg_b[...], kept_b[...])
     pieces = []
     for level in range(levels):
@@ -223,9 +214,9 @@
         mixed = mixed[0:16] + mixed[16:32] + dot(coef[0:16], coup_low[level])
         pieces.append(jnp.concatenate(split_two(mixed), axis=0))
     both = both + far_scale * dot(jnp.concatenate(pieces, axis=1), basis[...])
-    base = rhs[...]
+    base = given[0:16, :]
     value = first[...]
-    image = signal[0] * (both[0:16] + both[16:32] + row_sum[...] * value)
+    image = SCALE * (both[0:16] + both[16:32] + row_sum[...] * value)
     weight = row_total(base, base)
     shift = jnp.where(weight > 0.0, row_total(base, value) / jnp.where(weight > 0.0, weight, 1.0), 0.0)
     value = value - shift * base
@@ -233,7 +224,7 @@
     first_rest[...] = value
     second_rest[...] = image
     shift_out[...] = jnp.broadcast_to(shift, shift_out.shape)
-    slope = slope_image[...]
+    slope = slope_sum[...]
     parts = (
         shift,
         weight,
@@ -252,7 +243,7 @@
     sums[...] = jnp.broadcast_to(jnp.sum(packed, axis=0, keepdims=True), sums.shape)
 
 
-def last_kernel(point_total, noise, table, shift_in, first_rest, second_rest, rhs, out, res, trace):
+def last_kernel(point_total, signal, noise, numbers, table, shift_in, first_rest, second_rest, given, out, res, trace):
     gathered = table[...]
     shift = gathered
 
@@ -264,6 +255,8 @@
     def total(value):
         return jnp.sum(value, axis=0, keepdims=True)
 
+    gain = signal[0] / SCALE
+    rate = numbers[0:1, :]
     norm = total(weight)
     center = total(shift * weight + rw) / norm
     off = shift - center
@@ -275,7 +268,11 @@
     )
     held = total(rs)
     along = total(ws + off * rs)
-    level = noise[0] + center
+    cross = gain * cross
+    square = (gain * gain) * square
+    mixed = (gain * gain) * mixed
+    second = (gain * gain) * gain * second
+    level = noise[0] + gain * center
     lead = level * norm + cross
     alpha = norm / lead
     part = cross / lead
@@ -284,7 +281,8 @@
     direction = lean * lean * norm - 2.0 * lean * alpha * cross + alpha * alpha * square
     bend = lean * lean * cross - lean * alpha * (mixed + square) + alpha * alpha * second
     beta = norm_next / (level * direction + bend)
-    trace[...] = (((alpha + beta * lean) * held - beta * alpha * along) / point_total)[:, 0:16]
+    factor = signal[0] * (rate * rate)
+    trace[...] = (((alpha + beta * lean) * held - beta * alpha * gain * along) * factor / point_total)[:, 0:16]
 
     lane = lax.broadcasted_iota(jnp.int32, (16, 128), 1)
     row = lax.broadcasted_iota(jnp.int32, (16, 128), 0)
@@ -293,16 +291,21 @@
         return jnp.sum(jnp.where(lane == row, value, 0.0), axis=1, keepdims=True)
 
     own_off = shift_in[:, 0:1] - column(center)
-    base = rhs[...]
+    base = given[0:16, :]
     rest = first_rest[...]
     value = rest + own_off * base
     image = second_rest[...] + (2.0 * own_off) * rest + (own_off * own_off) * base
-    out[...] = column(alpha + beta * lean) * base - column(beta * alpha) * value
+    out[...] = column(alpha + beta * lean) * base - column(beta * alpha * gain) * value
     res[...] = (
         column(part - beta * level * lean) * base
-        - column(alpha - beta * level * alpha + beta * lean) * value
-        + column(beta * alpha) * image
-    )
+        - column((alpha - beta * level * alpha + beta * lean) * gain) * value
+        + column(beta * alpha * gain * gain) * image
+    )
+
+
+def slope_kernel(signal, numbers, source, dest):
+    rate = numbers[0:1, 0:1]
+    dest[...] = (signal[0] * rate * rate) * source[...]
 
 
 def call(kernel, outs, spaces, scratch=(), flops=0):
@@ -334,35 +337,36 @@
     def sides(value):
         return lax.ppermute(value, "loc", beside), lax.ppermute(value, "loc", across)
 
-    msg, target, basis, skel_target, rhs, *lev = call(
+    height = -(-(24 + levels) // 8) * 8
+    given = jnp.pad(right_sides, ((0, height - probes), (0, 0)))
+    given += jnp.pad(points, ((16, height - 19), (0, 0)))
+    given += jnp.pad(skeleton, ((24, height - 24 - levels), (0, rows - rank))).astype(FULL)
+    msg, target, basis, skel_target, numbers, *lev = call(
         functools.partial(front_kernel, levels),
         [
             ((MSG_ROWS, rows), HALF),
             ((SRC_ROWS, rows), HALF),
             ((levels * rank, rows), HALF),
             ((levels, SRC_ROWS, rank), HALF),
-            ((probes, rows), FULL),
+            ((8, 128), FULL),
         ]
         + [((96, rank), HALF)] * levels,
-        [SMEM] + [pltpu.HBM] * 3,
+        [SMEM, SMEM, VMEM],
         [
             VMEM((SRC_ROWS, rows), FULL),
             VMEM((2 * SRC_ROWS, rows), HALF),
             VMEM((levels * rank, SRC_ROWS), HALF),
-            VMEM(points.shape, FULL),
-            VMEM(skeleton.shape, jnp.int32),
-            pltpu.SemaphoreType.DMA((3,)),
         ],
-    )(far_length, points, right_sides, skeleton)
+    )(lengthscale, far_length, given)
     msg_a, msg_b = sides(msg)
     lev = [partner(value, level) for level, value in enumerate(lev)]
     kept, image, slopes = call(
         own_kernel,
         [((rows, rows), HALF), ((32, rows), FULL), ((probes, rows), FULL)],
-        [SMEM] + [VMEM] * 2,
+        [VMEM] * 3,
         [VMEM((rows, SRC_ROWS), HALF)],
-    )(lengthscale, msg, target)
-    kept_a, kept_b, coup_high, coup_low, row_sum, slope_image, slope_copy, first, wmsg, *wlev = call(
+    )(numbers, msg, target)
+    kept_a, kept_b, coup_high, coup_low, row_sum, slope_sum, first, wmsg, *wlev = call(
         functools.partial(side_kernel, levels, far_scale),
         [
             ((rows, rows), HALF),
@@ -372,21 +376,19 @@
             ((1, rows), FULL),
             ((probes, rows), FULL),
             ((probes, rows), FULL),
-            ((probes, rows), FULL),
             ((2 * probes, rows), HALF),
         ]
         + [((2 * probes, rank), HALF)] * levels,
-        [SMEM] * 3 + [VMEM] * (8 + levels),
+        [VMEM] * (9 + levels),
         [VMEM((rows, SRC_ROWS), HALF)] * 2,
-    )(lengthscale, far_length, signal, msg_a, msg_b, target, image, slopes, rhs, basis, skel_target, *lev)
+    )(numbers, msg_a, msg_b, target, image, slopes, given, basis, skel_target, *lev)
     wmsg_a, wmsg_b = sides(wmsg)
     wlev = [partner(value, level) for level, value in enumerate(wlev)]
     sums, first_rest, second_rest, shift = call(
         functools.partial(second_kernel, levels, far_scale),
         [((count, 128), FULL), ((probes, rows), FULL), ((probes, rows), FULL), ((probes, 128), FULL)],
-        [SMEM] + [VMEM] * (13 + levels),
+        [VMEM] * (13 + levels),
     )(
-        signal,
         wmsg,
         wmsg_a,
         wmsg_b,
@@ -398,16 +400,17 @@
         coup_low,
         row_sum,
         first,
-        rhs,
-        slope_copy,
+        given,
+        slope_sum,
         *wlev,
     )
     table = lax.all_to_all(sums, "loc", 0, 0, tiled=True)
+    (slope_image,) = call(slope_kernel, [((probes, rows), FULL)], [SMEM, VMEM, VMEM])(signal, numbers, slope_sum)
     solution, residual, trace = call(
         functools.partial(last_kernel, float(rows * count)),
         [((probes, rows), FULL), ((probes, rows), FULL), ((1, probes), FULL)],
-        [SMEM] + [VMEM] * 5,
-    )(noise_var, table, shift, first_rest, second_rest, rhs)
+        [SMEM, SMEM] + [VMEM] * 6,
+    )(signal, noise_var, numbers, table, shift, first_rest, second_rest, given)
     return (solution, residual, slope_image, trace.reshape(probes))
 
 

time: 56 us -> 54.3 us (0.970)
  local copies, waits for them, and re-layouts: 2.24 us -> 0 us
  starting transfers between devices: 25.7 us -> 26.8 us
  waiting for transfers between devices: 9.64 us -> 8.54 us
  other arithmetic: 0 us -> 0.88 us
    unnamed x6 -> x0, local copies, waits for them, and re-layouts: 2.24 us -> none
    all_to_all x1, waiting for transfers between devices: 6.43 us -> 5.11 us  [shards(): table = lax.all_to_all(sums, 'loc', 0, 0, tiled=True)]
    ppermute x8, starting transfers between devices: 20 us -> 21.3 us  [partner(): lax.ppermute(value, 'loc', [(i, i ^ 2 << level) for i in range(count)])]
    add x0 -> x1, other arithmetic: none -> 0.88 us  [shards(): given += jnp.pad(skeleton, ((24, height - 24 - levels), (0, rows - rank))...]
    pallas_call x0 -> x1, Pallas kernels: none -> 0.67 us  [shards(): call(slope_kernel, [((probes, rows), FULL)], [SMEM, VMEM, VMEM])]
  transfers between devices with their start and end apart: 13 -> 13, of which waited for: 5 -> 5; matrix products, arithmetic and copies ran while one was open for 0% -> 0% of each run, Pallas kernels for 4% -> 5%
where the time goes in v3:
time: 54.3 us; the launch traced here: 54.1 us
  starting transfers between devices  26.8 us (49%)
  Pallas kernels  14.5 us (27%)
  waiting for transfers between devices  8.54 us (16%)
  between operations  3.28 us (6%)
  other arithmetic  0.88 us (2%)
    ppermute x8, starting transfers between devices, partner(): lax.ppermute(value, 'loc', [(i, i ^ 2 << level) for i in range(count)])  21.3 us
    pallas_call x1, Pallas kernels, shards(): call(functools.partial(side_kernel, levels, far_scale), [((rows, rows), H...  5.73 us
    all_to_all x1, waiting for transfers between devices, shards(): table = lax.all_to_all(sums, 'loc', 0, 0, tiled=True)  5.11 us
    all_to_all x1, starting transfers between devices, shards(): table = lax.all_to_all(sums, 'loc', 0, 0, tiled=True)  3.71 us
    ppermute x8, waiting for transfers between devices, partner(): lax.ppermute(value, 'loc', [(i, i ^ 2 << level) for i in range(count)])  3.42 us
    pallas_call x1, Pallas kernels, shards(): call(functools.partial(front_kernel, levels), [((MSG_ROWS, rows), HALF),...  2.84 us
    pallas_call x1, Pallas kernels, shards(): call(functools.partial(second_kernel, levels, far_scale), [((count, 128),...  2.37 us
    pallas_call x1, Pallas kernels, shards(): call(own_kernel, [((rows, rows), HALF), ((32, rows), FULL), ((probes, row...  2.01 us
  transfers between devices with their start and end apart: 13, of which 5 were waited for; matrix products, arithmetic and copies ran while one was open for 0% of the time, Pallas kernels for 5%

profile of v3, /device:TPU:0, one launch (start us, length us, event | category | flops | bytes accessed | tf_op | source)
XLA Modules:
  0.0 54.1 jit_solution(16934543821423557670)
XLA Ops:
  1.9 0.9 %convert_add_fusion.refs_2_.refs_6_.refs_11_.given = f32[32,1024]{1,0:T(8,128)S(1)} fusion(s32[4,256]{1,0:T(4,128)} %param.9, f32[3,1024]{1,0:T(4,128)} %param.7, f32[16,1024]{1,0:T(8,128)} %param.8), kind=kLoop, calls=%fused_computation | loop fusion | flops 98304 | bytes 212992 | tf_op jit(solution)/shard_map/add | solution.py:343
  2.8 2.8 %shard_map.102 = (bf16[64,1024]{1,0:T(8,128)(2,1)S(1)}, bf16[32,1024]{1,0:T(8,128)(2,1)S(1)}, bf16[1024,1024]{1,0:T(8,128)(2,1)S(1)}, bf16[4,32,256]{2,1,0:T(8,1...) custom-call(f32[1]{0:T(128)S(6)} %copy.12.refs_0_, ...), custom_call_target="tpu_custom_call" | custom-call | bytes 1048576 | tf_op jit(solution)/shard_map/pallas_call | solution.py:344
  5.7 0.5 collective-permute-start
  6.2 0.7 %collective-permute-start.1 = (bf16[64,1024]{1,0:T(8,128)(2,1)S(1)}, bf16[64,1024]{1,0:T(8,128)(2,1)S(1)}, u32[]{:S(2)}, u32[]{:S(2)}) collective-permute-start(bf16[64,1024]{1,0:T(8,128)(2,1)S(1)} %get-tuple-element.36.msg), channel_id=1, source_target_pairs={{1,2},{3,4},{5,6},{7,8},{9,10},{11,12},{13,14},{15,16},{17,18},{19... | collective-permute-start | bytes 393224 | tf_op jit(solution)/shard_map/ppermute | solution.py:338
  6.8 3.8 %collective-permute-start.2 = (bf16[96,256]{1,0:T(8,128)(2,1)S(1)}, bf16[96,256]{1,0:T(8,128)(2,1)S(1)}, u32[]{:S(2)}, u32[]{:S(2)}) collective-permute-start(bf16[96,256]{1,0:T(8,128)(2,1)S(1)} %get-tuple-element.42), channel_id=1, source_target_pairs={{0,2},{1,3},{2,0},{3,1},{4,6},{5,7},{6,4},{7,5},{8,10},{9,11},{10,... | collective-permute-start | bytes 147464 | tf_op jit(solution)/shard_map/ppermute | solution.py:335
  10.7 2.1 %collective-permute-start.3 = (bf16[96,256]{1,0:T(8,128)(2,1)S(1)}, bf16[96,256]{1,0:T(8,128)(2,1)S(1)}, u32[]{:S(2)}, u32[]{:S(2)}) collective-permute-start(bf16[96,256]{1,0:T(8,128)(2,1)S(1)} %get-tuple-element.43), channel_id=1, source_target_pairs={{0,4},{1,5},{2,6},{3,7},{4,0},{5,1},{6,2},{7,3},{8,12},{9,13},{10,... | collective-permute-start | bytes 147464 | tf_op jit(solution)/shard_map/ppermute | solution.py:335
  12.8 1.6 %collective-permute-start.4 = (bf16[96,256]{1,0:T(8,128)(2,1)S(1)}, bf16[96,256]{1,0:T(8,128)(2,1)S(1)}, u32[]{:S(2)}, u32[]{:S(2)}) collective-permute-start(bf16[96,256]{1,0:T(8,128)(2,1)S(1)} %get-tuple-element.44), channel_id=1, source_target_pairs={{0,8},{1,9},{2,10},{3,11},{4,12},{5,13},{6,14},{7,15},{8,0},{9,1},... | collective-permute-start | bytes 147464 | tf_op jit(solution)/shard_map/ppermute | solution.py:335
  14.4 0.7 %collective-permute-done.2.refs_9_ = bf16[96,256]{1,0:T(8,128)(2,1)S(1)} collective-permute-done((bf16[96,256]{1,0:T(8,128)(2,1)S(1)}, bf16[96,256]{1,0:T(8,128)(2,1)S(1)}, u32[]{:S(2)}, u32[]{:S(2)}) %collective-permute-start.2) | collective-permute-done | bytes 49184 | tf_op jit(solution)/shard_map/ppermute | solution.py:335
  15.1 3.8 %collective-permute-start.5 = (bf16[96,256]{1,0:T(8,128)(2,1)S(1)}, bf16[96,256]{1,0:T(8,128)(2,1)S(1)}, u32[]{:S(2)}, u32[]{:S(2)}) collective-permute-start(bf16[96,256]{1,0:T(8,128)(2,1)S(1)} %get-tuple-element.45), channel_id=1, source_target_pairs={{0,16},{1,17},{2,18},{3,19},{4,20},{5,21},{6,22},{7,23},{8,24},{9,... | collective-permute-start | bytes 147464 | tf_op jit(solution)/shard_map/ppermute | solution.py:335
  18.9 2.0 %shard_map.103 = (bf16[1024,1024]{1,0:T(8,128)(2,1)S(1)}, f32[32,1024]{1,0:T(8,128)S(1)}, f32[16,1024]{1,0:T(8,128)S(1)}) custom-call(f32[8,128]{1,0:T(8,128)S(1)} %get-tuple-element.35.numbers.refs_0_, bf16[64,1024]{1,0:T(8,128)(2,1)S(1)} %get-tuple-element.36.msg, bf16[32,1024]{1,0:T(8,128)(2,1)S(1)} %get-tuple-element.37.target.refs_3_), custom_call_target="tpu_custom_call" | custom-call | bytes 1048576 | tf_op jit(solution)/shard_map/pallas_call | solution.py:363
  21.0 0.2 collective-permute-done.5.refs_12_
  21.2 5.7 %shard_map.104 = (bf16[1024,1024]{1,0:T(8,128)(2,1)S(1)}, bf16[1024,1024]{1,0:T(8,128)(2,1)S(1)}, bf16[4,256,256]{2,1,0:T(8,128)(2,1)S(1)}, bf16[4,256,256]{2,1,...) custom-call(f32[8,128]{1,0:T(8,128)S(1)} %get-tuple-element.35.numbe, ...), custom_call_target="tpu_custom_call" | custom-call | bytes 1048576 | tf_op jit(solution)/shard_map/pallas_call | solution.py:369
  27.0 0.7 %collective-permute-start.7 = (bf16[32,1024]{1,0:T(8,128)(2,1)S(1)}, bf16[32,1024]{1,0:T(8,128)(2,1)S(1)}, u32[]{:S(2)}, u32[]{:S(2)}) collective-permute-start(bf16[32,1024]{1,0:T(8,128)(2,1)S(1)} %get-tuple-element.46.refs_0_), channel_id=1, source_target_pairs={{1,2},{3,4},{5,6},{7,8},{9,10},{11,12},{13,14},{15,16},{17,18},{19... | collective-permute-start | bytes 196616 | tf_op jit(solution)/shard_map/ppermute | solution.py:338
  27.6 5.2 %collective-permute-start.10 = (bf16[32,256]{1,0:T(8,128)(2,1)S(1)}, bf16[32,256]{1,0:T(8,128)(2,1)S(1)}, u32[]{:S(2)}, u32[]{:S(2)}) collective-permute-start(bf16[32,256]{1,0:T(8,128)(2,1)S(1)} %get-tuple-element.57), channel_id=1, source_target_pairs={{0,8},{1,9},{2,10},{3,11},{4,12},{5,13},{6,14},{7,15},{8,0},{9,1},... | collective-permute-start | bytes 49160 | tf_op jit(solution)/shard_map/ppermute | solution.py:335
  32.8 2.5 %collective-permute-start.11 = (bf16[32,256]{1,0:T(8,128)(2,1)S(1)}, bf16[32,256]{1,0:T(8,128)(2,1)S(1)}, u32[]{:S(2)}, u32[]{:S(2)}) collective-permute-start(bf16[32,256]{1,0:T(8,128)(2,1)S(1)} %get-tuple-element.58), channel_id=1, source_target_pairs={{0,16},{1,17},{2,18},{3,19},{4,20},{5,21},{6,22},{7,23},{8,24},{9,... | collective-permute-start | bytes 49160 | tf_op jit(solution)/shard_map/ppermute | solution.py:335
  35.3 0.9 %collective-permute-start.8 = (bf16[32,256]{1,0:T(8,128)(2,1)S(1)}, bf16[32,256]{1,0:T(8,128)(2,1)S(1)}, u32[]{:S(2)}, u32[]{:S(2)}) collective-permute-start(bf16[32,256]{1,0:T(8,128)(2,1)S(1)} %get-tuple-element.55), channel_id=1, source_target_pairs={{0,2},{1,3},{2,0},{3,1},{4,6},{5,7},{6,4},{7,5},{8,10},{9,11},{10,... | collective-permute-start | bytes 49160 | tf_op jit(solution)/shard_map/ppermute | solution.py:335
  36.3 1.3 %collective-permute-start.9 = (bf16[32,256]{1,0:T(8,128)(2,1)S(1)}, bf16[32,256]{1,0:T(8,128)(2,1)S(1)}, u32[]{:S(2)}, u32[]{:S(2)}) collective-permute-start(bf16[32,256]{1,0:T(8,128)(2,1)S(1)} %get-tuple-element.56), channel_id=1, source_target_pairs={{0,4},{1,5},{2,6},{3,7},{4,0},{5,1},{6,2},{7,3},{8,12},{9,13},{10,... | collective-permute-start | bytes 49160 | tf_op jit(solution)/shard_map/ppermute | solution.py:335
  37.6 1.5 %collective-permute-done.8.refs_13_ = bf16[32,256]{1,0:T(8,128)(2,1)S(1)} collective-permute-done((bf16[32,256]{1,0:T(8,128)(2,1)S(1)}, bf16[32,256]{1,0:T(8,128)(2,1)S(1)}, u32[]{:S(2)}, u32[]{:S(2)}) %collective-permute-start.8) | collective-permute-done | bytes 16416 | tf_op jit(solution)/shard_map/ppermute | solution.py:335
  39.1 0.9 %collective-permute-done.9.refs_14_ = bf16[32,256]{1,0:T(8,128)(2,1)S(1)} collective-permute-done((bf16[32,256]{1,0:T(8,128)(2,1)S(1)}, bf16[32,256]{1,0:T(8,128)(2,1)S(1)}, u32[]{:S(2)}, u32[]{:S(2)}) %collective-permute-start.9) | collective-permute-done | bytes 16416 | tf_op jit(solution)/shard_map/ppermute | solution.py:335
  40.0 2.4 %shard_map.105 = (f32[32,128]{1,0:T(8,128)}, f32[16,1024]{1,0:T(8,128)S(1)}, f32[16,1024]{1,0:T(8,128)S(1)}, f32[16,128]{1,0:T(8,128)S(1)}) custom-call(bf16[32,1024]{1,0:T(8,128)(2,1)S(1)} %get-tuple-element.46.refs_0_, bf16[32,1024]{1,0:T(8,128)(2,1)S(1)} %collective-permute-done.6.refs_1_, bf16[32,1024]{1,0:T(8,128)(2,1)S(1)} %collective-permute-done.7.refs_2_, ...), custom_call_target="tpu_custom_call" | custom-call | bytes 1048576 | tf_op jit(solution)/shard_map/pallas_call | solution.py:387
  42.4 3.7 %all-to-all-start = ((f32[32,1,128]{2,1,0:T(1,128)}), f32[32,1,128]{2,1,0:T(1,128)S(1)}, u32[]{:S(2)}, u32[]{:S(2)}) async-start(f32[32,1,128]{2,1,0:T(1,128)} %bitcast.1), calls=%async_computation | async-start | bytes 32768 | tf_op jit(solution)/shard_map/all_to_all | solution.py:407
  47.4 0.7 %shard_map.107 = f32[16,1024]{1,0:T(8,128)} custom-call(f32[1]{0:T(128)S(6)} %copy.14.signal, f32[8,128]{1,0:T(8,128)S(1)} %get-tuple-element.35.numbers.refs_0_, f32[16,1024]{1,0:T(8,128)S(1)} %get-tuple-element.54.refs_12_.source), custom_call_target="tpu_custom_call" | custom-call | bytes 1048576 | tf_op jit(solution)/shard_map/pallas_call | solution.py:408
  48.1 5.1 %all-to-all-done = f32[32,1,128]{2,1,0:T(1,128)S(1)} async-done(((f32[32,1,128]{2,1,0:T(1,128)}), f32[32,1,128]{2,1,0:T(1,128)S(1)}, u32[]{:S(2)}, u32[]{:S(2)}) %all-to-all-start) | async-done | bytes 16416 | tf_op jit(solution)/shard_map/all_to_all | solution.py:407
  53.2 0.9 %shard_map.106 = (f32[16,1024]{1,0:T(8,128)}, f32[16,1024]{1,0:T(8,128)}, f32[1,16]{1,0:T(1,128)}) custom-call(f32[1]{0:T(128)S(6)} %copy.14.signal, f32[1]{0:T(128)S(6)} %copy.15.noise, f32[8,128]{1,0:T(8,128)S(1)} %get-tuple-element.35.numbers.refs_0_, f32[32,128]{1,0:T(8,128)S(1)} %bitcast.5, f32[16,128]{1,0:T(8,128)S(1)} %get-tuple-element.60.shift_in, ...), custom_call_target="tpu_custom_call" | custom-call | bytes 1048576 | tf_op jit(solution)/shard_map/pallas_call | solution.py:409
  (9 shorter events, 0.1 us)
Async XLA Ops:
  5.7 15.6 %collective-permute-start = (bf16[64,1024]{1,0:T(8,128)(2,1)S(1)}, bf16[64,1024]{1,0:T(8,128)(2,1)S(1)}, u32[]{:S(2)}, u32[]{:S(2)}) collective-permute-start(bf16[64,1024]{1,0:T(8,128)(2,1)S(1)} %get-tuple-element.36.msg), channel_id=1, source_target_pairs={{0,1},{1,0},{2,3},{3,2},{4,5},{5,4},{6,7},{7,6},{8,9},{9,8},{10,11... | collective-permute-start | bytes 393224 | tf_op jit(solution)/shard_map/ppermute | solution.py:338
  6.2 15.0 %collective-permute-start.1 = (bf16[64,1024]{1,0:T(8,128)(2,1)S(1)}, bf16[64,1024]{1,0:T(8,128)(2,1)S(1)}, u32[]{:S(2)}, u32[]{:S(2)}) collective-permute-start(bf16[64,1024]{1,0:T(8,128)(2,1)S(1)} %get-tuple-element.36.msg), channel_id=1, source_target_pairs={{1,2},{3,4},{5,6},{7,8},{9,10},{11,12},{13,14},{15,16},{17,18},{19... | collective-permute-start | bytes 393224 | tf_op jit(solution)/shard_map/ppermute | solution.py:338
  6.8 8.2 %collective-permute-start.2 = (bf16[96,256]{1,0:T(8,128)(2,1)S(1)}, bf16[96,256]{1,0:T(8,128)(2,1)S(1)}, u32[]{:S(2)}, u32[]{:S(2)}) collective-permute-start(bf16[96,256]{1,0:T(8,128)(2,1)S(1)} %get-tuple-element.42), channel_id=1, source_target_pairs={{0,2},{1,3},{2,0},{3,1},{4,6},{5,7},{6,4},{7,5},{8,10},{9,11},{10,... | collective-permute-start | bytes 147464 | tf_op jit(solution)/shard_map/ppermute | solution.py:335
  10.7 10.2 %collective-permute-start.3 = (bf16[96,256]{1,0:T(8,128)(2,1)S(1)}, bf16[96,256]{1,0:T(8,128)(2,1)S(1)}, u32[]{:S(2)}, u32[]{:S(2)}) collective-permute-start(bf16[96,256]{1,0:T(8,128)(2,1)S(1)} %get-tuple-element.43), channel_id=1, source_target_pairs={{0,4},{1,5},{2,6},{3,7},{4,0},{5,1},{6,2},{7,3},{8,12},{9,13},{10,... | collective-permute-start | bytes 147464 | tf_op jit(solution)/shard_map/ppermute | solution.py:335
  12.8 8.2 %collective-permute-start.4 = (bf16[96,256]{1,0:T(8,128)(2,1)S(1)}, bf16[96,256]{1,0:T(8,128)(2,1)S(1)}, u32[]{:S(2)}, u32[]{:S(2)}) collective-permute-start(bf16[96,256]{1,0:T(8,128)(2,1)S(1)} %get-tuple-element.44), channel_id=1, source_target_pairs={{0,8},{1,9},{2,10},{3,11},{4,12},{5,13},{6,14},{7,15},{8,0},{9,1},... | collective-permute-start | bytes 147464 | tf_op jit(solution)/shard_map/ppermute | solution.py:335
  15.1 6.1 %collective-permute-start.5 = (bf16[96,256]{1,0:T(8,128)(2,1)S(1)}, bf16[96,256]{1,0:T(8,128)(2,1)S(1)}, u32[]{:S(2)}, u32[]{:S(2)}) collective-permute-start(bf16[96,256]{1,0:T(8,128)(2,1)S(1)} %get-tuple-element.45), channel_id=1, source_target_pairs={{0,16},{1,17},{2,18},{3,19},{4,20},{5,21},{6,22},{7,23},{8,24},{9,... | collective-permute-start | bytes 147464 | tf_op jit(solution)/shard_map/ppermute | solution.py:335
  26.9 13.1 %collective-permute-start.6 = (bf16[32,1024]{1,0:T(8,128)(2,1)S(1)}, bf16[32,1024]{1,0:T(8,128)(2,1)S(1)}, u32[]{:S(2)}, u32[]{:S(2)}) collective-permute-start(bf16[32,1024]{1,0:T(8,128)(2,1)S(1)} %get-tuple-element.46.refs_0_), channel_id=1, source_target_pairs={{0,1},{1,0},{2,3},{3,2},{4,5},{5,4},{6,7},{7,6},{8,9},{9,8},{10,11... | collective-permute-start | bytes 196616 | tf_op jit(solution)/shard_map/ppermute | solution.py:338
  27.0 13.1 %collective-permute-start.7 = (bf16[32,1024]{1,0:T(8,128)(2,1)S(1)}, bf16[32,1024]{1,0:T(8,128)(2,1)S(1)}, u32[]{:S(2)}, u32[]{:S(2)}) collective-permute-start(bf16[32,1024]{1,0:T(8,128)(2,1)S(1)} %get-tuple-element.46.refs_0_), channel_id=1, source_target_pairs={{1,2},{3,4},{5,6},{7,8},{9,10},{11,12},{13,14},{15,16},{17,18},{19... | collective-permute-start | bytes 196616 | tf_op jit(solution)/shard_map/ppermute | solution.py:338
  27.6 8.6 %collective-permute-start.10 = (bf16[32,256]{1,0:T(8,128)(2,1)S(1)}, bf16[32,256]{1,0:T(8,128)(2,1)S(1)}, u32[]{:S(2)}, u32[]{:S(2)}) collective-permute-start(bf16[32,256]{1,0:T(8,128)(2,1)S(1)} %get-tuple-element.57), channel_id=1, source_target_pairs={{0,8},{1,9},{2,10},{3,11},{4,12},{5,13},{6,14},{7,15},{8,0},{9,1},... | collective-permute-start | bytes 49160 | tf_op jit(solution)/shard_map/ppermute | solution.py:335
  32.8 4.8 %collective-permute-start.11 = (bf16[32,256]{1,0:T(8,128)(2,1)S(1)}, bf16[32,256]{1,0:T(8,128)(2,1)S(1)}, u32[]{:S(2)}, u32[]{:S(2)}) collective-permute-start(bf16[32,256]{1,0:T(8,128)(2,1)S(1)} %get-tuple-element.58), channel_id=1, source_target_pairs={{0,16},{1,17},{2,18},{3,19},{4,20},{5,21},{6,22},{7,23},{8,24},{9,... | collective-permute-start | bytes 49160 | tf_op jit(solution)/shard_map/ppermute | solution.py:335
  35.3 3.7 %collective-permute-start.8 = (bf16[32,256]{1,0:T(8,128)(2,1)S(1)}, bf16[32,256]{1,0:T(8,128)(2,1)S(1)}, u32[]{:S(2)}, u32[]{:S(2)}) collective-permute-start(bf16[32,256]{1,0:T(8,128)(2,1)S(1)} %get-tuple-element.55), channel_id=1, source_target_pairs={{0,2},{1,3},{2,0},{3,1},{4,6},{5,7},{6,4},{7,5},{8,10},{9,11},{10,... | collective-permute-start | bytes 49160 | tf_op jit(solution)/shard_map/ppermute | solution.py:335
  36.3 3.7 %collective-permute-start.9 = (bf16[32,256]{1,0:T(8,128)(2,1)S(1)}, bf16[32,256]{1,0:T(8,128)(2,1)S(1)}, u32[]{:S(2)}, u32[]{:S(2)}) collective-permute-start(bf16[32,256]{1,0:T(8,128)(2,1)S(1)} %get-tuple-element.56), channel_id=1, source_target_pairs={{0,4},{1,5},{2,6},{3,7},{4,0},{5,1},{6,2},{7,3},{8,12},{9,13},{10,... | collective-permute-start | bytes 49160 | tf_op jit(solution)/shard_map/ppermute | solution.py:335
  42.4 10.8 %all-to-all-start = ((f32[32,1,128]{2,1,0:T(1,128)}), f32[32,1,128]{2,1,0:T(1,128)S(1)}, u32[]{:S(2)}, u32[]{:S(2)}) async-start(f32[32,1,128]{2,1,0:T(1,128)} %bitcast.1), calls=%async_computation | async-start | bytes 32768 | tf_op jit(solution)/shard_map/all_to_all | solution.py:407

commit v4 on v3

--- a/solution.py
+++ b/solution.py
@@ -97,11 +97,40 @@
     return jnp.concatenate([both[0:16] + both[16:32], both[32:48]], axis=0)
 
 
+def on_first_core():
+    return lax.rem(lax.axis_index("loc"), 2) == 0
+
+
+def share(values, keep, give):
+    first = on_first_core()
+    for slot in range(len(values) // 2):
+        even, odd = values[2 * slot], values[2 * slot + 1]
+        keep[slot] = jnp.where(first, even, odd)
+        give[slot] = jnp.where(first, odd, even)
+
+
+def gather_share(keep, got, packs):
+    first = on_first_core()
+    for slot, pack in enumerate(packs):
+        pack[0] = jnp.where(first, keep[slot], got[slot])
+        pack[1] = jnp.where(first, got[slot], keep[slot])
+
+
+def level_values(cross, other):
+    first = on_first_core()
+    values = []
+    for mine, theirs in zip(cross, other):
+        here = jnp.where(first, mine[0], mine[1])
+        there = jnp.where(first, theirs[0], theirs[1])
+        values.append(jnp.where(first, here, there))
+        values.append(jnp.where(first, there, here))
+    return values
+
+
 def front_kernel(levels, *refs):
     length, far_length, given = refs[:3]
-    msg, target, basis, skel_target, numbers = refs[3:8]
-    lev = refs[8 : 8 + levels]
-    buf, pair_buf, turned_src = refs[8 + levels :]
+    msg, target, basis, skel_target, numbers, keep, give = refs[3:10]
+    buf, pair_buf, turned_src = refs[10:]
     points = given[16:19, :]
     for slot, value in enumerate((length[0], far_length[0])):
         lengths = jnp.full((1, 128), value, FULL)
@@ -114,13 +143,14 @@
     pair_buf[0:SRC_ROWS, :] = buf[...].astype(HALF)
     msg[32:64, :] = buf[...].astype(HALF)
     rows, rank = points.shape[1], skel_target.shape[2]
+    sources = []
     for level in range(levels):
         spot = lax.broadcasted_iota(jnp.int32, (rows, rank), 0).astype(FULL)
         picks = jnp.where(spot == given[24 + level : 25 + level, 0:rank], 1.0, 0.0).astype(HALF)
         both = dot(pair_buf[...], picks)
         skel_target[level] = both[SRC_ROWS:].astype(HALF)
         skel_source = both[:SRC_ROWS]
-        lev[level][64:96, :] = skel_source.astype(HALF)
+        sources.append(skel_source.astype(HALF))
         turned_src[level * rank : (level + 1) * rank, :] = skel_source.T.astype(HALF)
     rates = numbers[1:2, :], numbers[3:4, :]
     for col in range(0, rows, TILE):
@@ -130,10 +160,11 @@
     msg[0:16, :] = low
     msg[16:32, :] = high
     coef = merged(dot_rows(msg[0:VEC_ROWS, :], basis[...]))
+    lev = []
     for level in range(levels):
         high, low = split_two(coef[:, level * rank : (level + 1) * rank])
-        lev[level][0:32, :] = high
-        lev[level][32:64, :] = low
+        lev.append(jnp.concatenate([high, low, sources[level]], axis=0))
+    share(lev, keep, give)
 
 
 def near_block(msg, target, turned_src, rates, kept):
@@ -149,71 +180,74 @@
         yield slice(col, col + TILE), merged(total[:, :TILE]), total[16:32, TILE:]
 
 
-def own_kernel(numbers, msg, target, kept, image, slopes, turned_src):
+def own_kernel(numbers, msg, target, keep, got, kept, image, slopes, *rest):
+    packs, turned_src = rest[:-1], rest[-1]
+    gather_share(keep, got, packs)
     rates = numbers[0:1, :], numbers[2:3, :]
     for span, part, slope in near_block(msg, target, turned_src, rates, kept):
         image[:, span] = part
         slopes[:, span] = slope
 
 
-def side_kernel(levels, far_scale, *refs):
-    numbers, msg_a, msg_b, target, image, slopes, given, basis, skel_target = refs[:9]
-    lev = refs[9 : 9 + levels]
-    outs = refs[9 + levels :]
-    kept_a, kept_b, coup_high, coup_low, row_sum, slope_sum, first, wmsg = outs[:8]
-    wlev = outs[8 : 8 + levels]
-    turned_a, turned_b = outs[8 + levels :]
+def side_kernel(numbers, msg, target, image_in, slopes_in, kept, image, slopes, turned_src):
+    rates = numbers[0:1, :], numbers[2:3, :]
+    for span, part, slope in near_block(msg, target, turned_src, rates, kept):
+        image[:, span] = image_in[:, span] + part
+        slopes[:, span] = slopes_in[:, span] + slope
+
+
+def far_kernel(half, far_scale, *refs):
+    numbers, image, given, basis, skel_target = refs[:5]
+    lev = level_values(refs[5 : 5 + half], refs[5 + half : 5 + 2 * half])
+    coup_high, coup_low, row_sum, first, wmsg, keep, give = refs[5 + 2 * half :]
     rank = skel_target.shape[2]
-    rates = numbers[0:1, :], numbers[2:3, :]
     far_rates = [jnp.concatenate([numbers[row : row + 1, :]] * (rank // 128), axis=1) for row in (1, 3)]
     mixed = []
-    for level in range(levels):
-        squared = dot(turned(lev[level][64:96, :]), skel_target[level])
+    for level, value in enumerate(lev):
+        squared = dot(turned(value[64:96]), skel_target[level])
         high, low = split_two(matern(squared, far_rates)[0])
         coup_high[level] = high
         coup_low[level] = low
-        both = dot(lev[level][0:64, :], high)
-        part = both[0:32] + both[32:64] + dot(lev[level][0:32, :], low)
+        both = dot(value[0:64], high)
+        part = both[0:32] + both[32:64] + dot(value[0:32], low)
         mixed.append(jnp.concatenate(split_two(part), axis=0))
     far = dot(jnp.concatenate(mixed, axis=1), basis[...])
-    far = far_scale * (far[0:32] + far[32:64])
-    side_a = near_block(msg_a, target, turned_a, rates, kept_a)
-    side_b = near_block(msg_b, target, turned_b, rates, kept_b)
-    for (span, image_a, slopes_a), (_, image_b, slopes_b) in zip(side_a, side_b):
-        slope_sum[:, span] = slopes[:, span] + slopes_a + slopes_b
-        total = image[:, span] + image_a + image_b + far[:, span]
-        sums = total[16:17, :]
-        row_sum[:, span] = sums
-        value = SCALE * (total[0:16] + sums * given[0:16, span])
-        first[:, span] = value
-        high, low = split_two(value)
-        wmsg[0:16, span] = high
-        wmsg[16:32, span] = low
+    total = image[...] + far_scale * (far[0:32] + far[32:64])
+    sums = total[16:17, :]
+    row_sum[...] = sums
+    value = SCALE * (total[0:16] + sums * given[0:16, :])
+    first[...] = value
+    high, low = split_two(value)
+    wmsg[0:16, :] = high
+    wmsg[16:32, :] = low
     both = dot_rows(wmsg[...], basis[...])
     high, low = split_two(both[0:16] + both[16:32])
-    for level in range(levels):
-        span = slice(level * rank, (level + 1) * rank)
-        wlev[level][0:16, :] = high[:, span]
-        wlev[level][16:32, :] = low[:, span]
+    both = jnp.concatenate([high, low], axis=0)
+    share([both[:, level * rank : (level + 1) * rank] for level in range(len(lev))], keep, give)
+
+
+def pack_kernel(keep, got, *packs):
+    gather_share(keep, got, packs)
+
+
+def near_kernel(wmsg, wmsg_a, wmsg_b, kept, kept_a, kept_b, out):
+    out[...] = dot(wmsg[...], kept[...]) + dot(wmsg_a[...], kept_a[...]) + dot(wmsg_b[...], kept_b[...])
 
 
 def row_total(a, b):
     return jnp.sum(a * b, axis=1, keepdims=True)
 
 
-def second_kernel(levels, far_scale, *refs):
-    wmsg, wmsg_a, wmsg_b, kept, kept_a, kept_b = refs[:6]
-    basis, coup_high, coup_low, row_sum, first, given, slope_sum = refs[6:13]
-    wlev = refs[13 : 13 + levels]
-    sums, first_rest, second_rest, shift_out = refs[13 + levels :]
-    both = dot(wmsg[...], kept[...]) + dot(wmsg_a[...], kept_a[...]) + dot(wmsg_b[...], kept_b[...])
+def second_kernel(half, far_scale, *refs):
+    near, basis, coup_high, coup_low, row_sum, first, given, slope_sum = refs[:8]
+    wlev = level_values(refs[8 : 8 + half], refs[8 + half : 8 + 2 * half])
+    sums, first_rest, second_rest, shift_out = refs[8 + 2 * half :]
     pieces = []
-    for level in range(levels):
-        coef = wlev[level][...]
+    for level, coef in enumerate(wlev):
         mixed = dot(coef, coup_high[level])
         mixed = mixed[0:16] + mixed[16:32] + dot(coef[0:16], coup_low[level])
         pieces.append(jnp.concatenate(split_two(mixed), axis=0))
-    both = both + far_scale * dot(jnp.concatenate(pieces, axis=1), basis[...])
+    both = near[...] + far_scale * dot(jnp.concatenate(pieces, axis=1), basis[...])
     base = given[0:16, :]
     value = first[...]
     image = SCALE * (both[0:16] + both[16:32] + row_sum[...] * value)
@@ -308,9 +342,9 @@
     dest[...] = (signal[0] * rate * rate) * source[...]
 
 
-def call(kernel, outs, spaces, scratch=(), flops=0):
+def call(kernel, outs, spaces, scratch=(), micros=2.0):
     params = pltpu.CompilerParams(vmem_limit_bytes=40 * 2**20)
-    cost = pl.CostEstimate(flops=flops, bytes_accessed=2**20, transcendentals=0)
+    cost = pl.CostEstimate(flops=int(micros * 1e9), bytes_accessed=2**16, transcendentals=0)
     return pl.pallas_call(
         kernel,
         out_shape=[jax.ShapeDtypeStruct(shape, kind) for shape, kind in outs],
@@ -325,14 +359,19 @@
 def shards(points, right_sides, skeleton, lengthscale, far_length, signal, noise_var):
     probes, rows = right_sides.shape
     levels, rank = skeleton.shape
+    half = levels // 2
     count = lax.axis_size("loc")
     far_scale = 1.0 / (rank * rank * levels)
     beside = [(i, i ^ 1) for i in range(count)]
     across = [(i, i + 1) for i in range(1, count - 1, 2)]
     across = across + [(j, i) for i, j in across]
 
-    def partner(value, level):
-        return lax.ppermute(value, "loc", [(i, i ^ (2 << level)) for i in range(count)])
+    def partner(value, slot):
+        pairs = [(i, i ^ (2 << (2 * slot + i % 2))) for i in range(count)]
+        return lax.ppermute(value, "loc", pairs)
+
+    def sibling(value):
+        return lax.ppermute(value, "loc", beside)
 
     def sides(value):
         return lax.ppermute(value, "loc", beside), lax.ppermute(value, "loc", across)
@@ -341,7 +380,7 @@
     given = jnp.pad(right_sides, ((0, height - probes), (0, 0)))
     given += jnp.pad(points, ((16, height - 19), (0, 0)))
     given += jnp.pad(skeleton, ((24, height - 24 - levels), (0, rows - rank))).astype(FULL)
-    msg, target, basis, skel_target, numbers, *lev = call(
+    msg, target, basis, skel_target, numbers, keep, give = call(
         functools.partial(front_kernel, levels),
         [
             ((MSG_ROWS, rows), HALF),
@@ -349,8 +388,9 @@
             ((levels * rank, rows), HALF),
             ((levels, SRC_ROWS, rank), HALF),
             ((8, 128), FULL),
-        ]
-        + [((96, rank), HALF)] * levels,
+            ((half, 96, rank), HALF),
+            ((half, 96, rank), HALF),
+        ],
         [SMEM, SMEM, VMEM],
         [
             VMEM((SRC_ROWS, rows), FULL),
@@ -358,54 +398,46 @@
             VMEM((levels * rank, SRC_ROWS), HALF),
         ],
     )(lengthscale, far_length, given)
+    got = sibling(give)
     msg_a, msg_b = sides(msg)
-    lev = [partner(value, level) for level, value in enumerate(lev)]
-    kept, image, slopes = call(
+    near_outs = [((rows, rows), HALF), ((32, rows), FULL), ((probes, rows), FULL)]
+    turned_buf = [VMEM((rows, SRC_ROWS), HALF)]
+    kept, image, slopes, *packs = call(
         own_kernel,
-        [((rows, rows), HALF), ((32, rows), FULL), ((probes, rows), FULL)],
-        [VMEM] * 3,
-        [VMEM((rows, SRC_ROWS), HALF)],
-    )(numbers, msg, target)
-    kept_a, kept_b, coup_high, coup_low, row_sum, slope_sum, first, wmsg, *wlev = call(
-        functools.partial(side_kernel, levels, far_scale),
+        near_outs + [((2, 96, rank), HALF)] * half,
+        [VMEM] * 5,
+        turned_buf,
+    )(numbers, msg, target, keep, got)
+    cross = [partner(pack, slot) for slot, pack in enumerate(packs)]
+    kept_a, image, slopes = call(side_kernel, near_outs, [VMEM] * 5, turned_buf)(numbers, msg_a, target, image, slopes)
+    other = [sibling(value) for value in cross]
+    kept_b, image, slopes = call(side_kernel, near_outs, [VMEM] * 5, turned_buf)(numbers, msg_b, target, image, slopes)
+    coup_high, coup_low, row_sum, first, wmsg, keep, give = call(
+        functools.partial(far_kernel, half, far_scale),
         [
-            ((rows, rows), HALF),
-            ((rows, rows), HALF),
             ((levels, rank, rank), HALF),
             ((levels, rank, rank), HALF),
             ((1, rows), FULL),
             ((probes, rows), FULL),
-            ((probes, rows), FULL),
             ((2 * probes, rows), HALF),
-        ]
-        + [((2 * probes, rank), HALF)] * levels,
-        [VMEM] * (9 + levels),
-        [VMEM((rows, SRC_ROWS), HALF)] * 2,
-    )(numbers, msg_a, msg_b, target, image, slopes, given, basis, skel_target, *lev)
+            ((half, 2 * probes, rank), HALF),
+            ((half, 2 * probes, rank), HALF),
+        ],
+        [VMEM] * (5 + levels),
+    )(numbers, image, given, basis, skel_target, *cross, *other)
+    got = sibling(give)
     wmsg_a, wmsg_b = sides(wmsg)
-    wlev = [partner(value, level) for level, value in enumerate(wlev)]
+    packs = call(pack_kernel, [((2, 2 * probes, rank), HALF)] * half, [VMEM] * 2, micros=0.1)(keep, got)
+    cross = [partner(pack, slot) for slot, pack in enumerate(packs)]
+    (near,) = call(near_kernel, [((2 * probes, rows), FULL)], [VMEM] * 6, micros=1.2)(wmsg, wmsg_a, wmsg_b, kept, kept_a, kept_b)
+    other = [sibling(value) for value in cross]
     sums, first_rest, second_rest, shift = call(
-        functools.partial(second_kernel, levels, far_scale),
+        functools.partial(second_kernel, half, far_scale),
         [((count, 128), FULL), ((probes, rows), FULL), ((probes, rows), FULL), ((probes, 128), FULL)],
-        [VMEM] * (13 + levels),
-    )(
-        wmsg,
-        wmsg_a,
-        wmsg_b,
-        kept,
-        kept_a,
-        kept_b,
-        basis,
-        coup_high,
-        coup_low,
-        row_sum,
-        first,
-        given,
-        slope_sum,
-        *wlev,
-    )
+        [VMEM] * (8 + levels),
+    )(near, basis, coup_high, coup_low, row_sum, first, given, slopes, *cross, *other)
     table = lax.all_to_all(sums, "loc", 0, 0, tiled=True)
-    (slope_image,) = call(slope_kernel, [((probes, rows), FULL)], [SMEM, VMEM, VMEM])(signal, numbers, slope_sum)
+    (slope_image,) = call(slope_kernel, [((probes, rows), FULL)], [SMEM, VMEM, VMEM])(signal, numbers, slopes)
     solution, residual, trace = call(
         functools.partial(last_kernel, float(rows * count)),
         [((probes, rows), FULL), ((probes, rows), FULL), ((1, probes), FULL)],

time: 54.3 us -> 49.1 us (0.904)
  starting transfers between devices: 26.8 us -> 20.5 us
  Pallas kernels: 14.5 us -> 15.2 us
    ppermute x8 -> x10, starting transfers between devices: 21.3 us -> 9.83 us  [the longest x4 7.76 us: partner(): return lax.ppermute(value, 'loc', pairs)]
    ppermute x2, starting transfers between devices: 0.52 us -> 4.01 us  [sides(): lax.ppermute(value, 'loc', beside)]
    all_to_all x1, starting transfers between devices: 3.71 us -> 5.36 us  [shards(): table = lax.all_to_all(sums, 'loc', 0, 0, tiled=True)]
    all_to_all x1, waiting for transfers between devices: 5.11 us -> 6.4 us  [shards(): table = lax.all_to_all(sums, 'loc', 0, 0, tiled=True)]
    ppermute x8 -> x10, waiting for transfers between devices: 3.42 us -> 2.5 us  [the longest x4 2.35 us: partner(): return lax.ppermute(value, 'loc', pairs)]
    pallas_call x3 -> x7, Pallas kernels: 10.1 us -> 10.7 us  [the longest x2 4.12 us: shards(): call(side_kernel, near_outs, [VMEM] * 5, turned_buf)]
  transfers between devices with their start and end apart: 13 -> 15, of which waited for: 5 -> 5; matrix products, arithmetic and copies ran while one was open for 0% -> 0% of each run, Pallas kernels for 5% -> 16%
where the time goes in v4:
time: 49.1 us; the launch traced here: 48.8 us
  starting transfers between devices  20.5 us (42%)
  Pallas kernels  15.2 us (31%)
  waiting for transfers between devices  8.91 us (18%)
  between operations  3.35 us (7%)
  other arithmetic  0.88 us (2%)
    ppermute x4, starting transfers between devices, partner(): return lax.ppermute(value, 'loc', pairs)  7.76 us
    all_to_all x1, waiting for transfers between devices, shards(): table = lax.all_to_all(sums, 'loc', 0, 0, tiled=True)  6.4 us
    all_to_all x1, starting transfers between devices, shards(): table = lax.all_to_all(sums, 'loc', 0, 0, tiled=True)  5.36 us
    pallas_call x2, Pallas kernels, shards(): call(side_kernel, near_outs, [VMEM] * 5, turned_buf)  4.12 us
    ppermute x2, starting transfers between devices, sides(): lax.ppermute(value, 'loc', beside)  4.01 us
    pallas_call x1, Pallas kernels, shards(): call(functools.partial(front_kernel, levels), [((MSG_ROWS, rows), HALF),...  2.84 us
    ppermute x4, waiting for transfers between devices, partner(): return lax.ppermute(value, 'loc', pairs)  2.35 us
    ppermute x6, starting transfers between devices, sibling(): return lax.ppermute(value, 'loc', beside)  2.07 us
  transfers between devices with their start and end apart: 15, of which 5 were waited for; matrix products, arithmetic and copies ran while one was open for 0% of the time, Pallas kernels for 16%

profile of v4, /device:TPU:0, one launch (start us, length us, event | category | flops | bytes accessed | tf_op | source)
XLA Modules:
  0.0 48.8 jit_solution(17748063032190067210)
XLA Ops:
  1.9 0.9 %convert_add_fusion.refs_2_.refs_6_.given = f32[32,1024]{1,0:T(8,128)S(1)} fusion(s32[4,256]{1,0:T(4,128)} %param.9, f32[3,1024]{1,0:T(4,128)} %param.7, f32[16,1024]{1,0:T(8,128)} %param.8), kind=kLoop, calls=%fused_computation | loop fusion | flops 98304 | bytes 212992 | tf_op jit(solution)/shard_map/add | solution.py:382
  2.8 2.8 %shard_map.102 = (bf16[64,1024]{1,0:T(8,128)(2,1)S(1)}, bf16[32,1024]{1,0:T(8,128)(2,1)S(1)}, bf16[1024,1024]{1,0:T(8,128)(2,1)S(1)}, bf16[4,32,256]{2,1,0:T(8,1...) custom-call(f32[1]{0:T(128)S(6)} %copy.12.refs_0_, ...), custom_call_target="tpu_custom_call" | custom-call | flops 2000000000 | bytes 65536 | tf_op jit(solution)/shard_map/pallas_call | solution.py:383
  5.7 0.5 %collective-permute-start.2 = (bf16[2,96,256]{2,1,0:T(8,128)(2,1)S(1)}, bf16[2,96,256]{2,1,0:T(8,128)(2,1)S(1)}, u32[]{:S(2)}, u32[]{:S(2)}) collective-permute-start(bf16[2,96,256]{2,1,0:T(8,128)(2,1)S(1)} %get-tuple-element.42), channel_id=1, source_target_pairs={{0,1},{1,0},{2,3},{3,2},{4,5},{5,4},{6,7},{7,6},{8,9},{9,8},{10,11... | collective-permute-start | bytes 294920 | tf_op jit(solution)/shard_map/ppermute | solution.py:374
  6.2 0.7 %collective-permute-start = (bf16[64,1024]{1,0:T(8,128)(2,1)S(1)}, bf16[64,1024]{1,0:T(8,128)(2,1)S(1)}, u32[]{:S(2)}, u32[]{:S(2)}) collective-permute-start(bf16[64,1024]{1,0:T(8,128)(2,1)S(1)} %get-tuple-element.39.msg), channel_id=1, source_target_pairs={{1,2},{3,4},{5,6},{7,8},{9,10},{11,12},{13,14},{15,16},{17,18},{19... | collective-permute-start | bytes 393224 | tf_op jit(solution)/shard_map/ppermute | solution.py:377
  6.8 3.9 %collective-permute-start.1 = (bf16[64,1024]{1,0:T(8,128)(2,1)S(1)}, bf16[64,1024]{1,0:T(8,128)(2,1)S(1)}, u32[]{:S(2)}, u32[]{:S(2)}) collective-permute-start(bf16[64,1024]{1,0:T(8,128)(2,1)S(1)} %get-tuple-element.39.msg), channel_id=1, source_target_pairs={{0,1},{1,0},{2,3},{3,2},{4,5},{5,4},{6,7},{7,6},{8,9},{9,8},{10,11... | collective-permute-start | bytes 393224 | tf_op jit(solution)/shard_map/ppermute | solution.py:377
  10.8 2.0 %shard_map.103 = (bf16[1024,1024]{1,0:T(8,128)(2,1)S(1)}, f32[32,1024]{1,0:T(8,128)S(1)}, f32[16,1024]{1,0:T(8,128)S(1)}, bf16[2,96,256]{2,1,0:T(8,128)(2,1)S(1)}, bf16[2,96,256]{2,1,0:T(8,128)(2,1)S(1)}) custom-call(f32[8,128]{1,0:T(8,128)S(1)} %get-tuple-element.38.numbers.refs_0_, bf16[64,1024]{1,0:T(8,128)(2,1)S(1)} %get-tuple-element.39.msg, ...), custom_call_target="tpu_custom_call" | custom-call | flops 2000000000 | bytes 65536 | tf_op jit(solution)/shard_map/pallas_call | solution.py:405
  12.8 1.5 %collective-permute-start.3 = (bf16[2,96,256]{2,1,0:T(8,128)(2,1)S(1)}, bf16[2,96,256]{2,1,0:T(8,128)(2,1)S(1)}, u32[]{:S(2)}, u32[]{:S(2)}) collective-permute-start(bf16[2,96,256]{2,1,0:T(8,128)(2,1)S(1)} %get-tuple-element.50), channel_id=1, source_target_pairs={{0,2},{1,5},{2,0},{3,7},{4,6},{5,1},{6,4},{7,3},{8,10},{9,13},{10,... | collective-permute-start | bytes 294920 | tf_op jit(solution)/shard_map/ppermute | solution.py:371
  14.3 1.6 %collective-permute-start.4 = (bf16[2,96,256]{2,1,0:T(8,128)(2,1)S(1)}, bf16[2,96,256]{2,1,0:T(8,128)(2,1)S(1)}, u32[]{:S(2)}, u32[]{:S(2)}) collective-permute-start(bf16[2,96,256]{2,1,0:T(8,128)(2,1)S(1)} %get-tuple-element.51), channel_id=1, source_target_pairs={{0,8},{1,17},{2,10},{3,19},{4,12},{5,21},{6,14},{7,23},{8,0},{9,25... | collective-permute-start | bytes 294920 | tf_op jit(solution)/shard_map/ppermute | solution.py:371
  15.9 2.1 %shard_map.104 = (bf16[1024,1024]{1,0:T(8,128)(2,1)S(1)}, f32[32,1024]{1,0:T(8,128)S(1)}, f32[16,1024]{1,0:T(8,128)S(1)}) custom-call(f32[8,128]{1,0:T(8,128)S(1)} %get-tuple-element.38.numbers.refs_0_, bf16[64,1024]{1,0:T(8,128)(2,1)S(1)} %collective-permute-done.1.msg, bf16[32,1024]{1,0:T(8,128)(2,1)S(1)} %get-tuple-element.40.target, ...), custom_call_target="tpu_custom_call" | custom-call | flops 2000000000 | bytes 65536 | tf_op jit(solution)/shard_map/pallas_call | solution.py:412
  18.0 1.0 %collective-permute-start.5 = (bf16[2,96,256]{2,1,0:T(8,128)(2,1)S(1)}, bf16[2,96,256]{2,1,0:T(8,128)(2,1)S(1)}, u32[]{:S(2)}, u32[]{:S(2)}) collective-permute-start(bf16[2,96,256]{2,1,0:T(8,128)(2,1)S(1)} %collective-permute-done.3.refs_5_), channel_id=1, source_target_pairs={{0,1},{1,0},{2,3},{3,2},{4,5},{5,4},{6,7},{7,6},{8,9},{9,8},{10,11... | collective-permute-start | bytes 294920 | tf_op jit(solution)/shard_map/ppermute | solution.py:374
  19.0 1.0 %collective-permute-done.4.refs_6_ = bf16[2,96,256]{2,1,0:T(8,128)(2,1)S(1)} collective-permute-done((bf16[2,96,256]{2,1,0:T(8,128)(2,1)S(1)}, bf16[2,96,256]{2,1,0:T(8,128)(2,1)S(1)}, u32[]{:S(2)}, u32[]{:S(2)}) %collective-permute-start.4) | collective-permute-done | bytes 98336 | tf_op jit(solution)/shard_map/ppermute | solution.py:371
  20.0 2.1 %shard_map.105 = (bf16[1024,1024]{1,0:T(8,128)(2,1)S(1)}, f32[32,1024]{1,0:T(8,128)S(1)}, f32[16,1024]{1,0:T(8,128)S(1)}) custom-call(f32[8,128]{1,0:T(8,128)S(1)} %get-tuple-element.38.numbers.refs_0_, bf16[64,1024]{1,0:T(8,128)(2,1)S(1)} %collective-permute-done.msg, bf16[32,1024]{1,0:T(8,128)(2,1)S(1)} %get-tuple-element.40.target, ...), custom_call_target="tpu_custom_call" | custom-call | flops 2000000000 | bytes 65536 | tf_op jit(solution)/shard_map/pallas_call | solution.py:414
  22.1 2.1 %shard_map.106 = (bf16[4,256,256]{2,1,0:T(8,128)(2,1)S(1)}, bf16[4,256,256]{2,1,0:T(8,128)(2,1)S(1)}, f32[1,1024]{1,0:T(1,128)S(1)}, f32[16,1024]{1,0:T(8,128)S(...) custom-call(f32[8,128]{1,0:T(8,128)S(1)} %get-tuple-element.38.numbers.refs_0_, ...), custom_call_target="tpu_custom_call" | custom-call | flops 2000000000 | bytes 65536 | tf_op jit(solution)/shard_map/pallas_call | solution.py:415
  24.2 0.6 %collective-permute-start.9 = (bf16[2,32,256]{2,1,0:T(8,128)(2,1)S(1)}, bf16[2,32,256]{2,1,0:T(8,128)(2,1)S(1)}, u32[]{:S(2)}, u32[]{:S(2)}) collective-permute-start(bf16[2,32,256]{2,1,0:T(8,128)(2,1)S(1)} %get-tuple-element.62), channel_id=1, source_target_pairs={{0,1},{1,0},{2,3},{3,2},{4,5},{5,4},{6,7},{7,6},{8,9},{9,8},{10,11... | collective-permute-start | bytes 98312 | tf_op jit(solution)/shard_map/ppermute | solution.py:374
  24.8 0.7 %collective-permute-start.8 = (bf16[32,1024]{1,0:T(8,128)(2,1)S(1)}, bf16[32,1024]{1,0:T(8,128)(2,1)S(1)}, u32[]{:S(2)}, u32[]{:S(2)}) collective-permute-start(bf16[32,1024]{1,0:T(8,128)(2,1)S(1)} %get-tuple-element.52.wmsg), channel_id=1, source_target_pairs={{1,2},{3,4},{5,6},{7,8},{9,10},{11,12},{13,14},{15,16},{17,18},{19... | collective-permute-start | bytes 196616 | tf_op jit(solution)/shard_map/ppermute | solution.py:377
  25.6 3.3 %collective-permute-start.10 = (bf16[2,32,256]{2,1,0:T(8,128)(2,1)S(1)}, bf16[2,32,256]{2,1,0:T(8,128)(2,1)S(1)}, u32[]{:S(2)}, u32[]{:S(2)}) collective-permute-start(bf16[2,32,256]{2,1,0:T(8,128)(2,1)S(1)} %get-tuple-element.63), channel_id=1, source_target_pairs={{0,2},{1,5},{2,0},{3,7},{4,6},{5,1},{6,4},{7,3},{8,10},{9,13},{10,... | collective-permute-start | bytes 98312 | tf_op jit(solution)/shard_map/ppermute | solution.py:371
  28.9 1.4 %collective-permute-start.11 = (bf16[2,32,256]{2,1,0:T(8,128)(2,1)S(1)}, bf16[2,32,256]{2,1,0:T(8,128)(2,1)S(1)}, u32[]{:S(2)}, u32[]{:S(2)}) collective-permute-start(bf16[2,32,256]{2,1,0:T(8,128)(2,1)S(1)} %get-tuple-element.64), channel_id=1, source_target_pairs={{0,8},{1,17},{2,10},{3,19},{4,12},{5,21},{6,14},{7,23},{8,0},{9,25... | collective-permute-start | bytes 98312 | tf_op jit(solution)/shard_map/ppermute | solution.py:371
  32.1 0.8 %collective-permute-done.11.refs_9_ = bf16[2,32,256]{2,1,0:T(8,128)(2,1)S(1)} collective-permute-done((bf16[2,32,256]{2,1,0:T(8,128)(2,1)S(1)}, bf16[2,32,256]{2,1,0:T(8,128)(2,1)S(1)}, u32[]{:S(2)}, u32[]{:S(2)}) %collective-permute-start.11) | collective-permute-done | bytes 32800 | tf_op jit(solution)/shard_map/ppermute | solution.py:371
  32.9 1.2 %shard_map.107.refs_0_ = f32[32,1024]{1,0:T(8,128)S(1)} custom-call(bf16[32,1024]{1,0:T(8,128)(2,1)S(1)} %get-tuple-element.52.wmsg, bf16[32,1024]{1,0:T(8,128)(2,1)S(1)} %collective-permute-done.7.wmsg_a, bf16[32,1024]{1,0:T(8,128)(2,1)S(1)} %collective-permute-done.8.wmsg_b, bf16[1024,1024]{1,0:T(8,128)(2,1)S(1)} %get-tuple-element.53.kept, ...), custom_call_target="tpu_custom_call" | custom-call | flops 1200000000 | bytes 65536 | tf_op jit(solution)/shard_map/pallas_call | solution.py:432
  34.1 1.4 %shard_map.109 = (f32[32,128]{1,0:T(8,128)}, f32[16,1024]{1,0:T(8,128)S(1)}, f32[16,1024]{1,0:T(8,128)S(1)}, f32[16,128]{1,0:T(8,128)S(1)}) custom-call(f32[32,1024]{1,0:T(8,128)S(1)} %shard_map.107.refs_0_, bf16[1024,1024]{1,0:T(8,128)(2,1)S(1)} %get-tuple-element.48.refs_3_.refs_1_, bf16[4,256,256]{2,1,0:T(8,128)(2,1)S(1)} %get-tuple-element.56.refs_2_, ...), custom_call_target="tpu_custom_call" | custom-call | flops 2000000000 | bytes 65536 | tf_op jit(solution)/shard_map/pallas_call | solution.py:434
  35.5 5.4 %all-to-all-start = ((f32[32,1,128]{2,1,0:T(1,128)}), f32[32,1,128]{2,1,0:T(1,128)S(1)}, u32[]{:S(2)}, u32[]{:S(2)}) async-start(f32[32,1,128]{2,1,0:T(1,128)} %bitcast.1), calls=%async_computation | async-start | bytes 32768 | tf_op jit(solution)/shard_map/all_to_all | solution.py:439
  40.8 0.7 %shard_map.111 = f32[16,1024]{1,0:T(8,128)} custom-call(f32[1]{0:T(128)S(6)} %copy.14.signal, f32[8,128]{1,0:T(8,128)S(1)} %get-tuple-element.38.numbers.refs_0_, f32[16,1024]{1,0:T(8,128)S(1)} %get-tuple-element.60.refs_7_.source), custom_call_target="tpu_custom_call" | custom-call | flops 2000000000 | bytes 65536 | tf_op jit(solution)/shard_map/pallas_call | solution.py:440
  41.5 6.4 %all-to-all-done = f32[32,1,128]{2,1,0:T(1,128)S(1)} async-done(((f32[32,1,128]{2,1,0:T(1,128)}), f32[32,1,128]{2,1,0:T(1,128)S(1)}, u32[]{:S(2)}, u32[]{:S(2)}) %all-to-all-start) | async-done | bytes 16416 | tf_op jit(solution)/shard_map/all_to_all | solution.py:439
  47.9 0.9 %shard_map.110 = (f32[16,1024]{1,0:T(8,128)}, f32[16,1024]{1,0:T(8,128)}, f32[1,16]{1,0:T(1,128)}) custom-call(f32[1]{0:T(128)S(6)} %copy.14.signal, f32[1]{0:T(128)S(6)} %copy.15.noise, f32[8,128]{1,0:T(8,128)S(1)} %get-tuple-element.38.numbers.refs_0_, f32[32,128]{1,0:T(8,128)S(1)} %bitcast.5, f32[16,128]{1,0:T(8,128)S(1)} %get-tuple-element.66.shift_in, ...), custom_call_target="tpu_custom_call" | custom-call | flops 2000000000 | bytes 65536 | tf_op jit(solution)/shard_map/pallas_call | solution.py:441
  (17 shorter events, 0.8 us)
Async XLA Ops:
  5.7 5.1 %collective-permute-start.2 = (bf16[2,96,256]{2,1,0:T(8,128)(2,1)S(1)}, bf16[2,96,256]{2,1,0:T(8,128)(2,1)S(1)}, u32[]{:S(2)}, u32[]{:S(2)}) collective-permute-start(bf16[2,96,256]{2,1,0:T(8,128)(2,1)S(1)} %get-tuple-element.42), channel_id=1, source_target_pairs={{0,1},{1,0},{2,3},{3,2},{4,5},{5,4},{6,7},{7,6},{8,9},{9,8},{10,11... | collective-permute-start | bytes 294920 | tf_op jit(solution)/shard_map/ppermute | solution.py:374
  6.2 13.8 %collective-permute-start = (bf16[64,1024]{1,0:T(8,128)(2,1)S(1)}, bf16[64,1024]{1,0:T(8,128)(2,1)S(1)}, u32[]{:S(2)}, u32[]{:S(2)}) collective-permute-start(bf16[64,1024]{1,0:T(8,128)(2,1)S(1)} %get-tuple-element.39.msg), channel_id=1, source_target_pairs={{1,2},{3,4},{5,6},{7,8},{9,10},{11,12},{13,14},{15,16},{17,18},{19... | collective-permute-start | bytes 393224 | tf_op jit(solution)/shard_map/ppermute | solution.py:377
  6.8 9.1 %collective-permute-start.1 = (bf16[64,1024]{1,0:T(8,128)(2,1)S(1)}, bf16[64,1024]{1,0:T(8,128)(2,1)S(1)}, u32[]{:S(2)}, u32[]{:S(2)}) collective-permute-start(bf16[64,1024]{1,0:T(8,128)(2,1)S(1)} %get-tuple-element.39.msg), channel_id=1, source_target_pairs={{0,1},{1,0},{2,3},{3,2},{4,5},{5,4},{6,7},{7,6},{8,9},{9,8},{10,11... | collective-permute-start | bytes 393224 | tf_op jit(solution)/shard_map/ppermute | solution.py:377
  12.8 5.2 %collective-permute-start.3 = (bf16[2,96,256]{2,1,0:T(8,128)(2,1)S(1)}, bf16[2,96,256]{2,1,0:T(8,128)(2,1)S(1)}, u32[]{:S(2)}, u32[]{:S(2)}) collective-permute-start(bf16[2,96,256]{2,1,0:T(8,128)(2,1)S(1)} %get-tuple-element.50), channel_id=1, source_target_pairs={{0,2},{1,5},{2,0},{3,7},{4,6},{5,1},{6,4},{7,3},{8,10},{9,13},{10,... | collective-permute-start | bytes 294920 | tf_op jit(solution)/shard_map/ppermute | solution.py:371
  14.3 5.7 %collective-permute-start.4 = (bf16[2,96,256]{2,1,0:T(8,128)(2,1)S(1)}, bf16[2,96,256]{2,1,0:T(8,128)(2,1)S(1)}, u32[]{:S(2)}, u32[]{:S(2)}) collective-permute-start(bf16[2,96,256]{2,1,0:T(8,128)(2,1)S(1)} %get-tuple-element.51), channel_id=1, source_target_pairs={{0,8},{1,17},{2,10},{3,19},{4,12},{5,21},{6,14},{7,23},{8,0},{9,25... | collective-permute-start | bytes 294920 | tf_op jit(solution)/shard_map/ppermute | solution.py:371
  18.0 4.1 %collective-permute-start.5 = (bf16[2,96,256]{2,1,0:T(8,128)(2,1)S(1)}, bf16[2,96,256]{2,1,0:T(8,128)(2,1)S(1)}, u32[]{:S(2)}, u32[]{:S(2)}) collective-permute-start(bf16[2,96,256]{2,1,0:T(8,128)(2,1)S(1)} %collective-permute-done.3.refs_5_), channel_id=1, source_target_pairs={{0,1},{1,0},{2,3},{3,2},{4,5},{5,4},{6,7},{7,6},{8,9},{9,8},{10,11... | collective-permute-start | bytes 294920 | tf_op jit(solution)/shard_map/ppermute | solution.py:374
  20.0 2.1 %collective-permute-start.6 = (bf16[2,96,256]{2,1,0:T(8,128)(2,1)S(1)}, bf16[2,96,256]{2,1,0:T(8,128)(2,1)S(1)}, u32[]{:S(2)}, u32[]{:S(2)}) collective-permute-start(bf16[2,96,256]{2,1,0:T(8,128)(2,1)S(1)} %collective-permute-done.4.refs_6_), channel_id=1, source_target_pairs={{0,1},{1,0},{2,3},{3,2},{4,5},{5,4},{6,7},{7,6},{8,9},{9,8},{10,11... | collective-permute-start | bytes 294920 | tf_op jit(solution)/shard_map/ppermute | solution.py:374
  24.2 1.4 %collective-permute-start.9 = (bf16[2,32,256]{2,1,0:T(8,128)(2,1)S(1)}, bf16[2,32,256]{2,1,0:T(8,128)(2,1)S(1)}, u32[]{:S(2)}, u32[]{:S(2)}) collective-permute-start(bf16[2,32,256]{2,1,0:T(8,128)(2,1)S(1)} %get-tuple-element.62), channel_id=1, source_target_pairs={{0,1},{1,0},{2,3},{3,2},{4,5},{5,4},{6,7},{7,6},{8,9},{9,8},{10,11... | collective-permute-start | bytes 98312 | tf_op jit(solution)/shard_map/ppermute | solution.py:374
  24.8 8.1 %collective-permute-start.7 = (bf16[32,1024]{1,0:T(8,128)(2,1)S(1)}, bf16[32,1024]{1,0:T(8,128)(2,1)S(1)}, u32[]{:S(2)}, u32[]{:S(2)}) collective-permute-start(bf16[32,1024]{1,0:T(8,128)(2,1)S(1)} %get-tuple-element.52.wmsg), channel_id=1, source_target_pairs={{0,1},{1,0},{2,3},{3,2},{4,5},{5,4},{6,7},{7,6},{8,9},{9,8},{10,11... | collective-permute-start | bytes 196616 | tf_op jit(solution)/shard_map/ppermute | solution.py:377
  24.8 8.1 %collective-permute-start.8 = (bf16[32,1024]{1,0:T(8,128)(2,1)S(1)}, bf16[32,1024]{1,0:T(8,128)(2,1)S(1)}, u32[]{:S(2)}, u32[]{:S(2)}) collective-permute-start(bf16[32,1024]{1,0:T(8,128)(2,1)S(1)} %get-tuple-element.52.wmsg), channel_id=1, source_target_pairs={{1,2},{3,4},{5,6},{7,8},{9,10},{11,12},{13,14},{15,16},{17,18},{19... | collective-permute-start | bytes 196616 | tf_op jit(solution)/shard_map/ppermute | solution.py:377
  25.6 6.4 %collective-permute-start.10 = (bf16[2,32,256]{2,1,0:T(8,128)(2,1)S(1)}, bf16[2,32,256]{2,1,0:T(8,128)(2,1)S(1)}, u32[]{:S(2)}, u32[]{:S(2)}) collective-permute-start(bf16[2,32,256]{2,1,0:T(8,128)(2,1)S(1)} %get-tuple-element.63), channel_id=1, source_target_pairs={{0,2},{1,5},{2,0},{3,7},{4,6},{5,1},{6,4},{7,3},{8,10},{9,13},{10,... | collective-permute-start | bytes 98312 | tf_op jit(solution)/shard_map/ppermute | solution.py:371
  28.9 4.0 %collective-permute-start.11 = (bf16[2,32,256]{2,1,0:T(8,128)(2,1)S(1)}, bf16[2,32,256]{2,1,0:T(8,128)(2,1)S(1)}, u32[]{:S(2)}, u32[]{:S(2)}) collective-permute-start(bf16[2,32,256]{2,1,0:T(8,128)(2,1)S(1)} %get-tuple-element.64), channel_id=1, source_target_pairs={{0,8},{1,17},{2,10},{3,19},{4,12},{5,21},{6,14},{7,23},{8,0},{9,25... | collective-permute-start | bytes 98312 | tf_op jit(solution)/shard_map/ppermute | solution.py:371
  32.1 2.0 %collective-permute-start.12 = (bf16[2,32,256]{2,1,0:T(8,128)(2,1)S(1)}, bf16[2,32,256]{2,1,0:T(8,128)(2,1)S(1)}, u32[]{:S(2)}, u32[]{:S(2)}) collective-permute-start(bf16[2,32,256]{2,1,0:T(8,128)(2,1)S(1)} %collective-permute-done.10.refs_8_), channel_id=1, source_target_pairs={{0,1},{1,0},{2,3},{3,2},{4,5},{5,4},{6,7},{7,6},{8,9},{9,8},{10,11... | collective-permute-start | bytes 98312 | tf_op jit(solution)/shard_map/ppermute | solution.py:374
  32.9 1.2 %collective-permute-start.13 = (bf16[2,32,256]{2,1,0:T(8,128)(2,1)S(1)}, bf16[2,32,256]{2,1,0:T(8,128)(2,1)S(1)}, u32[]{:S(2)}, u32[]{:S(2)}) collective-permute-start(bf16[2,32,256]{2,1,0:T(8,128)(2,1)S(1)} %collective-permute-done.11.refs_9_), channel_id=1, source_target_pairs={{0,1},{1,0},{2,3},{3,2},{4,5},{5,4},{6,7},{7,6},{8,9},{9,8},{10,11... | collective-permute-start | bytes 98312 | tf_op jit(solution)/shard_map/ppermute | solution.py:374
  35.5 12.4 %all-to-all-start = ((f32[32,1,128]{2,1,0:T(1,128)}), f32[32,1,128]{2,1,0:T(1,128)S(1)}, u32[]{:S(2)}, u32[]{:S(2)}) async-start(f32[32,1,128]{2,1,0:T(1,128)} %bitcast.1), calls=%async_computation | async-start | bytes 32768 | tf_op jit(solution)/shard_map/all_to_all | solution.py:439

commit v5 on v4

--- a/solution.py
+++ b/solution.py
@@ -17,6 +17,7 @@
 MSG_ROWS = 64
 VEC_ROWS = 48
 TILE = 128
+WIDE_TILE = 512
 VMEM = pltpu.VMEM
 SMEM = pltpu.SMEM
 
@@ -152,10 +153,10 @@
         skel_source = both[:SRC_ROWS]
         sources.append(skel_source.astype(HALF))
         turned_src[level * rank : (level + 1) * rank, :] = skel_source.T.astype(HALF)
-    rates = numbers[1:2, :], numbers[3:4, :]
-    for col in range(0, rows, TILE):
-        squared = dot(turned_src[...], target[:, col : col + TILE])
-        basis[:, col : col + TILE] = matern(squared, rates)[0].astype(HALF)
+    rates = [jnp.concatenate([numbers[row : row + 1, :]] * (WIDE_TILE // 128), axis=1) for row in (1, 3)]
+    for col in range(0, rows, WIDE_TILE):
+        squared = dot(turned_src[...], target[:, col : col + WIDE_TILE])
+        basis[:, col : col + WIDE_TILE] = matern(squared, rates)[0].astype(HALF)
     high, low = split_two(given[0:16, :])
     msg[0:16, :] = low
     msg[16:32, :] = high
@@ -436,6 +437,7 @@
         [((count, 128), FULL), ((probes, rows), FULL), ((probes, rows), FULL), ((probes, 128), FULL)],
         [VMEM] * (8 + levels),
     )(near, basis, coup_high, coup_low, row_sum, first, given, slopes, *cross, *other)
+    sums, signal, noise_var = lax.optimization_barrier((sums, signal, noise_var))
     table = lax.all_to_all(sums, "loc", 0, 0, tiled=True)
     (slope_image,) = call(slope_kernel, [((probes, rows), FULL)], [SMEM, VMEM, VMEM])(signal, numbers, slopes)
     solution, residual, trace = call(

time: 49.1 us -> 48.3 us (0.984)
  waiting for transfers between devices: 8.91 us -> 7 us
  starting transfers between devices: 20.5 us -> 21.9 us
    ppermute x2, starting transfers between devices: 4.01 us -> 0.16 us  [sides(): lax.ppermute(value, 'loc', beside)]
    ppermute x4, starting transfers between devices: 7.76 us -> 11.4 us  [partner(): return lax.ppermute(value, 'loc', pairs)]
    ppermute x4, waiting for transfers between devices: 2.35 us -> 0.25 us  [partner(): return lax.ppermute(value, 'loc', pairs)]
    ppermute x6, starting transfers between devices: 2.07 us -> 3.95 us  [sibling(): return lax.ppermute(value, 'loc', beside)]
  transfers between devices with their start and end apart: 15 -> 15, of which waited for: 5 -> 4; matrix products, arithmetic and copies ran while one was open for 0% -> 0% of each run, Pallas kernels for 16% -> 17%
where the time goes in v5:
time: 48.3 us; the launch traced here: 48.1 us
  starting transfers between devices  21.9 us (45%)
  Pallas kernels  14.9 us (31%)
  waiting for transfers between devices  7 us (14%)
  between operations  3.35 us (7%)
  other arithmetic  0.88 us (2%)
    ppermute x4, starting transfers between devices, partner(): return lax.ppermute(value, 'loc', pairs)  11.4 us
    all_to_all x1, waiting for transfers between devices, shards(): table = lax.all_to_all(sums, 'loc', 0, 0, tiled=True)  6.4 us
    all_to_all x1, starting transfers between devices, shards(): table = lax.all_to_all(sums, 'loc', 0, 0, tiled=True)  5.05 us
    pallas_call x2, Pallas kernels, shards(): call(side_kernel, near_outs, [VMEM] * 5, turned_buf)  4.12 us
    ppermute x6, starting transfers between devices, sibling(): return lax.ppermute(value, 'loc', beside)  3.95 us
    pallas_call x1, Pallas kernels, shards(): call(functools.partial(front_kernel, levels), [((MSG_ROWS, rows), HALF),...  2.63 us
    pallas_call x1, Pallas kernels, shards(): call(functools.partial(far_kernel, half, far_scale), [((levels, rank, ran...  2.07 us
    pallas_call x1, Pallas kernels, shards(): call(own_kernel, near_outs + [((2, 96, rank), HALF)] * half, [VMEM] * 5,...  2.01 us
  transfers between devices with their start and end apart: 15, of which 4 were waited for; matrix products, arithmetic and copies ran while one was open for 0% of the time, Pallas kernels for 17%

profile of v5, /device:TPU:0, one launch (start us, length us, event | category | flops | bytes accessed | tf_op | source)
XLA Modules:
  0.0 48.1 jit_solution(12943943607154754694)
XLA Ops:
  1.9 0.9 %convert_add_fusion.refs_2_.refs_6_.given = f32[32,1024]{1,0:T(8,128)S(1)} fusion(s32[4,256]{1,0:T(4,128)} %param.9, f32[3,1024]{1,0:T(4,128)} %param.7, f32[16,1024]{1,0:T(8,128)} %param.8), kind=kLoop, calls=%fused_computation | loop fusion | flops 98304 | bytes 212992 | tf_op jit(solution)/shard_map/add | solution.py:383
  2.8 2.6 %shard_map.102 = (bf16[64,1024]{1,0:T(8,128)(2,1)S(1)}, bf16[32,1024]{1,0:T(8,128)(2,1)S(1)}, bf16[1024,1024]{1,0:T(8,128)(2,1)S(1)}, bf16[4,32,256]{2,1,0:T(8,1...) custom-call(f32[1]{0:T(128)S(6)} %copy.12.refs_0_, ...), custom_call_target="tpu_custom_call" | custom-call | flops 2000000000 | bytes 65536 | tf_op jit(solution)/shard_map/pallas_call | solution.py:384
  5.4 0.5 %collective-permute-start.2 = (bf16[2,96,256]{2,1,0:T(8,128)(2,1)S(1)}, bf16[2,96,256]{2,1,0:T(8,128)(2,1)S(1)}, u32[]{:S(2)}, u32[]{:S(2)}) collective-permute-start(bf16[2,96,256]{2,1,0:T(8,128)(2,1)S(1)} %get-tuple-element.45), channel_id=1, source_target_pairs={{0,1},{1,0},{2,3},{3,2},{4,5},{5,4},{6,7},{7,6},{8,9},{9,8},{10,11... | collective-permute-start | bytes 294920 | tf_op jit(solution)/shard_map/ppermute | solution.py:375
  6.0 0.7 %collective-permute-start = (bf16[64,1024]{1,0:T(8,128)(2,1)S(1)}, bf16[64,1024]{1,0:T(8,128)(2,1)S(1)}, u32[]{:S(2)}, u32[]{:S(2)}) collective-permute-start(bf16[64,1024]{1,0:T(8,128)(2,1)S(1)} %get-tuple-element.42.msg), channel_id=1, source_target_pairs={{1,2},{3,4},{5,6},{7,8},{9,10},{11,12},{13,14},{15,16},{17,18},{19... | collective-permute-start | bytes 393224 | tf_op jit(solution)/shard_map/ppermute | solution.py:378
  6.9 2.0 %shard_map.103 = (bf16[1024,1024]{1,0:T(8,128)(2,1)S(1)}, f32[32,1024]{1,0:T(8,128)S(1)}, f32[16,1024]{1,0:T(8,128)S(1)}, bf16[2,96,256]{2,1,0:T(8,128)(2,1)S(1)}, bf16[2,96,256]{2,1,0:T(8,128)(2,1)S(1)}) custom-call(f32[8,128]{1,0:T(8,128)S(1)} %get-tuple-element.41.numbers.refs_0_, bf16[64,1024]{1,0:T(8,128)(2,1)S(1)} %get-tuple-element.42.msg, ...), custom_call_target="tpu_custom_call" | custom-call | flops 2000000000 | bytes 65536 | tf_op jit(solution)/shard_map/pallas_call | solution.py:406
  8.9 4.0 %collective-permute-start.3 = (bf16[2,96,256]{2,1,0:T(8,128)(2,1)S(1)}, bf16[2,96,256]{2,1,0:T(8,128)(2,1)S(1)}, u32[]{:S(2)}, u32[]{:S(2)}) collective-permute-start(bf16[2,96,256]{2,1,0:T(8,128)(2,1)S(1)} %get-tuple-element.53), channel_id=1, source_target_pairs={{0,2},{1,5},{2,0},{3,7},{4,6},{5,1},{6,4},{7,3},{8,10},{9,13},{10,... | collective-permute-start | bytes 294920 | tf_op jit(solution)/shard_map/ppermute | solution.py:372
  13.0 2.1 %collective-permute-start.4 = (bf16[2,96,256]{2,1,0:T(8,128)(2,1)S(1)}, bf16[2,96,256]{2,1,0:T(8,128)(2,1)S(1)}, u32[]{:S(2)}, u32[]{:S(2)}) collective-permute-start(bf16[2,96,256]{2,1,0:T(8,128)(2,1)S(1)} %get-tuple-element.54), channel_id=1, source_target_pairs={{0,8},{1,17},{2,10},{3,19},{4,12},{5,21},{6,14},{7,23},{8,0},{9,25... | collective-permute-start | bytes 294920 | tf_op jit(solution)/shard_map/ppermute | solution.py:372
  15.1 2.1 %shard_map.104 = (bf16[1024,1024]{1,0:T(8,128)(2,1)S(1)}, f32[32,1024]{1,0:T(8,128)S(1)}, f32[16,1024]{1,0:T(8,128)S(1)}) custom-call(f32[8,128]{1,0:T(8,128)S(1)} %get-tuple-element.41.numbers.refs_0_, bf16[64,1024]{1,0:T(8,128)(2,1)S(1)} %collective-permute-done.1.msg, bf16[32,1024]{1,0:T(8,128)(2,1)S(1)} %get-tuple-element.43.target, ...), custom_call_target="tpu_custom_call" | custom-call | flops 2000000000 | bytes 65536 | tf_op jit(solution)/shard_map/pallas_call | solution.py:413
  17.2 1.6 %collective-permute-start.5 = (bf16[2,96,256]{2,1,0:T(8,128)(2,1)S(1)}, bf16[2,96,256]{2,1,0:T(8,128)(2,1)S(1)}, u32[]{:S(2)}, u32[]{:S(2)}) collective-permute-start(bf16[2,96,256]{2,1,0:T(8,128)(2,1)S(1)} %collective-permute-done.3.refs_5_), channel_id=1, source_target_pairs={{0,1},{1,0},{2,3},{3,2},{4,5},{5,4},{6,7},{7,6},{8,9},{9,8},{10,11... | collective-permute-start | bytes 294920 | tf_op jit(solution)/shard_map/ppermute | solution.py:375
  18.9 2.1 %shard_map.105 = (bf16[1024,1024]{1,0:T(8,128)(2,1)S(1)}, f32[32,1024]{1,0:T(8,128)S(1)}, f32[16,1024]{1,0:T(8,128)S(1)}) custom-call(f32[8,128]{1,0:T(8,128)S(1)} %get-tuple-element.41.numbers.refs_0_, bf16[64,1024]{1,0:T(8,128)(2,1)S(1)} %collective-permute-done.msg, bf16[32,1024]{1,0:T(8,128)(2,1)S(1)} %get-tuple-element.43.target, ...), custom_call_target="tpu_custom_call" | custom-call | flops 2000000000 | bytes 65536 | tf_op jit(solution)/shard_map/pallas_call | solution.py:415
  21.0 2.1 %shard_map.106 = (bf16[4,256,256]{2,1,0:T(8,128)(2,1)S(1)}, bf16[4,256,256]{2,1,0:T(8,128)(2,1)S(1)}, f32[1,1024]{1,0:T(1,128)S(1)}, f32[16,1024]{1,0:T(8,128)S(...) custom-call(f32[8,128]{1,0:T(8,128)S(1)} %get-tuple-element.41.numbers.refs_0_, ...), custom_call_target="tpu_custom_call" | custom-call | flops 2000000000 | bytes 65536 | tf_op jit(solution)/shard_map/pallas_call | solution.py:416
  23.0 0.5 %collective-permute-start.9 = (bf16[2,32,256]{2,1,0:T(8,128)(2,1)S(1)}, bf16[2,32,256]{2,1,0:T(8,128)(2,1)S(1)}, u32[]{:S(2)}, u32[]{:S(2)}) collective-permute-start(bf16[2,32,256]{2,1,0:T(8,128)(2,1)S(1)} %get-tuple-element.65), channel_id=1, source_target_pairs={{0,1},{1,0},{2,3},{3,2},{4,5},{5,4},{6,7},{7,6},{8,9},{9,8},{10,11... | collective-permute-start | bytes 98312 | tf_op jit(solution)/shard_map/ppermute | solution.py:375
  23.6 0.7 %collective-permute-start.8 = (bf16[32,1024]{1,0:T(8,128)(2,1)S(1)}, bf16[32,1024]{1,0:T(8,128)(2,1)S(1)}, u32[]{:S(2)}, u32[]{:S(2)}) collective-permute-start(bf16[32,1024]{1,0:T(8,128)(2,1)S(1)} %get-tuple-element.55.wmsg), channel_id=1, source_target_pairs={{1,2},{3,4},{5,6},{7,8},{9,10},{11,12},{13,14},{15,16},{17,18},{19... | collective-permute-start | bytes 196616 | tf_op jit(solution)/shard_map/ppermute | solution.py:378
  24.4 3.3 %collective-permute-start.10 = (bf16[2,32,256]{2,1,0:T(8,128)(2,1)S(1)}, bf16[2,32,256]{2,1,0:T(8,128)(2,1)S(1)}, u32[]{:S(2)}, u32[]{:S(2)}) collective-permute-start(bf16[2,32,256]{2,1,0:T(8,128)(2,1)S(1)} %get-tuple-element.66), channel_id=1, source_target_pairs={{0,2},{1,5},{2,0},{3,7},{4,6},{5,1},{6,4},{7,3},{8,10},{9,13},{10,... | collective-permute-start | bytes 98312 | tf_op jit(solution)/shard_map/ppermute | solution.py:372
  27.7 2.0 %collective-permute-start.11 = (bf16[2,32,256]{2,1,0:T(8,128)(2,1)S(1)}, bf16[2,32,256]{2,1,0:T(8,128)(2,1)S(1)}, u32[]{:S(2)}, u32[]{:S(2)}) collective-permute-start(bf16[2,32,256]{2,1,0:T(8,128)(2,1)S(1)} %get-tuple-element.67), channel_id=1, source_target_pairs={{0,8},{1,17},{2,10},{3,19},{4,12},{5,21},{6,14},{7,23},{8,0},{9,25... | collective-permute-start | bytes 98312 | tf_op jit(solution)/shard_map/ppermute | solution.py:372
  31.0 0.9 %collective-permute-start.12 = (bf16[2,32,256]{2,1,0:T(8,128)(2,1)S(1)}, bf16[2,32,256]{2,1,0:T(8,128)(2,1)S(1)}, u32[]{:S(2)}, u32[]{:S(2)}) collective-permute-start(bf16[2,32,256]{2,1,0:T(8,128)(2,1)S(1)} %collective-permute-done.10.refs_8_), channel_id=1, source_target_pairs={{0,1},{1,0},{2,3},{3,2},{4,5},{5,4},{6,7},{7,6},{8,9},{9,8},{10,11... | collective-permute-start | bytes 98312 | tf_op jit(solution)/shard_map/ppermute | solution.py:375
  31.9 0.2 collective-permute-done.11.refs_9_
  32.1 0.4 collective-permute-start.13
  32.5 1.2 %shard_map.107.refs_0_ = f32[32,1024]{1,0:T(8,128)S(1)} custom-call(bf16[32,1024]{1,0:T(8,128)(2,1)S(1)} %get-tuple-element.55.wmsg, bf16[32,1024]{1,0:T(8,128)(2,1)S(1)} %collective-permute-done.7.wmsg_a, bf16[32,1024]{1,0:T(8,128)(2,1)S(1)} %collective-permute-done.8.wmsg_b, bf16[1024,1024]{1,0:T(8,128)(2,1)S(1)} %get-tuple-element.56.kept, ...), custom_call_target="tpu_custom_call" | custom-call | flops 1200000000 | bytes 65536 | tf_op jit(solution)/shard_map/pallas_call | solution.py:433
  33.7 1.4 %shard_map.109 = (f32[32,128]{1,0:T(8,128)}, f32[16,1024]{1,0:T(8,128)S(1)}, f32[16,1024]{1,0:T(8,128)S(1)}, f32[16,128]{1,0:T(8,128)S(1)}) custom-call(f32[32,1024]{1,0:T(8,128)S(1)} %shard_map.107.refs_0_, bf16[1024,1024]{1,0:T(8,128)(2,1)S(1)} %get-tuple-element.51.refs_3_.refs_1_, bf16[4,256,256]{2,1,0:T(8,128)(2,1)S(1)} %get-tuple-element.59.refs_2_, ...), custom_call_target="tpu_custom_call" | custom-call | flops 2000000000 | bytes 65536 | tf_op jit(solution)/shard_map/pallas_call | solution.py:435
  35.1 5.1 %all-to-all-start = ((f32[32,1,128]{2,1,0:T(1,128)}), f32[32,1,128]{2,1,0:T(1,128)S(1)}, u32[]{:S(2)}, u32[]{:S(2)}) async-start(f32[32,1,128]{2,1,0:T(1,128)} %bitcast.1), calls=%async_computation | async-start | bytes 32768 | tf_op jit(solution)/shard_map/all_to_all | solution.py:441
  40.1 0.7 %shard_map.111 = f32[16,1024]{1,0:T(8,128)} custom-call(f32[1]{0:T(128)S(6)} %copy.14.signal, f32[8,128]{1,0:T(8,128)S(1)} %get-tuple-element.41.numbers.refs_0_, f32[16,1024]{1,0:T(8,128)S(1)} %get-tuple-element.63.refs_7_.source), custom_call_target="tpu_custom_call" | custom-call | flops 2000000000 | bytes 65536 | tf_op jit(solution)/shard_map/pallas_call | solution.py:442
  40.8 6.4 %all-to-all-done = f32[32,1,128]{2,1,0:T(1,128)S(1)} async-done(((f32[32,1,128]{2,1,0:T(1,128)}), f32[32,1,128]{2,1,0:T(1,128)S(1)}, u32[]{:S(2)}, u32[]{:S(2)}) %all-to-all-start) | async-done | bytes 16416 | tf_op jit(solution)/shard_map/all_to_all | solution.py:441
  47.2 0.9 %shard_map.110 = (f32[16,1024]{1,0:T(8,128)}, f32[16,1024]{1,0:T(8,128)}, f32[1,16]{1,0:T(1,128)}) custom-call(f32[1]{0:T(128)S(6)} %copy.14.signal, f32[1]{0:T(128)S(6)} %copy.15.noise, f32[8,128]{1,0:T(8,128)S(1)} %get-tuple-element.41.numbers.refs_0_, f32[32,128]{1,0:T(8,128)S(1)} %bitcast.5, f32[16,128]{1,0:T(8,128)S(1)} %get-tuple-element.72.shift_in, ...), custom_call_target="tpu_custom_call" | custom-call | flops 2000000000 | bytes 65536 | tf_op jit(solution)/shard_map/pallas_call | solution.py:443
  (17 shorter events, 0.6 us)
Async XLA Ops:
  5.4 1.5 %collective-permute-start.2 = (bf16[2,96,256]{2,1,0:T(8,128)(2,1)S(1)}, bf16[2,96,256]{2,1,0:T(8,128)(2,1)S(1)}, u32[]{:S(2)}, u32[]{:S(2)}) collective-permute-start(bf16[2,96,256]{2,1,0:T(8,128)(2,1)S(1)} %get-tuple-element.45), channel_id=1, source_target_pairs={{0,1},{1,0},{2,3},{3,2},{4,5},{5,4},{6,7},{7,6},{8,9},{9,8},{10,11... | collective-permute-start | bytes 294920 | tf_op jit(solution)/shard_map/ppermute | solution.py:375
  6.0 9.1 %collective-permute-start.1 = (bf16[64,1024]{1,0:T(8,128)(2,1)S(1)}, bf16[64,1024]{1,0:T(8,128)(2,1)S(1)}, u32[]{:S(2)}, u32[]{:S(2)}) collective-permute-start(bf16[64,1024]{1,0:T(8,128)(2,1)S(1)} %get-tuple-element.42.msg), channel_id=1, source_target_pairs={{0,1},{1,0},{2,3},{3,2},{4,5},{5,4},{6,7},{7,6},{8,9},{9,8},{10,11... | collective-permute-start | bytes 393224 | tf_op jit(solution)/shard_map/ppermute | solution.py:378
  6.0 12.8 %collective-permute-start = (bf16[64,1024]{1,0:T(8,128)(2,1)S(1)}, bf16[64,1024]{1,0:T(8,128)(2,1)S(1)}, u32[]{:S(2)}, u32[]{:S(2)}) collective-permute-start(bf16[64,1024]{1,0:T(8,128)(2,1)S(1)} %get-tuple-element.42.msg), channel_id=1, source_target_pairs={{1,2},{3,4},{5,6},{7,8},{9,10},{11,12},{13,14},{15,16},{17,18},{19... | collective-permute-start | bytes 393224 | tf_op jit(solution)/shard_map/ppermute | solution.py:378
  8.9 8.3 %collective-permute-start.3 = (bf16[2,96,256]{2,1,0:T(8,128)(2,1)S(1)}, bf16[2,96,256]{2,1,0:T(8,128)(2,1)S(1)}, u32[]{:S(2)}, u32[]{:S(2)}) collective-permute-start(bf16[2,96,256]{2,1,0:T(8,128)(2,1)S(1)} %get-tuple-element.53), channel_id=1, source_target_pairs={{0,2},{1,5},{2,0},{3,7},{4,6},{5,1},{6,4},{7,3},{8,10},{9,13},{10,... | collective-permute-start | bytes 294920 | tf_op jit(solution)/shard_map/ppermute | solution.py:372
  13.0 5.8 %collective-permute-start.4 = (bf16[2,96,256]{2,1,0:T(8,128)(2,1)S(1)}, bf16[2,96,256]{2,1,0:T(8,128)(2,1)S(1)}, u32[]{:S(2)}, u32[]{:S(2)}) collective-permute-start(bf16[2,96,256]{2,1,0:T(8,128)(2,1)S(1)} %get-tuple-element.54), channel_id=1, source_target_pairs={{0,8},{1,17},{2,10},{3,19},{4,12},{5,21},{6,14},{7,23},{8,0},{9,25... | collective-permute-start | bytes 294920 | tf_op jit(solution)/shard_map/ppermute | solution.py:372
  17.2 3.7 %collective-permute-start.5 = (bf16[2,96,256]{2,1,0:T(8,128)(2,1)S(1)}, bf16[2,96,256]{2,1,0:T(8,128)(2,1)S(1)}, u32[]{:S(2)}, u32[]{:S(2)}) collective-permute-start(bf16[2,96,256]{2,1,0:T(8,128)(2,1)S(1)} %collective-permute-done.3.refs_5_), channel_id=1, source_target_pairs={{0,1},{1,0},{2,3},{3,2},{4,5},{5,4},{6,7},{7,6},{8,9},{9,8},{10,11... | collective-permute-start | bytes 294920 | tf_op jit(solution)/shard_map/ppermute | solution.py:375
  18.8 2.2 %collective-permute-start.6 = (bf16[2,96,256]{2,1,0:T(8,128)(2,1)S(1)}, bf16[2,96,256]{2,1,0:T(8,128)(2,1)S(1)}, u32[]{:S(2)}, u32[]{:S(2)}) collective-permute-start(bf16[2,96,256]{2,1,0:T(8,128)(2,1)S(1)} %collective-permute-done.4.refs_6_), channel_id=1, source_target_pairs={{0,1},{1,0},{2,3},{3,2},{4,5},{5,4},{6,7},{7,6},{8,9},{9,8},{10,11... | collective-permute-start | bytes 294920 | tf_op jit(solution)/shard_map/ppermute | solution.py:375
  23.0 1.4 %collective-permute-start.9 = (bf16[2,32,256]{2,1,0:T(8,128)(2,1)S(1)}, bf16[2,32,256]{2,1,0:T(8,128)(2,1)S(1)}, u32[]{:S(2)}, u32[]{:S(2)}) collective-permute-start(bf16[2,32,256]{2,1,0:T(8,128)(2,1)S(1)} %get-tuple-element.65), channel_id=1, source_target_pairs={{0,1},{1,0},{2,3},{3,2},{4,5},{5,4},{6,7},{7,6},{8,9},{9,8},{10,11... | collective-permute-start | bytes 98312 | tf_op jit(solution)/shard_map/ppermute | solution.py:375
  23.5 9.0 %collective-permute-start.7 = (bf16[32,1024]{1,0:T(8,128)(2,1)S(1)}, bf16[32,1024]{1,0:T(8,128)(2,1)S(1)}, u32[]{:S(2)}, u32[]{:S(2)}) collective-permute-start(bf16[32,1024]{1,0:T(8,128)(2,1)S(1)} %get-tuple-element.55.wmsg), channel_id=1, source_target_pairs={{0,1},{1,0},{2,3},{3,2},{4,5},{5,4},{6,7},{7,6},{8,9},{9,8},{10,11... | collective-permute-start | bytes 196616 | tf_op jit(solution)/shard_map/ppermute | solution.py:378
  23.6 8.9 %collective-permute-start.8 = (bf16[32,1024]{1,0:T(8,128)(2,1)S(1)}, bf16[32,1024]{1,0:T(8,128)(2,1)S(1)}, u32[]{:S(2)}, u32[]{:S(2)}) collective-permute-start(bf16[32,1024]{1,0:T(8,128)(2,1)S(1)} %get-tuple-element.55.wmsg), channel_id=1, source_target_pairs={{1,2},{3,4},{5,6},{7,8},{9,10},{11,12},{13,14},{15,16},{17,18},{19... | collective-permute-start | bytes 196616 | tf_op jit(solution)/shard_map/ppermute | solution.py:378
  24.4 6.6 %collective-permute-start.10 = (bf16[2,32,256]{2,1,0:T(8,128)(2,1)S(1)}, bf16[2,32,256]{2,1,0:T(8,128)(2,1)S(1)}, u32[]{:S(2)}, u32[]{:S(2)}) collective-permute-start(bf16[2,32,256]{2,1,0:T(8,128)(2,1)S(1)} %get-tuple-element.66), channel_id=1, source_target_pairs={{0,2},{1,5},{2,0},{3,7},{4,6},{5,1},{6,4},{7,3},{8,10},{9,13},{10,... | collective-permute-start | bytes 98312 | tf_op jit(solution)/shard_map/ppermute | solution.py:372
  27.7 4.4 %collective-permute-start.11 = (bf16[2,32,256]{2,1,0:T(8,128)(2,1)S(1)}, bf16[2,32,256]{2,1,0:T(8,128)(2,1)S(1)}, u32[]{:S(2)}, u32[]{:S(2)}) collective-permute-start(bf16[2,32,256]{2,1,0:T(8,128)(2,1)S(1)} %get-tuple-element.67), channel_id=1, source_target_pairs={{0,8},{1,17},{2,10},{3,19},{4,12},{5,21},{6,14},{7,23},{8,0},{9,25... | collective-permute-start | bytes 98312 | tf_op jit(solution)/shard_map/ppermute | solution.py:372
  31.0 2.7 %collective-permute-start.12 = (bf16[2,32,256]{2,1,0:T(8,128)(2,1)S(1)}, bf16[2,32,256]{2,1,0:T(8,128)(2,1)S(1)}, u32[]{:S(2)}, u32[]{:S(2)}) collective-permute-start(bf16[2,32,256]{2,1,0:T(8,128)(2,1)S(1)} %collective-permute-done.10.refs_8_), channel_id=1, source_target_pairs={{0,1},{1,0},{2,3},{3,2},{4,5},{5,4},{6,7},{7,6},{8,9},{9,8},{10,11... | collective-permute-start | bytes 98312 | tf_op jit(solution)/shard_map/ppermute | solution.py:375
  32.1 1.6 %collective-permute-start.13 = (bf16[2,32,256]{2,1,0:T(8,128)(2,1)S(1)}, bf16[2,32,256]{2,1,0:T(8,128)(2,1)S(1)}, u32[]{:S(2)}, u32[]{:S(2)}) collective-permute-start(bf16[2,32,256]{2,1,0:T(8,128)(2,1)S(1)} %collective-permute-done.11.refs_9_), channel_id=1, source_target_pairs={{0,1},{1,0},{2,3},{3,2},{4,5},{5,4},{6,7},{7,6},{8,9},{9,8},{10,11... | collective-permute-start | bytes 98312 | tf_op jit(solution)/shard_map/ppermute | solution.py:375
  35.1 12.1 %all-to-all-start = ((f32[32,1,128]{2,1,0:T(1,128)}), f32[32,1,128]{2,1,0:T(1,128)S(1)}, u32[]{:S(2)}, u32[]{:S(2)}) async-start(f32[32,1,128]{2,1,0:T(1,128)} %bitcast.1), calls=%async_computation | async-start | bytes 32768 | tf_op jit(solution)/shard_map/all_to_all | solution.py:441

commit v6 on v5

--- a/solution.py
+++ b/solution.py
@@ -102,14 +102,6 @@
     return lax.rem(lax.axis_index("loc"), 2) == 0
 
 
-def share(values, keep, give):
-    first = on_first_core()
-    for slot in range(len(values) // 2):
-        even, odd = values[2 * slot], values[2 * slot + 1]
-        keep[slot] = jnp.where(first, even, odd)
-        give[slot] = jnp.where(first, odd, even)
-
-
 def gather_share(keep, got, packs):
     first = on_first_core()
     for slot, pack in enumerate(packs):
@@ -117,15 +109,9 @@
         pack[1] = jnp.where(first, got[slot], keep[slot])
 
 
-def level_values(cross, other):
+def own_part(values):
     first = on_first_core()
-    values = []
-    for mine, theirs in zip(cross, other):
-        here = jnp.where(first, mine[0], mine[1])
-        there = jnp.where(first, theirs[0], theirs[1])
-        values.append(jnp.where(first, here, there))
-        values.append(jnp.where(first, there, here))
-    return values
+    return [jnp.where(first, value[0], value[1]) for value in values]
 
 
 def front_kernel(levels, *refs):
@@ -144,13 +130,25 @@
     pair_buf[0:SRC_ROWS, :] = buf[...].astype(HALF)
     msg[32:64, :] = buf[...].astype(HALF)
     rows, rank = points.shape[1], skel_target.shape[2]
+    first = on_first_core()
+    skel = [given[24 + level : 25 + level, 0:rank] for level in range(levels)]
+    order = [jnp.where(first, skel[level], skel[level + 1]) for level in range(0, levels, 2)]
+    order += [jnp.where(first, skel[level + 1], skel[level]) for level in range(0, levels, 2)]
+    stride = rows // rank
+    shift = stride.bit_length() - 1
+    spot = lax.broadcasted_iota(jnp.int32, (rows, rank), 0)
+    slot = lax.broadcasted_iota(jnp.int32, (rows, rank), 1)
+    group = jnp.where(lax.shift_right_logical(spot, shift) == slot, 1.0, 0.0).astype(HALF)
+    steps = lax.broadcasted_iota(jnp.int32, (len(order), rank), 1).astype(FULL) * stride
+    wanted = dot_rows((jnp.concatenate(order, axis=0) - steps).astype(HALF), group)
+    place = jnp.bitwise_and(lax.broadcasted_iota(jnp.int32, wanted.shape, 1), stride - 1).astype(FULL)
+    chosen = jnp.where(wanted == place, 1.0, 0.0).astype(HALF)
+    both_rows = pair_buf[...]
+    picked = dot(jnp.concatenate([both_rows * chosen[level : level + 1] for level in range(levels)], axis=0), group)
     sources = []
     for level in range(levels):
-        spot = lax.broadcasted_iota(jnp.int32, (rows, rank), 0).astype(FULL)
-        picks = jnp.where(spot == given[24 + level : 25 + level, 0:rank], 1.0, 0.0).astype(HALF)
-        both = dot(pair_buf[...], picks)
-        skel_target[level] = both[SRC_ROWS:].astype(HALF)
-        skel_source = both[:SRC_ROWS]
+        skel_source = picked[2 * SRC_ROWS * level : 2 * SRC_ROWS * level + SRC_ROWS]
+        skel_target[level] = picked[2 * SRC_ROWS * level + SRC_ROWS : 2 * SRC_ROWS * (level + 1)].astype(HALF)
         sources.append(skel_source.astype(HALF))
         turned_src[level * rank : (level + 1) * rank, :] = skel_source.T.astype(HALF)
     rates = [jnp.concatenate([numbers[row : row + 1, :]] * (WIDE_TILE // 128), axis=1) for row in (1, 3)]
@@ -161,11 +159,12 @@
     msg[0:16, :] = low
     msg[16:32, :] = high
     coef = merged(dot_rows(msg[0:VEC_ROWS, :], basis[...]))
-    lev = []
     for level in range(levels):
         high, low = split_two(coef[:, level * rank : (level + 1) * rank])
-        lev.append(jnp.concatenate([high, low, sources[level]], axis=0))
-    share(lev, keep, give)
+        dest = keep.at[level] if level < levels // 2 else give.at[level - levels // 2]
+        dest[0:32, :] = high
+        dest[32:64, :] = low
+        dest[64:96, :] = sources[level]
 
 
 def near_block(msg, target, turned_src, rates, kept):
@@ -197,23 +196,35 @@
         slopes[:, span] = slopes_in[:, span] + slope
 
 
-def far_kernel(half, far_scale, *refs):
-    numbers, image, given, basis, skel_target = refs[:5]
-    lev = level_values(refs[5 : 5 + half], refs[5 + half : 5 + 2 * half])
-    coup_high, coup_low, row_sum, first, wmsg, keep, give = refs[5 + 2 * half :]
+def far_part(lev, start, numbers, skel_target, basis, coup_high, coup_low):
     rank = skel_target.shape[2]
-    far_rates = [jnp.concatenate([numbers[row : row + 1, :]] * (rank // 128), axis=1) for row in (1, 3)]
+    rates = [jnp.concatenate([numbers[row : row + 1, :]] * (rank // 128), axis=1) for row in (1, 3)]
     mixed = []
-    for level, value in enumerate(lev):
-        squared = dot(turned(value[64:96]), skel_target[level])
-        high, low = split_two(matern(squared, far_rates)[0])
-        coup_high[level] = high
-        coup_low[level] = low
+    for slot, value in enumerate(lev):
+        squared = dot(turned(value[64:96]), skel_target[start + slot])
+        high, low = split_two(matern(squared, rates)[0])
+        coup_high[slot] = high
+        coup_low[slot] = low
         both = dot(value[0:64], high)
         part = both[0:32] + both[32:64] + dot(value[0:32], low)
         mixed.append(jnp.concatenate(split_two(part), axis=0))
-    far = dot(jnp.concatenate(mixed, axis=1), basis[...])
-    total = image[...] + far_scale * (far[0:32] + far[32:64])
+    far = dot(jnp.concatenate(mixed, axis=1), basis[start * rank : (start + len(lev)) * rank, :])
+    return far[0:32] + far[32:64]
+
+
+def carried_kernel(half, far_scale, *refs):
+    numbers, image_in, basis, skel_target = refs[:4]
+    lev = own_part(refs[4 : 4 + half])
+    image, coup_high, coup_low = refs[4 + half :]
+    image[...] = image_in[...] + far_scale * far_part(lev, 0, numbers, skel_target, basis, coup_high, coup_low)
+
+
+def far_kernel(half, far_scale, *refs):
+    numbers, image, given, basis, skel_target = refs[:5]
+    lev = own_part(refs[5 : 5 + half])
+    coup_high, coup_low, row_sum, first, wmsg, keep, give = refs[5 + half :]
+    rank = skel_target.shape[2]
+    total = image[...] + far_scale * far_part(lev, half, numbers, skel_target, basis, coup_high, coup_low)
     sums = total[16:17, :]
     row_sum[...] = sums
     value = SCALE * (total[0:16] + sums * given[0:16, :])
@@ -223,8 +234,11 @@
     wmsg[16:32, :] = low
     both = dot_rows(wmsg[...], basis[...])
     high, low = split_two(both[0:16] + both[16:32])
-    both = jnp.concatenate([high, low], axis=0)
-    share([both[:, level * rank : (level + 1) * rank] for level in range(len(lev))], keep, give)
+    for slot in range(2 * half):
+        dest = keep.at[slot] if slot < half else give.at[slot - half]
+        span = slice(slot * rank, (slot + 1) * rank)
+        dest[0:16, :] = high[:, span]
+        dest[16:32, :] = low[:, span]
 
 
 def pack_kernel(keep, got, *packs):
@@ -240,13 +254,15 @@
 
 
 def second_kernel(half, far_scale, *refs):
-    near, basis, coup_high, coup_low, row_sum, first, given, slope_sum = refs[:8]
-    wlev = level_values(refs[8 : 8 + half], refs[8 + half : 8 + 2 * half])
-    sums, first_rest, second_rest, shift_out = refs[8 + 2 * half :]
+    near, basis, own_high, own_low, other_high, other_low, row_sum, first, given, slope_sum = refs[:10]
+    wlev = own_part(refs[10 : 10 + 2 * half])
+    sums, first_rest, second_rest, shift_out = refs[10 + 2 * half :]
+    coup_high = [own_high[slot] for slot in range(half)] + [other_high[slot] for slot in range(half)]
+    coup_low = [own_low[slot] for slot in range(half)] + [other_low[slot] for slot in range(half)]
     pieces = []
-    for level, coef in enumerate(wlev):
-        mixed = dot(coef, coup_high[level])
-        mixed = mixed[0:16] + mixed[16:32] + dot(coef[0:16], coup_low[level])
+    for coef, high, low in zip(wlev, coup_high, coup_low):
+        mixed = dot(coef, high)
+        mixed = mixed[0:16] + mixed[16:32] + dot(coef[0:16], low)
         pieces.append(jnp.concatenate(split_two(mixed), axis=0))
     both = near[...] + far_scale * dot(jnp.concatenate(pieces, axis=1), basis[...])
     base = given[0:16, :]
@@ -411,21 +427,25 @@
     )(numbers, msg, target, keep, got)
     cross = [partner(pack, slot) for slot, pack in enumerate(packs)]
     kept_a, image, slopes = call(side_kernel, near_outs, [VMEM] * 5, turned_buf)(numbers, msg_a, target, image, slopes)
+    kept_b, image, slopes = call(side_kernel, near_outs, [VMEM] * 5, turned_buf)(numbers, msg_b, target, image, slopes)
+    image, cross = lax.optimization_barrier((image, cross))
     other = [sibling(value) for value in cross]
-    kept_b, image, slopes = call(side_kernel, near_outs, [VMEM] * 5, turned_buf)(numbers, msg_b, target, image, slopes)
-    coup_high, coup_low, row_sum, first, wmsg, keep, give = call(
+    couplings = [((half, rank, rank), HALF)] * 2
+    image, own_high, own_low = call(
+        functools.partial(carried_kernel, half, far_scale), [((32, rows), FULL)] + couplings, [VMEM] * (4 + half), micros=1.0
+    )(numbers, image, basis, skel_target, *cross)
+    other_high, other_low, row_sum, first, wmsg, keep, give = call(
         functools.partial(far_kernel, half, far_scale),
-        [
-            ((levels, rank, rank), HALF),
-            ((levels, rank, rank), HALF),
+        couplings
+        + [
             ((1, rows), FULL),
             ((probes, rows), FULL),
             ((2 * probes, rows), HALF),
             ((half, 2 * probes, rank), HALF),
             ((half, 2 * probes, rank), HALF),
         ],
-        [VMEM] * (5 + levels),
-    )(numbers, image, given, basis, skel_target, *cross, *other)
+        [VMEM] * (5 + half),
+    )(numbers, image, given, basis, skel_target, *other)
     got = sibling(give)
     wmsg_a, wmsg_b = sides(wmsg)
     packs = call(pack_kernel, [((2, 2 * probes, rank), HALF)] * half, [VMEM] * 2, micros=0.1)(keep, got)
@@ -435,8 +455,8 @@
     sums, first_rest, second_rest, shift = call(
         functools.partial(second_kernel, half, far_scale),
         [((count, 128), FULL), ((probes, rows), FULL), ((probes, rows), FULL), ((probes, 128), FULL)],
-        [VMEM] * (8 + levels),
-    )(near, basis, coup_high, coup_low, row_sum, first, given, slopes, *cross, *other)
+        [VMEM] * (10 + levels),
+    )(near, basis, own_high, own_low, other_high, other_low, row_sum, first, given, slopes, *cross, *other)
     sums, signal, noise_var = lax.optimization_barrier((sums, signal, noise_var))
     table = lax.all_to_all(sums, "loc", 0, 0, tiled=True)
     (slope_image,) = call(slope_kernel, [((probes, rows), FULL)], [SMEM, VMEM, VMEM])(signal, numbers, slopes)

time: 48.3 us -> 47.1 us (0.975)
  starting transfers between devices: 21.9 us -> 19 us
  waiting for transfers between devices: 7 us -> 8.2 us
  Pallas kernels: 14.9 us -> 15.4 us
    ppermute x6, starting transfers between devices: 3.95 us -> 2.48 us  [sibling(): return lax.ppermute(value, 'loc', beside)]
    all_to_all x1, starting transfers between devices: 5.05 us -> 3.97 us  [shards(): table = lax.all_to_all(sums, 'loc', 0, 0, tiled=True)]
    ppermute x4, waiting for transfers between devices: 0.25 us -> 1.27 us  [partner(): return lax.ppermute(value, 'loc', pairs)]
    ppermute x4, starting transfers between devices: 11.4 us -> 10.9 us  [partner(): return lax.ppermute(value, 'loc', pairs)]
    pallas_call x1 -> x2, Pallas kernels: 2.07 us -> 2.46 us  [the longest x1 1.52 us: shards(): call(functools.partial(far_kernel, half, far_scale), couplings + [((1, ro...]
  transfers between devices with their start and end apart: 15 -> 15, of which waited for: 4 -> 4; matrix products, arithmetic and copies ran while one was open for 0% -> 0% of each run, Pallas kernels for 17% -> 19%
where the time goes in v6:
time: 47.1 us; the launch traced here: 46.9 us
  starting transfers between devices  19 us (40%)
  Pallas kernels  15.4 us (33%)
  waiting for transfers between devices  8.2 us (17%)
  between operations  3.36 us (7%)
  other arithmetic  0.88 us (2%)
    ppermute x4, starting transfers between devices, partner(): return lax.ppermute(value, 'loc', pairs)  10.9 us
    all_to_all x1, waiting for transfers between devices, shards(): table = lax.all_to_all(sums, 'loc', 0, 0, tiled=True)  6.4 us
    pallas_call x2, Pallas kernels, shards(): call(side_kernel, near_outs, [VMEM] * 5, turned_buf)  4.12 us
    all_to_all x1, starting transfers between devices, shards(): table = lax.all_to_all(sums, 'loc', 0, 0, tiled=True)  3.97 us
    pallas_call x1, Pallas kernels, shards(): call(functools.partial(front_kernel, levels), [((MSG_ROWS, rows), HALF),...  2.67 us
    ppermute x6, starting transfers between devices, sibling(): return lax.ppermute(value, 'loc', beside)  2.48 us
    pallas_call x1, Pallas kernels, shards(): call(own_kernel, near_outs + [((2, 96, rank), HALF)] * half, [VMEM] * 5,...  2.01 us
    pallas_call x1, Pallas kernels, shards(): call(functools.partial(far_kernel, half, far_scale), couplings + [((1, ro...  1.52 us
  transfers between devices with their start and end apart: 15, of which 4 were waited for; matrix products, arithmetic and copies ran while one was open for 0% of the time, Pallas kernels for 19%

profile of v6, /device:TPU:0, one launch (start us, length us, event | category | flops | bytes accessed | tf_op | source)
XLA Modules:
  0.0 46.9 jit_solution(8562636814490966814)
XLA Ops:
  1.9 0.9 %convert_add_fusion.refs_2_.refs_8_.given = f32[32,1024]{1,0:T(8,128)S(1)} fusion(s32[4,256]{1,0:T(4,128)} %param.9, f32[3,1024]{1,0:T(4,128)} %param.7, f32[16,1024]{1,0:T(8,128)} %param.8), kind=kLoop, calls=%fused_computation | loop fusion | flops 98304 | bytes 212992 | tf_op jit(solution)/shard_map/add | solution.py:399
  2.8 2.7 %shard_map.102 = (bf16[64,1024]{1,0:T(8,128)(2,1)S(1)}, bf16[32,1024]{1,0:T(8,128)(2,1)S(1)}, bf16[1024,1024]{1,0:T(8,128)(2,1)S(1)}, bf16[4,32,256]{2,1,0:T(8,1...) custom-call(f32[1]{0:T(128)S(6)} %copy.12.refs_0_, ...), custom_call_target="tpu_custom_call" | custom-call | flops 2000000000 | bytes 65536 | tf_op jit(solution)/shard_map/pallas_call | solution.py:400
  5.5 0.5 %collective-permute-start.2 = (bf16[2,96,256]{2,1,0:T(8,128)(2,1)S(1)}, bf16[2,96,256]{2,1,0:T(8,128)(2,1)S(1)}, u32[]{:S(2)}, u32[]{:S(2)}) collective-permute-start(bf16[2,96,256]{2,1,0:T(8,128)(2,1)S(1)} %get-tuple-element.51), channel_id=1, source_target_pairs={{0,1},{1,0},{2,3},{3,2},{4,5},{5,4},{6,7},{7,6},{8,9},{9,8},{10,11... | collective-permute-start | bytes 294920 | tf_op jit(solution)/shard_map/ppermute | solution.py:391
  6.1 0.7 %collective-permute-start = (bf16[64,1024]{1,0:T(8,128)(2,1)S(1)}, bf16[64,1024]{1,0:T(8,128)(2,1)S(1)}, u32[]{:S(2)}, u32[]{:S(2)}) collective-permute-start(bf16[64,1024]{1,0:T(8,128)(2,1)S(1)} %get-tuple-element.48.msg), channel_id=1, source_target_pairs={{1,2},{3,4},{5,6},{7,8},{9,10},{11,12},{13,14},{15,16},{17,18},{19... | collective-permute-start | bytes 393224 | tf_op jit(solution)/shard_map/ppermute | solution.py:394
  6.9 2.0 %shard_map.103 = (bf16[1024,1024]{1,0:T(8,128)(2,1)S(1)}, f32[32,1024]{1,0:T(8,128)S(1)}, f32[16,1024]{1,0:T(8,128)S(1)}, bf16[2,96,256]{2,1,0:T(8,128)(2,1)S(1)}, bf16[2,96,256]{2,1,0:T(8,128)(2,1)S(1)}) custom-call(f32[8,128]{1,0:T(8,128)S(1)} %get-tuple-element.47.numbers.refs_0_, bf16[64,1024]{1,0:T(8,128)(2,1)S(1)} %get-tuple-element.48.msg, ...), custom_call_target="tpu_custom_call" | custom-call | flops 2000000000 | bytes 65536 | tf_op jit(solution)/shard_map/pallas_call | solution.py:422
  9.0 4.0 %collective-permute-start.3 = (bf16[2,96,256]{2,1,0:T(8,128)(2,1)S(1)}, bf16[2,96,256]{2,1,0:T(8,128)(2,1)S(1)}, u32[]{:S(2)}, u32[]{:S(2)}) collective-permute-start(bf16[2,96,256]{2,1,0:T(8,128)(2,1)S(1)} %get-tuple-element.57), channel_id=1, source_target_pairs={{0,2},{1,5},{2,0},{3,7},{4,6},{5,1},{6,4},{7,3},{8,10},{9,13},{10,... | collective-permute-start | bytes 294920 | tf_op jit(solution)/shard_map/ppermute | solution.py:388
  13.0 2.1 %collective-permute-start.4 = (bf16[2,96,256]{2,1,0:T(8,128)(2,1)S(1)}, bf16[2,96,256]{2,1,0:T(8,128)(2,1)S(1)}, u32[]{:S(2)}, u32[]{:S(2)}) collective-permute-start(bf16[2,96,256]{2,1,0:T(8,128)(2,1)S(1)} %get-tuple-element.58), channel_id=1, source_target_pairs={{0,8},{1,17},{2,10},{3,19},{4,12},{5,21},{6,14},{7,23},{8,0},{9,25... | collective-permute-start | bytes 294920 | tf_op jit(solution)/shard_map/ppermute | solution.py:388
  15.1 2.1 %shard_map.104 = (bf16[1024,1024]{1,0:T(8,128)(2,1)S(1)}, f32[32,1024]{1,0:T(8,128)S(1)}, f32[16,1024]{1,0:T(8,128)S(1)}) custom-call(f32[8,128]{1,0:T(8,128)S(1)} %get-tuple-element.47.numbers.refs_0_, bf16[64,1024]{1,0:T(8,128)(2,1)S(1)} %collective-permute-done.1.msg, bf16[32,1024]{1,0:T(8,128)(2,1)S(1)} %get-tuple-element.49.target, ...), custom_call_target="tpu_custom_call" | custom-call | flops 2000000000 | bytes 65536 | tf_op jit(solution)/shard_map/pallas_call | solution.py:429
  17.2 2.1 %shard_map.105 = (bf16[1024,1024]{1,0:T(8,128)(2,1)S(1)}, f32[32,1024]{1,0:T(8,128)S(1)}, f32[16,1024]{1,0:T(8,128)S(1)}) custom-call(f32[8,128]{1,0:T(8,128)S(1)} %get-tuple-element.47.numbers.refs_0_, bf16[64,1024]{1,0:T(8,128)(2,1)S(1)} %collective-permute-done.msg, bf16[32,1024]{1,0:T(8,128)(2,1)S(1)} %get-tuple-element.49.target, ...), custom_call_target="tpu_custom_call" | custom-call | flops 2000000000 | bytes 65536 | tf_op jit(solution)/shard_map/pallas_call | solution.py:430
  19.3 1.6 %collective-permute-start.5 = (bf16[2,96,256]{2,1,0:T(8,128)(2,1)S(1)}, bf16[2,96,256]{2,1,0:T(8,128)(2,1)S(1)}, u32[]{:S(2)}, u32[]{:S(2)}) collective-permute-start(bf16[2,96,256]{2,1,0:T(8,128)(2,1)S(1)} %collective-permute-done.3.refs_4_), channel_id=1, source_target_pairs={{0,1},{1,0},{2,3},{3,2},{4,5},{5,4},{6,7},{7,6},{8,9},{9,8},{10,11... | collective-permute-start | bytes 294920 | tf_op jit(solution)/shard_map/ppermute | solution.py:391
  21.0 0.9 %shard_map.106 = (f32[32,1024]{1,0:T(8,128)S(1)}, bf16[2,256,256]{2,1,0:T(8,128)(2,1)S(1)}, bf16[2,256,256]{2,1,0:T(8,128)(2,1)S(1)}) custom-call(f32[8,128]{1,0:T(8,128)S(1)} %get-tuple-element.47.numbers.refs_0_, f32[32,1024]{1,0:T(8,128)S(1)} %get-tuple-element.59.refs_1_, bf16[1024,1024]{1,0:T(8,128)(2,1)S(1)} %get-tuple-element.60.refs_2_.refs_3_.refs_1_, ...), custom_call_target="tpu_custom_call" | custom-call | flops 1000000000 | bytes 65536 | tf_op jit(solution)/shard_map/pallas_call | solution.py:434
  22.0 0.3 collective-permute-done.6.refs_6_
  22.2 1.5 %shard_map.107 = (bf16[2,256,256]{2,1,0:T(8,128)(2,1)S(1)}, bf16[2,256,256]{2,1,0:T(8,128)(2,1)S(1)}, f32[1,1024]{1,0:T(1,128)S(1)}, f32[16,1024]{1,0:T(8,128)S(...) custom-call(f32[8,128]{1,0:T(8,128)S(1)} %get-tuple-element.47.numbers.refs_0_, ...), custom_call_target="tpu_custom_call" | custom-call | flops 2000000000 | bytes 65536 | tf_op jit(solution)/shard_map/pallas_call | solution.py:437
  23.9 0.3 collective-permute-start.7
  24.3 0.7 %collective-permute-start.8 = (bf16[32,1024]{1,0:T(8,128)(2,1)S(1)}, bf16[32,1024]{1,0:T(8,128)(2,1)S(1)}, u32[]{:S(2)}, u32[]{:S(2)}) collective-permute-start(bf16[32,1024]{1,0:T(8,128)(2,1)S(1)} %get-tuple-element.65.wmsg), channel_id=1, source_target_pairs={{1,2},{3,4},{5,6},{7,8},{9,10},{11,12},{13,14},{15,16},{17,18},{19... | collective-permute-start | bytes 196616 | tf_op jit(solution)/shard_map/ppermute | solution.py:394
  25.0 3.1 %collective-permute-start.10 = (bf16[2,32,256]{2,1,0:T(8,128)(2,1)S(1)}, bf16[2,32,256]{2,1,0:T(8,128)(2,1)S(1)}, u32[]{:S(2)}, u32[]{:S(2)}) collective-permute-start(bf16[2,32,256]{2,1,0:T(8,128)(2,1)S(1)} %get-tuple-element.78), channel_id=1, source_target_pairs={{0,2},{1,5},{2,0},{3,7},{4,6},{5,1},{6,4},{7,3},{8,10},{9,13},{10,... | collective-permute-start | bytes 98312 | tf_op jit(solution)/shard_map/ppermute | solution.py:388
  28.1 1.6 %collective-permute-start.11 = (bf16[2,32,256]{2,1,0:T(8,128)(2,1)S(1)}, bf16[2,32,256]{2,1,0:T(8,128)(2,1)S(1)}, u32[]{:S(2)}, u32[]{:S(2)}) collective-permute-start(bf16[2,32,256]{2,1,0:T(8,128)(2,1)S(1)} %get-tuple-element.79), channel_id=1, source_target_pairs={{0,8},{1,17},{2,10},{3,19},{4,12},{5,21},{6,14},{7,23},{8,0},{9,25... | collective-permute-start | bytes 98312 | tf_op jit(solution)/shard_map/ppermute | solution.py:388
  31.1 1.3 %collective-permute-done.11.refs_11_ = bf16[2,32,256]{2,1,0:T(8,128)(2,1)S(1)} collective-permute-done((bf16[2,32,256]{2,1,0:T(8,128)(2,1)S(1)}, bf16[2,32,256]{2,1,0:T(8,128)(2,1)S(1)}, u32[]{:S(2)}, u32[]{:S(2)}) %collective-permute-start.11) | collective-permute-done | bytes 32800 | tf_op jit(solution)/shard_map/ppermute | solution.py:388
  32.3 1.2 %shard_map.108.refs_0_ = f32[32,1024]{1,0:T(8,128)S(1)} custom-call(bf16[32,1024]{1,0:T(8,128)(2,1)S(1)} %get-tuple-element.65.wmsg, bf16[32,1024]{1,0:T(8,128)(2,1)S(1)} %collective-permute-done.7.wmsg_a, bf16[32,1024]{1,0:T(8,128)(2,1)S(1)} %collective-permute-done.8.wmsg_b, bf16[1024,1024]{1,0:T(8,128)(2,1)S(1)} %get-tuple-element.66.kept, ...), custom_call_target="tpu_custom_call" | custom-call | flops 1200000000 | bytes 65536 | tf_op jit(solution)/shard_map/pallas_call | solution.py:453
  33.5 1.4 %shard_map.110 = (f32[32,128]{1,0:T(8,128)}, f32[16,1024]{1,0:T(8,128)S(1)}, f32[16,1024]{1,0:T(8,128)S(1)}, f32[16,128]{1,0:T(8,128)S(1)}) custom-call(f32[32,1024]{1,0:T(8,128)S(1)} %shard_map.108.refs_0_, bf16[1024,1024]{1,0:T(8,128)(2,1)S(1)} %get-tuple-element.60.refs_2_.refs_3_.refs_1_, bf16[2,256,256]{2,1,0:T(8,128)(2,1)S(1)} %get-tuple-element.69.refs_2_, ...), custom_call_target="tpu_custom_call" | custom-call | flops 2000000000 | bytes 65536 | tf_op jit(solution)/shard_map/pallas_call | solution.py:455
  34.9 4.0 %all-to-all-start = ((f32[32,1,128]{2,1,0:T(1,128)}), f32[32,1,128]{2,1,0:T(1,128)S(1)}, u32[]{:S(2)}, u32[]{:S(2)}) async-start(f32[32,1,128]{2,1,0:T(1,128)} %bitcast.1), calls=%async_computation | async-start | bytes 32768 | tf_op jit(solution)/shard_map/all_to_all | solution.py:461
  38.9 0.7 %shard_map.112 = f32[16,1024]{1,0:T(8,128)} custom-call(f32[1]{0:T(128)S(6)} %copy.14.signal, f32[8,128]{1,0:T(8,128)S(1)} %get-tuple-element.47.numbers.refs_0_, f32[16,1024]{1,0:T(8,128)S(1)} %get-tuple-element.75.refs_9_.source), custom_call_target="tpu_custom_call" | custom-call | flops 2000000000 | bytes 65536 | tf_op jit(solution)/shard_map/pallas_call | solution.py:462
  39.5 6.4 %all-to-all-done = f32[32,1,128]{2,1,0:T(1,128)S(1)} async-done(((f32[32,1,128]{2,1,0:T(1,128)}), f32[32,1,128]{2,1,0:T(1,128)S(1)}, u32[]{:S(2)}, u32[]{:S(2)}) %all-to-all-start) | async-done | bytes 16416 | tf_op jit(solution)/shard_map/all_to_all | solution.py:461
  46.0 0.9 %shard_map.111 = (f32[16,1024]{1,0:T(8,128)}, f32[16,1024]{1,0:T(8,128)}, f32[1,16]{1,0:T(1,128)}) custom-call(f32[1]{0:T(128)S(6)} %copy.14.signal, f32[1]{0:T(128)S(6)} %copy.15.noise, f32[8,128]{1,0:T(8,128)S(1)} %get-tuple-element.47.numbers.refs_0_, f32[32,128]{1,0:T(8,128)S(1)} %bitcast.5, f32[16,128]{1,0:T(8,128)S(1)} %get-tuple-element.84.shift_in, ...), custom_call_target="tpu_custom_call" | custom-call | flops 2000000000 | bytes 65536 | tf_op jit(solution)/shard_map/pallas_call | solution.py:463
  (18 shorter events, 0.8 us)
Async XLA Ops:
  5.5 1.5 %collective-permute-start.2 = (bf16[2,96,256]{2,1,0:T(8,128)(2,1)S(1)}, bf16[2,96,256]{2,1,0:T(8,128)(2,1)S(1)}, u32[]{:S(2)}, u32[]{:S(2)}) collective-permute-start(bf16[2,96,256]{2,1,0:T(8,128)(2,1)S(1)} %get-tuple-element.51), channel_id=1, source_target_pairs={{0,1},{1,0},{2,3},{3,2},{4,5},{5,4},{6,7},{7,6},{8,9},{9,8},{10,11... | collective-permute-start | bytes 294920 | tf_op jit(solution)/shard_map/ppermute | solution.py:391
  6.0 9.1 %collective-permute-start.1 = (bf16[64,1024]{1,0:T(8,128)(2,1)S(1)}, bf16[64,1024]{1,0:T(8,128)(2,1)S(1)}, u32[]{:S(2)}, u32[]{:S(2)}) collective-permute-start(bf16[64,1024]{1,0:T(8,128)(2,1)S(1)} %get-tuple-element.48.msg), channel_id=1, source_target_pairs={{0,1},{1,0},{2,3},{3,2},{4,5},{5,4},{6,7},{7,6},{8,9},{9,8},{10,11... | collective-permute-start | bytes 393224 | tf_op jit(solution)/shard_map/ppermute | solution.py:394
  6.1 11.1 %collective-permute-start = (bf16[64,1024]{1,0:T(8,128)(2,1)S(1)}, bf16[64,1024]{1,0:T(8,128)(2,1)S(1)}, u32[]{:S(2)}, u32[]{:S(2)}) collective-permute-start(bf16[64,1024]{1,0:T(8,128)(2,1)S(1)} %get-tuple-element.48.msg), channel_id=1, source_target_pairs={{1,2},{3,4},{5,6},{7,8},{9,10},{11,12},{13,14},{15,16},{17,18},{19... | collective-permute-start | bytes 393224 | tf_op jit(solution)/shard_map/ppermute | solution.py:394
  9.0 10.4 %collective-permute-start.3 = (bf16[2,96,256]{2,1,0:T(8,128)(2,1)S(1)}, bf16[2,96,256]{2,1,0:T(8,128)(2,1)S(1)}, u32[]{:S(2)}, u32[]{:S(2)}) collective-permute-start(bf16[2,96,256]{2,1,0:T(8,128)(2,1)S(1)} %get-tuple-element.57), channel_id=1, source_target_pairs={{0,2},{1,5},{2,0},{3,7},{4,6},{5,1},{6,4},{7,3},{8,10},{9,13},{10,... | collective-permute-start | bytes 294920 | tf_op jit(solution)/shard_map/ppermute | solution.py:388
  13.0 6.3 %collective-permute-start.4 = (bf16[2,96,256]{2,1,0:T(8,128)(2,1)S(1)}, bf16[2,96,256]{2,1,0:T(8,128)(2,1)S(1)}, u32[]{:S(2)}, u32[]{:S(2)}) collective-permute-start(bf16[2,96,256]{2,1,0:T(8,128)(2,1)S(1)} %get-tuple-element.58), channel_id=1, source_target_pairs={{0,8},{1,17},{2,10},{3,19},{4,12},{5,21},{6,14},{7,23},{8,0},{9,25... | collective-permute-start | bytes 294920 | tf_op jit(solution)/shard_map/ppermute | solution.py:388
  19.3 2.6 %collective-permute-start.5 = (bf16[2,96,256]{2,1,0:T(8,128)(2,1)S(1)}, bf16[2,96,256]{2,1,0:T(8,128)(2,1)S(1)}, u32[]{:S(2)}, u32[]{:S(2)}) collective-permute-start(bf16[2,96,256]{2,1,0:T(8,128)(2,1)S(1)} %collective-permute-done.3.refs_4_), channel_id=1, source_target_pairs={{0,1},{1,0},{2,3},{3,2},{4,5},{5,4},{6,7},{7,6},{8,9},{9,8},{10,11... | collective-permute-start | bytes 294920 | tf_op jit(solution)/shard_map/ppermute | solution.py:391
  20.9 1.3 %collective-permute-start.6 = (bf16[2,96,256]{2,1,0:T(8,128)(2,1)S(1)}, bf16[2,96,256]{2,1,0:T(8,128)(2,1)S(1)}, u32[]{:S(2)}, u32[]{:S(2)}) collective-permute-start(bf16[2,96,256]{2,1,0:T(8,128)(2,1)S(1)} %collective-permute-done.4.refs_5_), channel_id=1, source_target_pairs={{0,1},{1,0},{2,3},{3,2},{4,5},{5,4},{6,7},{7,6},{8,9},{9,8},{10,11... | collective-permute-start | bytes 294920 | tf_op jit(solution)/shard_map/ppermute | solution.py:391
  23.7 1.2 %collective-permute-start.9 = (bf16[2,32,256]{2,1,0:T(8,128)(2,1)S(1)}, bf16[2,32,256]{2,1,0:T(8,128)(2,1)S(1)}, u32[]{:S(2)}, u32[]{:S(2)}) collective-permute-start(bf16[2,32,256]{2,1,0:T(8,128)(2,1)S(1)} %get-tuple-element.77), channel_id=1, source_target_pairs={{0,1},{1,0},{2,3},{3,2},{4,5},{5,4},{6,7},{7,6},{8,9},{9,8},{10,11... | collective-permute-start | bytes 98312 | tf_op jit(solution)/shard_map/ppermute | solution.py:391
  23.9 8.4 %collective-permute-start.7 = (bf16[32,1024]{1,0:T(8,128)(2,1)S(1)}, bf16[32,1024]{1,0:T(8,128)(2,1)S(1)}, u32[]{:S(2)}, u32[]{:S(2)}) collective-permute-start(bf16[32,1024]{1,0:T(8,128)(2,1)S(1)} %get-tuple-element.65.wmsg), channel_id=1, source_target_pairs={{0,1},{1,0},{2,3},{3,2},{4,5},{5,4},{6,7},{7,6},{8,9},{9,8},{10,11... | collective-permute-start | bytes 196616 | tf_op jit(solution)/shard_map/ppermute | solution.py:394
  24.3 8.1 %collective-permute-start.8 = (bf16[32,1024]{1,0:T(8,128)(2,1)S(1)}, bf16[32,1024]{1,0:T(8,128)(2,1)S(1)}, u32[]{:S(2)}, u32[]{:S(2)}) collective-permute-start(bf16[32,1024]{1,0:T(8,128)(2,1)S(1)} %get-tuple-element.65.wmsg), channel_id=1, source_target_pairs={{1,2},{3,4},{5,6},{7,8},{9,10},{11,12},{13,14},{15,16},{17,18},{19... | collective-permute-start | bytes 196616 | tf_op jit(solution)/shard_map/ppermute | solution.py:394
  25.0 6.0 %collective-permute-start.10 = (bf16[2,32,256]{2,1,0:T(8,128)(2,1)S(1)}, bf16[2,32,256]{2,1,0:T(8,128)(2,1)S(1)}, u32[]{:S(2)}, u32[]{:S(2)}) collective-permute-start(bf16[2,32,256]{2,1,0:T(8,128)(2,1)S(1)} %get-tuple-element.78), channel_id=1, source_target_pairs={{0,2},{1,5},{2,0},{3,7},{4,6},{5,1},{6,4},{7,3},{8,10},{9,13},{10,... | collective-permute-start | bytes 98312 | tf_op jit(solution)/shard_map/ppermute | solution.py:388
  28.1 4.2 %collective-permute-start.11 = (bf16[2,32,256]{2,1,0:T(8,128)(2,1)S(1)}, bf16[2,32,256]{2,1,0:T(8,128)(2,1)S(1)}, u32[]{:S(2)}, u32[]{:S(2)}) collective-permute-start(bf16[2,32,256]{2,1,0:T(8,128)(2,1)S(1)} %get-tuple-element.79), channel_id=1, source_target_pairs={{0,8},{1,17},{2,10},{3,19},{4,12},{5,21},{6,14},{7,23},{8,0},{9,25... | collective-permute-start | bytes 98312 | tf_op jit(solution)/shard_map/ppermute | solution.py:388
  31.0 2.5 %collective-permute-start.12 = (bf16[2,32,256]{2,1,0:T(8,128)(2,1)S(1)}, bf16[2,32,256]{2,1,0:T(8,128)(2,1)S(1)}, u32[]{:S(2)}, u32[]{:S(2)}) collective-permute-start(bf16[2,32,256]{2,1,0:T(8,128)(2,1)S(1)} %collective-permute-done.10.refs_10_), channel_id=1, source_target_pairs={{0,1},{1,0},{2,3},{3,2},{4,5},{5,4},{6,7},{7,6},{8,9},{9,8},{10,11... | collective-permute-start | bytes 98312 | tf_op jit(solution)/shard_map/ppermute | solution.py:391
  32.3 1.2 %collective-permute-start.13 = (bf16[2,32,256]{2,1,0:T(8,128)(2,1)S(1)}, bf16[2,32,256]{2,1,0:T(8,128)(2,1)S(1)}, u32[]{:S(2)}, u32[]{:S(2)}) collective-permute-start(bf16[2,32,256]{2,1,0:T(8,128)(2,1)S(1)} %collective-permute-done.11.refs_11_), channel_id=1, source_target_pairs={{0,1},{1,0},{2,3},{3,2},{4,5},{5,4},{6,7},{7,6},{8,9},{9,8},{10,11... | collective-permute-start | bytes 98312 | tf_op jit(solution)/shard_map/ppermute | solution.py:391
  34.9 11.0 %all-to-all-start = ((f32[32,1,128]{2,1,0:T(1,128)}), f32[32,1,128]{2,1,0:T(1,128)S(1)}, u32[]{:S(2)}, u32[]{:S(2)}) async-start(f32[32,1,128]{2,1,0:T(1,128)} %bitcast.1), calls=%async_computation | async-start | bytes 32768 | tf_op jit(solution)/shard_map/all_to_all | solution.py:461

commit v7 on v6

--- a/solution.py
+++ b/solution.py
@@ -17,7 +17,7 @@
 MSG_ROWS = 64
 VEC_ROWS = 48
 TILE = 128
-WIDE_TILE = 512
+WIDE_TILE = 256
 VMEM = pltpu.VMEM
 SMEM = pltpu.SMEM
 
@@ -134,27 +134,20 @@
     skel = [given[24 + level : 25 + level, 0:rank] for level in range(levels)]
     order = [jnp.where(first, skel[level], skel[level + 1]) for level in range(0, levels, 2)]
     order += [jnp.where(first, skel[level + 1], skel[level]) for level in range(0, levels, 2)]
-    stride = rows // rank
-    shift = stride.bit_length() - 1
-    spot = lax.broadcasted_iota(jnp.int32, (rows, rank), 0)
-    slot = lax.broadcasted_iota(jnp.int32, (rows, rank), 1)
-    group = jnp.where(lax.shift_right_logical(spot, shift) == slot, 1.0, 0.0).astype(HALF)
-    steps = lax.broadcasted_iota(jnp.int32, (len(order), rank), 1).astype(FULL) * stride
-    wanted = dot_rows((jnp.concatenate(order, axis=0) - steps).astype(HALF), group)
-    place = jnp.bitwise_and(lax.broadcasted_iota(jnp.int32, wanted.shape, 1), stride - 1).astype(FULL)
-    chosen = jnp.where(wanted == place, 1.0, 0.0).astype(HALF)
-    both_rows = pair_buf[...]
-    picked = dot(jnp.concatenate([both_rows * chosen[level : level + 1] for level in range(levels)], axis=0), group)
+    spot = lax.broadcasted_iota(jnp.int32, (rows, rank), 0).astype(FULL)
     sources = []
     for level in range(levels):
-        skel_source = picked[2 * SRC_ROWS * level : 2 * SRC_ROWS * level + SRC_ROWS]
-        skel_target[level] = picked[2 * SRC_ROWS * level + SRC_ROWS : 2 * SRC_ROWS * (level + 1)].astype(HALF)
+        picks = jnp.where(spot == order[level], 1.0, 0.0).astype(HALF)
+        both = dot(pair_buf[...], picks)
+        skel_target[level] = both[SRC_ROWS:].astype(HALF)
+        skel_source = both[:SRC_ROWS]
         sources.append(skel_source.astype(HALF))
         turned_src[level * rank : (level + 1) * rank, :] = skel_source.T.astype(HALF)
     rates = [jnp.concatenate([numbers[row : row + 1, :]] * (WIDE_TILE // 128), axis=1) for row in (1, 3)]
-    for col in range(0, rows, WIDE_TILE):
-        squared = dot(turned_src[...], target[:, col : col + WIDE_TILE])
-        basis[:, col : col + WIDE_TILE] = matern(squared, rates)[0].astype(HALF)
+    for row in range(0, levels * rank, 1024):
+        for col in range(0, rows, WIDE_TILE):
+            squared = dot(turned_src[row : row + 1024, :], target[:, col : col + WIDE_TILE])
+            basis[row : row + 1024, col : col + WIDE_TILE] = matern(squared, rates)[0].astype(HALF)
     high, low = split_two(given[0:16, :])
     msg[0:16, :] = low
     msg[16:32, :] = high
@@ -222,7 +215,7 @@
 def far_kernel(half, far_scale, *refs):
     numbers, image, given, basis, skel_target = refs[:5]
     lev = own_part(refs[5 : 5 + half])
-    coup_high, coup_low, row_sum, first, wmsg, keep, give = refs[5 + half :]
+    coup_high, coup_low, row_sum, first, wmsg, keep, beside = refs[5 + half :]
     rank = skel_target.shape[2]
     total = image[...] + far_scale * far_part(lev, half, numbers, skel_target, basis, coup_high, coup_low)
     sums = total[16:17, :]
@@ -230,23 +223,30 @@
     value = SCALE * (total[0:16] + sums * given[0:16, :])
     first[...] = value
     high, low = split_two(value)
+    rows = wmsg.shape[1]
     wmsg[0:16, :] = high
     wmsg[16:32, :] = low
+    beside[0:16, 0:rows] = high
+    beside[16:32, 0:rows] = low
     both = dot_rows(wmsg[...], basis[...])
     high, low = split_two(both[0:16] + both[16:32])
-    for slot in range(2 * half):
-        dest = keep.at[slot] if slot < half else give.at[slot - half]
-        span = slice(slot * rank, (slot + 1) * rank)
-        dest[0:16, :] = high[:, span]
-        dest[16:32, :] = low[:, span]
+    keep[0:16, :] = high[:, : half * rank]
+    keep[16:32, :] = low[:, : half * rank]
+    beside[0:16, rows:] = high[:, half * rank :]
+    beside[16:32, rows:] = low[:, half * rank :]
 
 
 def pack_kernel(keep, got, *packs):
-    gather_share(keep, got, packs)
+    rank = packs[0].shape[2]
+    start = got.shape[1] - keep.shape[1]
+    spans = [slice(slot * rank, (slot + 1) * rank) for slot in range(len(packs))]
+    there = [slice(start + span.start, start + span.stop) for span in spans]
+    gather_share([keep[:, span] for span in spans], [got[:, span] for span in there], packs)
 
 
 def near_kernel(wmsg, wmsg_a, wmsg_b, kept, kept_a, kept_b, out):
-    out[...] = dot(wmsg[...], kept[...]) + dot(wmsg_a[...], kept_a[...]) + dot(wmsg_b[...], kept_b[...])
+    rows = kept_a.shape[0]
+    out[...] = dot(wmsg[...], kept[...]) + dot(wmsg_a[:, 0:rows], kept_a[...]) + dot(wmsg_b[...], kept_b[...])
 
 
 def row_total(a, b):
@@ -434,21 +434,21 @@
     image, own_high, own_low = call(
         functools.partial(carried_kernel, half, far_scale), [((32, rows), FULL)] + couplings, [VMEM] * (4 + half), micros=1.0
     )(numbers, image, basis, skel_target, *cross)
-    other_high, other_low, row_sum, first, wmsg, keep, give = call(
+    other_high, other_low, row_sum, first, wmsg, keep, beside_msg = call(
         functools.partial(far_kernel, half, far_scale),
         couplings
         + [
             ((1, rows), FULL),
             ((probes, rows), FULL),
             ((2 * probes, rows), HALF),
-            ((half, 2 * probes, rank), HALF),
-            ((half, 2 * probes, rank), HALF),
+            ((2 * probes, half * rank), HALF),
+            ((2 * probes, rows + half * rank), HALF),
         ],
         [VMEM] * (5 + half),
     )(numbers, image, given, basis, skel_target, *other)
-    got = sibling(give)
-    wmsg_a, wmsg_b = sides(wmsg)
-    packs = call(pack_kernel, [((2, 2 * probes, rank), HALF)] * half, [VMEM] * 2, micros=0.1)(keep, got)
+    wmsg_a = sibling(beside_msg)
+    wmsg_b = lax.ppermute(wmsg, "loc", across)
+    packs = call(pack_kernel, [((2, 2 * probes, rank), HALF)] * half, [VMEM] * 2, micros=0.1)(keep, wmsg_a)
     cross = [partner(pack, slot) for slot, pack in enumerate(packs)]
     (near,) = call(near_kernel, [((2 * probes, rows), FULL)], [VMEM] * 6, micros=1.2)(wmsg, wmsg_a, wmsg_b, kept, kept_a, kept_b)
     other = [sibling(value) for value in cross]

time: 47.1 us -> 46.8 us (level)
  starting transfers between devices: 19 us -> 18.5 us
    ppermute x0 -> x1, starting transfers between devices: none -> 0.65 us  [shards(): wmsg_b = lax.ppermute(wmsg, 'loc', across)]
    ppermute x2 -> x1, starting transfers between devices: 1.31 us -> 0.66 us  [sides(): lax.ppermute(value, 'loc', across)]
  transfers between devices with their start and end apart: 15 -> 14, of which waited for: 4 -> 5; matrix products, arithmetic and copies ran while one was open for 0% -> 0% of each run, Pallas kernels for 19% -> 19%
where the time goes in v7:
time: 46.8 us; the launch traced here: 46.6 us
  starting transfers between devices  18.5 us (40%)
  Pallas kernels  15.3 us (33%)
  waiting for transfers between devices  8.55 us (18%)
  between operations  3.35 us (7%)
  other arithmetic  0.88 us (2%)
    ppermute x4, starting transfers between devices, partner(): return lax.ppermute(value, 'loc', pairs)  10.6 us
    all_to_all x1, waiting for transfers between devices, shards(): table = lax.all_to_all(sums, 'loc', 0, 0, tiled=True)  6.4 us
    pallas_call x2, Pallas kernels, shards(): call(side_kernel, near_outs, [VMEM] * 5, turned_buf)  4.12 us
    all_to_all x1, starting transfers between devices, shards(): table = lax.all_to_all(sums, 'loc', 0, 0, tiled=True)  4.02 us
    pallas_call x1, Pallas kernels, shards(): call(functools.partial(front_kernel, levels), [((MSG_ROWS, rows), HALF),...  2.62 us
    ppermute x6, starting transfers between devices, sibling(): return lax.ppermute(value, 'loc', beside)  2.49 us
    pallas_call x1, Pallas kernels, shards(): call(own_kernel, near_outs + [((2, 96, rank), HALF)] * half, [VMEM] * 5,...  2.01 us
    pallas_call x1, Pallas kernels, shards(): call(functools.partial(far_kernel, half, far_scale), couplings + [((1, ro...  1.51 us
  transfers between devices with their start and end apart: 14, of which 5 were waited for; matrix products, arithmetic and copies ran while one was open for 0% of the time, Pallas kernels for 19%

profile of v7, /device:TPU:0, one launch (start us, length us, event | category | flops | bytes accessed | tf_op | source)
XLA Modules:
  0.0 46.6 jit_solution(11188131062310641036)
XLA Ops:
  1.9 0.9 %convert_add_fusion.refs_2_.refs_8_.given = f32[32,1024]{1,0:T(8,128)S(1)} fusion(s32[4,256]{1,0:T(4,128)} %param.9, f32[3,1024]{1,0:T(4,128)} %param.7, f32[16,1024]{1,0:T(8,128)} %param.8), kind=kLoop, calls=%fused_computation | loop fusion | flops 98304 | bytes 212992 | tf_op jit(solution)/shard_map/add | solution.py:399
  2.8 2.6 %shard_map.102 = (bf16[64,1024]{1,0:T(8,128)(2,1)S(1)}, bf16[32,1024]{1,0:T(8,128)(2,1)S(1)}, bf16[1024,1024]{1,0:T(8,128)(2,1)S(1)}, bf16[4,32,256]{2,1,0:T(8,1...) custom-call(f32[1]{0:T(128)S(6)} %copy.12.refs_0_, ...), custom_call_target="tpu_custom_call" | custom-call | flops 2000000000 | bytes 65536 | tf_op jit(solution)/shard_map/pallas_call | solution.py:400
  5.4 0.5 %collective-permute-start.2 = (bf16[2,96,256]{2,1,0:T(8,128)(2,1)S(1)}, bf16[2,96,256]{2,1,0:T(8,128)(2,1)S(1)}, u32[]{:S(2)}, u32[]{:S(2)}) collective-permute-start(bf16[2,96,256]{2,1,0:T(8,128)(2,1)S(1)} %get-tuple-element.51), channel_id=1, source_target_pairs={{0,1},{1,0},{2,3},{3,2},{4,5},{5,4},{6,7},{7,6},{8,9},{9,8},{10,11... | collective-permute-start | bytes 294920 | tf_op jit(solution)/shard_map/ppermute | solution.py:391
  6.0 0.7 %collective-permute-start = (bf16[64,1024]{1,0:T(8,128)(2,1)S(1)}, bf16[64,1024]{1,0:T(8,128)(2,1)S(1)}, u32[]{:S(2)}, u32[]{:S(2)}) collective-permute-start(bf16[64,1024]{1,0:T(8,128)(2,1)S(1)} %get-tuple-element.48.msg), channel_id=1, source_target_pairs={{1,2},{3,4},{5,6},{7,8},{9,10},{11,12},{13,14},{15,16},{17,18},{19... | collective-permute-start | bytes 393224 | tf_op jit(solution)/shard_map/ppermute | solution.py:394
  6.9 2.0 %shard_map.103 = (bf16[1024,1024]{1,0:T(8,128)(2,1)S(1)}, f32[32,1024]{1,0:T(8,128)S(1)}, f32[16,1024]{1,0:T(8,128)S(1)}, bf16[2,96,256]{2,1,0:T(8,128)(2,1)S(1)}, bf16[2,96,256]{2,1,0:T(8,128)(2,1)S(1)}) custom-call(f32[8,128]{1,0:T(8,128)S(1)} %get-tuple-element.47.numbers.refs_0_, bf16[64,1024]{1,0:T(8,128)(2,1)S(1)} %get-tuple-element.48.msg, ...), custom_call_target="tpu_custom_call" | custom-call | flops 2000000000 | bytes 65536 | tf_op jit(solution)/shard_map/pallas_call | solution.py:422
  8.9 4.0 %collective-permute-start.3 = (bf16[2,96,256]{2,1,0:T(8,128)(2,1)S(1)}, bf16[2,96,256]{2,1,0:T(8,128)(2,1)S(1)}, u32[]{:S(2)}, u32[]{:S(2)}) collective-permute-start(bf16[2,96,256]{2,1,0:T(8,128)(2,1)S(1)} %get-tuple-element.57), channel_id=1, source_target_pairs={{0,2},{1,5},{2,0},{3,7},{4,6},{5,1},{6,4},{7,3},{8,10},{9,13},{10,... | collective-permute-start | bytes 294920 | tf_op jit(solution)/shard_map/ppermute | solution.py:388
  12.9 2.1 %collective-permute-start.4 = (bf16[2,96,256]{2,1,0:T(8,128)(2,1)S(1)}, bf16[2,96,256]{2,1,0:T(8,128)(2,1)S(1)}, u32[]{:S(2)}, u32[]{:S(2)}) collective-permute-start(bf16[2,96,256]{2,1,0:T(8,128)(2,1)S(1)} %get-tuple-element.58), channel_id=1, source_target_pairs={{0,8},{1,17},{2,10},{3,19},{4,12},{5,21},{6,14},{7,23},{8,0},{9,25... | collective-permute-start | bytes 294920 | tf_op jit(solution)/shard_map/ppermute | solution.py:388
  15.1 2.1 %shard_map.104 = (bf16[1024,1024]{1,0:T(8,128)(2,1)S(1)}, f32[32,1024]{1,0:T(8,128)S(1)}, f32[16,1024]{1,0:T(8,128)S(1)}) custom-call(f32[8,128]{1,0:T(8,128)S(1)} %get-tuple-element.47.numbers.refs_0_, bf16[64,1024]{1,0:T(8,128)(2,1)S(1)} %collective-permute-done.1.msg, bf16[32,1024]{1,0:T(8,128)(2,1)S(1)} %get-tuple-element.49.target, ...), custom_call_target="tpu_custom_call" | custom-call | flops 2000000000 | bytes 65536 | tf_op jit(solution)/shard_map/pallas_call | solution.py:429
  17.2 2.1 %shard_map.105 = (bf16[1024,1024]{1,0:T(8,128)(2,1)S(1)}, f32[32,1024]{1,0:T(8,128)S(1)}, f32[16,1024]{1,0:T(8,128)S(1)}) custom-call(f32[8,128]{1,0:T(8,128)S(1)} %get-tuple-element.47.numbers.refs_0_, bf16[64,1024]{1,0:T(8,128)(2,1)S(1)} %collective-permute-done.msg, bf16[32,1024]{1,0:T(8,128)(2,1)S(1)} %get-tuple-element.49.target, ...), custom_call_target="tpu_custom_call" | custom-call | flops 2000000000 | bytes 65536 | tf_op jit(solution)/shard_map/pallas_call | solution.py:430
  19.3 1.6 %collective-permute-start.5 = (bf16[2,96,256]{2,1,0:T(8,128)(2,1)S(1)}, bf16[2,96,256]{2,1,0:T(8,128)(2,1)S(1)}, u32[]{:S(2)}, u32[]{:S(2)}) collective-permute-start(bf16[2,96,256]{2,1,0:T(8,128)(2,1)S(1)} %collective-permute-done.3.refs_4_), channel_id=1, source_target_pairs={{0,1},{1,0},{2,3},{3,2},{4,5},{5,4},{6,7},{7,6},{8,9},{9,8},{10,11... | collective-permute-start | bytes 294920 | tf_op jit(solution)/shard_map/ppermute | solution.py:391
  20.9 0.9 %shard_map.106 = (f32[32,1024]{1,0:T(8,128)S(1)}, bf16[2,256,256]{2,1,0:T(8,128)(2,1)S(1)}, bf16[2,256,256]{2,1,0:T(8,128)(2,1)S(1)}) custom-call(f32[8,128]{1,0:T(8,128)S(1)} %get-tuple-element.47.numbers.refs_0_, f32[32,1024]{1,0:T(8,128)S(1)} %get-tuple-element.59.refs_1_, bf16[1024,1024]{1,0:T(8,128)(2,1)S(1)} %get-tuple-element.60.refs_2_.refs_3_.refs_1_, ...), custom_call_target="tpu_custom_call" | custom-call | flops 1000000000 | bytes 65536 | tf_op jit(solution)/shard_map/pallas_call | solution.py:434
  21.9 0.2 collective-permute-done.6.refs_6_
  22.2 1.5 %shard_map.107 = (bf16[2,256,256]{2,1,0:T(8,128)(2,1)S(1)}, bf16[2,256,256]{2,1,0:T(8,128)(2,1)S(1)}, f32[1,1024]{1,0:T(1,128)S(1)}, f32[16,1024]{1,0:T(8,128)S(...) custom-call(f32[8,128]{1,0:T(8,128)S(1)} %get-tuple-element.47.numbers.refs_0_, ...), custom_call_target="tpu_custom_call" | custom-call | flops 2000000000 | bytes 65536 | tf_op jit(solution)/shard_map/pallas_call | solution.py:437
  23.9 0.7 %collective-permute-start.8 = (bf16[32,1024]{1,0:T(8,128)(2,1)S(1)}, bf16[32,1024]{1,0:T(8,128)(2,1)S(1)}, u32[]{:S(2)}, u32[]{:S(2)}) collective-permute-start(bf16[32,1024]{1,0:T(8,128)(2,1)S(1)} %get-tuple-element.65.wmsg), channel_id=1, source_target_pairs={{1,2},{3,4},{5,6},{7,8},{9,10},{11,12},{13,14},{15,16},{17,18},{19... | collective-permute-start | bytes 196616 | tf_op jit(solution)/shard_map/ppermute | solution.py:450
  24.6 0.4 collective-permute-done.7.wmsg_a.got
  25.0 2.8 %collective-permute-start.9 = (bf16[2,32,256]{2,1,0:T(8,128)(2,1)S(1)}, bf16[2,32,256]{2,1,0:T(8,128)(2,1)S(1)}, u32[]{:S(2)}, u32[]{:S(2)}) collective-permute-start(bf16[2,32,256]{2,1,0:T(8,128)(2,1)S(1)} %get-tuple-element.78), channel_id=1, source_target_pairs={{0,2},{1,5},{2,0},{3,7},{4,6},{5,1},{6,4},{7,3},{8,10},{9,13},{10,... | collective-permute-start | bytes 98312 | tf_op jit(solution)/shard_map/ppermute | solution.py:388
  27.8 1.6 %collective-permute-start.10 = (bf16[2,32,256]{2,1,0:T(8,128)(2,1)S(1)}, bf16[2,32,256]{2,1,0:T(8,128)(2,1)S(1)}, u32[]{:S(2)}, u32[]{:S(2)}) collective-permute-start(bf16[2,32,256]{2,1,0:T(8,128)(2,1)S(1)} %get-tuple-element.79), channel_id=1, source_target_pairs={{0,8},{1,17},{2,10},{3,19},{4,12},{5,21},{6,14},{7,23},{8,0},{9,25... | collective-permute-start | bytes 98312 | tf_op jit(solution)/shard_map/ppermute | solution.py:388
  30.8 1.2 %collective-permute-done.10.refs_11_ = bf16[2,32,256]{2,1,0:T(8,128)(2,1)S(1)} collective-permute-done((bf16[2,32,256]{2,1,0:T(8,128)(2,1)S(1)}, bf16[2,32,256]{2,1,0:T(8,128)(2,1)S(1)}, u32[]{:S(2)}, u32[]{:S(2)}) %collective-permute-start.10) | collective-permute-done | bytes 32800 | tf_op jit(solution)/shard_map/ppermute | solution.py:388
  32.0 1.2 %shard_map.108.refs_0_ = f32[32,1024]{1,0:T(8,128)S(1)} custom-call(bf16[32,1024]{1,0:T(8,128)(2,1)S(1)} %get-tuple-element.65.wmsg, bf16[32,1536]{1,0:T(8,128)(2,1)S(1)} %collective-permute-done.7.wmsg_a.got, bf16[32,1024]{1,0:T(8,128)(2,1)S(1)} %collective-permute-done.8.wmsg_b, bf16[1024,1024]{1,0:T(8,128)(2,1)S(1)} %get-tuple-element.67.kept, ...), custom_call_target="tpu_custom_call" | custom-call | flops 1200000000 | bytes 65536 | tf_op jit(solution)/shard_map/pallas_call | solution.py:453
  33.2 1.4 %shard_map.110 = (f32[32,128]{1,0:T(8,128)}, f32[16,1024]{1,0:T(8,128)S(1)}, f32[16,1024]{1,0:T(8,128)S(1)}, f32[16,128]{1,0:T(8,128)S(1)}) custom-call(f32[32,1024]{1,0:T(8,128)S(1)} %shard_map.108.refs_0_, bf16[1024,1024]{1,0:T(8,128)(2,1)S(1)} %get-tuple-element.60.refs_2_.refs_3_.refs_1_, bf16[2,256,256]{2,1,0:T(8,128)(2,1)S(1)} %get-tuple-element.70.refs_2_, ...), custom_call_target="tpu_custom_call" | custom-call | flops 2000000000 | bytes 65536 | tf_op jit(solution)/shard_map/pallas_call | solution.py:455
  34.6 4.0 %all-to-all-start = ((f32[32,1,128]{2,1,0:T(1,128)}), f32[32,1,128]{2,1,0:T(1,128)S(1)}, u32[]{:S(2)}, u32[]{:S(2)}) async-start(f32[32,1,128]{2,1,0:T(1,128)} %bitcast.1), calls=%async_computation | async-start | bytes 32768 | tf_op jit(solution)/shard_map/all_to_all | solution.py:461
  38.6 0.7 %shard_map.112 = f32[16,1024]{1,0:T(8,128)} custom-call(f32[1]{0:T(128)S(6)} %copy.14.signal, f32[8,128]{1,0:T(8,128)S(1)} %get-tuple-element.47.numbers.refs_0_, f32[16,1024]{1,0:T(8,128)S(1)} %get-tuple-element.76.refs_9_.source), custom_call_target="tpu_custom_call" | custom-call | flops 2000000000 | bytes 65536 | tf_op jit(solution)/shard_map/pallas_call | solution.py:462
  39.3 6.4 %all-to-all-done = f32[32,1,128]{2,1,0:T(1,128)S(1)} async-done(((f32[32,1,128]{2,1,0:T(1,128)}), f32[32,1,128]{2,1,0:T(1,128)S(1)}, u32[]{:S(2)}, u32[]{:S(2)}) %all-to-all-start) | async-done | bytes 16416 | tf_op jit(solution)/shard_map/all_to_all | solution.py:461
  45.7 0.9 %shard_map.111 = (f32[16,1024]{1,0:T(8,128)}, f32[16,1024]{1,0:T(8,128)}, f32[1,16]{1,0:T(1,128)}) custom-call(f32[1]{0:T(128)S(6)} %copy.14.signal, f32[1]{0:T(128)S(6)} %copy.15.noise, f32[8,128]{1,0:T(8,128)S(1)} %get-tuple-element.47.numbers.refs_0_, f32[32,128]{1,0:T(8,128)S(1)} %bitcast.5, f32[16,128]{1,0:T(8,128)S(1)} %get-tuple-element.84.shift_in, ...), custom_call_target="tpu_custom_call" | custom-call | flops 2000000000 | bytes 65536 | tf_op jit(solution)/shard_map/pallas_call | solution.py:463
  (16 shorter events, 0.7 us)
Async XLA Ops:
  5.4 1.5 %collective-permute-start.2 = (bf16[2,96,256]{2,1,0:T(8,128)(2,1)S(1)}, bf16[2,96,256]{2,1,0:T(8,128)(2,1)S(1)}, u32[]{:S(2)}, u32[]{:S(2)}) collective-permute-start(bf16[2,96,256]{2,1,0:T(8,128)(2,1)S(1)} %get-tuple-element.51), channel_id=1, source_target_pairs={{0,1},{1,0},{2,3},{3,2},{4,5},{5,4},{6,7},{7,6},{8,9},{9,8},{10,11... | collective-permute-start | bytes 294920 | tf_op jit(solution)/shard_map/ppermute | solution.py:391
  6.0 9.1 %collective-permute-start.1 = (bf16[64,1024]{1,0:T(8,128)(2,1)S(1)}, bf16[64,1024]{1,0:T(8,128)(2,1)S(1)}, u32[]{:S(2)}, u32[]{:S(2)}) collective-permute-start(bf16[64,1024]{1,0:T(8,128)(2,1)S(1)} %get-tuple-element.48.msg), channel_id=1, source_target_pairs={{0,1},{1,0},{2,3},{3,2},{4,5},{5,4},{6,7},{7,6},{8,9},{9,8},{10,11... | collective-permute-start | bytes 393224 | tf_op jit(solution)/shard_map/ppermute | solution.py:394
  6.0 11.1 %collective-permute-start = (bf16[64,1024]{1,0:T(8,128)(2,1)S(1)}, bf16[64,1024]{1,0:T(8,128)(2,1)S(1)}, u32[]{:S(2)}, u32[]{:S(2)}) collective-permute-start(bf16[64,1024]{1,0:T(8,128)(2,1)S(1)} %get-tuple-element.48.msg), channel_id=1, source_target_pairs={{1,2},{3,4},{5,6},{7,8},{9,10},{11,12},{13,14},{15,16},{17,18},{19... | collective-permute-start | bytes 393224 | tf_op jit(solution)/shard_map/ppermute | solution.py:394
  8.9 10.4 %collective-permute-start.3 = (bf16[2,96,256]{2,1,0:T(8,128)(2,1)S(1)}, bf16[2,96,256]{2,1,0:T(8,128)(2,1)S(1)}, u32[]{:S(2)}, u32[]{:S(2)}) collective-permute-start(bf16[2,96,256]{2,1,0:T(8,128)(2,1)S(1)} %get-tuple-element.57), channel_id=1, source_target_pairs={{0,2},{1,5},{2,0},{3,7},{4,6},{5,1},{6,4},{7,3},{8,10},{9,13},{10,... | collective-permute-start | bytes 294920 | tf_op jit(solution)/shard_map/ppermute | solution.py:388
  12.9 6.3 %collective-permute-start.4 = (bf16[2,96,256]{2,1,0:T(8,128)(2,1)S(1)}, bf16[2,96,256]{2,1,0:T(8,128)(2,1)S(1)}, u32[]{:S(2)}, u32[]{:S(2)}) collective-permute-start(bf16[2,96,256]{2,1,0:T(8,128)(2,1)S(1)} %get-tuple-element.58), channel_id=1, source_target_pairs={{0,8},{1,17},{2,10},{3,19},{4,12},{5,21},{6,14},{7,23},{8,0},{9,25... | collective-permute-start | bytes 294920 | tf_op jit(solution)/shard_map/ppermute | solution.py:388
  19.3 2.6 %collective-permute-start.5 = (bf16[2,96,256]{2,1,0:T(8,128)(2,1)S(1)}, bf16[2,96,256]{2,1,0:T(8,128)(2,1)S(1)}, u32[]{:S(2)}, u32[]{:S(2)}) collective-permute-start(bf16[2,96,256]{2,1,0:T(8,128)(2,1)S(1)} %collective-permute-done.3.refs_4_), channel_id=1, source_target_pairs={{0,1},{1,0},{2,3},{3,2},{4,5},{5,4},{6,7},{7,6},{8,9},{9,8},{10,11... | collective-permute-start | bytes 294920 | tf_op jit(solution)/shard_map/ppermute | solution.py:391
  20.9 1.3 %collective-permute-start.6 = (bf16[2,96,256]{2,1,0:T(8,128)(2,1)S(1)}, bf16[2,96,256]{2,1,0:T(8,128)(2,1)S(1)}, u32[]{:S(2)}, u32[]{:S(2)}) collective-permute-start(bf16[2,96,256]{2,1,0:T(8,128)(2,1)S(1)} %collective-permute-done.4.refs_5_), channel_id=1, source_target_pairs={{0,1},{1,0},{2,3},{3,2},{4,5},{5,4},{6,7},{7,6},{8,9},{9,8},{10,11... | collective-permute-start | bytes 294920 | tf_op jit(solution)/shard_map/ppermute | solution.py:391
  23.7 1.3 %collective-permute-start.7 = (bf16[32,1536]{1,0:T(8,128)(2,1)S(1)}, bf16[32,1536]{1,0:T(8,128)(2,1)S(1)}, u32[]{:S(2)}, u32[]{:S(2)}) collective-permute-start(bf16[32,1536]{1,0:T(8,128)(2,1)S(1)} %get-tuple-element.66), channel_id=1, source_target_pairs={{0,1},{1,0},{2,3},{3,2},{4,5},{5,4},{6,7},{7,6},{8,9},{9,8},{10,11... | collective-permute-start | bytes 294920 | tf_op jit(solution)/shard_map/ppermute | solution.py:391
  23.9 8.1 %collective-permute-start.8 = (bf16[32,1024]{1,0:T(8,128)(2,1)S(1)}, bf16[32,1024]{1,0:T(8,128)(2,1)S(1)}, u32[]{:S(2)}, u32[]{:S(2)}) collective-permute-start(bf16[32,1024]{1,0:T(8,128)(2,1)S(1)} %get-tuple-element.65.wmsg), channel_id=1, source_target_pairs={{1,2},{3,4},{5,6},{7,8},{9,10},{11,12},{13,14},{15,16},{17,18},{19... | collective-permute-start | bytes 196616 | tf_op jit(solution)/shard_map/ppermute | solution.py:450
  25.0 5.7 %collective-permute-start.9 = (bf16[2,32,256]{2,1,0:T(8,128)(2,1)S(1)}, bf16[2,32,256]{2,1,0:T(8,128)(2,1)S(1)}, u32[]{:S(2)}, u32[]{:S(2)}) collective-permute-start(bf16[2,32,256]{2,1,0:T(8,128)(2,1)S(1)} %get-tuple-element.78), channel_id=1, source_target_pairs={{0,2},{1,5},{2,0},{3,7},{4,6},{5,1},{6,4},{7,3},{8,10},{9,13},{10,... | collective-permute-start | bytes 98312 | tf_op jit(solution)/shard_map/ppermute | solution.py:388
  27.8 4.2 %collective-permute-start.10 = (bf16[2,32,256]{2,1,0:T(8,128)(2,1)S(1)}, bf16[2,32,256]{2,1,0:T(8,128)(2,1)S(1)}, u32[]{:S(2)}, u32[]{:S(2)}) collective-permute-start(bf16[2,32,256]{2,1,0:T(8,128)(2,1)S(1)} %get-tuple-element.79), channel_id=1, source_target_pairs={{0,8},{1,17},{2,10},{3,19},{4,12},{5,21},{6,14},{7,23},{8,0},{9,25... | collective-permute-start | bytes 98312 | tf_op jit(solution)/shard_map/ppermute | solution.py:388
  30.7 2.5 %collective-permute-start.11 = (bf16[2,32,256]{2,1,0:T(8,128)(2,1)S(1)}, bf16[2,32,256]{2,1,0:T(8,128)(2,1)S(1)}, u32[]{:S(2)}, u32[]{:S(2)}) collective-permute-start(bf16[2,32,256]{2,1,0:T(8,128)(2,1)S(1)} %collective-permute-done.9.refs_10_), channel_id=1, source_target_pairs={{0,1},{1,0},{2,3},{3,2},{4,5},{5,4},{6,7},{7,6},{8,9},{9,8},{10,11... | collective-permute-start | bytes 98312 | tf_op jit(solution)/shard_map/ppermute | solution.py:391
  32.0 1.2 %collective-permute-start.12 = (bf16[2,32,256]{2,1,0:T(8,128)(2,1)S(1)}, bf16[2,32,256]{2,1,0:T(8,128)(2,1)S(1)}, u32[]{:S(2)}, u32[]{:S(2)}) collective-permute-start(bf16[2,32,256]{2,1,0:T(8,128)(2,1)S(1)} %collective-permute-done.10.refs_11_), channel_id=1, source_target_pairs={{0,1},{1,0},{2,3},{3,2},{4,5},{5,4},{6,7},{7,6},{8,9},{9,8},{10,11... | collective-permute-start | bytes 98312 | tf_op jit(solution)/shard_map/ppermute | solution.py:391
  34.6 11.1 %all-to-all-start = ((f32[32,1,128]{2,1,0:T(1,128)}), f32[32,1,128]{2,1,0:T(1,128)S(1)}, u32[]{:S(2)}, u32[]{:S(2)}) async-start(f32[32,1,128]{2,1,0:T(1,128)} %bitcast.1), calls=%async_computation | async-start | bytes 32768 | tf_op jit(solution)/shard_map/all_to_all | solution.py:461

commit v8 on v7

--- a/solution.py
+++ b/solution.py
@@ -116,7 +116,7 @@
 
 def front_kernel(levels, *refs):
     length, far_length, given = refs[:3]
-    msg, target, basis, skel_target, numbers, keep, give = refs[3:10]
+    msg, target, basis, skel_target, numbers, keep, beside = refs[3:10]
     buf, pair_buf, turned_src = refs[10:]
     points = given[16:19, :]
     for slot, value in enumerate((length[0], far_length[0])):
@@ -154,28 +154,38 @@
     coef = merged(dot_rows(msg[0:VEC_ROWS, :], basis[...]))
     for level in range(levels):
         high, low = split_two(coef[:, level * rank : (level + 1) * rank])
-        dest = keep.at[level] if level < levels // 2 else give.at[level - levels // 2]
-        dest[0:32, :] = high
-        dest[32:64, :] = low
-        dest[64:96, :] = sources[level]
+        if level < levels // 2:
+            keep[level, 0:32, :] = high
+            keep[level, 32:64, :] = low
+            keep[level, 64:96, :] = sources[level]
+        else:
+            start = rows + (level - levels // 2) * 2 * rank
+            beside[0:32, start : start + rank] = high
+            beside[32:64, start : start + rank] = low
+            beside[0:32, start + rank : start + 2 * rank] = sources[level]
+            beside[32:64, start + rank : start + 2 * rank] = sources[level]
+    beside[:, 0:rows] = msg[...]
 
 
 def near_block(msg, target, turned_src, rates, kept):
     rows = target.shape[1]
-    turned_src[...] = turned(msg[32:64, :])
+    turned_src[...] = turned(msg[32:64, 0:rows])
     for col in range(0, rows, TILE):
         squared = dot(turned_src[...], target[:, col : col + TILE])
         value, slope = matern(squared, rates)
         value = value.astype(HALF)
         kept[:, col : col + TILE] = value
         pair = jnp.concatenate([value, slope.astype(HALF)], axis=1)
-        total = dot(msg[0:VEC_ROWS, :], pair)
+        total = dot(msg[0:VEC_ROWS, 0:rows], pair)
         yield slice(col, col + TILE), merged(total[:, :TILE]), total[16:32, TILE:]
 
 
 def own_kernel(numbers, msg, target, keep, got, kept, image, slopes, *rest):
     packs, turned_src = rest[:-1], rest[-1]
-    gather_share(keep, got, packs)
+    rows, rank = target.shape[1], keep.shape[2]
+    starts = [rows + 2 * rank * slot for slot in range(len(packs))]
+    parts = [(got[:, start : start + rank], got[0:32, start + rank : start + 2 * rank]) for start in starts]
+    gather_share(keep, [jnp.concatenate(part, axis=0) for part in parts], packs)
     rates = numbers[0:1, :], numbers[2:3, :]
     for span, part, slope in near_block(msg, target, turned_src, rates, kept):
         image[:, span] = part
@@ -390,14 +400,11 @@
     def sibling(value):
         return lax.ppermute(value, "loc", beside)
 
-    def sides(value):
-        return lax.ppermute(value, "loc", beside), lax.ppermute(value, "loc", across)
-
     height = -(-(24 + levels) // 8) * 8
     given = jnp.pad(right_sides, ((0, height - probes), (0, 0)))
     given += jnp.pad(points, ((16, height - 19), (0, 0)))
     given += jnp.pad(skeleton, ((24, height - 24 - levels), (0, rows - rank))).astype(FULL)
-    msg, target, basis, skel_target, numbers, keep, give = call(
+    msg, target, basis, skel_target, numbers, keep, beside_msg = call(
         functools.partial(front_kernel, levels),
         [
             ((MSG_ROWS, rows), HALF),
@@ -406,7 +413,7 @@
             ((levels, SRC_ROWS, rank), HALF),
             ((8, 128), FULL),
             ((half, 96, rank), HALF),
-            ((half, 96, rank), HALF),
+            ((MSG_ROWS, rows + 2 * half * rank), HALF),
         ],
         [SMEM, SMEM, VMEM],
         [
@@ -415,8 +422,8 @@
             VMEM((levels * rank, SRC_ROWS), HALF),
         ],
     )(lengthscale, far_length, given)
-    got = sibling(give)
-    msg_a, msg_b = sides(msg)
+    msg_a = sibling(beside_msg)
+    msg_b = lax.ppermute(msg, "loc", across)
     near_outs = [((rows, rows), HALF), ((32, rows), FULL), ((probes, rows), FULL)]
     turned_buf = [VMEM((rows, SRC_ROWS), HALF)]
     kept, image, slopes, *packs = call(
@@ -424,7 +431,7 @@
         near_outs + [((2, 96, rank), HALF)] * half,
         [VMEM] * 5,
         turned_buf,
-    )(numbers, msg, target, keep, got)
+    )(numbers, msg, target, keep, msg_a)
     cross = [partner(pack, slot) for slot, pack in enumerate(packs)]
     kept_a, image, slopes = call(side_kernel, near_outs, [VMEM] * 5, turned_buf)(numbers, msg_a, target, image, slopes)
     kept_b, image, slopes = call(side_kernel, near_outs, [VMEM] * 5, turned_buf)(numbers, msg_b, target, image, slopes)

time: 46.8 us -> 46.7 us (level)
  transfers between devices with their start and end apart: 14 -> 13, of which waited for: 5 -> 5; matrix products, arithmetic and copies ran while one was open for 0% -> 0% of each run, Pallas kernels for 19% -> 19%
where the time goes in v8:
time: 46.7 us; the launch traced here: 46.4 us
  starting transfers between devices  18.4 us (39%)
  Pallas kernels  15.3 us (33%)
  waiting for transfers between devices  8.45 us (18%)
  between operations  3.35 us (7%)
  other arithmetic  0.88 us (2%)
    ppermute x4, starting transfers between devices, partner(): return lax.ppermute(value, 'loc', pairs)  10.3 us
    all_to_all x1, waiting for transfers between devices, shards(): table = lax.all_to_all(sums, 'loc', 0, 0, tiled=True)  6.4 us
    all_to_all x1, starting transfers between devices, shards(): table = lax.all_to_all(sums, 'loc', 0, 0, tiled=True)  4.34 us
    pallas_call x2, Pallas kernels, shards(): call(side_kernel, near_outs, [VMEM] * 5, turned_buf)  4.12 us
    pallas_call x1, Pallas kernels, shards(): call(functools.partial(front_kernel, levels), [((MSG_ROWS, rows), HALF),...  2.63 us
    ppermute x6, starting transfers between devices, sibling(): return lax.ppermute(value, 'loc', beside)  2.48 us
    pallas_call x1, Pallas kernels, shards(): call(own_kernel, near_outs + [((2, 96, rank), HALF)] * half, [VMEM] * 5,...  2.01 us
    pallas_call x1, Pallas kernels, shards(): call(functools.partial(far_kernel, half, far_scale), couplings + [((1, ro...  1.52 us
  transfers between devices with their start and end apart: 13, of which 5 were waited for; matrix products, arithmetic and copies ran while one was open for 0% of the time, Pallas kernels for 19%

profile of v8, /device:TPU:0, one launch (start us, length us, event | category | flops | bytes accessed | tf_op | source)
XLA Modules:
  0.0 46.4 jit_solution(412972997112853815)
XLA Ops:
  1.9 0.9 %convert_add_fusion.refs_2_.refs_8_.given = f32[32,1024]{1,0:T(8,128)S(1)} fusion(s32[4,256]{1,0:T(4,128)} %param.9, f32[3,1024]{1,0:T(4,128)} %param.7, f32[16,1024]{1,0:T(8,128)} %param.8), kind=kLoop, calls=%fused_computation | loop fusion | flops 98304 | bytes 212992 | tf_op jit(solution)/shard_map/add | solution.py:406
  2.8 2.6 %shard_map.102 = (bf16[64,1024]{1,0:T(8,128)(2,1)S(1)}, bf16[32,1024]{1,0:T(8,128)(2,1)S(1)}, bf16[1024,1024]{1,0:T(8,128)(2,1)S(1)}, bf16[4,32,256]{2,1,0:T(8,1...) custom-call(f32[1]{0:T(128)S(6)} %copy.12.refs_0_, ...), custom_call_target="tpu_custom_call" | custom-call | flops 2000000000 | bytes 65536 | tf_op jit(solution)/shard_map/pallas_call | solution.py:407
  5.4 0.5 %collective-permute-start.1 = (bf16[64,2048]{1,0:T(8,128)(2,1)S(1)}, bf16[64,2048]{1,0:T(8,128)(2,1)S(1)}, u32[]{:S(2)}, u32[]{:S(2)}) collective-permute-start(bf16[64,2048]{1,0:T(8,128)(2,1)S(1)} %get-tuple-element.50), channel_id=1, source_target_pairs={{0,1},{1,0},{2,3},{3,2},{4,5},{5,4},{6,7},{7,6},{8,9},{9,8},{10,11... | collective-permute-start | bytes 786440 | tf_op jit(solution)/shard_map/ppermute | solution.py:401
  6.0 0.7 %collective-permute-start = (bf16[64,1024]{1,0:T(8,128)(2,1)S(1)}, bf16[64,1024]{1,0:T(8,128)(2,1)S(1)}, u32[]{:S(2)}, u32[]{:S(2)}) collective-permute-start(bf16[64,1024]{1,0:T(8,128)(2,1)S(1)} %get-tuple-element.48.msg), channel_id=1, source_target_pairs={{1,2},{3,4},{5,6},{7,8},{9,10},{11,12},{13,14},{15,16},{17,18},{19... | collective-permute-start | bytes 393224 | tf_op jit(solution)/shard_map/ppermute | solution.py:426
  6.6 0.5 %collective-permute-done.1.got.msg = bf16[64,2048]{1,0:T(8,128)(2,1)S(1)} collective-permute-done((bf16[64,2048]{1,0:T(8,128)(2,1)S(1)}, bf16[64,2048]{1,0:T(8,128)(2,1)S(1)}, u32[]{:S(2)}, u32[]{:S(2)}) %collective-permute-start.1) | collective-permute-done | bytes 262176 | tf_op jit(solution)/shard_map/ppermute | solution.py:401
  7.1 2.0 %shard_map.103 = (bf16[1024,1024]{1,0:T(8,128)(2,1)S(1)}, f32[32,1024]{1,0:T(8,128)S(1)}, f32[16,1024]{1,0:T(8,128)S(1)}, bf16[2,96,256]{2,1,0:T(8,128)(2,1)S(1)}, bf16[2,96,256]{2,1,0:T(8,128)(2,1)S(1)}) custom-call(f32[8,128]{1,0:T(8,128)S(1)} %get-tuple-element.47.numbers.refs_0_, bf16[64,1024]{1,0:T(8,128)(2,1)S(1)} %get-tuple-element.48.msg, ...), custom_call_target="tpu_custom_call" | custom-call | flops 2000000000 | bytes 65536 | tf_op jit(solution)/shard_map/pallas_call | solution.py:429
  9.1 3.3 %collective-permute-start.2 = (bf16[2,96,256]{2,1,0:T(8,128)(2,1)S(1)}, bf16[2,96,256]{2,1,0:T(8,128)(2,1)S(1)}, u32[]{:S(2)}, u32[]{:S(2)}) collective-permute-start(bf16[2,96,256]{2,1,0:T(8,128)(2,1)S(1)} %get-tuple-element.57), channel_id=1, source_target_pairs={{0,2},{1,5},{2,0},{3,7},{4,6},{5,1},{6,4},{7,3},{8,10},{9,13},{10,... | collective-permute-start | bytes 294920 | tf_op jit(solution)/shard_map/ppermute | solution.py:398
  12.5 2.6 %collective-permute-start.3 = (bf16[2,96,256]{2,1,0:T(8,128)(2,1)S(1)}, bf16[2,96,256]{2,1,0:T(8,128)(2,1)S(1)}, u32[]{:S(2)}, u32[]{:S(2)}) collective-permute-start(bf16[2,96,256]{2,1,0:T(8,128)(2,1)S(1)} %get-tuple-element.58), channel_id=1, source_target_pairs={{0,8},{1,17},{2,10},{3,19},{4,12},{5,21},{6,14},{7,23},{8,0},{9,25... | collective-permute-start | bytes 294920 | tf_op jit(solution)/shard_map/ppermute | solution.py:398
  15.0 2.1 %shard_map.104 = (bf16[1024,1024]{1,0:T(8,128)(2,1)S(1)}, f32[32,1024]{1,0:T(8,128)S(1)}, f32[16,1024]{1,0:T(8,128)S(1)}) custom-call(f32[8,128]{1,0:T(8,128)S(1)} %get-tuple-element.47.numbers.refs_0_, bf16[64,2048]{1,0:T(8,128)(2,1)S(1)} %collective-permute-done.1.got.msg, bf16[32,1024]{1,0:T(8,128)(2,1)S(1)} %get-tuple-element.49.target, ...), custom_call_target="tpu_custom_call" | custom-call | flops 2000000000 | bytes 65536 | tf_op jit(solution)/shard_map/pallas_call | solution.py:436
  17.1 2.1 %shard_map.105 = (bf16[1024,1024]{1,0:T(8,128)(2,1)S(1)}, f32[32,1024]{1,0:T(8,128)S(1)}, f32[16,1024]{1,0:T(8,128)S(1)}) custom-call(f32[8,128]{1,0:T(8,128)S(1)} %get-tuple-element.47.numbers.refs_0_, bf16[64,1024]{1,0:T(8,128)(2,1)S(1)} %collective-permute-done.msg, bf16[32,1024]{1,0:T(8,128)(2,1)S(1)} %get-tuple-element.49.target, ...), custom_call_target="tpu_custom_call" | custom-call | flops 2000000000 | bytes 65536 | tf_op jit(solution)/shard_map/pallas_call | solution.py:437
  19.2 1.2 %collective-permute-start.4 = (bf16[2,96,256]{2,1,0:T(8,128)(2,1)S(1)}, bf16[2,96,256]{2,1,0:T(8,128)(2,1)S(1)}, u32[]{:S(2)}, u32[]{:S(2)}) collective-permute-start(bf16[2,96,256]{2,1,0:T(8,128)(2,1)S(1)} %collective-permute-done.2.refs_4_), channel_id=1, source_target_pairs={{0,1},{1,0},{2,3},{3,2},{4,5},{5,4},{6,7},{7,6},{8,9},{9,8},{10,11... | collective-permute-start | bytes 294920 | tf_op jit(solution)/shard_map/ppermute | solution.py:401
  20.5 0.9 %shard_map.106 = (f32[32,1024]{1,0:T(8,128)S(1)}, bf16[2,256,256]{2,1,0:T(8,128)(2,1)S(1)}, bf16[2,256,256]{2,1,0:T(8,128)(2,1)S(1)}) custom-call(f32[8,128]{1,0:T(8,128)S(1)} %get-tuple-element.47.numbers.refs_0_, f32[32,1024]{1,0:T(8,128)S(1)} %get-tuple-element.59.refs_1_, bf16[1024,1024]{1,0:T(8,128)(2,1)S(1)} %get-tuple-element.60.refs_2_.refs_3_.refs_1_, ...), custom_call_target="tpu_custom_call" | custom-call | flops 1000000000 | bytes 65536 | tf_op jit(solution)/shard_map/pallas_call | solution.py:441
  21.7 1.5 %shard_map.107 = (bf16[2,256,256]{2,1,0:T(8,128)(2,1)S(1)}, bf16[2,256,256]{2,1,0:T(8,128)(2,1)S(1)}, f32[1,1024]{1,0:T(1,128)S(1)}, f32[16,1024]{1,0:T(8,128)S(...) custom-call(f32[8,128]{1,0:T(8,128)S(1)} %get-tuple-element.47.numbers.refs_0_, ...), custom_call_target="tpu_custom_call" | custom-call | flops 2000000000 | bytes 65536 | tf_op jit(solution)/shard_map/pallas_call | solution.py:444
  23.4 0.7 %collective-permute-start.7 = (bf16[32,1024]{1,0:T(8,128)(2,1)S(1)}, bf16[32,1024]{1,0:T(8,128)(2,1)S(1)}, u32[]{:S(2)}, u32[]{:S(2)}) collective-permute-start(bf16[32,1024]{1,0:T(8,128)(2,1)S(1)} %get-tuple-element.65.wmsg), channel_id=1, source_target_pairs={{1,2},{3,4},{5,6},{7,8},{9,10},{11,12},{13,14},{15,16},{17,18},{19... | collective-permute-start | bytes 196616 | tf_op jit(solution)/shard_map/ppermute | solution.py:457
  24.5 2.8 %collective-permute-start.8 = (bf16[2,32,256]{2,1,0:T(8,128)(2,1)S(1)}, bf16[2,32,256]{2,1,0:T(8,128)(2,1)S(1)}, u32[]{:S(2)}, u32[]{:S(2)}) collective-permute-start(bf16[2,32,256]{2,1,0:T(8,128)(2,1)S(1)} %get-tuple-element.78), channel_id=1, source_target_pairs={{0,2},{1,5},{2,0},{3,7},{4,6},{5,1},{6,4},{7,3},{8,10},{9,13},{10,... | collective-permute-start | bytes 98312 | tf_op jit(solution)/shard_map/ppermute | solution.py:398
  27.4 1.6 %collective-permute-start.9 = (bf16[2,32,256]{2,1,0:T(8,128)(2,1)S(1)}, bf16[2,32,256]{2,1,0:T(8,128)(2,1)S(1)}, u32[]{:S(2)}, u32[]{:S(2)}) collective-permute-start(bf16[2,32,256]{2,1,0:T(8,128)(2,1)S(1)} %get-tuple-element.79), channel_id=1, source_target_pairs={{0,8},{1,17},{2,10},{3,19},{4,12},{5,21},{6,14},{7,23},{8,0},{9,25... | collective-permute-start | bytes 98312 | tf_op jit(solution)/shard_map/ppermute | solution.py:398
  30.3 0.5 %collective-permute-start.10 = (bf16[2,32,256]{2,1,0:T(8,128)(2,1)S(1)}, bf16[2,32,256]{2,1,0:T(8,128)(2,1)S(1)}, u32[]{:S(2)}, u32[]{:S(2)}) collective-permute-start(bf16[2,32,256]{2,1,0:T(8,128)(2,1)S(1)} %collective-permute-done.8.refs_10_), channel_id=1, source_target_pairs={{0,1},{1,0},{2,3},{3,2},{4,5},{5,4},{6,7},{7,6},{8,9},{9,8},{10,11... | collective-permute-start | bytes 98312 | tf_op jit(solution)/shard_map/ppermute | solution.py:401
  30.7 0.8 %collective-permute-done.9.refs_11_ = bf16[2,32,256]{2,1,0:T(8,128)(2,1)S(1)} collective-permute-done((bf16[2,32,256]{2,1,0:T(8,128)(2,1)S(1)}, bf16[2,32,256]{2,1,0:T(8,128)(2,1)S(1)}, u32[]{:S(2)}, u32[]{:S(2)}) %collective-permute-start.9) | collective-permute-done | bytes 32800 | tf_op jit(solution)/shard_map/ppermute | solution.py:398
  31.6 1.2 %shard_map.108.refs_0_ = f32[32,1024]{1,0:T(8,128)S(1)} custom-call(bf16[32,1024]{1,0:T(8,128)(2,1)S(1)} %get-tuple-element.65.wmsg, bf16[32,1536]{1,0:T(8,128)(2,1)S(1)} %collective-permute-done.6.wmsg_a.got, bf16[32,1024]{1,0:T(8,128)(2,1)S(1)} %collective-permute-done.7.wmsg_b, bf16[1024,1024]{1,0:T(8,128)(2,1)S(1)} %get-tuple-element.67.kept, ...), custom_call_target="tpu_custom_call" | custom-call | flops 1200000000 | bytes 65536 | tf_op jit(solution)/shard_map/pallas_call | solution.py:460
  32.8 1.4 %shard_map.110 = (f32[32,128]{1,0:T(8,128)}, f32[16,1024]{1,0:T(8,128)S(1)}, f32[16,1024]{1,0:T(8,128)S(1)}, f32[16,128]{1,0:T(8,128)S(1)}) custom-call(f32[32,1024]{1,0:T(8,128)S(1)} %shard_map.108.refs_0_, bf16[1024,1024]{1,0:T(8,128)(2,1)S(1)} %get-tuple-element.60.refs_2_.refs_3_.refs_1_, bf16[2,256,256]{2,1,0:T(8,128)(2,1)S(1)} %get-tuple-element.70.refs_2_, ...), custom_call_target="tpu_custom_call" | custom-call | flops 2000000000 | bytes 65536 | tf_op jit(solution)/shard_map/pallas_call | solution.py:462
  34.1 4.3 %all-to-all-start = ((f32[32,1,128]{2,1,0:T(1,128)}), f32[32,1,128]{2,1,0:T(1,128)S(1)}, u32[]{:S(2)}, u32[]{:S(2)}) async-start(f32[32,1,128]{2,1,0:T(1,128)} %bitcast.1), calls=%async_computation | async-start | bytes 32768 | tf_op jit(solution)/shard_map/all_to_all | solution.py:468
  38.5 0.7 %shard_map.112 = f32[16,1024]{1,0:T(8,128)} custom-call(f32[1]{0:T(128)S(6)} %copy.14.signal, f32[8,128]{1,0:T(8,128)S(1)} %get-tuple-element.47.numbers.refs_0_, f32[16,1024]{1,0:T(8,128)S(1)} %get-tuple-element.76.refs_9_.source), custom_call_target="tpu_custom_call" | custom-call | flops 2000000000 | bytes 65536 | tf_op jit(solution)/shard_map/pallas_call | solution.py:469
  39.1 6.4 %all-to-all-done = f32[32,1,128]{2,1,0:T(1,128)S(1)} async-done(((f32[32,1,128]{2,1,0:T(1,128)}), f32[32,1,128]{2,1,0:T(1,128)S(1)}, u32[]{:S(2)}, u32[]{:S(2)}) %all-to-all-start) | async-done | bytes 16416 | tf_op jit(solution)/shard_map/all_to_all | solution.py:468
  45.5 0.9 %shard_map.111 = (f32[16,1024]{1,0:T(8,128)}, f32[16,1024]{1,0:T(8,128)}, f32[1,16]{1,0:T(1,128)}) custom-call(f32[1]{0:T(128)S(6)} %copy.14.signal, f32[1]{0:T(128)S(6)} %copy.15.noise, f32[8,128]{1,0:T(8,128)S(1)} %get-tuple-element.47.numbers.refs_0_, f32[32,128]{1,0:T(8,128)S(1)} %bitcast.5, f32[16,128]{1,0:T(8,128)S(1)} %get-tuple-element.84.shift_in, ...), custom_call_target="tpu_custom_call" | custom-call | flops 2000000000 | bytes 65536 | tf_op jit(solution)/shard_map/pallas_call | solution.py:470
  (14 shorter events, 1.1 us)
Async XLA Ops:
  5.4 1.7 %collective-permute-start.1 = (bf16[64,2048]{1,0:T(8,128)(2,1)S(1)}, bf16[64,2048]{1,0:T(8,128)(2,1)S(1)}, u32[]{:S(2)}, u32[]{:S(2)}) collective-permute-start(bf16[64,2048]{1,0:T(8,128)(2,1)S(1)} %get-tuple-element.50), channel_id=1, source_target_pairs={{0,1},{1,0},{2,3},{3,2},{4,5},{5,4},{6,7},{7,6},{8,9},{9,8},{10,11... | collective-permute-start | bytes 786440 | tf_op jit(solution)/shard_map/ppermute | solution.py:401
  6.0 11.1 %collective-permute-start = (bf16[64,1024]{1,0:T(8,128)(2,1)S(1)}, bf16[64,1024]{1,0:T(8,128)(2,1)S(1)}, u32[]{:S(2)}, u32[]{:S(2)}) collective-permute-start(bf16[64,1024]{1,0:T(8,128)(2,1)S(1)} %get-tuple-element.48.msg), channel_id=1, source_target_pairs={{1,2},{3,4},{5,6},{7,8},{9,10},{11,12},{13,14},{15,16},{17,18},{19... | collective-permute-start | bytes 393224 | tf_op jit(solution)/shard_map/ppermute | solution.py:426
  9.1 10.1 %collective-permute-start.2 = (bf16[2,96,256]{2,1,0:T(8,128)(2,1)S(1)}, bf16[2,96,256]{2,1,0:T(8,128)(2,1)S(1)}, u32[]{:S(2)}, u32[]{:S(2)}) collective-permute-start(bf16[2,96,256]{2,1,0:T(8,128)(2,1)S(1)} %get-tuple-element.57), channel_id=1, source_target_pairs={{0,2},{1,5},{2,0},{3,7},{4,6},{5,1},{6,4},{7,3},{8,10},{9,13},{10,... | collective-permute-start | bytes 294920 | tf_op jit(solution)/shard_map/ppermute | solution.py:398
  12.5 6.7 %collective-permute-start.3 = (bf16[2,96,256]{2,1,0:T(8,128)(2,1)S(1)}, bf16[2,96,256]{2,1,0:T(8,128)(2,1)S(1)}, u32[]{:S(2)}, u32[]{:S(2)}) collective-permute-start(bf16[2,96,256]{2,1,0:T(8,128)(2,1)S(1)} %get-tuple-element.58), channel_id=1, source_target_pairs={{0,8},{1,17},{2,10},{3,19},{4,12},{5,21},{6,14},{7,23},{8,0},{9,25... | collective-permute-start | bytes 294920 | tf_op jit(solution)/shard_map/ppermute | solution.py:398
  19.2 2.2 %collective-permute-start.4 = (bf16[2,96,256]{2,1,0:T(8,128)(2,1)S(1)}, bf16[2,96,256]{2,1,0:T(8,128)(2,1)S(1)}, u32[]{:S(2)}, u32[]{:S(2)}) collective-permute-start(bf16[2,96,256]{2,1,0:T(8,128)(2,1)S(1)} %collective-permute-done.2.refs_4_), channel_id=1, source_target_pairs={{0,1},{1,0},{2,3},{3,2},{4,5},{5,4},{6,7},{7,6},{8,9},{9,8},{10,11... | collective-permute-start | bytes 294920 | tf_op jit(solution)/shard_map/ppermute | solution.py:401
  20.4 1.3 %collective-permute-start.5 = (bf16[2,96,256]{2,1,0:T(8,128)(2,1)S(1)}, bf16[2,96,256]{2,1,0:T(8,128)(2,1)S(1)}, u32[]{:S(2)}, u32[]{:S(2)}) collective-permute-start(bf16[2,96,256]{2,1,0:T(8,128)(2,1)S(1)} %collective-permute-done.3.refs_5_), channel_id=1, source_target_pairs={{0,1},{1,0},{2,3},{3,2},{4,5},{5,4},{6,7},{7,6},{8,9},{9,8},{10,11... | collective-permute-start | bytes 294920 | tf_op jit(solution)/shard_map/ppermute | solution.py:401
  23.2 1.3 %collective-permute-start.6 = (bf16[32,1536]{1,0:T(8,128)(2,1)S(1)}, bf16[32,1536]{1,0:T(8,128)(2,1)S(1)}, u32[]{:S(2)}, u32[]{:S(2)}) collective-permute-start(bf16[32,1536]{1,0:T(8,128)(2,1)S(1)} %get-tuple-element.66), channel_id=1, source_target_pairs={{0,1},{1,0},{2,3},{3,2},{4,5},{5,4},{6,7},{7,6},{8,9},{9,8},{10,11... | collective-permute-start | bytes 294920 | tf_op jit(solution)/shard_map/ppermute | solution.py:401
  23.4 8.1 %collective-permute-start.7 = (bf16[32,1024]{1,0:T(8,128)(2,1)S(1)}, bf16[32,1024]{1,0:T(8,128)(2,1)S(1)}, u32[]{:S(2)}, u32[]{:S(2)}) collective-permute-start(bf16[32,1024]{1,0:T(8,128)(2,1)S(1)} %get-tuple-element.65.wmsg), channel_id=1, source_target_pairs={{1,2},{3,4},{5,6},{7,8},{9,10},{11,12},{13,14},{15,16},{17,18},{19... | collective-permute-start | bytes 196616 | tf_op jit(solution)/shard_map/ppermute | solution.py:457
  24.5 5.7 %collective-permute-start.8 = (bf16[2,32,256]{2,1,0:T(8,128)(2,1)S(1)}, bf16[2,32,256]{2,1,0:T(8,128)(2,1)S(1)}, u32[]{:S(2)}, u32[]{:S(2)}) collective-permute-start(bf16[2,32,256]{2,1,0:T(8,128)(2,1)S(1)} %get-tuple-element.78), channel_id=1, source_target_pairs={{0,2},{1,5},{2,0},{3,7},{4,6},{5,1},{6,4},{7,3},{8,10},{9,13},{10,... | collective-permute-start | bytes 98312 | tf_op jit(solution)/shard_map/ppermute | solution.py:398
  27.4 4.2 %collective-permute-start.9 = (bf16[2,32,256]{2,1,0:T(8,128)(2,1)S(1)}, bf16[2,32,256]{2,1,0:T(8,128)(2,1)S(1)}, u32[]{:S(2)}, u32[]{:S(2)}) collective-permute-start(bf16[2,32,256]{2,1,0:T(8,128)(2,1)S(1)} %get-tuple-element.79), channel_id=1, source_target_pairs={{0,8},{1,17},{2,10},{3,19},{4,12},{5,21},{6,14},{7,23},{8,0},{9,25... | collective-permute-start | bytes 98312 | tf_op jit(solution)/shard_map/ppermute | solution.py:398
  30.3 2.5 %collective-permute-start.10 = (bf16[2,32,256]{2,1,0:T(8,128)(2,1)S(1)}, bf16[2,32,256]{2,1,0:T(8,128)(2,1)S(1)}, u32[]{:S(2)}, u32[]{:S(2)}) collective-permute-start(bf16[2,32,256]{2,1,0:T(8,128)(2,1)S(1)} %collective-permute-done.8.refs_10_), channel_id=1, source_target_pairs={{0,1},{1,0},{2,3},{3,2},{4,5},{5,4},{6,7},{7,6},{8,9},{9,8},{10,11... | collective-permute-start | bytes 98312 | tf_op jit(solution)/shard_map/ppermute | solution.py:401
  31.5 1.2 %collective-permute-start.11 = (bf16[2,32,256]{2,1,0:T(8,128)(2,1)S(1)}, bf16[2,32,256]{2,1,0:T(8,128)(2,1)S(1)}, u32[]{:S(2)}, u32[]{:S(2)}) collective-permute-start(bf16[2,32,256]{2,1,0:T(8,128)(2,1)S(1)} %collective-permute-done.9.refs_11_), channel_id=1, source_target_pairs={{0,1},{1,0},{2,3},{3,2},{4,5},{5,4},{6,7},{7,6},{8,9},{9,8},{10,11... | collective-permute-start | bytes 98312 | tf_op jit(solution)/shard_map/ppermute | solution.py:401
  34.1 11.4 %all-to-all-start = ((f32[32,1,128]{2,1,0:T(1,128)}), f32[32,1,128]{2,1,0:T(1,128)S(1)}, u32[]{:S(2)}, u32[]{:S(2)}) async-start(f32[32,1,128]{2,1,0:T(1,128)} %bitcast.1), calls=%async_computation | async-start | bytes 32768 | tf_op jit(solution)/shard_map/all_to_all | solution.py:468

commit v9 on v8

--- a/solution.py
+++ b/solution.py
@@ -180,12 +180,15 @@
         yield slice(col, col + TILE), merged(total[:, :TILE]), total[16:32, TILE:]
 
 
-def own_kernel(numbers, msg, target, keep, got, kept, image, slopes, *rest):
-    packs, turned_src = rest[:-1], rest[-1]
-    rows, rank = target.shape[1], keep.shape[2]
+def first_pack_kernel(keep, got, *packs):
+    rank = keep.shape[2]
+    rows = got.shape[1] - 2 * rank * len(packs)
     starts = [rows + 2 * rank * slot for slot in range(len(packs))]
     parts = [(got[:, start : start + rank], got[0:32, start + rank : start + 2 * rank]) for start in starts]
     gather_share(keep, [jnp.concatenate(part, axis=0) for part in parts], packs)
+
+
+def own_kernel(numbers, msg, target, kept, image, slopes, turned_src):
     rates = numbers[0:1, :], numbers[2:3, :]
     for span, part, slope in near_block(msg, target, turned_src, rates, kept):
         image[:, span] = part
@@ -426,12 +429,9 @@
     msg_b = lax.ppermute(msg, "loc", across)
     near_outs = [((rows, rows), HALF), ((32, rows), FULL), ((probes, rows), FULL)]
     turned_buf = [VMEM((rows, SRC_ROWS), HALF)]
-    kept, image, slopes, *packs = call(
-        own_kernel,
-        near_outs + [((2, 96, rank), HALF)] * half,
-        [VMEM] * 5,
-        turned_buf,
-    )(numbers, msg, target, keep, msg_a)
+    packs = call(first_pack_kernel, [((2, 96, rank), HALF)] * half, [VMEM] * 2, micros=0.1)(keep, msg_a)
+    msg, packs = lax.optimization_barrier((msg, packs))
+    kept, image, slopes = call(own_kernel, near_outs, [VMEM] * 3, turned_buf)(numbers, msg, target)
     cross = [partner(pack, slot) for slot, pack in enumerate(packs)]
     kept_a, image, slopes = call(side_kernel, near_outs, [VMEM] * 5, turned_buf)(numbers, msg_a, target, image, slopes)
     kept_b, image, slopes = call(side_kernel, near_outs, [VMEM] * 5, turned_buf)(numbers, msg_b, target, image, slopes)

time: 46.7 us -> 46.7 us (level)
    pallas_call x1 -> x2, Pallas kernels: 2.01 us -> 2.04 us  [the longest x1 2.01 us: shards(): call(own_kernel, near_outs, [VMEM] * 3, turned_buf)(numbers, msg, target)]
where the time goes in v9:
time: 46.7 us; the launch traced here: 46.4 us
  starting transfers between devices  18.5 us (40%)
  Pallas kernels  15.4 us (33%)
  waiting for transfers between devices  8.34 us (18%)
  between operations  3.35 us (7%)
  other arithmetic  0.88 us (2%)
    ppermute x4, starting transfers between devices, partner(): return lax.ppermute(value, 'loc', pairs)  10.3 us
    all_to_all x1, waiting for transfers between devices, shards(): table = lax.all_to_all(sums, 'loc', 0, 0, tiled=True)  6.4 us
    all_to_all x1, starting transfers between devices, shards(): table = lax.all_to_all(sums, 'loc', 0, 0, tiled=True)  4.35 us
    pallas_call x2, Pallas kernels, shards(): call(side_kernel, near_outs, [VMEM] * 5, turned_buf)  4.16 us
    pallas_call x1, Pallas kernels, shards(): call(functools.partial(front_kernel, levels), [((MSG_ROWS, rows), HALF),...  2.63 us
    ppermute x6, starting transfers between devices, sibling(): return lax.ppermute(value, 'loc', beside)  2.46 us
    pallas_call x1, Pallas kernels, shards(): call(own_kernel, near_outs, [VMEM] * 3, turned_buf)(numbers, msg, target)  2.01 us
    pallas_call x1, Pallas kernels, shards(): call(functools.partial(far_kernel, half, far_scale), couplings + [((1, ro...  1.52 us
  transfers between devices with their start and end apart: 13, of which 5 were waited for; matrix products, arithmetic and copies ran while one was open for 0% of the time, Pallas kernels for 19%

profile of v9, /device:TPU:0, one launch (start us, length us, event | category | flops | bytes accessed | tf_op | source)
XLA Modules:
  0.0 46.4 jit_solution(5837396451134516129)
XLA Ops:
  1.9 0.9 %convert_add_fusion.refs_2_.refs_8_.given = f32[32,1024]{1,0:T(8,128)S(1)} fusion(s32[4,256]{1,0:T(4,128)} %param.9, f32[3,1024]{1,0:T(4,128)} %param.7, f32[16,1024]{1,0:T(8,128)} %param.8), kind=kLoop, calls=%fused_computation | loop fusion | flops 98304 | bytes 212992 | tf_op jit(solution)/shard_map/add | solution.py:409
  2.8 2.6 %shard_map.102 = (bf16[64,1024]{1,0:T(8,128)(2,1)S(1)}, bf16[32,1024]{1,0:T(8,128)(2,1)S(1)}, bf16[1024,1024]{1,0:T(8,128)(2,1)S(1)}, bf16[4,32,256]{2,1,0:T(8,1...) custom-call(f32[1]{0:T(128)S(6)} %copy.12.refs_0_, ...), custom_call_target="tpu_custom_call" | custom-call | flops 2000000000 | bytes 65536 | tf_op jit(solution)/shard_map/pallas_call | solution.py:410
  5.4 0.5 %collective-permute-start.1 = (bf16[64,2048]{1,0:T(8,128)(2,1)S(1)}, bf16[64,2048]{1,0:T(8,128)(2,1)S(1)}, u32[]{:S(2)}, u32[]{:S(2)}) collective-permute-start(bf16[64,2048]{1,0:T(8,128)(2,1)S(1)} %get-tuple-element.53), channel_id=1, source_target_pairs={{0,1},{1,0},{2,3},{3,2},{4,5},{5,4},{6,7},{7,6},{8,9},{9,8},{10,11... | collective-permute-start | bytes 786440 | tf_op jit(solution)/shard_map/ppermute | solution.py:404
  6.0 0.7 %collective-permute-start = (bf16[64,1024]{1,0:T(8,128)(2,1)S(1)}, bf16[64,1024]{1,0:T(8,128)(2,1)S(1)}, u32[]{:S(2)}, u32[]{:S(2)}) collective-permute-start(bf16[64,1024]{1,0:T(8,128)(2,1)S(1)} %get-tuple-element.57.msg), channel_id=1, source_target_pairs={{1,2},{3,4},{5,6},{7,8},{9,10},{11,12},{13,14},{15,16},{17,18},{19... | collective-permute-start | bytes 393224 | tf_op jit(solution)/shard_map/ppermute | solution.py:429
  6.6 0.5 %collective-permute-done.1.got.msg = bf16[64,2048]{1,0:T(8,128)(2,1)S(1)} collective-permute-done((bf16[64,2048]{1,0:T(8,128)(2,1)S(1)}, bf16[64,2048]{1,0:T(8,128)(2,1)S(1)}, u32[]{:S(2)}, u32[]{:S(2)}) %collective-permute-start.1) | collective-permute-done | bytes 262176 | tf_op jit(solution)/shard_map/ppermute | solution.py:404
  7.2 3.3 %collective-permute-start.2 = (bf16[2,96,256]{2,1,0:T(8,128)(2,1)S(1)}, bf16[2,96,256]{2,1,0:T(8,128)(2,1)S(1)}, u32[]{:S(2)}, u32[]{:S(2)}) collective-permute-start(bf16[2,96,256]{2,1,0:T(8,128)(2,1)S(1)} %get-tuple-element.63), channel_id=1, source_target_pairs={{0,2},{1,5},{2,0},{3,7},{4,6},{5,1},{6,4},{7,3},{8,10},{9,13},{10,... | collective-permute-start | bytes 294920 | tf_op jit(solution)/shard_map/ppermute | solution.py:401
  10.5 2.6 %collective-permute-start.3 = (bf16[2,96,256]{2,1,0:T(8,128)(2,1)S(1)}, bf16[2,96,256]{2,1,0:T(8,128)(2,1)S(1)}, u32[]{:S(2)}, u32[]{:S(2)}) collective-permute-start(bf16[2,96,256]{2,1,0:T(8,128)(2,1)S(1)} %get-tuple-element.64), channel_id=1, source_target_pairs={{0,8},{1,17},{2,10},{3,19},{4,12},{5,21},{6,14},{7,23},{8,0},{9,25... | collective-permute-start | bytes 294920 | tf_op jit(solution)/shard_map/ppermute | solution.py:401
  13.1 2.0 %shard_map.104 = (bf16[1024,1024]{1,0:T(8,128)(2,1)S(1)}, f32[32,1024]{1,0:T(8,128)S(1)}, f32[16,1024]{1,0:T(8,128)S(1)}) custom-call(f32[8,128]{1,0:T(8,128)S(1)} %get-tuple-element.50.numbers.refs_0_, bf16[64,1024]{1,0:T(8,128)(2,1)S(1)} %get-tuple-element.57.msg, bf16[32,1024]{1,0:T(8,128)(2,1)S(1)} %get-tuple-element.52.target), custom_call_target="tpu_custom_call" | custom-call | flops 2000000000 | bytes 65536 | tf_op jit(solution)/shard_map/pallas_call | solution.py:434
  15.1 2.1 %shard_map.105 = (bf16[1024,1024]{1,0:T(8,128)(2,1)S(1)}, f32[32,1024]{1,0:T(8,128)S(1)}, f32[16,1024]{1,0:T(8,128)S(1)}) custom-call(f32[8,128]{1,0:T(8,128)S(1)} %get-tuple-element.50.numbers.refs_0_, bf16[64,2048]{1,0:T(8,128)(2,1)S(1)} %collective-permute-done.1.got.msg, bf16[32,1024]{1,0:T(8,128)(2,1)S(1)} %get-tuple-element.52.target, ...), custom_call_target="tpu_custom_call" | custom-call | flops 2000000000 | bytes 65536 | tf_op jit(solution)/shard_map/pallas_call | solution.py:436
  17.2 2.1 %shard_map.106 = (bf16[1024,1024]{1,0:T(8,128)(2,1)S(1)}, f32[32,1024]{1,0:T(8,128)S(1)}, f32[16,1024]{1,0:T(8,128)S(1)}) custom-call(f32[8,128]{1,0:T(8,128)S(1)} %get-tuple-element.50.numbers.refs_0_, bf16[64,1024]{1,0:T(8,128)(2,1)S(1)} %collective-permute-done.msg, bf16[32,1024]{1,0:T(8,128)(2,1)S(1)} %get-tuple-element.52.target, ...), custom_call_target="tpu_custom_call" | custom-call | flops 2000000000 | bytes 65536 | tf_op jit(solution)/shard_map/pallas_call | solution.py:437
  19.3 1.1 %collective-permute-start.4 = (bf16[2,96,256]{2,1,0:T(8,128)(2,1)S(1)}, bf16[2,96,256]{2,1,0:T(8,128)(2,1)S(1)}, u32[]{:S(2)}, u32[]{:S(2)}) collective-permute-start(bf16[2,96,256]{2,1,0:T(8,128)(2,1)S(1)} %collective-permute-done.2.refs_4_), channel_id=1, source_target_pairs={{0,1},{1,0},{2,3},{3,2},{4,5},{5,4},{6,7},{7,6},{8,9},{9,8},{10,11... | collective-permute-start | bytes 294920 | tf_op jit(solution)/shard_map/ppermute | solution.py:404
  20.5 0.9 %shard_map.107 = (f32[32,1024]{1,0:T(8,128)S(1)}, bf16[2,256,256]{2,1,0:T(8,128)(2,1)S(1)}, bf16[2,256,256]{2,1,0:T(8,128)(2,1)S(1)}) custom-call(f32[8,128]{1,0:T(8,128)S(1)} %get-tuple-element.50.numbers.refs_0_, f32[32,1024]{1,0:T(8,128)S(1)} %get-tuple-element.65.refs_1_, bf16[1024,1024]{1,0:T(8,128)(2,1)S(1)} %get-tuple-element.66.refs_2_.refs_3_.refs_1_, ...), custom_call_target="tpu_custom_call" | custom-call | flops 1000000000 | bytes 65536 | tf_op jit(solution)/shard_map/pallas_call | solution.py:441
  21.8 1.5 %shard_map.108 = (bf16[2,256,256]{2,1,0:T(8,128)(2,1)S(1)}, bf16[2,256,256]{2,1,0:T(8,128)(2,1)S(1)}, f32[1,1024]{1,0:T(1,128)S(1)}, f32[16,1024]{1,0:T(8,128)S(...) custom-call(f32[8,128]{1,0:T(8,128)S(1)} %get-tuple-element.50.numbers.refs_0_, ...), custom_call_target="tpu_custom_call" | custom-call | flops 2000000000 | bytes 65536 | tf_op jit(solution)/shard_map/pallas_call | solution.py:444
  23.5 0.7 %collective-permute-start.7 = (bf16[32,1024]{1,0:T(8,128)(2,1)S(1)}, bf16[32,1024]{1,0:T(8,128)(2,1)S(1)}, u32[]{:S(2)}, u32[]{:S(2)}) collective-permute-start(bf16[32,1024]{1,0:T(8,128)(2,1)S(1)} %get-tuple-element.71.wmsg), channel_id=1, source_target_pairs={{1,2},{3,4},{5,6},{7,8},{9,10},{11,12},{13,14},{15,16},{17,18},{19... | collective-permute-start | bytes 196616 | tf_op jit(solution)/shard_map/ppermute | solution.py:457
  24.6 2.8 %collective-permute-start.8 = (bf16[2,32,256]{2,1,0:T(8,128)(2,1)S(1)}, bf16[2,32,256]{2,1,0:T(8,128)(2,1)S(1)}, u32[]{:S(2)}, u32[]{:S(2)}) collective-permute-start(bf16[2,32,256]{2,1,0:T(8,128)(2,1)S(1)} %get-tuple-element.84), channel_id=1, source_target_pairs={{0,2},{1,5},{2,0},{3,7},{4,6},{5,1},{6,4},{7,3},{8,10},{9,13},{10,... | collective-permute-start | bytes 98312 | tf_op jit(solution)/shard_map/ppermute | solution.py:401
  27.5 1.6 %collective-permute-start.9 = (bf16[2,32,256]{2,1,0:T(8,128)(2,1)S(1)}, bf16[2,32,256]{2,1,0:T(8,128)(2,1)S(1)}, u32[]{:S(2)}, u32[]{:S(2)}) collective-permute-start(bf16[2,32,256]{2,1,0:T(8,128)(2,1)S(1)} %get-tuple-element.85), channel_id=1, source_target_pairs={{0,8},{1,17},{2,10},{3,19},{4,12},{5,21},{6,14},{7,23},{8,0},{9,25... | collective-permute-start | bytes 98312 | tf_op jit(solution)/shard_map/ppermute | solution.py:401
  30.3 0.5 %collective-permute-start.10 = (bf16[2,32,256]{2,1,0:T(8,128)(2,1)S(1)}, bf16[2,32,256]{2,1,0:T(8,128)(2,1)S(1)}, u32[]{:S(2)}, u32[]{:S(2)}) collective-permute-start(bf16[2,32,256]{2,1,0:T(8,128)(2,1)S(1)} %collective-permute-done.8.refs_10_), channel_id=1, source_target_pairs={{0,1},{1,0},{2,3},{3,2},{4,5},{5,4},{6,7},{7,6},{8,9},{9,8},{10,11... | collective-permute-start | bytes 98312 | tf_op jit(solution)/shard_map/ppermute | solution.py:404
  30.8 0.7 %collective-permute-done.9.refs_11_ = bf16[2,32,256]{2,1,0:T(8,128)(2,1)S(1)} collective-permute-done((bf16[2,32,256]{2,1,0:T(8,128)(2,1)S(1)}, bf16[2,32,256]{2,1,0:T(8,128)(2,1)S(1)}, u32[]{:S(2)}, u32[]{:S(2)}) %collective-permute-start.9) | collective-permute-done | bytes 32800 | tf_op jit(solution)/shard_map/ppermute | solution.py:401
  31.5 1.2 %shard_map.109.refs_0_ = f32[32,1024]{1,0:T(8,128)S(1)} custom-call(bf16[32,1024]{1,0:T(8,128)(2,1)S(1)} %get-tuple-element.71.wmsg, bf16[32,1536]{1,0:T(8,128)(2,1)S(1)} %collective-permute-done.6.wmsg_a.got, bf16[32,1024]{1,0:T(8,128)(2,1)S(1)} %collective-permute-done.7.wmsg_b, bf16[1024,1024]{1,0:T(8,128)(2,1)S(1)} %get-tuple-element.73.kept, ...), custom_call_target="tpu_custom_call" | custom-call | flops 1200000000 | bytes 65536 | tf_op jit(solution)/shard_map/pallas_call | solution.py:460
  32.8 1.4 %shard_map.111 = (f32[32,128]{1,0:T(8,128)}, f32[16,1024]{1,0:T(8,128)S(1)}, f32[16,1024]{1,0:T(8,128)S(1)}, f32[16,128]{1,0:T(8,128)S(1)}) custom-call(f32[32,1024]{1,0:T(8,128)S(1)} %shard_map.109.refs_0_, bf16[1024,1024]{1,0:T(8,128)(2,1)S(1)} %get-tuple-element.66.refs_2_.refs_3_.refs_1_, bf16[2,256,256]{2,1,0:T(8,128)(2,1)S(1)} %get-tuple-element.76.refs_2_, ...), custom_call_target="tpu_custom_call" | custom-call | flops 2000000000 | bytes 65536 | tf_op jit(solution)/shard_map/pallas_call | solution.py:462
  34.1 4.4 %all-to-all-start = ((f32[32,1,128]{2,1,0:T(1,128)}), f32[32,1,128]{2,1,0:T(1,128)S(1)}, u32[]{:S(2)}, u32[]{:S(2)}) async-start(f32[32,1,128]{2,1,0:T(1,128)} %bitcast.1), calls=%async_computation | async-start | bytes 32768 | tf_op jit(solution)/shard_map/all_to_all | solution.py:468
  38.5 0.7 %shard_map.113 = f32[16,1024]{1,0:T(8,128)} custom-call(f32[1]{0:T(128)S(6)} %copy.14.signal, f32[8,128]{1,0:T(8,128)S(1)} %get-tuple-element.50.numbers.refs_0_, f32[16,1024]{1,0:T(8,128)S(1)} %get-tuple-element.82.refs_9_.source), custom_call_target="tpu_custom_call" | custom-call | flops 2000000000 | bytes 65536 | tf_op jit(solution)/shard_map/pallas_call | solution.py:469
  39.1 6.4 %all-to-all-done = f32[32,1,128]{2,1,0:T(1,128)S(1)} async-done(((f32[32,1,128]{2,1,0:T(1,128)}), f32[32,1,128]{2,1,0:T(1,128)S(1)}, u32[]{:S(2)}, u32[]{:S(2)}) %all-to-all-start) | async-done | bytes 16416 | tf_op jit(solution)/shard_map/all_to_all | solution.py:468
  45.5 0.9 %shard_map.112 = (f32[16,1024]{1,0:T(8,128)}, f32[16,1024]{1,0:T(8,128)}, f32[1,16]{1,0:T(1,128)}) custom-call(f32[1]{0:T(128)S(6)} %copy.14.signal, f32[1]{0:T(128)S(6)} %copy.15.noise, f32[8,128]{1,0:T(8,128)S(1)} %get-tuple-element.50.numbers.refs_0_, f32[32,128]{1,0:T(8,128)S(1)} %bitcast.5, f32[16,128]{1,0:T(8,128)S(1)} %get-tuple-element.90.shift_in, ...), custom_call_target="tpu_custom_call" | custom-call | flops 2000000000 | bytes 65536 | tf_op jit(solution)/shard_map/pallas_call | solution.py:470
  (15 shorter events, 1.1 us)
Async XLA Ops:
  5.4 1.7 %collective-permute-start.1 = (bf16[64,2048]{1,0:T(8,128)(2,1)S(1)}, bf16[64,2048]{1,0:T(8,128)(2,1)S(1)}, u32[]{:S(2)}, u32[]{:S(2)}) collective-permute-start(bf16[64,2048]{1,0:T(8,128)(2,1)S(1)} %get-tuple-element.53), channel_id=1, source_target_pairs={{0,1},{1,0},{2,3},{3,2},{4,5},{5,4},{6,7},{7,6},{8,9},{9,8},{10,11... | collective-permute-start | bytes 786440 | tf_op jit(solution)/shard_map/ppermute | solution.py:404
  6.0 11.3 %collective-permute-start = (bf16[64,1024]{1,0:T(8,128)(2,1)S(1)}, bf16[64,1024]{1,0:T(8,128)(2,1)S(1)}, u32[]{:S(2)}, u32[]{:S(2)}) collective-permute-start(bf16[64,1024]{1,0:T(8,128)(2,1)S(1)} %get-tuple-element.57.msg), channel_id=1, source_target_pairs={{1,2},{3,4},{5,6},{7,8},{9,10},{11,12},{13,14},{15,16},{17,18},{19... | collective-permute-start | bytes 393224 | tf_op jit(solution)/shard_map/ppermute | solution.py:429
  7.2 12.1 %collective-permute-start.2 = (bf16[2,96,256]{2,1,0:T(8,128)(2,1)S(1)}, bf16[2,96,256]{2,1,0:T(8,128)(2,1)S(1)}, u32[]{:S(2)}, u32[]{:S(2)}) collective-permute-start(bf16[2,96,256]{2,1,0:T(8,128)(2,1)S(1)} %get-tuple-element.63), channel_id=1, source_target_pairs={{0,2},{1,5},{2,0},{3,7},{4,6},{5,1},{6,4},{7,3},{8,10},{9,13},{10,... | collective-permute-start | bytes 294920 | tf_op jit(solution)/shard_map/ppermute | solution.py:401
  10.5 8.8 %collective-permute-start.3 = (bf16[2,96,256]{2,1,0:T(8,128)(2,1)S(1)}, bf16[2,96,256]{2,1,0:T(8,128)(2,1)S(1)}, u32[]{:S(2)}, u32[]{:S(2)}) collective-permute-start(bf16[2,96,256]{2,1,0:T(8,128)(2,1)S(1)} %get-tuple-element.64), channel_id=1, source_target_pairs={{0,8},{1,17},{2,10},{3,19},{4,12},{5,21},{6,14},{7,23},{8,0},{9,25... | collective-permute-start | bytes 294920 | tf_op jit(solution)/shard_map/ppermute | solution.py:401
  19.3 2.2 %collective-permute-start.4 = (bf16[2,96,256]{2,1,0:T(8,128)(2,1)S(1)}, bf16[2,96,256]{2,1,0:T(8,128)(2,1)S(1)}, u32[]{:S(2)}, u32[]{:S(2)}) collective-permute-start(bf16[2,96,256]{2,1,0:T(8,128)(2,1)S(1)} %collective-permute-done.2.refs_4_), channel_id=1, source_target_pairs={{0,1},{1,0},{2,3},{3,2},{4,5},{5,4},{6,7},{7,6},{8,9},{9,8},{10,11... | collective-permute-start | bytes 294920 | tf_op jit(solution)/shard_map/ppermute | solution.py:404
  20.5 1.3 %collective-permute-start.5 = (bf16[2,96,256]{2,1,0:T(8,128)(2,1)S(1)}, bf16[2,96,256]{2,1,0:T(8,128)(2,1)S(1)}, u32[]{:S(2)}, u32[]{:S(2)}) collective-permute-start(bf16[2,96,256]{2,1,0:T(8,128)(2,1)S(1)} %collective-permute-done.3.refs_5_), channel_id=1, source_target_pairs={{0,1},{1,0},{2,3},{3,2},{4,5},{5,4},{6,7},{7,6},{8,9},{9,8},{10,11... | collective-permute-start | bytes 294920 | tf_op jit(solution)/shard_map/ppermute | solution.py:404
  23.3 1.3 %collective-permute-start.6 = (bf16[32,1536]{1,0:T(8,128)(2,1)S(1)}, bf16[32,1536]{1,0:T(8,128)(2,1)S(1)}, u32[]{:S(2)}, u32[]{:S(2)}) collective-permute-start(bf16[32,1536]{1,0:T(8,128)(2,1)S(1)} %get-tuple-element.72), channel_id=1, source_target_pairs={{0,1},{1,0},{2,3},{3,2},{4,5},{5,4},{6,7},{7,6},{8,9},{9,8},{10,11... | collective-permute-start | bytes 294920 | tf_op jit(solution)/shard_map/ppermute | solution.py:404
  23.5 8.0 %collective-permute-start.7 = (bf16[32,1024]{1,0:T(8,128)(2,1)S(1)}, bf16[32,1024]{1,0:T(8,128)(2,1)S(1)}, u32[]{:S(2)}, u32[]{:S(2)}) collective-permute-start(bf16[32,1024]{1,0:T(8,128)(2,1)S(1)} %get-tuple-element.71.wmsg), channel_id=1, source_target_pairs={{1,2},{3,4},{5,6},{7,8},{9,10},{11,12},{13,14},{15,16},{17,18},{19... | collective-permute-start | bytes 196616 | tf_op jit(solution)/shard_map/ppermute | solution.py:457
  24.6 5.7 %collective-permute-start.8 = (bf16[2,32,256]{2,1,0:T(8,128)(2,1)S(1)}, bf16[2,32,256]{2,1,0:T(8,128)(2,1)S(1)}, u32[]{:S(2)}, u32[]{:S(2)}) collective-permute-start(bf16[2,32,256]{2,1,0:T(8,128)(2,1)S(1)} %get-tuple-element.84), channel_id=1, source_target_pairs={{0,2},{1,5},{2,0},{3,7},{4,6},{5,1},{6,4},{7,3},{8,10},{9,13},{10,... | collective-permute-start | bytes 98312 | tf_op jit(solution)/shard_map/ppermute | solution.py:401
  27.5 4.1 %collective-permute-start.9 = (bf16[2,32,256]{2,1,0:T(8,128)(2,1)S(1)}, bf16[2,32,256]{2,1,0:T(8,128)(2,1)S(1)}, u32[]{:S(2)}, u32[]{:S(2)}) collective-permute-start(bf16[2,32,256]{2,1,0:T(8,128)(2,1)S(1)} %get-tuple-element.85), channel_id=1, source_target_pairs={{0,8},{1,17},{2,10},{3,19},{4,12},{5,21},{6,14},{7,23},{8,0},{9,25... | collective-permute-start | bytes 98312 | tf_op jit(solution)/shard_map/ppermute | solution.py:401
  30.3 2.4 %collective-permute-start.10 = (bf16[2,32,256]{2,1,0:T(8,128)(2,1)S(1)}, bf16[2,32,256]{2,1,0:T(8,128)(2,1)S(1)}, u32[]{:S(2)}, u32[]{:S(2)}) collective-permute-start(bf16[2,32,256]{2,1,0:T(8,128)(2,1)S(1)} %collective-permute-done.8.refs_10_), channel_id=1, source_target_pairs={{0,1},{1,0},{2,3},{3,2},{4,5},{5,4},{6,7},{7,6},{8,9},{9,8},{10,11... | collective-permute-start | bytes 98312 | tf_op jit(solution)/shard_map/ppermute | solution.py:404
  31.5 1.2 %collective-permute-start.11 = (bf16[2,32,256]{2,1,0:T(8,128)(2,1)S(1)}, bf16[2,32,256]{2,1,0:T(8,128)(2,1)S(1)}, u32[]{:S(2)}, u32[]{:S(2)}) collective-permute-start(bf16[2,32,256]{2,1,0:T(8,128)(2,1)S(1)} %collective-permute-done.9.refs_11_), channel_id=1, source_target_pairs={{0,1},{1,0},{2,3},{3,2},{4,5},{5,4},{6,7},{7,6},{8,9},{9,8},{10,11... | collective-permute-start | bytes 98312 | tf_op jit(solution)/shard_map/ppermute | solution.py:404
  34.1 11.4 %all-to-all-start = ((f32[32,1,128]{2,1,0:T(1,128)}), f32[32,1,128]{2,1,0:T(1,128)S(1)}, u32[]{:S(2)}, u32[]{:S(2)}) async-start(f32[32,1,128]{2,1,0:T(1,128)} %bitcast.1), calls=%async_computation | async-start | bytes 32768 | tf_op jit(solution)/shard_map/all_to_all | solution.py:468

commit v10 on v9

--- a/solution.py
+++ b/solution.py
@@ -202,17 +202,16 @@
         slopes[:, span] = slopes_in[:, span] + slope
 
 
-def far_part(lev, start, numbers, skel_target, basis, coup_high, coup_low):
+def far_part(lev, start, numbers, skel_target, basis, coup_high):
     rank = skel_target.shape[2]
     rates = [jnp.concatenate([numbers[row : row + 1, :]] * (rank // 128), axis=1) for row in (1, 3)]
     mixed = []
     for slot, value in enumerate(lev):
         squared = dot(turned(value[64:96]), skel_target[start + slot])
-        high, low = split_two(matern(squared, rates)[0])
+        high = matern(squared, rates)[0].astype(HALF)
         coup_high[slot] = high
-        coup_low[slot] = low
         both = dot(value[0:64], high)
-        part = both[0:32] + both[32:64] + dot(value[0:32], low)
+        part = both[0:32] + both[32:64]
         mixed.append(jnp.concatenate(split_two(part), axis=0))
     far = dot(jnp.concatenate(mixed, axis=1), basis[start * rank : (start + len(lev)) * rank, :])
     return far[0:32] + far[32:64]
@@ -221,16 +220,16 @@
 def carried_kernel(half, far_scale, *refs):
     numbers, image_in, basis, skel_target = refs[:4]
     lev = own_part(refs[4 : 4 + half])
-    image, coup_high, coup_low = refs[4 + half :]
-    image[...] = image_in[...] + far_scale * far_part(lev, 0, numbers, skel_target, basis, coup_high, coup_low)
+    image, coup_high = refs[4 + half :]
+    image[...] = image_in[...] + far_scale * far_part(lev, 0, numbers, skel_target, basis, coup_high)
 
 
 def far_kernel(half, far_scale, *refs):
     numbers, image, given, basis, skel_target = refs[:5]
     lev = own_part(refs[5 : 5 + half])
-    coup_high, coup_low, row_sum, first, wmsg, keep, beside = refs[5 + half :]
+    coup_high, row_sum, first, wmsg, keep, beside = refs[5 + half :]
     rank = skel_target.shape[2]
-    total = image[...] + far_scale * far_part(lev, half, numbers, skel_target, basis, coup_high, coup_low)
+    total = image[...] + far_scale * far_part(lev, half, numbers, skel_target, basis, coup_high)
     sums = total[16:17, :]
     row_sum[...] = sums
     value = SCALE * (total[0:16] + sums * given[0:16, :])
@@ -267,15 +266,14 @@
 
 
 def second_kernel(half, far_scale, *refs):
-    near, basis, own_high, own_low, other_high, other_low, row_sum, first, given, slope_sum = refs[:10]
-    wlev = own_part(refs[10 : 10 + 2 * half])
-    sums, first_rest, second_rest, shift_out = refs[10 + 2 * half :]
+    near, basis, own_high, other_high, row_sum, first, given, slope_sum = refs[:8]
+    wlev = own_part(refs[8 : 8 + 2 * half])
+    sums, first_rest, second_rest, shift_out = refs[8 + 2 * half :]
     coup_high = [own_high[slot] for slot in range(half)] + [other_high[slot] for slot in range(half)]
-    coup_low = [own_low[slot] for slot in range(half)] + [other_low[slot] for slot in range(half)]
     pieces = []
-    for coef, high, low in zip(wlev, coup_high, coup_low):
+    for coef, high in zip(wlev, coup_high):
         mixed = dot(coef, high)
-        mixed = mixed[0:16] + mixed[16:32] + dot(coef[0:16], low)
+        mixed = mixed[0:16] + mixed[16:32]
         pieces.append(jnp.concatenate(split_two(mixed), axis=0))
     both = near[...] + far_scale * dot(jnp.concatenate(pieces, axis=1), basis[...])
     base = given[0:16, :]
@@ -437,11 +435,11 @@
     kept_b, image, slopes = call(side_kernel, near_outs, [VMEM] * 5, turned_buf)(numbers, msg_b, target, image, slopes)
     image, cross = lax.optimization_barrier((image, cross))
     other = [sibling(value) for value in cross]
-    couplings = [((half, rank, rank), HALF)] * 2
-    image, own_high, own_low = call(
+    couplings = [((half, rank, rank), HALF)]
+    image, own_high = call(
         functools.partial(carried_kernel, half, far_scale), [((32, rows), FULL)] + couplings, [VMEM] * (4 + half), micros=1.0
     )(numbers, image, basis, skel_target, *cross)
-    other_high, other_low, row_sum, first, wmsg, keep, beside_msg = call(
+    other_high, row_sum, first, wmsg, keep, beside_msg = call(
         functools.partial(far_kernel, half, far_scale),
         couplings
         + [
@@ -462,8 +460,8 @@
     sums, first_rest, second_rest, shift = call(
         functools.partial(second_kernel, half, far_scale),
         [((count, 128), FULL), ((probes, rows), FULL), ((probes, rows), FULL), ((probes, 128), FULL)],
-        [VMEM] * (10 + levels),
-    )(near, basis, own_high, own_low, other_high, other_low, row_sum, first, given, slopes, *cross, *other)
+        [VMEM] * (8 + levels),
+    )(near, basis, own_high, other_high, row_sum, first, given, slopes, *cross, *other)
     sums, signal, noise_var = lax.optimization_barrier((sums, signal, noise_var))
     table = lax.all_to_all(sums, "loc", 0, 0, tiled=True)
     (slope_image,) = call(slope_kernel, [((probes, rows), FULL)], [SMEM, VMEM, VMEM])(signal, numbers, slopes)

time: 46.7 us -> 46.5 us (level)
  no operation moved by 1% of the time
where the time goes in v10:
time: 46.5 us; the launch traced here: 46.3 us
  starting transfers between devices  18.4 us (40%)
  Pallas kernels  15.2 us (33%)
  waiting for transfers between devices  8.45 us (18%)
  between operations  3.36 us (7%)
  other arithmetic  0.88 us (2%)
    ppermute x4, starting transfers between devices, partner(): return lax.ppermute(value, 'loc', pairs)  10.3 us
    all_to_all x1, waiting for transfers between devices, shards(): table = lax.all_to_all(sums, 'loc', 0, 0, tiled=True)  6.4 us
    all_to_all x1, starting transfers between devices, shards(): table = lax.all_to_all(sums, 'loc', 0, 0, tiled=True)  4.35 us
    pallas_call x2, Pallas kernels, shards(): call(side_kernel, near_outs, [VMEM] * 5, turned_buf)  4.16 us
    pallas_call x1, Pallas kernels, shards(): call(functools.partial(front_kernel, levels), [((MSG_ROWS, rows), HALF),...  2.63 us
    ppermute x6, starting transfers between devices, sibling(): return lax.ppermute(value, 'loc', beside)  2.41 us
    pallas_call x1, Pallas kernels, shards(): call(own_kernel, near_outs, [VMEM] * 3, turned_buf)(numbers, msg, target)  2.01 us
    pallas_call x1, Pallas kernels, shards(): call(functools.partial(far_kernel, half, far_scale), couplings + [((1, ro...  1.45 us
  transfers between devices with their start and end apart: 13, of which 5 were waited for; matrix products, arithmetic and copies ran while one was open for 0% of the time, Pallas kernels for 19%

profile of v10, /device:TPU:0, one launch (start us, length us, event | category | flops | bytes accessed | tf_op | source)
XLA Modules:
  0.0 46.3 jit_solution(1798659298845564982)
XLA Ops:
  1.9 0.9 %convert_add_fusion.refs_2_.refs_6_.given = f32[32,1024]{1,0:T(8,128)S(1)} fusion(s32[4,256]{1,0:T(4,128)} %param.9, f32[3,1024]{1,0:T(4,128)} %param.7, f32[16,1024]{1,0:T(8,128)} %param.8), kind=kLoop, calls=%fused_computation | loop fusion | flops 98304 | bytes 212992 | tf_op jit(solution)/shard_map/add | solution.py:407
  2.8 2.6 %shard_map.102 = (bf16[64,1024]{1,0:T(8,128)(2,1)S(1)}, bf16[32,1024]{1,0:T(8,128)(2,1)S(1)}, bf16[1024,1024]{1,0:T(8,128)(2,1)S(1)}, bf16[4,32,256]{2,1,0:T(8,1...) custom-call(f32[1]{0:T(128)S(6)} %copy.12.refs_0_, ...), custom_call_target="tpu_custom_call" | custom-call | flops 2000000000 | bytes 65536 | tf_op jit(solution)/shard_map/pallas_call | solution.py:408
  5.4 0.5 %collective-permute-start.1 = (bf16[64,2048]{1,0:T(8,128)(2,1)S(1)}, bf16[64,2048]{1,0:T(8,128)(2,1)S(1)}, u32[]{:S(2)}, u32[]{:S(2)}) collective-permute-start(bf16[64,2048]{1,0:T(8,128)(2,1)S(1)} %get-tuple-element.51), channel_id=1, source_target_pairs={{0,1},{1,0},{2,3},{3,2},{4,5},{5,4},{6,7},{7,6},{8,9},{9,8},{10,11... | collective-permute-start | bytes 786440 | tf_op jit(solution)/shard_map/ppermute | solution.py:402
  6.0 0.7 %collective-permute-start = (bf16[64,1024]{1,0:T(8,128)(2,1)S(1)}, bf16[64,1024]{1,0:T(8,128)(2,1)S(1)}, u32[]{:S(2)}, u32[]{:S(2)}) collective-permute-start(bf16[64,1024]{1,0:T(8,128)(2,1)S(1)} %get-tuple-element.55.msg), channel_id=1, source_target_pairs={{1,2},{3,4},{5,6},{7,8},{9,10},{11,12},{13,14},{15,16},{17,18},{19... | collective-permute-start | bytes 393224 | tf_op jit(solution)/shard_map/ppermute | solution.py:427
  6.6 0.5 %collective-permute-done.1.got.msg = bf16[64,2048]{1,0:T(8,128)(2,1)S(1)} collective-permute-done((bf16[64,2048]{1,0:T(8,128)(2,1)S(1)}, bf16[64,2048]{1,0:T(8,128)(2,1)S(1)}, u32[]{:S(2)}, u32[]{:S(2)}) %collective-permute-start.1) | collective-permute-done | bytes 262176 | tf_op jit(solution)/shard_map/ppermute | solution.py:402
  7.2 3.3 %collective-permute-start.2 = (bf16[2,96,256]{2,1,0:T(8,128)(2,1)S(1)}, bf16[2,96,256]{2,1,0:T(8,128)(2,1)S(1)}, u32[]{:S(2)}, u32[]{:S(2)}) collective-permute-start(bf16[2,96,256]{2,1,0:T(8,128)(2,1)S(1)} %get-tuple-element.61), channel_id=1, source_target_pairs={{0,2},{1,5},{2,0},{3,7},{4,6},{5,1},{6,4},{7,3},{8,10},{9,13},{10,... | collective-permute-start | bytes 294920 | tf_op jit(solution)/shard_map/ppermute | solution.py:399
  10.5 2.6 %collective-permute-start.3 = (bf16[2,96,256]{2,1,0:T(8,128)(2,1)S(1)}, bf16[2,96,256]{2,1,0:T(8,128)(2,1)S(1)}, u32[]{:S(2)}, u32[]{:S(2)}) collective-permute-start(bf16[2,96,256]{2,1,0:T(8,128)(2,1)S(1)} %get-tuple-element.62), channel_id=1, source_target_pairs={{0,8},{1,17},{2,10},{3,19},{4,12},{5,21},{6,14},{7,23},{8,0},{9,25... | collective-permute-start | bytes 294920 | tf_op jit(solution)/shard_map/ppermute | solution.py:399
  13.1 2.0 %shard_map.104 = (bf16[1024,1024]{1,0:T(8,128)(2,1)S(1)}, f32[32,1024]{1,0:T(8,128)S(1)}, f32[16,1024]{1,0:T(8,128)S(1)}) custom-call(f32[8,128]{1,0:T(8,128)S(1)} %get-tuple-element.48.numbers.refs_0_, bf16[64,1024]{1,0:T(8,128)(2,1)S(1)} %get-tuple-element.55.msg, bf16[32,1024]{1,0:T(8,128)(2,1)S(1)} %get-tuple-element.50.target), custom_call_target="tpu_custom_call" | custom-call | flops 2000000000 | bytes 65536 | tf_op jit(solution)/shard_map/pallas_call | solution.py:432
  15.1 2.1 %shard_map.105 = (bf16[1024,1024]{1,0:T(8,128)(2,1)S(1)}, f32[32,1024]{1,0:T(8,128)S(1)}, f32[16,1024]{1,0:T(8,128)S(1)}) custom-call(f32[8,128]{1,0:T(8,128)S(1)} %get-tuple-element.48.numbers.refs_0_, bf16[64,2048]{1,0:T(8,128)(2,1)S(1)} %collective-permute-done.1.got.msg, bf16[32,1024]{1,0:T(8,128)(2,1)S(1)} %get-tuple-element.50.target, ...), custom_call_target="tpu_custom_call" | custom-call | flops 2000000000 | bytes 65536 | tf_op jit(solution)/shard_map/pallas_call | solution.py:434
  17.2 2.1 %shard_map.106 = (bf16[1024,1024]{1,0:T(8,128)(2,1)S(1)}, f32[32,1024]{1,0:T(8,128)S(1)}, f32[16,1024]{1,0:T(8,128)S(1)}) custom-call(f32[8,128]{1,0:T(8,128)S(1)} %get-tuple-element.48.numbers.refs_0_, bf16[64,1024]{1,0:T(8,128)(2,1)S(1)} %collective-permute-done.msg, bf16[32,1024]{1,0:T(8,128)(2,1)S(1)} %get-tuple-element.50.target, ...), custom_call_target="tpu_custom_call" | custom-call | flops 2000000000 | bytes 65536 | tf_op jit(solution)/shard_map/pallas_call | solution.py:435
  19.3 1.1 %collective-permute-start.4 = (bf16[2,96,256]{2,1,0:T(8,128)(2,1)S(1)}, bf16[2,96,256]{2,1,0:T(8,128)(2,1)S(1)}, u32[]{:S(2)}, u32[]{:S(2)}) collective-permute-start(bf16[2,96,256]{2,1,0:T(8,128)(2,1)S(1)} %collective-permute-done.2.refs_4_), channel_id=1, source_target_pairs={{0,1},{1,0},{2,3},{3,2},{4,5},{5,4},{6,7},{7,6},{8,9},{9,8},{10,11... | collective-permute-start | bytes 294920 | tf_op jit(solution)/shard_map/ppermute | solution.py:402
  20.5 0.9 %shard_map.107 = (f32[32,1024]{1,0:T(8,128)S(1)}, bf16[2,256,256]{2,1,0:T(8,128)(2,1)S(1)}) custom-call(f32[8,128]{1,0:T(8,128)S(1)} %get-tuple-element.48.numbers.refs_0_, f32[32,1024]{1,0:T(8,128)S(1)} %get-tuple-element.63.refs_1_, bf16[1024,1024]{1,0:T(8,128)(2,1)S(1)} %get-tuple-element.64.refs_2_.refs_3_.refs_1_, ...), custom_call_target="tpu_custom_call" | custom-call | flops 1000000000 | bytes 65536 | tf_op jit(solution)/shard_map/pallas_call | solution.py:439
  21.8 1.4 %shard_map.108 = (bf16[2,256,256]{2,1,0:T(8,128)(2,1)S(1)}, f32[1,1024]{1,0:T(1,128)S(1)}, f32[16,1024]{1,0:T(8,128)S(1)}, bf16[32,1024]{1,0:T(8,128)(2,1)S(1)},...) custom-call(f32[8,128]{1,0:T(8,128)S(1)} %get-tuple-element.48.numbers.refs_0_, ...), custom_call_target="tpu_custom_call" | custom-call | flops 2000000000 | bytes 65536 | tf_op jit(solution)/shard_map/pallas_call | solution.py:442
  23.4 0.7 %collective-permute-start.7 = (bf16[32,1024]{1,0:T(8,128)(2,1)S(1)}, bf16[32,1024]{1,0:T(8,128)(2,1)S(1)}, u32[]{:S(2)}, u32[]{:S(2)}) collective-permute-start(bf16[32,1024]{1,0:T(8,128)(2,1)S(1)} %get-tuple-element.69.wmsg), channel_id=1, source_target_pairs={{1,2},{3,4},{5,6},{7,8},{9,10},{11,12},{13,14},{15,16},{17,18},{19... | collective-permute-start | bytes 196616 | tf_op jit(solution)/shard_map/ppermute | solution.py:455
  24.6 2.8 %collective-permute-start.8 = (bf16[2,32,256]{2,1,0:T(8,128)(2,1)S(1)}, bf16[2,32,256]{2,1,0:T(8,128)(2,1)S(1)}, u32[]{:S(2)}, u32[]{:S(2)}) collective-permute-start(bf16[2,32,256]{2,1,0:T(8,128)(2,1)S(1)} %get-tuple-element.80), channel_id=1, source_target_pairs={{0,2},{1,5},{2,0},{3,7},{4,6},{5,1},{6,4},{7,3},{8,10},{9,13},{10,... | collective-permute-start | bytes 98312 | tf_op jit(solution)/shard_map/ppermute | solution.py:399
  27.4 1.6 %collective-permute-start.9 = (bf16[2,32,256]{2,1,0:T(8,128)(2,1)S(1)}, bf16[2,32,256]{2,1,0:T(8,128)(2,1)S(1)}, u32[]{:S(2)}, u32[]{:S(2)}) collective-permute-start(bf16[2,32,256]{2,1,0:T(8,128)(2,1)S(1)} %get-tuple-element.81), channel_id=1, source_target_pairs={{0,8},{1,17},{2,10},{3,19},{4,12},{5,21},{6,14},{7,23},{8,0},{9,25... | collective-permute-start | bytes 98312 | tf_op jit(solution)/shard_map/ppermute | solution.py:399
  30.3 0.5 %collective-permute-start.10 = (bf16[2,32,256]{2,1,0:T(8,128)(2,1)S(1)}, bf16[2,32,256]{2,1,0:T(8,128)(2,1)S(1)}, u32[]{:S(2)}, u32[]{:S(2)}) collective-permute-start(bf16[2,32,256]{2,1,0:T(8,128)(2,1)S(1)} %collective-permute-done.8.refs_8_), channel_id=1, source_target_pairs={{0,1},{1,0},{2,3},{3,2},{4,5},{5,4},{6,7},{7,6},{8,9},{9,8},{10,11... | collective-permute-start | bytes 98312 | tf_op jit(solution)/shard_map/ppermute | solution.py:402
  30.8 0.7 %collective-permute-done.9.refs_9_ = bf16[2,32,256]{2,1,0:T(8,128)(2,1)S(1)} collective-permute-done((bf16[2,32,256]{2,1,0:T(8,128)(2,1)S(1)}, bf16[2,32,256]{2,1,0:T(8,128)(2,1)S(1)}, u32[]{:S(2)}, u32[]{:S(2)}) %collective-permute-start.9) | collective-permute-done | bytes 32800 | tf_op jit(solution)/shard_map/ppermute | solution.py:399
  31.4 1.2 %shard_map.109.refs_0_ = f32[32,1024]{1,0:T(8,128)S(1)} custom-call(bf16[32,1024]{1,0:T(8,128)(2,1)S(1)} %get-tuple-element.69.wmsg, bf16[32,1536]{1,0:T(8,128)(2,1)S(1)} %collective-permute-done.6.wmsg_a.got, bf16[32,1024]{1,0:T(8,128)(2,1)S(1)} %collective-permute-done.7.wmsg_b, bf16[1024,1024]{1,0:T(8,128)(2,1)S(1)} %get-tuple-element.71.kept, ...), custom_call_target="tpu_custom_call" | custom-call | flops 1200000000 | bytes 65536 | tf_op jit(solution)/shard_map/pallas_call | solution.py:458
  32.6 1.3 %shard_map.111 = (f32[32,128]{1,0:T(8,128)}, f32[16,1024]{1,0:T(8,128)S(1)}, f32[16,1024]{1,0:T(8,128)S(1)}, f32[16,128]{1,0:T(8,128)S(1)}) custom-call(f32[32,1024]{1,0:T(8,128)S(1)} %shard_map.109.refs_0_, bf16[1024,1024]{1,0:T(8,128)(2,1)S(1)} %get-tuple-element.64.refs_2_.refs_3_.refs_1_, bf16[2,256,256]{2,1,0:T(8,128)(2,1)S(1)} %get-tuple-element.74.refs_2_, ...), custom_call_target="tpu_custom_call" | custom-call | flops 2000000000 | bytes 65536 | tf_op jit(solution)/shard_map/pallas_call | solution.py:460
  34.0 4.4 %all-to-all-start = ((f32[32,1,128]{2,1,0:T(1,128)}), f32[32,1,128]{2,1,0:T(1,128)S(1)}, u32[]{:S(2)}, u32[]{:S(2)}) async-start(f32[32,1,128]{2,1,0:T(1,128)} %bitcast.1), calls=%async_computation | async-start | bytes 32768 | tf_op jit(solution)/shard_map/all_to_all | solution.py:466
  38.3 0.7 %shard_map.113 = f32[16,1024]{1,0:T(8,128)} custom-call(f32[1]{0:T(128)S(6)} %copy.14.signal, f32[8,128]{1,0:T(8,128)S(1)} %get-tuple-element.48.numbers.refs_0_, f32[16,1024]{1,0:T(8,128)S(1)} %get-tuple-element.78.refs_7_.source), custom_call_target="tpu_custom_call" | custom-call | flops 2000000000 | bytes 65536 | tf_op jit(solution)/shard_map/pallas_call | solution.py:467
  39.0 6.4 %all-to-all-done = f32[32,1,128]{2,1,0:T(1,128)S(1)} async-done(((f32[32,1,128]{2,1,0:T(1,128)}), f32[32,1,128]{2,1,0:T(1,128)S(1)}, u32[]{:S(2)}, u32[]{:S(2)}) %all-to-all-start) | async-done | bytes 16416 | tf_op jit(solution)/shard_map/all_to_all | solution.py:466
  45.4 0.9 %shard_map.112 = (f32[16,1024]{1,0:T(8,128)}, f32[16,1024]{1,0:T(8,128)}, f32[1,16]{1,0:T(1,128)}) custom-call(f32[1]{0:T(128)S(6)} %copy.14.signal, f32[1]{0:T(128)S(6)} %copy.15.noise, f32[8,128]{1,0:T(8,128)S(1)} %get-tuple-element.48.numbers.refs_0_, f32[32,128]{1,0:T(8,128)S(1)} %bitcast.5, f32[16,128]{1,0:T(8,128)S(1)} %get-tuple-element.86.shift_in, ...), custom_call_target="tpu_custom_call" | custom-call | flops 2000000000 | bytes 65536 | tf_op jit(solution)/shard_map/pallas_call | solution.py:468
  (15 shorter events, 1.2 us)
Async XLA Ops:
  5.4 1.7 %collective-permute-start.1 = (bf16[64,2048]{1,0:T(8,128)(2,1)S(1)}, bf16[64,2048]{1,0:T(8,128)(2,1)S(1)}, u32[]{:S(2)}, u32[]{:S(2)}) collective-permute-start(bf16[64,2048]{1,0:T(8,128)(2,1)S(1)} %get-tuple-element.51), channel_id=1, source_target_pairs={{0,1},{1,0},{2,3},{3,2},{4,5},{5,4},{6,7},{7,6},{8,9},{9,8},{10,11... | collective-permute-start | bytes 786440 | tf_op jit(solution)/shard_map/ppermute | solution.py:402
  6.0 11.3 %collective-permute-start = (bf16[64,1024]{1,0:T(8,128)(2,1)S(1)}, bf16[64,1024]{1,0:T(8,128)(2,1)S(1)}, u32[]{:S(2)}, u32[]{:S(2)}) collective-permute-start(bf16[64,1024]{1,0:T(8,128)(2,1)S(1)} %get-tuple-element.55.msg), channel_id=1, source_target_pairs={{1,2},{3,4},{5,6},{7,8},{9,10},{11,12},{13,14},{15,16},{17,18},{19... | collective-permute-start | bytes 393224 | tf_op jit(solution)/shard_map/ppermute | solution.py:427
  7.2 12.1 %collective-permute-start.2 = (bf16[2,96,256]{2,1,0:T(8,128)(2,1)S(1)}, bf16[2,96,256]{2,1,0:T(8,128)(2,1)S(1)}, u32[]{:S(2)}, u32[]{:S(2)}) collective-permute-start(bf16[2,96,256]{2,1,0:T(8,128)(2,1)S(1)} %get-tuple-element.61), channel_id=1, source_target_pairs={{0,2},{1,5},{2,0},{3,7},{4,6},{5,1},{6,4},{7,3},{8,10},{9,13},{10,... | collective-permute-start | bytes 294920 | tf_op jit(solution)/shard_map/ppermute | solution.py:399
  10.5 8.8 %collective-permute-start.3 = (bf16[2,96,256]{2,1,0:T(8,128)(2,1)S(1)}, bf16[2,96,256]{2,1,0:T(8,128)(2,1)S(1)}, u32[]{:S(2)}, u32[]{:S(2)}) collective-permute-start(bf16[2,96,256]{2,1,0:T(8,128)(2,1)S(1)} %get-tuple-element.62), channel_id=1, source_target_pairs={{0,8},{1,17},{2,10},{3,19},{4,12},{5,21},{6,14},{7,23},{8,0},{9,25... | collective-permute-start | bytes 294920 | tf_op jit(solution)/shard_map/ppermute | solution.py:399
  19.3 2.1 %collective-permute-start.4 = (bf16[2,96,256]{2,1,0:T(8,128)(2,1)S(1)}, bf16[2,96,256]{2,1,0:T(8,128)(2,1)S(1)}, u32[]{:S(2)}, u32[]{:S(2)}) collective-permute-start(bf16[2,96,256]{2,1,0:T(8,128)(2,1)S(1)} %collective-permute-done.2.refs_4_), channel_id=1, source_target_pairs={{0,1},{1,0},{2,3},{3,2},{4,5},{5,4},{6,7},{7,6},{8,9},{9,8},{10,11... | collective-permute-start | bytes 294920 | tf_op jit(solution)/shard_map/ppermute | solution.py:402
  20.5 1.3 %collective-permute-start.5 = (bf16[2,96,256]{2,1,0:T(8,128)(2,1)S(1)}, bf16[2,96,256]{2,1,0:T(8,128)(2,1)S(1)}, u32[]{:S(2)}, u32[]{:S(2)}) collective-permute-start(bf16[2,96,256]{2,1,0:T(8,128)(2,1)S(1)} %collective-permute-done.3.refs_5_), channel_id=1, source_target_pairs={{0,1},{1,0},{2,3},{3,2},{4,5},{5,4},{6,7},{7,6},{8,9},{9,8},{10,11... | collective-permute-start | bytes 294920 | tf_op jit(solution)/shard_map/ppermute | solution.py:402
  23.2 1.3 %collective-permute-start.6 = (bf16[32,1536]{1,0:T(8,128)(2,1)S(1)}, bf16[32,1536]{1,0:T(8,128)(2,1)S(1)}, u32[]{:S(2)}, u32[]{:S(2)}) collective-permute-start(bf16[32,1536]{1,0:T(8,128)(2,1)S(1)} %get-tuple-element.70), channel_id=1, source_target_pairs={{0,1},{1,0},{2,3},{3,2},{4,5},{5,4},{6,7},{7,6},{8,9},{9,8},{10,11... | collective-permute-start | bytes 294920 | tf_op jit(solution)/shard_map/ppermute | solution.py:402
  23.4 8.0 %collective-permute-start.7 = (bf16[32,1024]{1,0:T(8,128)(2,1)S(1)}, bf16[32,1024]{1,0:T(8,128)(2,1)S(1)}, u32[]{:S(2)}, u32[]{:S(2)}) collective-permute-start(bf16[32,1024]{1,0:T(8,128)(2,1)S(1)} %get-tuple-element.69.wmsg), channel_id=1, source_target_pairs={{1,2},{3,4},{5,6},{7,8},{9,10},{11,12},{13,14},{15,16},{17,18},{19... | collective-permute-start | bytes 196616 | tf_op jit(solution)/shard_map/ppermute | solution.py:455
  24.6 5.7 %collective-permute-start.8 = (bf16[2,32,256]{2,1,0:T(8,128)(2,1)S(1)}, bf16[2,32,256]{2,1,0:T(8,128)(2,1)S(1)}, u32[]{:S(2)}, u32[]{:S(2)}) collective-permute-start(bf16[2,32,256]{2,1,0:T(8,128)(2,1)S(1)} %get-tuple-element.80), channel_id=1, source_target_pairs={{0,2},{1,5},{2,0},{3,7},{4,6},{5,1},{6,4},{7,3},{8,10},{9,13},{10,... | collective-permute-start | bytes 98312 | tf_op jit(solution)/shard_map/ppermute | solution.py:399
  27.4 4.0 %collective-permute-start.9 = (bf16[2,32,256]{2,1,0:T(8,128)(2,1)S(1)}, bf16[2,32,256]{2,1,0:T(8,128)(2,1)S(1)}, u32[]{:S(2)}, u32[]{:S(2)}) collective-permute-start(bf16[2,32,256]{2,1,0:T(8,128)(2,1)S(1)} %get-tuple-element.81), channel_id=1, source_target_pairs={{0,8},{1,17},{2,10},{3,19},{4,12},{5,21},{6,14},{7,23},{8,0},{9,25... | collective-permute-start | bytes 98312 | tf_op jit(solution)/shard_map/ppermute | solution.py:399
  30.3 2.3 %collective-permute-start.10 = (bf16[2,32,256]{2,1,0:T(8,128)(2,1)S(1)}, bf16[2,32,256]{2,1,0:T(8,128)(2,1)S(1)}, u32[]{:S(2)}, u32[]{:S(2)}) collective-permute-start(bf16[2,32,256]{2,1,0:T(8,128)(2,1)S(1)} %collective-permute-done.8.refs_8_), channel_id=1, source_target_pairs={{0,1},{1,0},{2,3},{3,2},{4,5},{5,4},{6,7},{7,6},{8,9},{9,8},{10,11... | collective-permute-start | bytes 98312 | tf_op jit(solution)/shard_map/ppermute | solution.py:402
  31.4 1.2 %collective-permute-start.11 = (bf16[2,32,256]{2,1,0:T(8,128)(2,1)S(1)}, bf16[2,32,256]{2,1,0:T(8,128)(2,1)S(1)}, u32[]{:S(2)}, u32[]{:S(2)}) collective-permute-start(bf16[2,32,256]{2,1,0:T(8,128)(2,1)S(1)} %collective-permute-done.9.refs_9_), channel_id=1, source_target_pairs={{0,1},{1,0},{2,3},{3,2},{4,5},{5,4},{6,7},{7,6},{8,9},{9,8},{10,11... | collective-permute-start | bytes 98312 | tf_op jit(solution)/shard_map/ppermute | solution.py:402
  34.0 11.4 %all-to-all-start = ((f32[32,1,128]{2,1,0:T(1,128)}), f32[32,1,128]{2,1,0:T(1,128)S(1)}, u32[]{:S(2)}, u32[]{:S(2)}) async-start(f32[32,1,128]{2,1,0:T(1,128)} %bitcast.1), calls=%async_computation | async-start | bytes 32768 | tf_op jit(solution)/shard_map/all_to_all | solution.py:466

commit v11 on v10

--- a/solution.py
+++ b/solution.py
@@ -36,11 +36,16 @@
     return first, second, third
 
 
-def matern(squared, rates):
+def matern(squared, rates, packed=False):
     rate, falling_rate = rates
     squared = jnp.maximum(squared, TINY)
     radius = squared * lax.rsqrt(squared)
     decay = jnp.exp2(radius * falling_rate)
+    if packed:
+        scaled = (radius * rate).astype(HALF)
+        decay = decay.astype(HALF)
+        falling = scaled * decay
+        return decay + falling, scaled * falling
     falling = radius * decay
     return decay + rate * falling, radius * falling
 
@@ -172,7 +177,7 @@
     turned_src[...] = turned(msg[32:64, 0:rows])
     for col in range(0, rows, TILE):
         squared = dot(turned_src[...], target[:, col : col + TILE])
-        value, slope = matern(squared, rates)
+        value, slope = matern(squared, rates, True)
         value = value.astype(HALF)
         kept[:, col : col + TILE] = value
         pair = jnp.concatenate([value, slope.astype(HALF)], axis=1)
@@ -343,7 +348,7 @@
     direction = lean * lean * norm - 2.0 * lean * alpha * cross + alpha * alpha * square
     bend = lean * lean * cross - lean * alpha * (mixed + square) + alpha * alpha * second
     beta = norm_next / (level * direction + bend)
-    factor = signal[0] * (rate * rate)
+    factor = signal[0]
     trace[...] = (((alpha + beta * lean) * held - beta * alpha * gain * along) * factor / point_total)[:, 0:16]
 
     lane = lax.broadcasted_iota(jnp.int32, (16, 128), 1)
@@ -366,8 +371,7 @@
 
 
 def slope_kernel(signal, numbers, source, dest):
-    rate = numbers[0:1, 0:1]
-    dest[...] = (signal[0] * rate * rate) * source[...]
+    dest[...] = signal[0] * source[...]
 
 
 def call(kernel, outs, spaces, scratch=(), micros=2.0):

time: 46.5 us -> 46 us (0.989)
  Pallas kernels: 15.2 us -> 14.5 us
  transfers between devices with their start and end apart: 13 -> 13, of which waited for: 5 -> 5; matrix products, arithmetic and copies ran while one was open for 0% -> 0% of each run, Pallas kernels for 19% -> 18%
where the time goes in v11:
time: 46 us; the launch traced here: 45.7 us
  starting transfers between devices  18.4 us (40%)
  Pallas kernels  14.5 us (32%)
  waiting for transfers between devices  8.53 us (19%)
  between operations  3.33 us (7%)
  other arithmetic  0.88 us (2%)
    ppermute x4, starting transfers between devices, partner(): return lax.ppermute(value, 'loc', pairs)  10.3 us
    all_to_all x1, waiting for transfers between devices, shards(): table = lax.all_to_all(sums, 'loc', 0, 0, tiled=True)  6.44 us
    all_to_all x1, starting transfers between devices, shards(): table = lax.all_to_all(sums, 'loc', 0, 0, tiled=True)  4.41 us
    pallas_call x2, Pallas kernels, shards(): call(side_kernel, near_outs, [VMEM] * 5, turned_buf)  3.71 us
    pallas_call x1, Pallas kernels, shards(): call(functools.partial(front_kernel, levels), [((MSG_ROWS, rows), HALF),...  2.63 us
    ppermute x6, starting transfers between devices, sibling(): return lax.ppermute(value, 'loc', beside)  2.4 us
    pallas_call x1, Pallas kernels, shards(): call(own_kernel, near_outs, [VMEM] * 3, turned_buf)(numbers, msg, target)  1.8 us
    pallas_call x1, Pallas kernels, shards(): call(functools.partial(far_kernel, half, far_scale), couplings + [((1, ro...  1.45 us
  transfers between devices with their start and end apart: 13, of which 5 were waited for; matrix products, arithmetic and copies ran while one was open for 0% of the time, Pallas kernels for 18%

profile of v11, /device:TPU:0, one launch (start us, length us, event | category | flops | bytes accessed | tf_op | source)
XLA Modules:
  0.0 45.7 jit_solution(16063005142724016358)
XLA Ops:
  1.9 0.9 %convert_add_fusion.refs_2_.refs_6_.given = f32[32,1024]{1,0:T(8,128)S(1)} fusion(s32[4,256]{1,0:T(4,128)} %param.9, f32[3,1024]{1,0:T(4,128)} %param.7, f32[16,1024]{1,0:T(8,128)} %param.8), kind=kLoop, calls=%fused_computation | loop fusion | flops 98304 | bytes 212992 | tf_op jit(solution)/shard_map/add | solution.py:411
  2.8 2.6 %shard_map.102 = (bf16[64,1024]{1,0:T(8,128)(2,1)S(1)}, bf16[32,1024]{1,0:T(8,128)(2,1)S(1)}, bf16[1024,1024]{1,0:T(8,128)(2,1)S(1)}, bf16[4,32,256]{2,1,0:T(8,1...) custom-call(f32[1]{0:T(128)S(6)} %copy.12.refs_0_, ...), custom_call_target="tpu_custom_call" | custom-call | flops 2000000000 | bytes 65536 | tf_op jit(solution)/shard_map/pallas_call | solution.py:412
  5.4 0.5 %collective-permute-start.1 = (bf16[64,2048]{1,0:T(8,128)(2,1)S(1)}, bf16[64,2048]{1,0:T(8,128)(2,1)S(1)}, u32[]{:S(2)}, u32[]{:S(2)}) collective-permute-start(bf16[64,2048]{1,0:T(8,128)(2,1)S(1)} %get-tuple-element.51), channel_id=1, source_target_pairs={{0,1},{1,0},{2,3},{3,2},{4,5},{5,4},{6,7},{7,6},{8,9},{9,8},{10,11... | collective-permute-start | bytes 786440 | tf_op jit(solution)/shard_map/ppermute | solution.py:406
  6.0 0.7 %collective-permute-start = (bf16[64,1024]{1,0:T(8,128)(2,1)S(1)}, bf16[64,1024]{1,0:T(8,128)(2,1)S(1)}, u32[]{:S(2)}, u32[]{:S(2)}) collective-permute-start(bf16[64,1024]{1,0:T(8,128)(2,1)S(1)} %get-tuple-element.55.msg), channel_id=1, source_target_pairs={{1,2},{3,4},{5,6},{7,8},{9,10},{11,12},{13,14},{15,16},{17,18},{19... | collective-permute-start | bytes 393224 | tf_op jit(solution)/shard_map/ppermute | solution.py:431
  6.6 0.5 %collective-permute-done.1.got.msg = bf16[64,2048]{1,0:T(8,128)(2,1)S(1)} collective-permute-done((bf16[64,2048]{1,0:T(8,128)(2,1)S(1)}, bf16[64,2048]{1,0:T(8,128)(2,1)S(1)}, u32[]{:S(2)}, u32[]{:S(2)}) %collective-permute-start.1) | collective-permute-done | bytes 262176 | tf_op jit(solution)/shard_map/ppermute | solution.py:406
  7.2 3.3 %collective-permute-start.2 = (bf16[2,96,256]{2,1,0:T(8,128)(2,1)S(1)}, bf16[2,96,256]{2,1,0:T(8,128)(2,1)S(1)}, u32[]{:S(2)}, u32[]{:S(2)}) collective-permute-start(bf16[2,96,256]{2,1,0:T(8,128)(2,1)S(1)} %get-tuple-element.61), channel_id=1, source_target_pairs={{0,2},{1,5},{2,0},{3,7},{4,6},{5,1},{6,4},{7,3},{8,10},{9,13},{10,... | collective-permute-start | bytes 294920 | tf_op jit(solution)/shard_map/ppermute | solution.py:403
  10.5 2.6 %collective-permute-start.3 = (bf16[2,96,256]{2,1,0:T(8,128)(2,1)S(1)}, bf16[2,96,256]{2,1,0:T(8,128)(2,1)S(1)}, u32[]{:S(2)}, u32[]{:S(2)}) collective-permute-start(bf16[2,96,256]{2,1,0:T(8,128)(2,1)S(1)} %get-tuple-element.62), channel_id=1, source_target_pairs={{0,8},{1,17},{2,10},{3,19},{4,12},{5,21},{6,14},{7,23},{8,0},{9,25... | collective-permute-start | bytes 294920 | tf_op jit(solution)/shard_map/ppermute | solution.py:403
  13.1 1.8 %shard_map.104 = (bf16[1024,1024]{1,0:T(8,128)(2,1)S(1)}, f32[32,1024]{1,0:T(8,128)S(1)}, f32[16,1024]{1,0:T(8,128)S(1)}) custom-call(f32[8,128]{1,0:T(8,128)S(1)} %get-tuple-element.48.numbers.refs_0_, bf16[64,1024]{1,0:T(8,128)(2,1)S(1)} %get-tuple-element.55.msg, bf16[32,1024]{1,0:T(8,128)(2,1)S(1)} %get-tuple-element.50.target), custom_call_target="tpu_custom_call" | custom-call | flops 2000000000 | bytes 65536 | tf_op jit(solution)/shard_map/pallas_call | solution.py:436
  14.9 1.9 %shard_map.105 = (bf16[1024,1024]{1,0:T(8,128)(2,1)S(1)}, f32[32,1024]{1,0:T(8,128)S(1)}, f32[16,1024]{1,0:T(8,128)S(1)}) custom-call(f32[8,128]{1,0:T(8,128)S(1)} %get-tuple-element.48.numbers.refs_0_, bf16[64,2048]{1,0:T(8,128)(2,1)S(1)} %collective-permute-done.1.got.msg, bf16[32,1024]{1,0:T(8,128)(2,1)S(1)} %get-tuple-element.50.target, ...), custom_call_target="tpu_custom_call" | custom-call | flops 2000000000 | bytes 65536 | tf_op jit(solution)/shard_map/pallas_call | solution.py:438
  16.8 1.8 %shard_map.106 = (bf16[1024,1024]{1,0:T(8,128)(2,1)S(1)}, f32[32,1024]{1,0:T(8,128)S(1)}, f32[16,1024]{1,0:T(8,128)S(1)}) custom-call(f32[8,128]{1,0:T(8,128)S(1)} %get-tuple-element.48.numbers.refs_0_, bf16[64,1024]{1,0:T(8,128)(2,1)S(1)} %collective-permute-done.msg, bf16[32,1024]{1,0:T(8,128)(2,1)S(1)} %get-tuple-element.50.target, ...), custom_call_target="tpu_custom_call" | custom-call | flops 2000000000 | bytes 65536 | tf_op jit(solution)/shard_map/pallas_call | solution.py:439
  18.7 1.1 %collective-permute-start.4 = (bf16[2,96,256]{2,1,0:T(8,128)(2,1)S(1)}, bf16[2,96,256]{2,1,0:T(8,128)(2,1)S(1)}, u32[]{:S(2)}, u32[]{:S(2)}) collective-permute-start(bf16[2,96,256]{2,1,0:T(8,128)(2,1)S(1)} %collective-permute-done.2.refs_4_), channel_id=1, source_target_pairs={{0,1},{1,0},{2,3},{3,2},{4,5},{5,4},{6,7},{7,6},{8,9},{9,8},{10,11... | collective-permute-start | bytes 294920 | tf_op jit(solution)/shard_map/ppermute | solution.py:406
  19.9 0.9 %shard_map.107 = (f32[32,1024]{1,0:T(8,128)S(1)}, bf16[2,256,256]{2,1,0:T(8,128)(2,1)S(1)}) custom-call(f32[8,128]{1,0:T(8,128)S(1)} %get-tuple-element.48.numbers.refs_0_, f32[32,1024]{1,0:T(8,128)S(1)} %get-tuple-element.63.refs_1_, bf16[1024,1024]{1,0:T(8,128)(2,1)S(1)} %get-tuple-element.64.refs_2_.refs_3_.refs_1_, ...), custom_call_target="tpu_custom_call" | custom-call | flops 1000000000 | bytes 65536 | tf_op jit(solution)/shard_map/pallas_call | solution.py:443
  21.1 1.4 %shard_map.108 = (bf16[2,256,256]{2,1,0:T(8,128)(2,1)S(1)}, f32[1,1024]{1,0:T(1,128)S(1)}, f32[16,1024]{1,0:T(8,128)S(1)}, bf16[32,1024]{1,0:T(8,128)(2,1)S(1)},...) custom-call(f32[8,128]{1,0:T(8,128)S(1)} %get-tuple-element.48.numbers.refs_0_, ...), custom_call_target="tpu_custom_call" | custom-call | flops 2000000000 | bytes 65536 | tf_op jit(solution)/shard_map/pallas_call | solution.py:446
  22.8 0.7 %collective-permute-start.7 = (bf16[32,1024]{1,0:T(8,128)(2,1)S(1)}, bf16[32,1024]{1,0:T(8,128)(2,1)S(1)}, u32[]{:S(2)}, u32[]{:S(2)}) collective-permute-start(bf16[32,1024]{1,0:T(8,128)(2,1)S(1)} %get-tuple-element.69.wmsg), channel_id=1, source_target_pairs={{1,2},{3,4},{5,6},{7,8},{9,10},{11,12},{13,14},{15,16},{17,18},{19... | collective-permute-start | bytes 196616 | tf_op jit(solution)/shard_map/ppermute | solution.py:459
  23.4 0.5 %collective-permute-done.6.wmsg_a.got = bf16[32,1536]{1,0:T(8,128)(2,1)S(1)} collective-permute-done((bf16[32,1536]{1,0:T(8,128)(2,1)S(1)}, bf16[32,1536]{1,0:T(8,128)(2,1)S(1)}, u32[]{:S(2)}, u32[]{:S(2)}) %collective-permute-start.6) | collective-permute-done | bytes 98336 | tf_op jit(solution)/shard_map/ppermute | solution.py:406
  23.9 2.8 %collective-permute-start.8 = (bf16[2,32,256]{2,1,0:T(8,128)(2,1)S(1)}, bf16[2,32,256]{2,1,0:T(8,128)(2,1)S(1)}, u32[]{:S(2)}, u32[]{:S(2)}) collective-permute-start(bf16[2,32,256]{2,1,0:T(8,128)(2,1)S(1)} %get-tuple-element.80), channel_id=1, source_target_pairs={{0,2},{1,5},{2,0},{3,7},{4,6},{5,1},{6,4},{7,3},{8,10},{9,13},{10,... | collective-permute-start | bytes 98312 | tf_op jit(solution)/shard_map/ppermute | solution.py:403
  26.8 1.6 %collective-permute-start.9 = (bf16[2,32,256]{2,1,0:T(8,128)(2,1)S(1)}, bf16[2,32,256]{2,1,0:T(8,128)(2,1)S(1)}, u32[]{:S(2)}, u32[]{:S(2)}) collective-permute-start(bf16[2,32,256]{2,1,0:T(8,128)(2,1)S(1)} %get-tuple-element.81), channel_id=1, source_target_pairs={{0,8},{1,17},{2,10},{3,19},{4,12},{5,21},{6,14},{7,23},{8,0},{9,25... | collective-permute-start | bytes 98312 | tf_op jit(solution)/shard_map/ppermute | solution.py:403
  30.1 0.7 %collective-permute-done.9.refs_9_ = bf16[2,32,256]{2,1,0:T(8,128)(2,1)S(1)} collective-permute-done((bf16[2,32,256]{2,1,0:T(8,128)(2,1)S(1)}, bf16[2,32,256]{2,1,0:T(8,128)(2,1)S(1)}, u32[]{:S(2)}, u32[]{:S(2)}) %collective-permute-start.9) | collective-permute-done | bytes 32800 | tf_op jit(solution)/shard_map/ppermute | solution.py:403
  30.8 1.2 %shard_map.109.refs_0_ = f32[32,1024]{1,0:T(8,128)S(1)} custom-call(bf16[32,1024]{1,0:T(8,128)(2,1)S(1)} %get-tuple-element.69.wmsg, bf16[32,1536]{1,0:T(8,128)(2,1)S(1)} %collective-permute-done.6.wmsg_a.got, bf16[32,1024]{1,0:T(8,128)(2,1)S(1)} %collective-permute-done.7.wmsg_b, bf16[1024,1024]{1,0:T(8,128)(2,1)S(1)} %get-tuple-element.71.kept, ...), custom_call_target="tpu_custom_call" | custom-call | flops 1200000000 | bytes 65536 | tf_op jit(solution)/shard_map/pallas_call | solution.py:462
  32.0 1.3 %shard_map.111 = (f32[32,128]{1,0:T(8,128)}, f32[16,1024]{1,0:T(8,128)S(1)}, f32[16,1024]{1,0:T(8,128)S(1)}, f32[16,128]{1,0:T(8,128)S(1)}) custom-call(f32[32,1024]{1,0:T(8,128)S(1)} %shard_map.109.refs_0_, bf16[1024,1024]{1,0:T(8,128)(2,1)S(1)} %get-tuple-element.64.refs_2_.refs_3_.refs_1_, bf16[2,256,256]{2,1,0:T(8,128)(2,1)S(1)} %get-tuple-element.74.refs_2_, ...), custom_call_target="tpu_custom_call" | custom-call | flops 2000000000 | bytes 65536 | tf_op jit(solution)/shard_map/pallas_call | solution.py:464
  33.3 4.4 %all-to-all-start = ((f32[32,1,128]{2,1,0:T(1,128)}), f32[32,1,128]{2,1,0:T(1,128)S(1)}, u32[]{:S(2)}, u32[]{:S(2)}) async-start(f32[32,1,128]{2,1,0:T(1,128)} %bitcast.1), calls=%async_computation | async-start | bytes 32768 | tf_op jit(solution)/shard_map/all_to_all | solution.py:470
  37.7 0.6 %shard_map.113 = f32[16,1024]{1,0:T(8,128)} custom-call(f32[1]{0:T(128)S(6)} %copy.14.signal, f32[8,128]{1,0:T(8,128)S(1)} %get-tuple-element.48.numbers.refs_0_, f32[16,1024]{1,0:T(8,128)S(1)} %get-tuple-element.78.refs_7_.source), custom_call_target="tpu_custom_call" | custom-call | flops 2000000000 | bytes 65536 | tf_op jit(solution)/shard_map/pallas_call | solution.py:471
  38.4 6.4 %all-to-all-done = f32[32,1,128]{2,1,0:T(1,128)S(1)} async-done(((f32[32,1,128]{2,1,0:T(1,128)}), f32[32,1,128]{2,1,0:T(1,128)S(1)}, u32[]{:S(2)}, u32[]{:S(2)}) %all-to-all-start) | async-done | bytes 16416 | tf_op jit(solution)/shard_map/all_to_all | solution.py:470
  44.8 0.9 %shard_map.112 = (f32[16,1024]{1,0:T(8,128)}, f32[16,1024]{1,0:T(8,128)}, f32[1,16]{1,0:T(1,128)}) custom-call(f32[1]{0:T(128)S(6)} %copy.14.signal, f32[1]{0:T(128)S(6)} %copy.15.noise, f32[8,128]{1,0:T(8,128)S(1)} %get-tuple-element.48.numbers.refs_0_, f32[32,128]{1,0:T(8,128)S(1)} %bitcast.5, f32[16,128]{1,0:T(8,128)S(1)} %get-tuple-element.86.shift_in, ...), custom_call_target="tpu_custom_call" | custom-call | flops 2000000000 | bytes 65536 | tf_op jit(solution)/shard_map/pallas_call | solution.py:472
  (15 shorter events, 1.2 us)
Async XLA Ops:
  5.4 1.7 %collective-permute-start.1 = (bf16[64,2048]{1,0:T(8,128)(2,1)S(1)}, bf16[64,2048]{1,0:T(8,128)(2,1)S(1)}, u32[]{:S(2)}, u32[]{:S(2)}) collective-permute-start(bf16[64,2048]{1,0:T(8,128)(2,1)S(1)} %get-tuple-element.51), channel_id=1, source_target_pairs={{0,1},{1,0},{2,3},{3,2},{4,5},{5,4},{6,7},{7,6},{8,9},{9,8},{10,11... | collective-permute-start | bytes 786440 | tf_op jit(solution)/shard_map/ppermute | solution.py:406
  6.0 10.8 %collective-permute-start = (bf16[64,1024]{1,0:T(8,128)(2,1)S(1)}, bf16[64,1024]{1,0:T(8,128)(2,1)S(1)}, u32[]{:S(2)}, u32[]{:S(2)}) collective-permute-start(bf16[64,1024]{1,0:T(8,128)(2,1)S(1)} %get-tuple-element.55.msg), channel_id=1, source_target_pairs={{1,2},{3,4},{5,6},{7,8},{9,10},{11,12},{13,14},{15,16},{17,18},{19... | collective-permute-start | bytes 393224 | tf_op jit(solution)/shard_map/ppermute | solution.py:431
  7.2 11.5 %collective-permute-start.2 = (bf16[2,96,256]{2,1,0:T(8,128)(2,1)S(1)}, bf16[2,96,256]{2,1,0:T(8,128)(2,1)S(1)}, u32[]{:S(2)}, u32[]{:S(2)}) collective-permute-start(bf16[2,96,256]{2,1,0:T(8,128)(2,1)S(1)} %get-tuple-element.61), channel_id=1, source_target_pairs={{0,2},{1,5},{2,0},{3,7},{4,6},{5,1},{6,4},{7,3},{8,10},{9,13},{10,... | collective-permute-start | bytes 294920 | tf_op jit(solution)/shard_map/ppermute | solution.py:403
  10.5 8.2 %collective-permute-start.3 = (bf16[2,96,256]{2,1,0:T(8,128)(2,1)S(1)}, bf16[2,96,256]{2,1,0:T(8,128)(2,1)S(1)}, u32[]{:S(2)}, u32[]{:S(2)}) collective-permute-start(bf16[2,96,256]{2,1,0:T(8,128)(2,1)S(1)} %get-tuple-element.62), channel_id=1, source_target_pairs={{0,8},{1,17},{2,10},{3,19},{4,12},{5,21},{6,14},{7,23},{8,0},{9,25... | collective-permute-start | bytes 294920 | tf_op jit(solution)/shard_map/ppermute | solution.py:403
  18.7 2.1 %collective-permute-start.4 = (bf16[2,96,256]{2,1,0:T(8,128)(2,1)S(1)}, bf16[2,96,256]{2,1,0:T(8,128)(2,1)S(1)}, u32[]{:S(2)}, u32[]{:S(2)}) collective-permute-start(bf16[2,96,256]{2,1,0:T(8,128)(2,1)S(1)} %collective-permute-done.2.refs_4_), channel_id=1, source_target_pairs={{0,1},{1,0},{2,3},{3,2},{4,5},{5,4},{6,7},{7,6},{8,9},{9,8},{10,11... | collective-permute-start | bytes 294920 | tf_op jit(solution)/shard_map/ppermute | solution.py:406
  19.8 1.3 %collective-permute-start.5 = (bf16[2,96,256]{2,1,0:T(8,128)(2,1)S(1)}, bf16[2,96,256]{2,1,0:T(8,128)(2,1)S(1)}, u32[]{:S(2)}, u32[]{:S(2)}) collective-permute-start(bf16[2,96,256]{2,1,0:T(8,128)(2,1)S(1)} %collective-permute-done.3.refs_5_), channel_id=1, source_target_pairs={{0,1},{1,0},{2,3},{3,2},{4,5},{5,4},{6,7},{7,6},{8,9},{9,8},{10,11... | collective-permute-start | bytes 294920 | tf_op jit(solution)/shard_map/ppermute | solution.py:406
  22.6 1.3 %collective-permute-start.6 = (bf16[32,1536]{1,0:T(8,128)(2,1)S(1)}, bf16[32,1536]{1,0:T(8,128)(2,1)S(1)}, u32[]{:S(2)}, u32[]{:S(2)}) collective-permute-start(bf16[32,1536]{1,0:T(8,128)(2,1)S(1)} %get-tuple-element.70), channel_id=1, source_target_pairs={{0,1},{1,0},{2,3},{3,2},{4,5},{5,4},{6,7},{7,6},{8,9},{9,8},{10,11... | collective-permute-start | bytes 294920 | tf_op jit(solution)/shard_map/ppermute | solution.py:406
  22.8 8.0 %collective-permute-start.7 = (bf16[32,1024]{1,0:T(8,128)(2,1)S(1)}, bf16[32,1024]{1,0:T(8,128)(2,1)S(1)}, u32[]{:S(2)}, u32[]{:S(2)}) collective-permute-start(bf16[32,1024]{1,0:T(8,128)(2,1)S(1)} %get-tuple-element.69.wmsg), channel_id=1, source_target_pairs={{1,2},{3,4},{5,6},{7,8},{9,10},{11,12},{13,14},{15,16},{17,18},{19... | collective-permute-start | bytes 196616 | tf_op jit(solution)/shard_map/ppermute | solution.py:459
  23.9 5.7 %collective-permute-start.8 = (bf16[2,32,256]{2,1,0:T(8,128)(2,1)S(1)}, bf16[2,32,256]{2,1,0:T(8,128)(2,1)S(1)}, u32[]{:S(2)}, u32[]{:S(2)}) collective-permute-start(bf16[2,32,256]{2,1,0:T(8,128)(2,1)S(1)} %get-tuple-element.80), channel_id=1, source_target_pairs={{0,2},{1,5},{2,0},{3,7},{4,6},{5,1},{6,4},{7,3},{8,10},{9,13},{10,... | collective-permute-start | bytes 98312 | tf_op jit(solution)/shard_map/ppermute | solution.py:403
  26.8 4.0 %collective-permute-start.9 = (bf16[2,32,256]{2,1,0:T(8,128)(2,1)S(1)}, bf16[2,32,256]{2,1,0:T(8,128)(2,1)S(1)}, u32[]{:S(2)}, u32[]{:S(2)}) collective-permute-start(bf16[2,32,256]{2,1,0:T(8,128)(2,1)S(1)} %get-tuple-element.81), channel_id=1, source_target_pairs={{0,8},{1,17},{2,10},{3,19},{4,12},{5,21},{6,14},{7,23},{8,0},{9,25... | collective-permute-start | bytes 98312 | tf_op jit(solution)/shard_map/ppermute | solution.py:403
  29.6 2.3 %collective-permute-start.10 = (bf16[2,32,256]{2,1,0:T(8,128)(2,1)S(1)}, bf16[2,32,256]{2,1,0:T(8,128)(2,1)S(1)}, u32[]{:S(2)}, u32[]{:S(2)}) collective-permute-start(bf16[2,32,256]{2,1,0:T(8,128)(2,1)S(1)} %collective-permute-done.8.refs_8_), channel_id=1, source_target_pairs={{0,1},{1,0},{2,3},{3,2},{4,5},{5,4},{6,7},{7,6},{8,9},{9,8},{10,11... | collective-permute-start | bytes 98312 | tf_op jit(solution)/shard_map/ppermute | solution.py:406
  30.8 1.2 %collective-permute-start.11 = (bf16[2,32,256]{2,1,0:T(8,128)(2,1)S(1)}, bf16[2,32,256]{2,1,0:T(8,128)(2,1)S(1)}, u32[]{:S(2)}, u32[]{:S(2)}) collective-permute-start(bf16[2,32,256]{2,1,0:T(8,128)(2,1)S(1)} %collective-permute-done.9.refs_9_), channel_id=1, source_target_pairs={{0,1},{1,0},{2,3},{3,2},{4,5},{5,4},{6,7},{7,6},{8,9},{9,8},{10,11... | collective-permute-start | bytes 98312 | tf_op jit(solution)/shard_map/ppermute | solution.py:406
  33.3 11.5 %all-to-all-start = ((f32[32,1,128]{2,1,0:T(1,128)}), f32[32,1,128]{2,1,0:T(1,128)S(1)}, u32[]{:S(2)}, u32[]{:S(2)}) async-start(f32[32,1,128]{2,1,0:T(1,128)} %bitcast.1), calls=%async_computation | async-start | bytes 32768 | tf_op jit(solution)/shard_map/all_to_all | solution.py:470
